TPU v7x, 32 devices: a whole 2x2x4 slice. The times are simulated.
32 devices in a mesh: seq: 8 (over y, x, core), head: 4 (over z).
Axes of the slice: x: 2, y: 2, z: 4, core: 2. Of those that a mesh axis runs over, the one named last changes fastest.
Arguments:
- inputs: bfloat16 [4096, 1536], P(('seq', 'head')), may hold values from -6 to 6
- norm_gain_attn: bfloat16 [1536], P(('seq', 'head')), may hold values from 0.099609375 to 1.8984375
- qkv_weight: bfloat16 [1536, 2048], P(('seq', 'head')), may hold values from -0.15625 to 0.15625
- qkv_bias: bfloat16 [2048], P(('seq', 'head')), may hold values from -3 to 3
- out_weight: bfloat16 [1536, 1536], P('head', 'seq'), may hold values from -1.75 to 1.75
- norm_gain_mlp: bfloat16 [1536], P(('seq', 'head')), may hold values from 0.099609375 to 1.8984375
- gate_weight: bfloat16 [1536, 8960], P('seq', 'head'), may hold values from -0.15625 to 0.15625
- up_weight: bfloat16 [1536, 8960], P('seq', 'head'), may hold values from -0.15625 to 0.15625
- down_weight: bfloat16 [8960, 1536], P('head', 'seq'), may hold values from -0.0625 to 0.0625
- cotangent: bfloat16 [4096, 1536], P(('seq', 'head')), may hold values from -6 to 6
- segment_ids: int32 [4096], P(('seq', 'head')), may hold values from 0 to 2, as said below
- positions: int32 [4096], P(('seq', 'head')), may hold values from 0 to 3071, as said below
Outputs:
- output: bfloat16 [4096, 1536], P(('seq', 'head'))
- grad_inputs: bfloat16 [4096, 1536], P(('seq', 'head'))
- grad_gain_attn: float32 [1536], P(('seq', 'head'))
- grad_qkv: float32 [1536, 2048], P(('seq', 'head'))
- grad_bias: float32 [1792], P(('seq', 'head'))
- grad_value_bias: float32 [256], P(('seq', 'head'))
- grad_out: float32 [1536, 1536], P('head', 'seq')
- grad_gain_mlp: float32 [1536], P(('seq', 'head'))
- grad_gate: float32 [1536, 8960], P('seq', 'head')
- grad_up: float32 [1536, 8960], P('seq', 'head')
- grad_down: float32 [8960, 1536], P('head', 'seq')
Inputs may be any that keep to these rules, and one draw needn't show every extreme that they name: `segment_ids`: the 2048 prompt tokens have segment 0; continuation c, for c from 1 to 2, has 1024 tokens of segment c. On each device the first half of its 128 rows are prompt tokens and the second half continuation tokens; every token of the group stands once. A prompt token's position is its place in the prompt; a continuation token's is 2048 plus its place in its continuation; with segment_ids, positions name each token once.
All inputs are finite; a program needn't handle non-finite values.
Results may differ from a plain program's by a relative error of at most 0.028.
Values may be sent and summed in bfloat16 or wider, within the bound.
No kernel may reach another device: no remote copies, remote signals or barrier semaphores. Data moves between devices by JAX's collectives and lax.ppermute only.
A program may use at most 768 MiB of HBM per device.

v0:
```python
import math

import jax
import jax.numpy as jnp
from jax import lax
from jax.sharding import PartitionSpec as P

HEADS = 12
KV_HEADS = 2
HD = 128
QD = 1536
KD = 256
QKV = 2048


EPS = 1e-06
ROPE_BASE = 1000000.0
MASKED = -1e30


def swapped(block, axis, apart):
    count = lax.axis_size(axis)
    route = []
    for low in range(count):
        high = low | 1 << apart
        if high != low and high < count:
            route += [(low, high), (high, low)]
    return lax.ppermute(block, axis, route)


def rope_tables(positions):
    freq_index = jnp.arange(HD // 2, dtype=jnp.float32) * 2.0 / HD
    inverse = 1.0 / ROPE_BASE**freq_index
    angles = positions.astype(jnp.float32)[:, None] * inverse[None, :]
    return (jnp.cos(angles)[:, None, :], jnp.sin(angles)[:, None, :])


def rotate(values, cosine_part, sine_part):
    front_half = values[..., : HD // 2]
    back_half = values[..., HD // 2 :]
    return jnp.concatenate(
        [
            front_half * cosine_part - back_half * sine_part,
            back_half * cosine_part + front_half * sine_part,
        ],
        axis=-1,
    )


def rotate_back(grad_in, cosine_part, sine_part):
    front_half = grad_in[..., : HD // 2]
    back_half = grad_in[..., HD // 2 :]
    return jnp.concatenate(
        [
            front_half * cosine_part + back_half * sine_part,
            back_half * cosine_part - front_half * sine_part,
        ],
        axis=-1,
    )


def norm_forward(values, gain_vec):
    inv_norm = lax.rsqrt(jnp.mean(values * values, axis=-1, keepdims=True) + EPS)
    return (values * inv_norm * gain_vec, inv_norm)


def norm_backward(values, inv_norm, gain_vec, grad_in):
    scaled = grad_in * gain_vec
    gain_grad = jnp.sum(grad_in * values * inv_norm, axis=0)
    inner_mean = jnp.mean(scaled * values, axis=-1, keepdims=True)
    return (inv_norm * scaled - values * inv_norm**3 * inner_mean, gain_grad)


def over_keys(key_group, value_group, update, init_state):
    return update(
        init_state,
        (
            lax.all_gather(key_group, "seq", axis=0, tiled=True),
            lax.all_gather(value_group, "seq", axis=0, tiled=True),
        ),
        jnp.int32(0),
    )


def collect_qkv(qkv_weight):
    return lax.all_gather(qkv_weight, ("seq", "head"), axis=0, tiled=True)


def collect_layer(out_weight, pair_local, down_weight):
    return (
        lax.all_gather(out_weight, "seq", axis=1, tiled=True),
        lax.all_gather(pair_local, "seq", axis=0, tiled=True),
        lax.all_gather(down_weight, "seq", axis=1, tiled=True),
    )


def collect_heads(pair_part, down_part):
    return (
        lax.all_gather(pair_part, "head", axis=1, tiled=True),
        lax.all_gather(down_part, "head", axis=0, tiled=True),
    )


def to_group(values):
    return lax.all_gather(values, "head", axis=0, tiled=True)


def to_own(values):
    return lax.psum_scatter(
        values.astype(jnp.bfloat16), "head", scatter_dimension=0, tiled=True
    ).astype(jnp.float32)


def key_visible(query_seg, query_pos, key_seg, key_pos):
    shared_seg = (key_seg[None, :] == query_seg[:, None]) | (key_seg[None, :] == 0)
    return shared_seg & (key_pos[None, :] <= query_pos[:, None])


def times_transpose(grad_in, whole_weight):
    return lax.dot_general(
        grad_in, whole_weight, (((1,), (1,)), ((), ())), preferred_element_type=jnp.float32
    )


def rows_product(left_side, right_side):
    return lax.dot_general(
        left_side, right_side, (((0,), (0,)), ((), ())), preferred_element_type=jnp.float32
    )


def per_device(
    inputs,
    norm_gain_attn,
    qkv_weight,
    qkv_bias,
    out_weight,
    norm_gain_mlp,
    gate_weight,
    up_weight,
    down_weight,
    cotangent,
    segment_ids,
    positions,
):
    tok_rows = inputs.shape[0]
    heads_dev = lax.axis_size("head")
    heads_here = HEADS // heads_dev
    copies = heads_dev // KV_HEADS
    group_rows = heads_dev * tok_rows
    score_scale = HD ** (-0.5)
    query_cols = heads_here * HD
    quarter_ff = gate_weight.shape[1]
    head_index = lax.axis_index("head")
    kv_slot = head_index // copies
    pair_share = 1.0 / copies
    query_start = head_index * query_cols
    key_start = QD + kv_slot * HD
    value_start = QD + KD + kv_slot * HD

    def pick_columns(values):
        last = values.ndim - 1
        return jnp.concatenate(
            [
                lax.dynamic_slice_in_dim(values, query_start, query_cols, last),
                lax.dynamic_slice_in_dim(values, key_start, HD, last),
                lax.dynamic_slice_in_dim(values, value_start, HD, last),
            ],
            axis=last,
        )

    def place_columns(values):
        last = values.ndim - 1
        padded = jnp.zeros(values.shape[:-1] + (QKV,), values.dtype)
        padded = lax.dynamic_update_slice_in_dim(
            padded, values[..., :query_cols], query_start, last
        )
        padded = lax.dynamic_update_slice_in_dim(
            padded, values[..., query_cols : query_cols + HD], key_start, last
        )
        return lax.dynamic_update_slice_in_dim(
            padded, values[..., query_cols + HD :], value_start, last
        )

    seg_all, pos_all = (
        lax.all_gather(segment_ids, ("seq", "head"), axis=0, tiled=True),
        lax.all_gather(positions, ("seq", "head"), axis=0, tiled=True),
    )
    gain_attn, bias_all, gain_mlp = (
        lax.all_gather(norm_gain_attn, ("seq", "head"), axis=0, tiled=True),
        lax.all_gather(qkv_bias, ("seq", "head"), axis=0, tiled=True),
        lax.all_gather(norm_gain_mlp, ("seq", "head"), axis=0, tiled=True),
    )
    gain_attn = gain_attn.astype(jnp.float32)
    bias_cols = pick_columns(bias_all.astype(jnp.float32))
    gain_mlp = gain_mlp.astype(jnp.float32)
    pair_local = jnp.concatenate([gate_weight, up_weight], axis=1)
    cols_weight = pick_columns(collect_qkv(qkv_weight))
    out_part, pair_part, down_part = collect_layer(out_weight, pair_local, down_weight)
    inputs_f = inputs.astype(jnp.float32)
    normed_one, inv_one = norm_forward(inputs_f, gain_attn)
    normed_one = normed_one.astype(jnp.bfloat16)
    normed_grp = to_group(normed_one)
    group_start = lax.axis_index("seq") * group_rows
    query_seg = lax.dynamic_slice_in_dim(seg_all, group_start, group_rows)
    query_pos = lax.dynamic_slice_in_dim(pos_all, group_start, group_rows)
    total_rows = seg_all.shape[0]
    cosine_part, sine_part = rope_tables(query_pos)
    qkv_grp = jnp.dot(normed_grp, cols_weight, preferred_element_type=jnp.float32) + bias_cols
    query_grp = rotate(
        qkv_grp[:, :query_cols].reshape(group_rows, heads_here, HD), cosine_part, sine_part
    ).astype(jnp.bfloat16)
    key_grp = rotate(qkv_grp[:, query_cols : query_cols + HD][:, None, :], cosine_part, sine_part)[
        :, 0
    ].astype(jnp.bfloat16)
    value_grp = qkv_grp[:, query_cols + HD :].astype(jnp.bfloat16)

    def forward_update(fold_state, pieces, first_row):
        key_piece, value_piece = pieces
        piece_rows = key_piece.shape[0]
        tile_rows = math.gcd(piece_rows, group_rows)
        tile_count = piece_rows // tile_rows

        def forward_one_tile(running, tile_item):
            key_tile, value_tile, number = tile_item
            offset = number * tile_rows
            visible = key_visible(
                query_seg,
                query_pos,
                lax.dynamic_slice_in_dim(seg_all, offset, tile_rows),
                lax.dynamic_slice_in_dim(pos_all, offset, tile_rows),
            )
            running_max, running_sum, accumulated = running
            scores = (
                jnp.einsum("qhd,kd->qhk", query_grp, key_tile, preferred_element_type=jnp.float32)
                * score_scale
            )
            scores = jnp.where(visible[:, None, :], scores, MASKED)
            new_max = jnp.maximum(running_max, jnp.max(scores, axis=-1))
            weights = jnp.where(visible[:, None, :], jnp.exp(scores - new_max[..., None]), 0.0)
            factor = jnp.exp(running_max - new_max)
            running_sum = running_sum * factor + jnp.sum(weights, axis=-1)
            accumulated = accumulated * factor[..., None] + jnp.einsum(
                "qhk,kd->qhd",
                weights.astype(jnp.bfloat16),
                value_tile,
                preferred_element_type=jnp.float32,
            )
            return ((new_max, running_sum, accumulated), None)

        tiles = (
            key_piece.reshape(tile_count, tile_rows, HD),
            value_piece.reshape(tile_count, tile_rows, HD),
            jnp.arange(tile_count, dtype=jnp.int32),
        )
        fold_state, unused = lax.scan(forward_one_tile, fold_state, tiles)
        return fold_state

    start_state = (
        jnp.full((group_rows, heads_here), MASKED, jnp.float32),
        jnp.zeros((group_rows, heads_here), jnp.float32),
        jnp.zeros((group_rows, heads_here, HD), jnp.float32),
    )
    running_max, running_sum, accumulated = over_keys(
        key_grp, value_grp, forward_update, start_state
    )
    mixed_f = accumulated / running_sum[..., None]
    log_total = running_max + jnp.log(running_sum)
    mixed_grp = mixed_f.astype(jnp.bfloat16).reshape(group_rows, query_cols)
    hidden = inputs_f + to_own(jnp.dot(mixed_grp, out_part, preferred_element_type=jnp.float32))
    normed_two, inv_two = norm_forward(hidden, gain_mlp)
    normed_two = normed_two.astype(jnp.bfloat16)
    whole_pair, whole_down = collect_heads(pair_part, down_part)
    pair_pre = jnp.dot(normed_two, whole_pair, preferred_element_type=jnp.float32)
    pair_pre = pair_pre.reshape(tok_rows, heads_dev, 2, quarter_ff)
    gate_pre = pair_pre[:, :, 0]
    up_pre = pair_pre[:, :, 1]
    gate_sig = 1.0 / (1.0 + jnp.exp(-gate_pre))
    activated = gate_pre * gate_sig
    middle = (activated * up_pre).astype(jnp.bfloat16)
    output = (
        hidden
        + jnp.dot(
            middle.reshape(tok_rows, heads_dev * quarter_ff),
            whole_down,
            preferred_element_type=jnp.float32,
        )
    ).astype(jnp.bfloat16)
    back_cols = pick_columns(collect_qkv(qkv_weight))
    back_out, back_pair, back_down = collect_layer(out_weight, pair_local, down_weight)
    full_pair, full_down = collect_heads(back_pair, back_down)
    grad_middle = times_transpose(cotangent, full_down).reshape(tok_rows, heads_dev, quarter_ff)
    d_gate = grad_middle * up_pre * gate_sig * (1.0 + gate_pre * (1.0 - gate_sig))
    d_up = grad_middle * activated
    d_pair = (
        jnp.stack([d_gate, d_up], axis=2)
        .reshape(tok_rows, heads_dev * 2 * quarter_ff)
        .astype(jnp.bfloat16)
    )
    d_normed_two = times_transpose(d_pair, full_pair)
    pair_quarters = d_pair.reshape(tok_rows, heads_dev, 2 * quarter_ff)
    pair_term = jnp.einsum(
        "td,tqf->qdf", normed_two, pair_quarters, preferred_element_type=jnp.float32
    )
    down_term = jnp.einsum("td,tqf->qdf", cotangent, middle, preferred_element_type=jnp.float32)
    head_sum = lax.psum_scatter(
        jnp.concatenate([pair_term, down_term], axis=2).astype(jnp.bfloat16),
        "head",
        scatter_dimension=0,
        tiled=True,
    ).astype(jnp.float32)[0]
    d_norm_two, grad_gain_two = norm_backward(hidden, inv_two, gain_mlp, d_normed_two)
    d_hidden = cotangent.astype(jnp.float32) + d_norm_two
    d_branch = d_hidden.astype(jnp.bfloat16)
    branch_grp = to_group(d_branch)
    dout_grp = (
        times_transpose(branch_grp, back_out)
        .astype(jnp.bfloat16)
        .reshape(group_rows, heads_here, HD)
    )
    delta = jnp.sum(dout_grp.astype(jnp.float32) * mixed_f, axis=-1)

    def backward_update(fold_state, pieces, first_row):
        key_piece, value_piece = pieces
        piece_rows = key_piece.shape[0]
        tile_rows = math.gcd(piece_rows, group_rows)
        tile_count = piece_rows // tile_rows

        def backward_one_tile(running, tile_item):
            key_tile, value_tile, number = tile_item
            grad_query, grad_keys, grad_values = running
            offset = number * tile_rows
            visible = key_visible(
                query_seg,
                query_pos,
                lax.dynamic_slice_in_dim(seg_all, offset, tile_rows),
                lax.dynamic_slice_in_dim(pos_all, offset, tile_rows),
            )
            scores = (
                jnp.einsum("qhd,kd->qhk", query_grp, key_tile, preferred_element_type=jnp.float32)
                * score_scale
            )
            probabilities = jnp.where(
                visible[:, None, :], jnp.exp(scores - log_total[..., None]), 0.0
            )
            grad_probs = jnp.einsum(
                "qhd,kd->qhk", dout_grp, value_tile, preferred_element_type=jnp.float32
            )
            grad_scores = (probabilities * (grad_probs - delta[..., None])).astype(jnp.bfloat16)
            grad_query = (
                grad_query
                + jnp.einsum(
                    "qhk,kd->qhd", grad_scores, key_tile, preferred_element_type=jnp.float32
                )
                * score_scale
            )
            key_term = (
                jnp.einsum(
                    "qhk,qhd->kd", grad_scores, query_grp, preferred_element_type=jnp.float32
                )
                * score_scale
            )
            value_term = jnp.einsum(
                "qhk,qhd->kd",
                probabilities.astype(jnp.bfloat16),
                dout_grp,
                preferred_element_type=jnp.float32,
            )
            grad_keys = lax.dynamic_update_slice_in_dim(
                grad_keys,
                lax.dynamic_slice_in_dim(grad_keys, offset, tile_rows, 0) + key_term,
                offset,
                0,
            )
            grad_values = lax.dynamic_update_slice_in_dim(
                grad_values,
                lax.dynamic_slice_in_dim(grad_values, offset, tile_rows, 0) + value_term,
                offset,
                0,
            )
            return ((grad_query, grad_keys, grad_values), None)

        tiles = (
            key_piece.reshape(tile_count, tile_rows, HD),
            value_piece.reshape(tile_count, tile_rows, HD),
            jnp.arange(tile_count, dtype=jnp.int32),
        )
        fold_state, unused = lax.scan(backward_one_tile, fold_state, tiles)
        return fold_state

    back_state = (
        jnp.zeros((group_rows, heads_here, HD), jnp.float32),
        jnp.zeros((total_rows, HD), jnp.float32),
        jnp.zeros((total_rows, HD), jnp.float32),
    )
    grad_query, keys_all, values_all = over_keys(key_grp, value_grp, backward_update, back_state)
    grad_key_grp, grad_value_grp = (
        lax.psum_scatter(
            keys_all.astype(jnp.bfloat16), "seq", scatter_dimension=0, tiled=True
        ).astype(jnp.float32),
        lax.psum_scatter(
            values_all.astype(jnp.bfloat16), "seq", scatter_dimension=0, tiled=True
        ).astype(jnp.float32),
    )
    kv_stack = jnp.stack([grad_key_grp, grad_value_grp], axis=0)
    kv_total = kv_stack + swapped(kv_stack.astype(jnp.bfloat16), "head", 0).astype(kv_stack.dtype)
    d_queries = grad_query.astype(jnp.bfloat16).astype(jnp.float32)
    d_keys = kv_total[0].astype(jnp.bfloat16).astype(jnp.float32)
    d_values = kv_total[1].astype(jnp.bfloat16).astype(jnp.float32)
    d_cols = jnp.concatenate(
        [
            rotate_back(d_queries, cosine_part, sine_part).reshape(group_rows, query_cols),
            rotate_back(d_keys[:, None, :], cosine_part, sine_part)[:, 0] * pair_share,
            d_values * pair_share,
        ],
        axis=1,
    ).astype(jnp.bfloat16)
    bias_padded = place_columns(jnp.sum(d_cols.astype(jnp.float32), axis=0))
    d_normed_one = to_own(times_transpose(d_cols, back_cols))
    d_norm_one, grad_gain_one = norm_backward(inputs_f, inv_one, gain_attn, d_normed_one)
    grad_inputs = (d_hidden + d_norm_one).astype(jnp.bfloat16)
    grad_qkv = lax.psum_scatter(
        place_columns(rows_product(normed_grp, d_cols)),
        ("seq", "head"),
        scatter_dimension=0,
        tiled=True,
    )
    out_term = rows_product(branch_grp, mixed_grp)
    flat_grads = lax.psum_scatter(
        jnp.concatenate([out_term, head_sum], axis=1).astype(jnp.bfloat16),
        "seq",
        scatter_dimension=0,
        tiled=True,
    ).astype(jnp.float32)
    grad_out = flat_grads[:, :query_cols].T
    grad_gate = flat_grads[:, query_cols : query_cols + quarter_ff]
    grad_up = flat_grads[:, query_cols + quarter_ff : query_cols + 2 * quarter_ff]
    grad_down = flat_grads[:, query_cols + 2 * quarter_ff :].T
    grad_gain_attn, grad_bias, grad_value_bias, grad_gain_mlp = (
        lax.psum_scatter(grad_gain_one, ("seq", "head"), scatter_dimension=0, tiled=True),
        lax.psum_scatter(bias_padded[: QD + KD], ("seq", "head"), scatter_dimension=0, tiled=True),
        lax.psum_scatter(bias_padded[QD + KD :], ("seq", "head"), scatter_dimension=0, tiled=True),
        lax.psum_scatter(grad_gain_two, ("seq", "head"), scatter_dimension=0, tiled=True),
    )
    return (
        output,
        grad_inputs,
        grad_gain_attn,
        grad_qkv,
        grad_bias,
        grad_value_bias,
        grad_out,
        grad_gain_mlp,
        grad_gate,
        grad_up,
        grad_down,
    )


def solution(mesh):
    in_specs = (
        P(("seq", "head"), None),
        P(("seq", "head")),
        P(("seq", "head"), None),
        P(("seq", "head")),
        P("head", "seq"),
        P(("seq", "head")),
        P("seq", "head"),
        P("seq", "head"),
        P("head", "seq"),
        P(("seq", "head"), None),
        P(("seq", "head")),
        P(("seq", "head")),
    )
    out_specs = (
        P(("seq", "head"), None),
        P(("seq", "head"), None),
        P(("seq", "head")),
        P(("seq", "head"), None),
        P(("seq", "head")),
        P(("seq", "head")),
        P("head", "seq"),
        P(("seq", "head")),
        P("seq", "head"),
        P("seq", "head"),
        P("head", "seq"),
    )
    return jax.shard_map(
        per_device, mesh=mesh, in_specs=in_specs, out_specs=out_specs, check_vma=False
    )
```

profile of v0, /device:TPU:0, one launch (start us, length us, event | category | flops | bytes accessed | tf_op | source)
XLA Modules:
  0.0 3799.3 jit_solution(16707743115222050394)
XLA Ops:
  10.5 43.2 %all-reduce.8 = (bf16[2048]{0:T(1024)(128)(2,1)S(1)}, bf16[1536]{0:T(1024)(128)(2,1)S(1)}, bf16[1536]{0:T(1024)(128)(2,1)}) all-reduce(bf16[2048]{0:T(1024)(128)(2,1)S(1)} %dynamic-update-slice.1, bf16[1536]{0:T(1024)(128)(2,1)S(1)} %dynamic-update-slice, ...), channel_id=1, replica_groups=mesh['seq'=8,'head'=4] {'seq','head'}, use_global_device_ids=true, to_apply=%add.1 | all-reduce | flops 5120 | bytes 20480
  58.1 25.3 all-gather.16.cloned.1.call-done
  86.3 34.9 all-gather.14.cloned.1.call-done
  121.2 2.8 convolution_add_fusion.1
  124.8 65.8 %all-gather.2 = s32[32,1,128]{2,1,0:T(1,128)S(1)} all-gather(s32[1,1,128]{2,1,0:T(1,128)S(1)} %bitcast.274), channel_id=1, replica_groups=mesh['seq'=8,'head'=4] {'seq','head'}, dimensions={0}, use_global_device_ids=true | all-gather | bytes 16896 | tf_op jit(solution)/shard_map/all_gather | solution.py:186
  195.6 63.0 %all-gather.1 = s32[32,1,128]{2,1,0:T(1,128)S(1)} all-gather(s32[1,1,128]{2,1,0:T(1,128)S(1)} %bitcast.275), channel_id=1, replica_groups=mesh['seq'=8,'head'=4] {'seq','head'}, dimensions={0}, use_global_device_ids=true | all-gather | bytes 16896 | tf_op jit(solution)/shard_map/all_gather | solution.py:185
  260.6 51.9 %while.30 = (s32[]{:T(128)}, f32[512,3]{0,1:T(4,128)S(1)}, f32[512,3]{0,1:T(4,128)S(1)}, f32[512,3,128]{2,0,1:T(8,128)S(1)}, s32[8]{0:T(128)S(1)}, /*index=5*/s3...) while((s32[]{:T(128)}, f32[512,3]{0,1:T(4,128)S(1)}, ...), condition=%wide.region_4.5_spmd.clone, body=%wide.region_1.4_spmd.clone.sunk | while | flops 414523392 | bytes 12829939 | solution.py:255
  264.8 2.2 fusion.171
  271.3 2.2 fusion.171
  277.7 2.2 fusion.171
  284.2 2.2 fusion.171
  290.7 2.2 fusion.171
  297.2 2.2 fusion.171
  303.7 2.2 fusion.171
  310.2 2.2 fusion.171
  315.2 3.6 convolution_convert_fusion.3
  318.9 10.3 copy.86
  329.2 39.5 %all-gather.22.cloned.1.call-done = bf16[1536,4480]{1,0:T(8,128)(2,1)} async-done(((bf16[192,4480]{1,0:T(8,128)(2,1)}), bf16[1536,4480]{1,0:T(8,128)(2,1)}) %all-gather.22.cloned.1.call-update) | async-done | bytes 13762576 | tf_op jit(solution)/shard_map/all_gather | solution.py:92
  370.1 36.9 reduce-scatter.10.cloned.1.call-done
  408.2 462.8 %all-gather.28.cloned.1.call-done = bf16[8960,1536]{1,0:T(8,128)(2,1)} async-done(((bf16[2240,1536]{1,0:T(8,128)(2,1)}), bf16[8960,1536]{1,0:T(8,128)(2,1)}) %all-gather.28.cloned.1.call-update) | async-done | bytes 27525136 | tf_op jit(solution)/shard_map/all_gather | solution.py:100
  871.0 18.5 fusion.116
  889.4 895.8 %all-gather.24.cloned.1.call-done = bf16[1536,17920]{1,0:T(8,128)(2,1)} async-done(((bf16[1536,4480]{1,0:T(8,128)(2,1)}), bf16[1536,17920]{1,0:T(8,128)(2,1)}) %all-gather.24.cloned.1.call-update) | async-done | bytes 55050256 | tf_op jit(solution)/shard_map/all_gather | solution.py:99
  1785.3 29.6 fusion.108
  1814.8 6.2 fusion.65
  1821.4 2.4 copy.89
  1823.8 23.8 multiply_reduce_fusion
  1851.1 32.9 fusion.50
  1884.0 2.7 all-gather.30.cloned.1.call-done
  1886.7 2.6 convolution_convert_fusion.5
  1892.6 106.0 %while.31 = (s32[]{:T(128)}, f32[512,3,128]{2,0,1:T(8,128)S(1)}, f32[4096,128]{1,0:T(8,128)}, f32[4096,128]{1,0:T(8,128)}, s32[8]{0:T(128)S(1)}, /*index=5*/s32[...) while((s32[]{:T(128)}, f32[512,3,128]{2,0,1:T(8,128)S(1)}, ...), condition=%wide.region_10.11_spmd.clone, body=%wide.region_9.10_spmd.clone.sunk | while | flops 1016332800 | bytes 19565844 | solution.py:387
  1899.3 2.5 fusion.186
  1903.6 2.2 fusion.185
  1912.6 2.5 fusion.186
  1916.9 2.2 fusion.185
  1925.8 2.5 fusion.186
  1930.1 2.2 fusion.185
  1939.1 2.5 fusion.186
  1943.4 2.3 fusion.185
  1952.4 2.5 fusion.186
  1956.7 2.2 fusion.185
  1965.6 2.5 fusion.186
  1969.9 2.2 fusion.185
  1978.9 2.5 fusion.186
  1983.2 2.2 fusion.185
  1992.1 2.5 fusion.186
  1996.4 2.2 fusion.185
  1998.7 2.7 convert_element_type.163
  2001.5 16.2 fusion.51
  2018.8 71.3 %pad_maximum_fusion = bf16[4,1536,6720]{1,2,0:T(8,128)(2,1)} fusion(bf16[4,1536,2240]{1,2,0:T(8,128)(2,1)} %fusion.51, bf16[4,1536,4480]{1,2,0:T(8,128)(2,1)} %fusion.50), kind=kLoop, calls=%fused_computation.54 | loop fusion | flops 165150720 | bytes 165150720 | tf_op jit(solution)/shard_map/concatenate | solution.py:306
  2092.3 14.4 collective-permute-done
  2109.5 3.9 convolution_convert_fusion.2
  2115.7 1321.6 %reduce-scatter.20.cloned.1.call-done = bf16[1,1536,6720]{1,2,0:T(8,128)(2,1)} async-done(((bf16[4,1536,6720]{1,2,0:T(8,128)(2,1)}), bf16[1,1536,6720]{1,2,0:T(8,128)(2,1)}) %reduce-scatter.20.cloned.1.call-update) | async-done | bytes 20643856 | tf_op jit(solution)/shard_map/reduce_scatter | solution.py:305
  3437.2 19.3 pad_maximum_fusion.1
  3456.6 28.8 copy.104
  3488.2 7.1 broadcast_in_dim.48
  3498.9 6.5 fusion.113
  3507.1 16.3 fusion.69
  3525.2 42.1 %all-reduce.7 = (f32[1536]{0:T(1024)S(1)}, f32[1792]{0:T(1024)S(1)}, f32[256]{0:T(256)S(1)}, f32[1536]{0:T(1024)S(1)}) all-reduce(f32[1536]{0:T(1024)S(1)} %get-tuple-element.389, f32[1792]{0:T(1024)S(1)} %bitcast.273, f32[256]{0:T(256)S(1)} %slice.130, f32[1536]{0:T(1024)S(1)} %copy-done.40), channel_id=7, replica_groups=mesh['seq'=8,'head'=4] {'seq','head'}, use_global_device_ids=true, to_apply=%region_16.17.clone | all-reduce | flops 5120 | bytes 40960
  3569.7 2.3 fusion.75
  3572.0 57.4 %reduce-scatter.22.cloned.1.call-done = bf16[192,7104]{1,0:T(8,128)(2,1)} async-done(((bf16[1536,7104]{1,0:T(8,128)(2,1)}), bf16[192,7104]{1,0:T(8,128)(2,1)}) %reduce-scatter.22.cloned.1.call-update) | async-done | bytes 2727952
  3629.4 5.5 copy.105
  3634.9 5.6 convert_element_type.174
  3642.4 2.9 copy.98
  3653.0 139.4 %reduce-scatter.18.cloned.1.call-done = f32[48,2048]{1,0:T(8,128)} async-done(((f32[1536,2048]{1,0:T(8,128)}), f32[48,2048]{1,0:T(8,128)}) %reduce-scatter.18.cloned.1.call-update) | async-done | bytes 393232 | tf_op jit(solution)/shard_map/reduce_scatter | solution.py:421
  (367 shorter events, 151.6 us)
Async XLA Ops:
  7.2 76.3 %all-gather.16.cloned.1.call-start = ((), (), s32[]{:S(2)}) async-start(), calls=%async_computation.8 | async-start | bytes 6488064 | tf_op jit(solution)/shard_map/all_gather | solution.py:86
  7.9 113.3 %all-gather.14.cloned.1.call-start = ((), (), s32[]{:S(2)}) async-start(), calls=%async_computation.7 | async-start | bytes 1966080 | tf_op jit(solution)/shard_map/all_gather | solution.py:105
  53.7 1.7 copy-start.34
  57.9 202.2 %all-gather.18.cloned.1.call-start = ((), (), s32[]{:S(2)}) async-start(), calls=%async_computation.9 | async-start | bytes 1179648 | tf_op jit(solution)/shard_map/all_gather | solution.py:79
  84.6 39.4 %copy-start.26 = (bf16[1536,128]{1,0:T(8,128)(2,1)}, bf16[1536,128]{1,0:T(8,128)(2,1)S(1)}, u32[]{:S(2)}) copy-start(bf16[1536,128]{1,0:T(8,128)(2,1)S(1)} %get-tuple-element.466) | copy-start | bytes 1179652
  84.6 39.4 %copy-start.28 = (bf16[1536,128]{1,0:T(8,128)(2,1)}, bf16[1536,128]{1,0:T(8,128)(2,1)S(1)}, u32[]{:S(2)}) copy-start(bf16[1536,128]{1,0:T(8,128)(2,1)S(1)} %get-tuple-element.467) | copy-start | bytes 1179652
  86.3 37.7 copy-start.13
  121.2 3.6 copy-start.54
  124.7 69.2 %copy-start.18 = (bf16[192,2240]{1,0:T(8,128)(2,1)S(1)}, bf16[192,2240]{1,0:T(8,128)(2,1)}, u32[]{:S(2)}) copy-start(bf16[192,2240]{1,0:T(8,128)(2,1)} %param.23) | copy-start | bytes 2580484
  124.7 69.2 %copy-start.19 = (bf16[192,2240]{1,0:T(8,128)(2,1)S(1)}, bf16[192,2240]{1,0:T(8,128)(2,1)}, u32[]{:S(2)}) copy-start(bf16[192,2240]{1,0:T(8,128)(2,1)} %param.22) | copy-start | bytes 2580484
  124.8 135.3 %all-gather.32.cloned.1.call-start = ((), (), s32[]{:S(2)}) async-start(), calls=%async_computation.22 | async-start | bytes 1179648 | tf_op jit(solution)/shard_map/all_gather | solution.py:78
  190.6 68.2 %copy-start.46 = (f32[64]{0:T(128)}, f32[64]{0:T(128)S(1)}, u32[]{:S(2)}) copy-start(f32[64]{0:T(128)S(1)} %negate_power_fusion) | copy-start | bytes 772
  190.7 68.1 %copy-start.38 = (f32[512]{0:T(512)}, f32[512]{0:T(512)S(1)}, u32[]{:S(2)}) copy-start(f32[512]{0:T(512)S(1)} %get-tuple-element.458) | copy-start | bytes 6148
  192.7 2.9 copy-start.55
  192.7 122.5 %all-gather.20.cloned.1.call-start = ((), (), s32[]{:S(2)}) async-start(), calls=%async_computation.10 | async-start | bytes 1327104 | tf_op jit(solution)/shard_map/all_gather | solution.py:91
  193.3 125.5 %all-gather.26.cloned.1.call-start = ((), (), s32[]{:S(2)}) async-start(), calls=%async_computation.14 | async-start | bytes 7962624 | tf_op jit(solution)/shard_map/all_gather | solution.py:93
  193.9 174.9 %all-gather.22.cloned.1.call-start = ((), (), s32[]{:S(2)}) async-start(), calls=%async_computation.12 | async-start | bytes 15482880 | tf_op jit(solution)/shard_map/all_gather | solution.py:92
  195.5 211.4 %reduce-scatter.10.cloned.1.call-start = ((), (), s32[]{:S(2)}) async-start(), calls=%async_computation.11 | async-start | bytes 1966080 | tf_op jit(solution)/shard_map/reduce_scatter | solution.py:109
  259.3 1.2 copy-start.14
  314.8 4.0 copy-start.23
  315.2 14.0 copy-start.11
  318.8 552.2 %all-gather.28.cloned.1.call-start = ((), (), s32[]{:S(2)}) async-start(), calls=%async_computation.15 | async-start | bytes 34406400 | tf_op jit(solution)/shard_map/all_gather | solution.py:100
  329.2 1456.1 %all-gather.24.cloned.1.call-start = ((), (), s32[]{:S(2)}) async-start(), calls=%async_computation.13 | async-start | bytes 68812800 | tf_op jit(solution)/shard_map/all_gather | solution.py:99
  368.8 38.2 %copy-start = (bf16[128,1536]{1,0:T(8,128)(2,1)S(1)}, bf16[128,1536]{1,0:T(8,128)(2,1)}, u32[]{:S(2)}) copy-start(bf16[128,1536]{1,0:T(8,128)(2,1)} %param.16) | copy-start | bytes 1179652
  368.8 502.2 %copy-start.8 = (bf16[128,1536]{1,0:T(8,128)(2,1)S(1)}, bf16[128,1536]{1,0:T(8,128)(2,1)}, u32[]{:S(2)}) copy-start(bf16[128,1536]{1,0:T(8,128)(2,1)} %param.25) | copy-start | bytes 1179652
  368.8 1517.9 %all-gather.30.cloned.1.call-start = ((), (), s32[]{:S(2)}) async-start(), calls=%async_computation.16 | async-start | bytes 1966080 | tf_op jit(solution)/shard_map/all_gather | solution.py:105
  369.5 1481.6 %copy-start.21 = (f32[1536]{0:T(1024)}, f32[1536]{0:T(1024)S(1)}, u32[]{:S(2)}) copy-start(f32[1536]{0:T(1024)S(1)} %convert_element_type.150) | copy-start | bytes 18436
  408.2 1440.1 %copy-start.49 = (f32[128]{0:T(128)}, f32[128]{0:T(128)S(1)}, u32[]{:S(2)}) copy-start(f32[128]{0:T(128)S(1)} %get-tuple-element.484) | copy-start | bytes 1540
  408.2 1442.9 %copy-start.41 = (f32[128]{0:T(128)}, f32[128]{0:T(128)S(1)}, u32[]{:S(2)}) copy-start(f32[128]{0:T(128)S(1)} %get-tuple-element.485) | copy-start | bytes 1540
  408.2 1377.0 %copy-start.3 = (bf16[128,1536]{1,0:T(8,128)(2,1)S(1)}, bf16[128,1536]{1,0:T(8,128)(2,1)}, u32[]{:S(2)}) copy-start(bf16[128,1536]{1,0:T(8,128)(2,1)} %reduce-scatter.10.cloned.1.call-done) | copy-start | bytes 1179652
  1847.6 36.4 copy-start.6
  1851.0 239.5 %reduce-scatter.14.cloned.1.call-start = ((), (), s32[]{:S(2)}) async-start(), calls=%async_computation.18 | async-start | bytes 1179648 | tf_op jit(solution)/shard_map/reduce_scatter | solution.py:400
  1884.0 5.3 copy-start.25
  1889.3 3.4 copy-start.31
  1889.3 3.3 copy-start.33
  1889.3 3.3 copy-start.43
  1998.7 2.8 copy-start.9
  2001.4 89.1 %reduce-scatter.12.cloned.1.call-start = ((), (), s32[]{:S(2)}) async-start(), calls=%async_computation.17 | async-start | bytes 1179648 | tf_op jit(solution)/shard_map/reduce_scatter | solution.py:397
  2001.5 16.2 copy-start.5
  2018.7 1418.5 %reduce-scatter.20.cloned.1.call-start = ((), (), s32[]{:S(2)}) async-start(), calls=%async_computation.21 | async-start | bytes 103219200 | tf_op jit(solution)/shard_map/reduce_scatter | solution.py:305
  2090.1 2.1 copy-start.15
  2090.1 2.1 copy-start.17
  2090.1 1433.7 %reduce-scatter.16.cloned.1.call-start = ((), (), s32[]{:S(2)}) async-start(), calls=%async_computation.19 | async-start | bytes 1966080 | tf_op jit(solution)/shard_map/reduce_scatter | solution.py:109
  2090.2 17.8 copy-start.39
  2090.2 17.8 copy-start.47
  2090.5 18.9 copy-start.27
  2090.5 18.9 copy-start.29
  2091.6 15.1 collective-permute-start
  2109.5 4.0 copy-start.12
  2113.4 1516.0 %reduce-scatter.22.cloned.1.call-start = ((), (), s32[]{:S(2)}) async-start(), calls=%async_computation.23 | async-start | bytes 24772608
  3485.3 1.4 copy-start.10
  3485.4 307.0 %reduce-scatter.18.cloned.1.call-start = ((), (), s32[]{:S(2)}) async-start(), calls=%async_computation.20 | async-start | bytes 12976128 | tf_op jit(solution)/shard_map/reduce_scatter | solution.py:421
  3505.4 1.5 copy-start.1
  3505.5 1.5 copy-start.4
  3507.0 16.9 copy-start.35
  3507.0 16.9 copy-start.45
  3507.0 18.1 copy-start.40
  3507.0 62.6 %copy-start.7 = (f32[128,1536]{1,0:T(8,128)S(1)}, f32[128,1536]{1,0:T(8,128)}, u32[]{:S(2)}) copy-start(f32[128,1536]{1,0:T(8,128)} %copy-done.6) | copy-start | bytes 2359300
  3507.0 62.6 %copy-start.22 = (f32[1536]{0:T(1024)S(1)}, f32[1536]{0:T(1024)}, u32[]{:S(2)}) copy-start(f32[1536]{0:T(1024)} %copy-done.21) | copy-start | bytes 18436
  3507.0 62.6 %copy-start.42 = (f32[128]{0:T(128)S(1)}, f32[128]{0:T(128)}, u32[]{:S(2)}) copy-start(f32[128]{0:T(128)} %copy-done.41) | copy-start | bytes 1540
  3507.1 62.6 %copy-start.50 = (f32[128]{0:T(128)S(1)}, f32[128]{0:T(128)}, u32[]{:S(2)}) copy-start(f32[128]{0:T(128)} %copy-done.49) | copy-start | bytes 1540
  3507.1 62.6 %copy-start.52 = (f32[128]{0:T(128)S(1)}, f32[128]{0:T(128)}, u32[]{:S(2)}) copy-start(f32[128]{0:T(128)} %copy-done.51) | copy-start | bytes 1540
  3507.1 62.6 %copy-start.53 = (f32[128]{0:T(128)S(1)}, f32[128]{0:T(128)}, u32[]{:S(2)}) copy-start(f32[128]{0:T(128)} %get-tuple-element.482) | copy-start | bytes 1540
  3634.9 5.6 copy-start.2
  (10 other events, 7.2 us)
Sparse Core Ops, SparseCore 0:
  10.9 72.5 all-gather.15
  85.6 35.5 all-gather.13
  124.9 22.3 all-gather.17
  192.9 19.8 all-gather.31
  214.4 24.0 all-gather.19
  240.3 48.8 all-gather.25
  291.6 77.1 all-gather.21
  371.7 35.2 reduce-scatter.9
  408.6 462.3 all-gather.27
  872.4 912.7 all-gather.23
  1851.1 35.5 all-gather.29
  2001.5 34.8 reduce-scatter.13
  2040.2 35.9 reduce-scatter.11
  2090.3 1346.9 reduce-scatter.19
  3440.1 37.0 reduce-scatter.15
  3485.5 143.8 reduce-scatter.21
  3636.9 155.3 reduce-scatter.17
where the time goes:
time: 3810 us; the launch traced here: 3800 us
  waiting for transfers between devices  3030 us (80%)
  matrix products  265 us (7%)
  blocking collectives  214 us (6%)
  other arithmetic  147 us (4%)
  local copies, waits for them, and re-layouts  112 us (3%)
    reduce_scatter x1, waiting for transfers between devices, per_device(): lax.psum_scatter(jnp.concatenate([pair_term, down_term], axis=2).astype(j...  1320 us
    all_gather x1, waiting for transfers between devices, collect_heads(): lax.all_gather(pair_part, 'head', axis=1, tiled=True)  896 us
    all_gather x1, waiting for transfers between devices, collect_heads(): lax.all_gather(down_part, 'head', axis=0, tiled=True)  463 us
    reduce_scatter x1, waiting for transfers between devices, per_device(): lax.psum_scatter(place_columns(rows_product(normed_grp, d_cols)), ('seq',...  139 us
    unnamed x2, blocking collectives  85.3 us
  transfers between devices with their start and end apart: 18, of which 11 were waited for; matrix products, arithmetic and copies ran while one was open for 9% of the time, Pallas kernels for 0%

commit v1 on v0

v1 whole, which is shorter than its diff:
```python
import functools

import jax
import jax.numpy as jnp
from jax import lax
from jax.experimental import pallas as pl
from jax.experimental.pallas import tpu as pltpu
from jax.sharding import PartitionSpec as P

HEADS = 12
KV_HEADS = 2
HD = 128
QD = 1536
KD = 256
QKV = 2048


EPS = 1e-06
ROPE_BASE = 1000000.0
MASKED = -1e30
SEG_STEP = 1 << 20

BF = jnp.bfloat16
F32 = jnp.float32


def bits_of(axis):
    return (lax.axis_size(axis) - 1).bit_length()


def bit_value(axis, bit):
    return (lax.axis_index(axis) >> bit) & 1


def swap(block, axis, bit):
    count = lax.axis_size(axis)
    return lax.ppermute(block, axis, [(j, j ^ (1 << bit)) for j in range(count)])


def from_next(block, axis, apart=1):
    count = lax.axis_size(axis)
    return lax.ppermute(block, axis, [(j, (j - apart) % count) for j in range(count)])


def to_next(block, axis):
    count = lax.axis_size(axis)
    return lax.ppermute(block, axis, [(j, (j + 1) % count) for j in range(count)])


def ring_gather(block, axis):
    blocks = [block]
    for _ in range(lax.axis_size(axis) - 1):
        blocks.append(from_next(blocks[-1], axis))
    return blocks


def ring_sum(pieces, axis):
    total = pieces[-1]
    for piece in pieces[-2::-1]:
        total = piece + to_next(total.astype(BF), axis).astype(F32)
    return total


def gather_ordered(block, steps):
    done = []
    ranks = sorted(steps, reverse=True)
    for axis, bit, rank in steps:
        other = swap(block, axis, bit)
        upper = bit_value(axis, bit) == 1
        low = jnp.where(upper, other, block)
        high = jnp.where(upper, block, other)
        place = sum(1 for known in done if known > rank)
        block = jnp.stack([low, high], axis=place)
        done.append(rank)
    del ranks
    return block


def sum_ordered(block, steps, wide):
    left = sorted((rank for _, _, rank in steps), reverse=True)
    for axis, bit, rank in steps:
        place = left.index(rank)
        low = lax.index_in_dim(block, 0, place, keepdims=False)
        high = lax.index_in_dim(block, 1, place, keepdims=False)
        upper = bit_value(axis, bit) == 1
        sent = jnp.where(upper, low, high)
        kept = jnp.where(upper, high, low)
        if wide:
            block = kept + swap(sent, axis, bit)
        else:
            block = kept.astype(F32) + swap(sent.astype(BF), axis, bit).astype(F32)
        left.pop(place)
    return block


def gather_xor(block, steps):
    blocks = {0: block}
    for axis, bit in steps:
        masks = sorted(blocks)
        moved = swap(jnp.stack([blocks[m] for m in masks]), axis, bit)
        for place, mask in enumerate(masks):
            blocks[mask | 1 << bit] = moved[place]
    return blocks


def sum_xor(blocks, steps):
    for axis, bit in steps:
        masks = sorted(blocks)
        sent = [m for m in masks if m >> bit & 1]
        moved = swap(jnp.stack([blocks[m].astype(BF) for m in sent]), axis, bit)
        blocks = {m: blocks[m].astype(F32) for m in masks if not m >> bit & 1}
        for place, mask in enumerate(sent):
            blocks[mask ^ 1 << bit] = blocks[mask ^ 1 << bit] + moved[place].astype(F32)
    return blocks[0]


def roll_blocks(stacked, shift, axis=0):
    count = stacked.shape[axis]
    return lax.dynamic_slice_in_dim(
        jnp.concatenate([stacked, stacked], axis=axis), shift, count, axis
    )


def rope_tables(positions):
    freq_index = jnp.arange(HD // 2, dtype=F32) * 2.0 / HD
    inverse = 1.0 / ROPE_BASE**freq_index
    angles = positions.astype(F32)[:, None] * inverse[None, :]
    return (jnp.cos(angles)[:, None, :], jnp.sin(angles)[:, None, :])


def rotate(values, cosine_part, sine_part):
    front_half = values[..., : HD // 2]
    back_half = values[..., HD // 2 :]
    return jnp.concatenate(
        [
            front_half * cosine_part - back_half * sine_part,
            back_half * cosine_part + front_half * sine_part,
        ],
        axis=-1,
    )


def rotate_back(grad_in, cosine_part, sine_part):
    return rotate(grad_in, cosine_part, -sine_part)


def inverse_norm(values):
    return lax.rsqrt(jnp.mean(values * values, axis=-1, keepdims=True) + EPS)


def dot_nn(left, right):
    return jnp.dot(left, right, preferred_element_type=F32)


def dot_nt(left, right):
    return lax.dot_general(left, right, (((1,), (1,)), ((), ())), preferred_element_type=F32)


def dot_tn(left, right):
    return lax.dot_general(left, right, (((0,), (0,)), ((), ())), preferred_element_type=F32)


def joined(block_ref, half):
    block = block_ref[:, half]
    return block.reshape(block.shape[0] * block.shape[1], block.shape[2])


def visible_of(key_code, query_code, half):
    seen = key_code <= query_code
    if half == 1:
        seen &= key_code >= (query_code // SEG_STEP) * SEG_STEP
    return seen


PAIRS = ((0, 0), (0, 1), (1, 1))


def attend_kernel(scale, q_ref, k_ref, v_ref, kc_ref, qc_ref, mixed_ref, lse_ref, top, total, acc):
    step = pl.program_id(0)

    @pl.when(step == 0)
    def _():
        top[...] = jnp.full(top.shape, MASKED, F32)
        total[...] = jnp.zeros(total.shape, F32)
        acc[...] = jnp.zeros(acc.shape, F32)

    for key_half, query_half in PAIRS:
        keys = joined(k_ref, key_half)
        values = joined(v_ref, key_half)
        scores = dot_nt(keys, q_ref[query_half]) * scale
        if key_half == query_half:
            seen = visible_of(joined(kc_ref, key_half), qc_ref[query_half], key_half)
            scores = jnp.where(seen, scores, MASKED)
        old = top[query_half]
        new = jnp.maximum(old, jnp.max(scores, axis=0, keepdims=True))
        weights = jnp.exp(scores - new)
        if key_half == query_half:
            weights = jnp.where(seen, weights, 0.0)
        factor = jnp.exp(old - new)
        top[query_half] = new
        total[query_half] = total[query_half] * factor + jnp.sum(weights, axis=0, keepdims=True)
        acc[query_half] = acc[query_half] * factor + dot_tn(values, weights.astype(BF))

    @pl.when(step == pl.num_programs(0) - 1)
    def _():
        for half in range(2):
            mixed_ref[half] = jnp.transpose(acc[half] / total[half])
            lse_ref[half] = top[half] + jnp.log(total[half])


def whole(shape):
    return pl.BlockSpec(shape, lambda i: (0,) * len(shape))


def per_step(shape, some):
    return pl.BlockSpec((some,) + shape[1:], lambda i: (i,) + (0,) * (len(shape) - 1))


SEQ_STEP = 2


def attend(queries, keys, values, key_code, query_code):
    _, rows, _ = queries.shape
    count = keys.shape[0]
    work = 3 * rows * keys.shape[0] * keys.shape[2]
    return pl.pallas_call(
        functools.partial(attend_kernel, HD**-0.5),
        grid=(count // SEQ_STEP,),
        in_specs=[
            whole(queries.shape),
            per_step(keys.shape, SEQ_STEP),
            per_step(values.shape, SEQ_STEP),
            per_step(key_code.shape, SEQ_STEP),
            whole(query_code.shape),
        ],
        out_specs=[whole((2, rows, HD)), whole((2, 1, rows))],
        out_shape=[
            jax.ShapeDtypeStruct((2, rows, HD), F32),
            jax.ShapeDtypeStruct((2, 1, rows), F32),
        ],
        scratch_shapes=[
            pltpu.VMEM((2, 1, rows), F32),
            pltpu.VMEM((2, 1, rows), F32),
            pltpu.VMEM((2, HD, rows), F32),
        ],
        compiler_params=pltpu.CompilerParams(vmem_limit_bytes=48 * 2**20),
        cost_estimate=pl.CostEstimate(
            flops=4 * HD * work, bytes_accessed=4 * 2**20, transcendentals=work
        ),
        name="attend",
    )(queries, keys, values, key_code, query_code)


def attend_back_kernel(
    scale, q_ref, do_ref, k_ref, v_ref, kc_ref, qc_ref, lse_ref, delta_ref, dq_ref, dk_ref, dv_ref, acc
):
    step = pl.program_id(0)

    @pl.when(step == 0)
    def _():
        acc[...] = jnp.zeros(acc.shape, F32)

    for key_half in range(2):
        keys = joined(k_ref, key_half)
        values = joined(v_ref, key_half)
        grad_keys, grad_values = None, None
        for query_half in range(key_half, 2):
            queries = q_ref[query_half]
            grads = do_ref[query_half]
            scores = dot_nt(keys, queries) * scale
            weights = jnp.exp(scores - lse_ref[query_half])
            if key_half == query_half:
                seen = visible_of(joined(kc_ref, key_half), qc_ref[query_half], key_half)
                weights = jnp.where(seen, weights, 0.0)
            grad_weights = dot_nt(values, grads)
            grad_scores = (weights * (grad_weights - delta_ref[query_half])).astype(BF)
            value_term = dot_nn(weights.astype(BF), grads)
            key_term = dot_nn(grad_scores, queries)
            grad_keys = key_term if grad_keys is None else grad_keys + key_term
            grad_values = value_term if grad_values is None else grad_values + value_term
            acc[query_half] += dot_tn(keys, grad_scores)
        shape = (dk_ref.shape[0],) + dk_ref.shape[2:]
        dk_ref[:, key_half] = (grad_keys * scale).reshape(shape).astype(dk_ref.dtype)
        dv_ref[:, key_half] = grad_values.reshape(shape).astype(dv_ref.dtype)

    @pl.when(step == pl.num_programs(0) - 1)
    def _():
        for half in range(2):
            dq_ref[half] = jnp.transpose(acc[half] * scale)


def attend_back(queries, grads, keys, values, key_code, query_code, log_total, delta):
    _, rows, _ = queries.shape
    count = keys.shape[0]
    work = 3 * rows * keys.shape[0] * keys.shape[2]
    return pl.pallas_call(
        functools.partial(attend_back_kernel, HD**-0.5),
        grid=(count // SEQ_STEP,),
        in_specs=[
            whole(queries.shape),
            whole(grads.shape),
            per_step(keys.shape, SEQ_STEP),
            per_step(values.shape, SEQ_STEP),
            per_step(key_code.shape, SEQ_STEP),
            whole(query_code.shape),
            whole(log_total.shape),
            whole(delta.shape),
        ],
        out_specs=[
            whole((2, rows, HD)),
            per_step(keys.shape, SEQ_STEP),
            per_step(values.shape, SEQ_STEP),
        ],
        out_shape=[
            jax.ShapeDtypeStruct((2, rows, HD), F32),
            jax.ShapeDtypeStruct(keys.shape, BF),
            jax.ShapeDtypeStruct(values.shape, BF),
        ],
        scratch_shapes=[pltpu.VMEM((2, HD, rows), F32)],
        compiler_params=pltpu.CompilerParams(vmem_limit_bytes=48 * 2**20),
        cost_estimate=pl.CostEstimate(
            flops=10 * HD * work, bytes_accessed=6 * 2**20, transcendentals=work
        ),
        name="attend_back",
    )(queries, grads, keys, values, key_code, query_code, log_total, delta)


def per_device(
    inputs,
    norm_gain_attn,
    qkv_weight,
    qkv_bias,
    out_weight,
    norm_gain_mlp,
    gate_weight,
    up_weight,
    down_weight,
    cotangent,
    segment_ids,
    positions,
):
    tok_rows = inputs.shape[0]
    width = inputs.shape[1]
    seq_dev = lax.axis_size("seq")
    heads_dev = lax.axis_size("head")
    heads_here = HEADS // heads_dev
    copies = heads_dev // KV_HEADS
    group_rows = heads_dev * tok_rows
    half_rows = group_rows // 2
    query_cols = heads_here * HD
    quarter_ff = gate_weight.shape[1]
    head_index = lax.axis_index("head")
    seq_index = lax.axis_index("seq")
    odd = head_index % 2 == 1
    seq_bits = bits_of("seq")
    head_bits = bits_of("head")
    far = list(range(1, seq_bits))
    one_way = [("seq", bit) for bit in far]
    other_way = one_way[::-1]
    near = [("seq", 0)]

    def ranked(steps):
        return [(axis, bit, bit) for axis, bit in steps]

    gain_cols = norm_gain_attn.shape[0]
    bias_cols = qkv_bias.shape[0]
    small = jnp.concatenate(
        [
            norm_gain_attn,
            norm_gain_mlp,
            qkv_bias,
            (positions >> 7).astype(BF),
            (positions & 127).astype(BF),
            segment_ids.astype(BF),
        ]
    )
    small_steps = [("head", bit, bit) for bit in range(head_bits)] + [
        ("seq", bit, bit + head_bits) for bit in range(seq_bits)
    ]
    small_all = gather_ordered(small, small_steps).reshape(seq_dev * heads_dev, small.shape[0])
    cuts, start = [], 0
    for size in (gain_cols, gain_cols, bias_cols, tok_rows, tok_rows, tok_rows):
        cuts.append(small_all[:, start : start + size])
        start += size
    gain_attn = cuts[0].reshape(-1).astype(F32)
    gain_mlp = cuts[1].reshape(-1).astype(F32)
    bias_all = cuts[2].reshape(-1).astype(F32)
    pos_all = (cuts[3].astype(jnp.int32) << 7) + cuts[4].astype(jnp.int32)
    seg_all = cuts[5].astype(jnp.int32)

    pos_all = roll_blocks(pos_all.reshape(seq_dev, heads_dev, tok_rows), head_index, 1)
    seg_all = roll_blocks(seg_all.reshape(seq_dev, heads_dev, tok_rows), head_index, 1)
    code_all = seg_all * SEG_STEP + pos_all
    query_pos = lax.dynamic_index_in_dim(pos_all, seq_index, 0, keepdims=False).reshape(-1)
    query_code = lax.dynamic_index_in_dim(code_all, seq_index, 0, keepdims=False)

    def halves_first(values):
        tail = values.shape[1:]
        return jnp.swapaxes(
            values.reshape((heads_dev, 2, tok_rows // 2) + tail), 0, 1
        ).reshape((2, half_rows) + tail)

    def halves_back(values):
        tail = values.shape[2:]
        return jnp.swapaxes(
            values.reshape((2, heads_dev, tok_rows // 2) + tail), 0, 1
        ).reshape((group_rows,) + tail)

    def to_heads(values):
        return jnp.swapaxes(halves_first(values), 1, 2).reshape(2, heads_here * half_rows, HD)

    def from_heads(values):
        return halves_back(jnp.swapaxes(values.reshape(2, heads_here, half_rows, HD), 1, 2))

    query_code = jnp.broadcast_to(
        halves_first(query_code.reshape(-1))[:, None, None, :], (2, 1, heads_here, half_rows)
    ).reshape(2, 1, heads_here * half_rows)
    key_code = jnp.stack(
        [
            lax.dynamic_index_in_dim(code_all, seq_index ^ mask, 0, keepdims=False)
            for mask in range(seq_dev)
        ]
    )
    key_code = jnp.swapaxes(
        key_code.reshape(seq_dev, heads_dev, 2, tok_rows // 2), 1, 2
    ).reshape(seq_dev, 2, half_rows, 1)

    pair_local = jnp.concatenate([gate_weight, up_weight], axis=1)
    pair_all = lax.all_gather(pair_local, "seq", axis=0, tiled=True)
    down_all = lax.all_gather(down_weight.T, "seq", axis=0, tiled=True)

    def head_columns(values, head):
        last = values.ndim - 1
        slot = head // copies
        return [
            lax.dynamic_slice_in_dim(values, head * query_cols, query_cols, last),
            lax.dynamic_slice_in_dim(values, QD + slot * HD, HD, last),
            lax.dynamic_slice_in_dim(values, QD + KD + slot * HD, HD, last),
        ]

    rows_of = [jnp.concatenate(head_columns(qkv_weight, head_index), axis=1)]
    for apart in range(1, heads_dev):
        target = (head_index - apart) % heads_dev
        block = jnp.concatenate(head_columns(qkv_weight, target), axis=1)
        rows_of.append(from_next(block, "head", apart))
    own_rows = roll_blocks(jnp.stack(rows_of), (heads_dev - head_index) % heads_dev)
    own_rows = own_rows.reshape(-1, query_cols + 2 * HD)
    query_weight = gather_ordered(own_rows[:, :query_cols], ranked(one_way + near)).reshape(
        width, query_cols
    )
    kv_weight = gather_ordered(own_rows[:, query_cols:], ranked(other_way + near)).reshape(
        width, 2 * HD
    )

    out_rows = jnp.concatenate([block.T for block in ring_gather(out_weight, "head")], axis=1)
    out_all = lax.all_gather(out_rows, "seq", axis=0, tiled=True)

    inputs_f = jnp.concatenate(ring_gather(inputs, "head")).astype(F32)
    inv_one = inverse_norm(inputs_f)
    normed_one = (inputs_f * inv_one * gain_attn).astype(BF)
    cosine_part, sine_part = rope_tables(query_pos)
    bias_here = head_columns(bias_all, head_index)
    queries = dot_nn(normed_one, query_weight) + bias_here[0]
    keys_values = dot_nn(normed_one, kv_weight) + jnp.concatenate(bias_here[1:])
    queries = rotate(
        queries.reshape(group_rows, heads_here, HD), cosine_part, sine_part
    ).astype(BF)
    keys = rotate(keys_values[:, None, :HD], cosine_part, sine_part)[:, 0].astype(BF)
    values = keys_values[:, HD:].astype(BF)
    keys_far = gather_xor(halves_first(keys), one_way)
    values_far = gather_xor(halves_first(values), other_way)
    far_masks = sorted(keys_far)
    kv_near = jnp.stack(
        [jnp.stack([blocks[mask] for mask in far_masks]) for blocks in (keys_far, values_far)]
    )
    kv_all = jnp.stack([kv_near, swap(kv_near, "seq", 0)], axis=2).reshape(
        2, seq_dev, 2, half_rows, HD
    )
    queries = to_heads(queries)
    mixed_f, log_total = attend(queries, kv_all[0], kv_all[1], key_code, query_code)
    mixed_f = from_heads(mixed_f)
    mixed = mixed_f.astype(BF).reshape(group_rows, query_cols)
    mixed_all = [
        jnp.concatenate([block[group_rows - far_by * tok_rows :], block[: group_rows - far_by * tok_rows]])
        for far_by, block in enumerate(ring_gather(mixed, "head"))
    ]
    hidden = inputs_f + dot_nt(jnp.concatenate(mixed_all, axis=1), out_all)

    inv_two = inverse_norm(hidden)
    normed_two = (hidden * inv_two * gain_mlp).astype(BF)
    cot_grp = jnp.concatenate(ring_gather(cotangent, "head"))
    pair_pre = dot_nn(normed_two, pair_all)
    gate_pre = pair_pre[:, :quarter_ff]
    up_pre = pair_pre[:, quarter_ff:]
    gate_sig = 1.0 / (1.0 + jnp.exp(-gate_pre))
    activated = gate_pre * gate_sig
    middle = (activated * up_pre).astype(BF)
    grad_middle = dot_nn(cot_grp, down_all)
    d_gate = grad_middle * up_pre * gate_sig * (1.0 + gate_pre * (1.0 - gate_sig))
    d_up = grad_middle * activated
    d_pair = jnp.concatenate([d_gate.astype(BF), d_up.astype(BF)], axis=1)
    d_normed_two = dot_nt(d_pair, pair_all)

    def split_rows(values):
        return [values[i * tok_rows : (i + 1) * tok_rows] for i in range(heads_dev)]

    d_normed_two = ring_sum(split_rows(d_normed_two), "head")
    own_hidden = hidden[:tok_rows]
    own_inv = inv_two[:tok_rows]
    scaled = d_normed_two * gain_mlp
    grad_gain_two = jnp.sum(d_normed_two * own_hidden * own_inv, axis=0)
    inner = jnp.mean(scaled * own_hidden, axis=-1, keepdims=True)
    d_hidden = cotangent.astype(F32) + own_inv * scaled - own_hidden * own_inv**3 * inner
    d_branch = d_hidden.astype(BF)

    d_mixed_own = dot_nn(d_branch, out_all).astype(BF)
    d_mixed = [d_mixed_own[:, :query_cols]]
    for apart in range(1, heads_dev):
        place = (heads_dev - apart) % heads_dev
        block = d_mixed_own[:, place * query_cols : (place + 1) * query_cols]
        d_mixed.append(from_next(block, "head", apart))
    d_mixed = jnp.concatenate(d_mixed).reshape(group_rows, heads_here, HD)
    delta = jnp.sum(d_mixed.astype(F32) * mixed_f, axis=-1)
    delta = jnp.swapaxes(halves_first(delta), 1, 2).reshape(2, 1, heads_here * half_rows)
    d_queries, d_keys_all, d_values_all = attend_back(
        queries, to_heads(d_mixed), kv_all[0], kv_all[1], key_code, query_code, log_total, delta
    )
    d_kv = jnp.stack([d_keys_all, d_values_all]).reshape(2, seq_dev // 2, 2, 2, half_rows, HD)
    d_kv = d_kv[:, :, 0].astype(F32) + swap(d_kv[:, :, 1], "seq", 0).astype(F32)
    d_keys = sum_xor({mask: d_kv[0, i] for i, mask in enumerate(far_masks)}, one_way[::-1])
    d_values = sum_xor({mask: d_kv[1, i] for i, mask in enumerate(far_masks)}, other_way[::-1])
    d_other = swap(jnp.where(odd, d_keys, d_values).astype(BF), "head", 0)
    d_kv_own = jnp.where(odd, d_values, d_keys).astype(F32)
    d_other = d_other.reshape(2, heads_dev, tok_rows // 2, HD)
    d_other = roll_blocks(d_other, jnp.where(odd, 1, heads_dev - 1), 1).reshape(2, half_rows, HD)
    d_kv_own = halves_back(d_kv_own + d_other.astype(F32)).astype(BF).astype(F32)
    d_queries = from_heads(d_queries).astype(BF).astype(F32)
    d_cols = jnp.concatenate(
        [
            rotate_back(d_queries, cosine_part, sine_part).reshape(group_rows, query_cols),
            jnp.where(
                odd, d_kv_own, rotate_back(d_kv_own[:, None, :], cosine_part, sine_part)[:, 0]
            ),
        ],
        axis=1,
    ).astype(BF)
    back_weight = jnp.concatenate(
        [query_weight, jnp.where(odd, kv_weight[:, HD:], kv_weight[:, :HD])], axis=1
    )
    d_normed_one = dot_nt(d_cols, back_weight)
    grad_gain_one = jnp.sum(d_normed_one * inputs_f * inv_one, axis=0)
    d_normed_one = ring_sum(split_rows(d_normed_one), "head")
    scaled = d_normed_one * gain_attn
    inner = jnp.mean(scaled * inputs_f[:tok_rows], axis=-1, keepdims=True)
    grad_inputs = (
        d_hidden + inv_one[:tok_rows] * scaled - inputs_f[:tok_rows] * inv_one[:tok_rows] ** 3 * inner
    ).astype(BF)

    grad_cols = dot_tn(normed_one, d_cols).astype(BF)
    grad_cols = grad_cols.reshape((2,) * seq_bits + (width // seq_dev, query_cols + HD))
    grad_cols = jnp.concatenate(
        [
            sum_ordered(grad_cols[..., : 2 * HD], ranked(near + one_way[::-1]), False),
            sum_ordered(grad_cols[..., 2 * HD :], ranked(near + other_way[::-1]), False),
        ],
        axis=1,
    )
    own_wide = width // (seq_dev * heads_dev)
    grad_blocks = grad_cols.reshape(heads_dev, own_wide, query_cols + HD)
    grad_qkv = jnp.zeros((own_wide, QKV), F32)
    for apart in range(heads_dev):
        source = (head_index + apart) % heads_dev
        target = (head_index - apart) % heads_dev
        block = lax.dynamic_index_in_dim(grad_blocks, target, 0, keepdims=False)
        if apart:
            block = from_next(block.astype(BF), "head", apart).astype(F32)
        kv_place = QD + source % 2 * KD + source // copies * HD
        grad_qkv = lax.dynamic_update_slice_in_dim(
            grad_qkv, block[:, :query_cols], source * query_cols, 1
        )
        grad_qkv = lax.dynamic_update_slice_in_dim(grad_qkv, block[:, query_cols:], kv_place, 1)

    branch_grp = jnp.concatenate(ring_gather(d_branch, "head"))
    grad_pair = lax.psum_scatter(
        dot_tn(normed_two, d_pair).astype(BF), "seq", scatter_dimension=0, tiled=True
    ).astype(F32)
    grad_down = lax.psum_scatter(
        dot_tn(cot_grp, middle).astype(BF), "seq", scatter_dimension=0, tiled=True
    ).astype(F32).T
    grad_out = lax.psum_scatter(
        dot_tn(branch_grp, mixed).astype(BF), "seq", scatter_dimension=0, tiled=True
    ).astype(F32).T

    output = ring_sum(split_rows(dot_nt(middle, down_all)), "head")
    output = (own_hidden + output).astype(BF)

    bias_cols_sum = jnp.sum(d_cols.astype(F32), axis=0)
    bias_sum = lax.dynamic_update_slice_in_dim(
        jnp.zeros((QKV,), F32), bias_cols_sum[:query_cols], head_index * query_cols, 0
    )
    bias_sum = lax.dynamic_update_slice_in_dim(
        bias_sum,
        bias_cols_sum[query_cols:],
        QD + head_index % 2 * KD + head_index // copies * HD,
        0,
    )
    devices = seq_dev * heads_dev
    small_grads = jnp.concatenate(
        [
            grad_gain_one.reshape(devices, -1),
            grad_gain_two.reshape(devices, -1),
            bias_sum[: QD + KD].reshape(devices, -1),
            bias_sum[QD + KD :].reshape(devices, -1),
        ],
        axis=1,
    )
    small_grads = sum_ordered(
        small_grads.reshape((2,) * (seq_bits + head_bits) + (-1,)), small_steps[::-1], True
    )
    one = gain_cols
    two = one + gain_cols
    three = two + (QD + KD) // devices
    return (
        output,
        grad_inputs,
        small_grads[:one],
        grad_qkv,
        small_grads[two:three],
        small_grads[three:],
        grad_out,
        small_grads[one:two],
        grad_pair[:, :quarter_ff],
        grad_pair[:, quarter_ff:],
        grad_down,
    )


def solution(mesh):
    both = ("seq", "head")
    in_specs = (
        P(both, None),
        P(both),
        P(both, None),
        P(both),
        P("head", "seq"),
        P(both),
        P("seq", "head"),
        P("seq", "head"),
        P("head", "seq"),
        P(both, None),
        P(both),
        P(both),
    )
    out_specs = (
        P(both, None),
        P(both, None),
        P(both),
        P(both, None),
        P(both),
        P(both),
        P("head", "seq"),
        P(both),
        P("seq", "head"),
        P("seq", "head"),
        P("head", "seq"),
    )
    return jax.shard_map(
        per_device, mesh=mesh, in_specs=in_specs, out_specs=out_specs, check_vma=False
    )
```

time: 3810 us -> 566 us (0.15)
  waiting for transfers between devices: 3030 us -> 255 us
  blocking collectives: 214 us -> 0 us
  matrix products: 265 us -> 91.3 us
  other arithmetic: 147 us -> 47 us
  starting transfers between devices: 1.48 us -> 89.8 us
  local copies, waits for them, and re-layouts: 112 us -> 30.1 us
    all_gather x10 -> x3, waiting for transfers between devices: 1460 us -> 5.48 us  [the longest x1 5.44 us: per_device(): down_all = lax.all_gather(down_weight.T, 'seq', axis=0, tiled=True)]
    reduce_scatter x6 -> x3, waiting for transfers between devices: 1500 us -> 51.4 us  [the longest x1 51.4 us: per_device(): lax.psum_scatter(dot_tn(normed_two, d_pair).astype(BF), 'seq', scatter_di...]
    ppermute x1 -> x66, waiting for transfers between devices: 14.4 us -> 198 us  [the longest x24 76.8 us: from_next(): lax.ppermute(block, axis, [(j, (j - apart) % count) for j in range(count)])]
    dot_general x68 -> x13, matrix products: 265 us -> 91.3 us  [the longest x5 33.5 us: dot_nn(): return jnp.dot(left, right, preferred_element_type=F32)]
    all_gather x2 -> x0, blocking collectives: 129 us -> none  [the longest x1 65.8 us: per_device(): lax.all_gather(positions, ('seq', 'head'), axis=0, tiled=True)]
    ppermute x1 -> x66, starting transfers between devices: 0.53 us -> 89.5 us  [the longest x24 56.9 us: from_next(): lax.ppermute(block, axis, [(j, (j - apart) % count) for j in range(count)])]
    concatenate x4 -> x8, other arithmetic: 90.7 us -> 1.97 us  [the longest x1 1.77 us: per_device(): jnp.concatenate([block.T for block in ring_gather(out_weight, 'head')], a...]
    unnamed x2 -> x0, blocking collectives: 85.3 us -> none
  transfers between devices with their start and end apart: 18 -> 72, of which waited for: 11 -> 46; matrix products, arithmetic and copies ran while one was open for 9% -> 24% of each run, Pallas kernels for 0% -> 5%
where the time goes in v1:
time: 566 us; the launch traced here: 558 us
  waiting for transfers between devices  255 us (45%)
  matrix products  91.3 us (16%)
  starting transfers between devices  89.8 us (16%)
  other arithmetic  47 us (8%)
  local copies, waits for them, and re-layouts  30.1 us (5%)
  Pallas kernels  28 us (5%)
  between operations  16.6 us (3%)
    ppermute x24, waiting for transfers between devices, from_next(): lax.ppermute(block, axis, [(j, (j - apart) % count) for j in range(count)])  76.8 us
    ppermute x33, waiting for transfers between devices, swap(): return lax.ppermute(block, axis, [(j, j ^ 1 << bit) for j in range(count)])  67.5 us
    ppermute x24, starting transfers between devices, from_next(): lax.ppermute(block, axis, [(j, (j - apart) % count) for j in range(count)])  56.9 us
    ppermute x9, waiting for transfers between devices, to_next(): lax.ppermute(block, axis, [(j, (j + 1) % count) for j in range(count)])  54.1 us
    reduce_scatter x1, waiting for transfers between devices, per_device(): lax.psum_scatter(dot_tn(normed_two, d_pair).astype(BF), 'seq', scatter_di...  51.4 us
    dot_general x5, matrix products, dot_nn(): return jnp.dot(left, right, preferred_element_type=F32)  33.5 us
    dot_general x4, matrix products, dot_nt(): lax.dot_general(left, right, (((1,), (1,)), ((), ())), preferred_element_...  30 us
    ppermute x33, starting transfers between devices, swap(): return lax.ppermute(block, axis, [(j, j ^ 1 << bit) for j in range(count)])  28 us
  transfers between devices with their start and end apart: 72, of which 46 were waited for; matrix products, arithmetic and copies ran while one was open for 24% of the time, Pallas kernels for 5%

profile of v1, /device:TPU:0, one launch (start us, length us, event | category | flops | bytes accessed | tf_op | source)
XLA Modules:
  0.0 558.3 jit_solution(12638673455281922390)
XLA Ops:
  7.2 5.1 collective-permute-start.25
  12.3 3.4 collective-permute-done.25
  15.7 4.2 collective-permute-start.26
  19.9 2.7 collective-permute-done.26
  22.6 4.3 collective-permute-start.27
  26.9 2.7 collective-permute-done.27
  31.4 3.1 pad_maximum_fusion.3
  35.1 4.3 collective-permute-start.8
  45.1 3.0 collective-permute-start
  49.8 2.2 collective-permute-done.6
  62.7 3.8 collective-permute-done.14
  67.9 3.2 collective-permute-done.11
  71.6 6.3 %collective-permute-done.15 = bf16[2,192,256]{2,1,0:T(8,128)(2,1)S(1)} collective-permute-done((bf16[2,192,256]{2,1,0:T(8,128)(2,1)S(1)}, bf16[2,192,256]{2,1,0:T(8,128)(2,1)S(1)}, u32[]{:S(2)}, u32[]{:S(2)}) %collective-permute-start.15) | collective-permute-done | bytes 196640 | tf_op jit(solution)/shard_map/ppermute | solution.py:37
  84.4 2.8 collective-permute-done.1
  91.4 4.7 collective-permute-done.2
  104.3 3.0 collective-permute-start.32
  112.7 4.4 collective-permute-done.19
  118.4 2.3 collective-permute-done.18
  125.2 2.3 convolution_add_fusion.1
  134.5 13.4 %attend.1 = (f32[2,768,128]{2,1,0:T(8,128)S(1)}, f32[2,1,768]{2,1,0:T(1,128)S(1)}) custom-call(bf16[2,768,128]{2,1,0:T(8,128)(2,1)S(1)} %bitcast.342, bf16[8,2,256,128]{3,2,1,0:T(8,128)(2,1)S(1)} %bitcast.337, bf16[8,2,256,128]{3,2,1,0:T(8,128)(2,1)S(1)} %bitcast.339, s32[8,2,256,1]{3,2,1,0:T(8,128)S(1)} %reshape.581.kc_ref, ...), custom_call_target="tpu_custom_call" | custom-call | flops 2415919104 | bytes 4194304 | tf_op jit(solution)/shard_map/attend/pallas_call | solution.py:226
  151.3 9.1 %collective-permute-done.22 = bf16[512,384]{1,0:T(8,128)(2,1)S(1)} collective-permute-done((bf16[512,384]{1,0:T(8,128)(2,1)S(1)}, bf16[512,384]{1,0:T(8,128)(2,1)S(1)}, u32[]{:S(2)}, u32[]{:S(2)}) %collective-permute-start.22) | collective-permute-done | bytes 393248 | tf_op jit(solution)/shard_map/ppermute | solution.py:42
  160.4 3.2 collective-permute-start.23
  167.1 9.8 %collective-permute-done.23 = bf16[512,384]{1,0:T(8,128)(2,1)S(1)} collective-permute-done((bf16[512,384]{1,0:T(8,128)(2,1)S(1)}, bf16[512,384]{1,0:T(8,128)(2,1)S(1)}, u32[]{:S(2)}, u32[]{:S(2)}) %collective-permute-start.23) | collective-permute-done | bytes 393248 | tf_op jit(solution)/shard_map/ppermute | solution.py:42
  176.9 3.6 collective-permute-start.24
  182.7 6.1 %collective-permute-done.24 = bf16[512,384]{1,0:T(8,128)(2,1)S(1)} collective-permute-done((bf16[512,384]{1,0:T(8,128)(2,1)S(1)}, bf16[512,384]{1,0:T(8,128)(2,1)S(1)}, u32[]{:S(2)}, u32[]{:S(2)}) %collective-permute-start.24) | collective-permute-done | bytes 393248 | tf_op jit(solution)/shard_map/ppermute | solution.py:42
  188.9 6.9 %multiply_reduce_fusion.1 = (f32[512]{0:T(512)S(1)}, f32[512,1536]{1,0:T(8,128)}) fusion(bf16[1536,1536]{1,0:T(8,128)(2,1)} %all-gather.4.cloned.1.call-done, bf16[128,384]{1,0:T(8,128)(2,1)S(1)} %slice.490, bf16[384,384]{1,0:T(8,128)(2,1)S(1)} %slice.489, bf16[256,384]{1,0:T(8,128)(2,1)S(1)} %get-tuple-element.69, ...), kind=kOutput, calls=%fused_computation.11 | convolution fusion | flops 2435579392 | bytes 11012096 | tf_op jit(solution)/shard_map/dot_general | solution.py:156
  195.9 15.4 %fusion.95 = f32[512,4480]{1,0:T(8,128)} fusion(bf16[1536,4480]{1,0:T(8,128)(2,1)} %all-gather.6.cloned.1.call-done, f32[512,1536]{1,0:T(8,128)} %get-tuple-element.122, f32[1536]{0:T(1024)S(1)} %reshape.563, f32[512]{0:T(512)S(1)} %add_rsqrt_fusion), kind=kOutput, calls=%fused_computation.325 | convolution fusion | flops 7048790016 | bytes 26091520 | tf_op jit(solution)/shard_map/dot_general | solution.py:152
  211.3 5.4 all-gather.8.cloned.1.call-done
  216.7 10.8 %multiply_convert_fusion.1 = (bf16[512,2240]{1,0:T(8,128)(2,1)S(1)}, bf16[512,2240]{1,0:T(8,128)(2,1)S(1)}, bf16[512,2240]{1,0:T(8,128)(2,1)S(1)}) fusion(f32[512,4480]{1,0:T(8,128)} %fusion.95, bf16[512,1536]{1,0:T(8,128)(2,1)} %constant_dynamic-update-slice_fusion.10, bf16[1536,2240]{1,0:T(8,128)(2,1)} %all-gather.8.cloned.1.call-done), kind=kOutput, calls=%fused_computation.3 | convolution fusion | flops 3540418560 | bytes 24510464 | tf_op jit(solution)/shard_map/dot_general | solution.py:152
  227.5 12.7 %fusion.1 = f32[512,1536]{1,0:T(8,128)S(1)} fusion(bf16[1536,4480]{1,0:T(8,128)(2,1)} %all-gather.6.cloned.1.call-done, bf16[512,2240]{1,0:T(8,128)(2,1)S(1)} %get-tuple-element.30, bf16[512,2240]{1,0:T(8,128)(2,1)S(1)} %get-tuple-element.29), kind=kOutput, calls=%fused_computation.15 | convolution fusion | flops 7055605760 | bytes 21495808 | tf_op jit(solution)/shard_map/dot_general | solution.py:156
  242.1 6.1 %fusion.109 = f32[512,1536]{1,0:T(8,128)S(1)} fusion(bf16[512,2240]{1,0:T(8,128)(2,1)S(1)} %get-tuple-element.31, bf16[1536,2240]{1,0:T(8,128)(2,1)} %all-gather.8.cloned.1.call-done), kind=kOutput, calls=%fused_computation.339 | convolution fusion | flops 3523215360 | bytes 12320768 | tf_op jit(solution)/shard_map/dot_general | solution.py:156
  249.8 4.5 collective-permute-done.34
  254.5 8.3 %collective-permute-done.28 = bf16[128,1536]{1,0:T(8,128)(2,1)S(1)} collective-permute-done((bf16[128,1536]{1,0:T(8,128)(2,1)S(1)}, bf16[128,1536]{1,0:T(8,128)(2,1)S(1)}, u32[]{:S(2)}, u32[]{:S(2)}) %collective-permute-start.28) | collective-permute-done | bytes 393248 | tf_op jit(solution)/shard_map/ppermute | solution.py:47
  262.9 8.3 %collective-permute-done.35 = bf16[128,1536]{1,0:T(8,128)(2,1)S(1)} collective-permute-done((bf16[128,1536]{1,0:T(8,128)(2,1)S(1)}, bf16[128,1536]{1,0:T(8,128)(2,1)S(1)}, u32[]{:S(2)}, u32[]{:S(2)}) %collective-permute-start.35) | collective-permute-done | bytes 393248 | tf_op jit(solution)/shard_map/ppermute | solution.py:47
  271.3 8.3 %collective-permute-done.29 = bf16[128,1536]{1,0:T(8,128)(2,1)S(1)} collective-permute-done((bf16[128,1536]{1,0:T(8,128)(2,1)S(1)}, bf16[128,1536]{1,0:T(8,128)(2,1)S(1)}, u32[]{:S(2)}, u32[]{:S(2)}) %collective-permute-start.29) | collective-permute-done | bytes 393248 | tf_op jit(solution)/shard_map/ppermute | solution.py:47
  279.7 8.3 %collective-permute-done.36 = bf16[128,1536]{1,0:T(8,128)(2,1)S(1)} collective-permute-done((bf16[128,1536]{1,0:T(8,128)(2,1)S(1)}, bf16[128,1536]{1,0:T(8,128)(2,1)S(1)}, u32[]{:S(2)}, u32[]{:S(2)}) %collective-permute-start.36) | collective-permute-done | bytes 393248 | tf_op jit(solution)/shard_map/ppermute | solution.py:47
  288.9 6.9 %collective-permute-done.30 = bf16[128,1536]{1,0:T(8,128)(2,1)S(1)} collective-permute-done((bf16[128,1536]{1,0:T(8,128)(2,1)S(1)}, bf16[128,1536]{1,0:T(8,128)(2,1)S(1)}, u32[]{:S(2)}, u32[]{:S(2)}) %collective-permute-start.30) | collective-permute-done | bytes 393248 | tf_op jit(solution)/shard_map/ppermute | solution.py:47
  298.7 9.0 %collective-permute-done.63 = bf16[128,1536]{1,0:T(8,128)(2,1)S(1)} collective-permute-done((bf16[128,1536]{1,0:T(8,128)(2,1)S(1)}, bf16[128,1536]{1,0:T(8,128)(2,1)S(1)}, u32[]{:S(2)}, u32[]{:S(2)}) %collective-permute-start.63) | collective-permute-done | bytes 393248 | tf_op jit(solution)/shard_map/ppermute | solution.py:42
  307.7 3.3 collective-permute-start.64
  311.0 7.1 %collective-permute-done.64 = bf16[128,1536]{1,0:T(8,128)(2,1)S(1)} collective-permute-done((bf16[128,1536]{1,0:T(8,128)(2,1)S(1)}, bf16[128,1536]{1,0:T(8,128)(2,1)S(1)}, u32[]{:S(2)}, u32[]{:S(2)}) %collective-permute-start.64) | collective-permute-done | bytes 393248 | tf_op jit(solution)/shard_map/ppermute | solution.py:42
  318.1 4.3 collective-permute-start.65
  322.3 6.1 %collective-permute-done.65 = bf16[128,1536]{1,0:T(8,128)(2,1)S(1)} collective-permute-done((bf16[128,1536]{1,0:T(8,128)(2,1)S(1)}, bf16[128,1536]{1,0:T(8,128)(2,1)S(1)}, u32[]{:S(2)}, u32[]{:S(2)}) %collective-permute-start.65) | collective-permute-done | bytes 393248 | tf_op jit(solution)/shard_map/ppermute | solution.py:42
  330.6 9.0 %convolution_convert_fusion.1 = bf16[1536,2240]{1,0:T(8,128)(2,1)} fusion(bf16[512,1536]{1,0:T(8,128)(2,1)} %constant_dynamic-update-slice_fusion.10, bf16[512,2240]{1,0:T(8,128)(2,1)} %copy-done.56), kind=kOutput, calls=%fused_computation.1 | convolution fusion | flops 3526656000 | bytes 10747904 | tf_op jit(solution)/shard_map/dot_general | solution.py:160
  339.6 14.1 %convolution_convert_fusion = bf16[1536,4480]{1,0:T(8,128)(2,1)} fusion(bf16[512,2240]{1,0:T(8,128)(2,1)} %copy-done.58, bf16[512,2240]{1,0:T(8,128)(2,1)} %copy-done.57, f32[512,1536]{1,0:T(8,128)} %get-tuple-element.122, f32[1536]{0:T(1024)S(1)} %reshape.563, f32[512]{0:T(512)S(1)} %add_rsqrt_fusion), kind=kOutput, calls=%fused_computation | convolution fusion | flops 7064846336 | bytes 21504000 | tf_op jit(solution)/shard_map/dot_general | solution.py:160
  353.7 3.1 convolution_convert_fusion.4
  357.0 4.9 collective-permute-start.38
  364.0 2.4 collective-permute-done.38
  370.3 14.6 %attend_back.1 = (f32[2,768,128]{2,1,0:T(8,128)S(1)}, bf16[8,2,256,128]{3,2,1,0:T(8,128)(2,1)S(1)}, bf16[8,2,256,128]{3,2,1,0:T(8,128)(2,1)S(1)}) custom-call(bf16[2,768,128]{2,1,0:T(8,128)(2,1)S(1)} %bitcast.343, bf16[2,768,128]{2,1,0:T(8,128)(2,1)S(1)} %bitcast.341, bf16[8,2,256,128]{3,2,1,0:T(8,128)(2,1)S(1)} %bitcast.338, ...), custom_call_target="tpu_custom_call" | custom-call | flops 6039797760 | bytes 6291456 | tf_op jit(solution)/shard_map/attend_back/pallas_call | solution.py:296
  390.1 3.0 fusion.98
  397.0 9.2 %collective-permute-done.43 = bf16[2,2,256,128]{3,2,1,0:T(8,128)(2,1)S(1)} collective-permute-done((bf16[2,2,256,128]{3,2,1,0:T(8,128)(2,1)}, bf16[2,2,256,128]{3,2,1,0:T(8,128)(2,1)S(1)}, u32[]{:S(2)}, u32[]{:S(2)}) %collective-permute-start.43) | collective-permute-done | bytes 262176 | tf_op jit(solution)/shard_map/ppermute | solution.py:37
  406.2 3.6 collective-permute-done.41
  412.4 5.6 %collective-permute-done.44 = bf16[1,2,256,128]{3,2,1,0:T(8,128)(2,1)S(1)} collective-permute-done((bf16[1,2,256,128]{3,2,1,0:T(8,128)(2,1)S(1)}, bf16[1,2,256,128]{3,2,1,0:T(8,128)(2,1)S(1)}, u32[]{:S(2)}, u32[]{:S(2)}) %collective-permute-start.44) | collective-permute-done | bytes 131104 | tf_op jit(solution)/shard_map/ppermute | solution.py:37
  420.4 3.9 collective-permute-done.45
  426.2 4.2 multiply_reduce_fusion
  441.3 2.7 convolution_convert_fusion.2
  444.2 4.6 collective-permute-done.52
  450.3 2.2 collective-permute-done.53
  458.6 2.6 collective-permute-done.58
  466.0 2.7 collective-permute-done.56
  473.0 7.6 %collective-permute-done.61 = bf16[48,512]{1,0:T(8,128)(2,1)S(1)} collective-permute-done((bf16[48,512]{1,0:T(8,128)(2,1)S(1)}, bf16[48,512]{1,0:T(8,128)(2,1)S(1)}, u32[]{:S(2)}, u32[]{:S(2)}) %collective-permute-start.61) | collective-permute-done | bytes 49184 | tf_op jit(solution)/shard_map/ppermute | solution.py:42
  481.0 9.5 %collective-permute-done.48 = bf16[128,1536]{1,0:T(8,128)(2,1)S(1)} collective-permute-done((bf16[128,1536]{1,0:T(8,128)(2,1)S(1)}, bf16[128,1536]{1,0:T(8,128)(2,1)S(1)}, u32[]{:S(2)}, u32[]{:S(2)}) %collective-permute-start.48) | collective-permute-done | bytes 393248 | tf_op jit(solution)/shard_map/ppermute | solution.py:47
  493.5 2.5 convert_bitcast_fusion
  496.0 51.4 %reduce-scatter.6.cloned.1.call-done = bf16[192,4480]{1,0:T(8,128)(2,1)} async-done(((bf16[1536,4480]{1,0:T(8,128)(2,1)}), bf16[192,4480]{1,0:T(8,128)(2,1)}) %reduce-scatter.6.cloned.1.call-update) | async-done | bytes 1720336 | tf_op jit(solution)/shard_map/reduce_scatter | solution.py:584
  547.4 3.6 fusion.101
  (443 shorter events, 130.1 us)
Async XLA Ops:
  7.2 181.7 %all-gather.4.cloned.1.call-start = ((), (), s32[]{:S(2)}) async-start(), calls=%async_computation.3 | async-start | bytes 5308416 | tf_op jit(solution)/shard_map/all_gather | solution.py:456
  7.2 8.5 %collective-permute-start.25 = (bf16[384,192]{0,1:T(8,128)(2,1)}, bf16[384,192]{0,1:T(8,128)(2,1)S(1)}, u32[]{:S(2)}, u32[]{:S(2)}) collective-permute-start(bf16[384,192]{0,1:T(8,128)(2,1)} %param.16), channel_id=1, source_target_pairs={{0,3},{1,0},{2,1},{3,2},{4,7},{5,4},{6,5},{7,6},{8,11},{9,8},{10,9... | collective-permute-start | bytes 442376 | tf_op jit(solution)/shard_map/ppermute | solution.py:42
  15.7 6.8 %collective-permute-start.26 = (bf16[384,192]{0,1:T(8,128)(2,1)S(1)}, bf16[384,192]{0,1:T(8,128)(2,1)S(1)}, u32[]{:S(2)}, u32[]{:S(2)}) collective-permute-start(bf16[384,192]{0,1:T(8,128)(2,1)S(1)} %collective-permute-done.25), channel_id=1, source_target_pairs={{0,3},{1,0},{2,1},{3,2},{4,7},{5,4},{6,5},{7,6},{8,11},{9,8},{10,9... | collective-permute-start | bytes 442376 | tf_op jit(solution)/shard_map/ppermute | solution.py:42
  22.6 6.9 %collective-permute-start.27 = (bf16[384,192]{0,1:T(8,128)(2,1)S(1)}, bf16[384,192]{0,1:T(8,128)(2,1)S(1)}, u32[]{:S(2)}, u32[]{:S(2)}) collective-permute-start(bf16[384,192]{0,1:T(8,128)(2,1)S(1)} %collective-permute-done.26), channel_id=1, source_target_pairs={{0,3},{1,0},{2,1},{3,2},{4,7},{5,4},{6,5},{7,6},{8,11},{9,8},{10,9... | collective-permute-start | bytes 442376 | tf_op jit(solution)/shard_map/ppermute | solution.py:42
  31.4 164.5 %all-gather.6.cloned.1.call-start = ((), (), s32[]{:S(2)}) async-start(), calls=%async_computation.4 | async-start | bytes 15482880 | tf_op jit(solution)/shard_map/all_gather | solution.py:429
  34.6 182.1 %all-gather.8.cloned.1.call-start = ((), (), s32[]{:S(2)}) async-start(), calls=%async_computation.5 | async-start | bytes 7962624 | tf_op jit(solution)/shard_map/all_gather | solution.py:430
  34.8 4.6 collective-permute-start.3
  35.1 24.2 %collective-permute-start.8 = (bf16[48,640]{1,0:T(8,128)(2,1)S(1)}, bf16[48,640]{1,0:T(8,128)(2,1)S(1)}, u32[]{:S(2)}, u32[]{:S(2)}) collective-permute-start(bf16[48,640]{1,0:T(8,128)(2,1)S(1)} %pad_maximum_fusion.26), channel_id=1, source_target_pairs={{0,3},{1,0},{2,1},{3,2},{4,7},{5,4},{6,5},{7,6},{8,11},{9,8},{10,9... | collective-permute-start | bytes 184328 | tf_op jit(solution)/shard_map/ppermute | solution.py:42
  39.5 4.6 collective-permute-start.4
  41.3 18.0 %collective-permute-start.9 = (bf16[48,640]{1,0:T(8,128)(2,1)S(1)}, bf16[48,640]{1,0:T(8,128)(2,1)S(1)}, u32[]{:S(2)}, u32[]{:S(2)}) collective-permute-start(bf16[48,640]{1,0:T(8,128)(2,1)S(1)} %pad_maximum_fusion.27), channel_id=1, source_target_pairs={{0,2},{1,3},{2,0},{3,1},{4,6},{5,7},{6,4},{7,5},{8,10},{9,11},{10,... | collective-permute-start | bytes 184328 | tf_op jit(solution)/shard_map/ppermute | solution.py:42
  44.2 15.2 %collective-permute-start.10 = (bf16[48,640]{1,0:T(8,128)(2,1)S(1)}, bf16[48,640]{1,0:T(8,128)(2,1)S(1)}, u32[]{:S(2)}, u32[]{:S(2)}) collective-permute-start(bf16[48,640]{1,0:T(8,128)(2,1)S(1)} %pad_maximum_fusion.28), channel_id=1, source_target_pairs={{0,1},{1,2},{2,3},{3,0},{4,5},{5,6},{6,7},{7,4},{8,9},{9,10},{10,1... | collective-permute-start | bytes 184328 | tf_op jit(solution)/shard_map/ppermute | solution.py:42
  45.1 32.9 %collective-permute-start = (bf16[128,1536]{1,0:T(8,128)(2,1)S(1)}, bf16[128,1536]{1,0:T(8,128)(2,1)}, u32[]{:S(2)}, u32[]{:S(2)}) collective-permute-start(bf16[128,1536]{1,0:T(8,128)(2,1)S(1)} %copy-done.17), channel_id=1, source_target_pairs={{0,3},{1,0},{2,1},{3,2},{4,7},{5,4},{6,5},{7,6},{8,11},{9,8},{10,9... | collective-permute-start | bytes 1179656 | tf_op jit(solution)/shard_map/ppermute | solution.py:42
  48.1 443.8 %reduce-scatter.4.cloned.1.call-start = ((), (), s32[]{:S(2)}) async-start(), calls=%async_computation.6 | async-start | bytes 1327104 | tf_op jit(solution)/shard_map/reduce_scatter | solution.py:590
  55.9 48.4 %collective-permute-start.31 = (bf16[128,1536]{1,0:T(8,128)(2,1)S(1)}, bf16[128,1536]{1,0:T(8,128)(2,1)}, u32[]{:S(2)}, u32[]{:S(2)}) collective-permute-start(bf16[128,1536]{1,0:T(8,128)(2,1)S(1)} %copy-done.15), channel_id=1, source_target_pairs={{0,3},{1,0},{2,1},{3,2},{4,7},{5,4},{6,5},{7,6},{8,11},{9,8},{10,9... | collective-permute-start | bytes 1179656 | tf_op jit(solution)/shard_map/ppermute | solution.py:42
  59.5 6.9 %collective-permute-start.14 = (bf16[192,256]{1,0:T(8,128)(2,1)S(1)}, bf16[192,256]{1,0:T(8,128)(2,1)S(1)}, u32[]{:S(2)}, u32[]{:S(2)}) collective-permute-start(bf16[192,256]{1,0:T(8,128)(2,1)S(1)} %slice.475), channel_id=1, source_target_pairs={{0,16},{4,20},{8,24},{12,28},{16,0},{20,4},{24,8},{28,12},{1,17},{... | collective-permute-start | bytes 294920 | tf_op jit(solution)/shard_map/ppermute | solution.py:37
  61.2 9.9 %collective-permute-start.11 = (bf16[192,384]{1,0:T(8,128)(2,1)S(1)}, bf16[192,384]{1,0:T(8,128)(2,1)S(1)}, u32[]{:S(2)}, u32[]{:S(2)}) collective-permute-start(bf16[192,384]{1,0:T(8,128)(2,1)S(1)} %slice.469), channel_id=1, source_target_pairs={{0,8},{4,12},{8,0},{12,4},{16,24},{20,28},{24,16},{28,20},{1,9},{5... | collective-permute-start | bytes 442376 | tf_op jit(solution)/shard_map/ppermute | solution.py:37
  66.5 11.5 %collective-permute-start.15 = (bf16[2,192,256]{2,1,0:T(8,128)(2,1)S(1)}, bf16[2,192,256]{2,1,0:T(8,128)(2,1)S(1)}, u32[]{:S(2)}, u32[]{:S(2)}) collective-permute-start(bf16[2,192,256]{2,1,0:T(8,128)(2,1)S(1)} %pad_maximum_fusion.22), channel_id=1, source_target_pairs={{0,8},{4,12},{8,0},{12,4},{16,24},{20,28},{24,16},{28,20},{1,9},{5... | collective-permute-start | bytes 589832 | tf_op jit(solution)/shard_map/ppermute | solution.py:37
  71.2 11.4 %collective-permute-start.12 = (bf16[2,192,384]{2,1,0:T(8,128)(2,1)S(1)}, bf16[2,192,384]{2,1,0:T(8,128)(2,1)}, u32[]{:S(2)}, u32[]{:S(2)}) collective-permute-start(bf16[2,192,384]{2,1,0:T(8,128)(2,1)S(1)} %pad_maximum_fusion.17), channel_id=1, source_target_pairs={{0,16},{4,20},{8,24},{12,28},{16,0},{20,4},{24,8},{28,12},{1,17},{... | collective-permute-start | bytes 884744 | tf_op jit(solution)/shard_map/ppermute | solution.py:37
  78.0 9.2 %collective-permute-start.1 = (bf16[128,1536]{1,0:T(8,128)(2,1)}, bf16[128,1536]{1,0:T(8,128)(2,1)}, u32[]{:S(2)}, u32[]{:S(2)}) collective-permute-start(bf16[128,1536]{1,0:T(8,128)(2,1)} %collective-permute-done), channel_id=1, source_target_pairs={{0,3},{1,0},{2,1},{3,2},{4,7},{5,4},{6,5},{7,6},{8,11},{9,8},{10,9... | collective-permute-start | bytes 1179656 | tf_op jit(solution)/shard_map/ppermute | solution.py:42
  79.5 10.7 %collective-permute-start.16 = (bf16[2,2,192,256]{3,2,0,1:T(8,128)(2,1)}, bf16[2,2,192,256]{3,2,0,1:T(8,128)(2,1)}, u32[]{:S(2)}, u32[]{:S(2)}) collective-permute-start(bf16[2,2,192,256]{3,2,0,1:T(8,128)(2,1)} %pad_maximum_fusion.13), channel_id=1, source_target_pairs={{0,4},{4,0},{8,12},{12,8},{16,20},{20,16},{24,28},{28,24},{1,5},{5... | collective-permute-start | bytes 1179656 | tf_op jit(solution)/shard_map/ppermute | solution.py:37
  87.2 9.0 %collective-permute-start.2 = (bf16[128,1536]{1,0:T(8,128)(2,1)}, bf16[128,1536]{1,0:T(8,128)(2,1)S(1)}, u32[]{:S(2)}, u32[]{:S(2)}) collective-permute-start(bf16[128,1536]{1,0:T(8,128)(2,1)} %collective-permute-done.1), channel_id=1, source_target_pairs={{0,3},{1,0},{2,1},{3,2},{4,7},{5,4},{6,5},{7,6},{8,11},{9,8},{10,9... | collective-permute-start | bytes 1179656 | tf_op jit(solution)/shard_map/ppermute | solution.py:42
  90.2 21.3 %collective-permute-start.13 = (bf16[2,2,192,384]{3,2,1,0:T(8,128)(2,1)}, bf16[2,2,192,384]{3,2,1,0:T(8,128)(2,1)}, u32[]{:S(2)}, u32[]{:S(2)}) collective-permute-start(bf16[2,2,192,384]{3,2,1,0:T(8,128)(2,1)} %pad_maximum_fusion.10), channel_id=1, source_target_pairs={{0,4},{4,0},{8,12},{12,8},{16,20},{20,16},{24,28},{28,24},{1,5},{5... | collective-permute-start | bytes 1769480 | tf_op jit(solution)/shard_map/ppermute | solution.py:37
  100.8 8.6 %collective-permute-start.17 = (bf16[1,2,256,128]{3,2,1,0:T(8,128)(2,1)S(1)}, bf16[1,2,256,128]{3,2,1,0:T(8,128)(2,1)}, u32[]{:S(2)}, u32[]{:S(2)}) collective-permute-start(bf16[1,2,256,128]{3,2,1,0:T(8,128)(2,1)S(1)} %bitcast.367), channel_id=1, source_target_pairs={{0,8},{4,12},{8,0},{12,4},{16,24},{20,28},{24,16},{28,20},{1,9},{5... | collective-permute-start | bytes 393224 | tf_op jit(solution)/shard_map/ppermute | solution.py:37
  104.3 46.5 %collective-permute-start.32 = (bf16[128,1536]{1,0:T(8,128)(2,1)}, bf16[128,1536]{1,0:T(8,128)(2,1)}, u32[]{:S(2)}, u32[]{:S(2)}) collective-permute-start(bf16[128,1536]{1,0:T(8,128)(2,1)} %collective-permute-done.31), channel_id=1, source_target_pairs={{0,3},{1,0},{2,1},{3,2},{4,7},{5,4},{6,5},{7,6},{8,11},{9,8},{10,9... | collective-permute-start | bytes 1179656 | tf_op jit(solution)/shard_map/ppermute | solution.py:42
  108.4 8.7 %collective-permute-start.19 = (bf16[1,2,256,128]{3,2,1,0:T(8,128)(2,1)S(1)}, bf16[1,2,256,128]{3,2,1,0:T(8,128)(2,1)S(1)}, u32[]{:S(2)}, u32[]{:S(2)}) collective-permute-start(bf16[1,2,256,128]{3,2,1,0:T(8,128)(2,1)S(1)} %bitcast.370), channel_id=1, source_target_pairs={{0,16},{4,20},{8,24},{12,28},{16,0},{20,4},{24,8},{28,12},{1,17},{... | collective-permute-start | bytes 393224 | tf_op jit(solution)/shard_map/ppermute | solution.py:37
  110.3 10.4 %collective-permute-start.18 = (bf16[2,2,256,128]{3,2,1,0:T(8,128)(2,1)S(1)}, bf16[2,2,256,128]{3,2,1,0:T(8,128)(2,1)S(1)}, u32[]{:S(2)}, u32[]{:S(2)}) collective-permute-start(bf16[2,2,256,128]{3,2,1,0:T(8,128)(2,1)S(1)} %pad_maximum_fusion.18), channel_id=1, source_target_pairs={{0,16},{4,20},{8,24},{12,28},{16,0},{20,4},{24,8},{28,12},{1,17},{... | collective-permute-start | bytes 786440 | tf_op jit(solution)/shard_map/ppermute | solution.py:37
  117.1 6.4 %collective-permute-start.20 = (bf16[2,2,256,128]{3,2,1,0:T(8,128)(2,1)S(1)}, bf16[2,2,256,128]{3,2,1,0:T(8,128)(2,1)S(1)}, u32[]{:S(2)}, u32[]{:S(2)}) collective-permute-start(bf16[2,2,256,128]{3,2,1,0:T(8,128)(2,1)S(1)} %pad_maximum_fusion.19), channel_id=1, source_target_pairs={{0,8},{4,12},{8,0},{12,4},{16,24},{20,28},{24,16},{28,20},{1,9},{5... | collective-permute-start | bytes 786440 | tf_op jit(solution)/shard_map/ppermute | solution.py:37
  125.1 7.3 %collective-permute-start.21 = (bf16[2,4,2,256,128]{4,3,2,1,0:T(8,128)(2,1)}, bf16[2,4,2,256,128]{4,3,2,1,0:T(8,128)(2,1)}, u32[]{:S(2)}, u32[]{:S(2)}) collective-permute-start(bf16[2,4,2,256,128]{4,3,2,1,0:T(8,128)(2,1)} %get-tuple-element.53), channel_id=1, source_target_pairs={{0,4},{4,0},{8,12},{12,8},{16,20},{20,16},{24,28},{28,24},{1,5},{5... | collective-permute-start | bytes 3145736 | tf_op jit(solution)/shard_map/ppermute | solution.py:37
  148.5 12.0 %collective-permute-start.22 = (bf16[512,384]{1,0:T(8,128)(2,1)S(1)}, bf16[512,384]{1,0:T(8,128)(2,1)S(1)}, u32[]{:S(2)}, u32[]{:S(2)}) collective-permute-start(bf16[512,384]{1,0:T(8,128)(2,1)S(1)} %bitcast.385), channel_id=1, source_target_pairs={{0,3},{1,0},{2,1},{3,2},{4,7},{5,4},{6,5},{7,6},{8,11},{9,8},{10,9... | collective-permute-start | bytes 1179656 | tf_op jit(solution)/shard_map/ppermute | solution.py:42
  150.7 29.8 %collective-permute-start.33 = (bf16[128,1536]{1,0:T(8,128)(2,1)}, bf16[128,1536]{1,0:T(8,128)(2,1)S(1)}, u32[]{:S(2)}, u32[]{:S(2)}) collective-permute-start(bf16[128,1536]{1,0:T(8,128)(2,1)} %collective-permute-done.32), channel_id=1, source_target_pairs={{0,3},{1,0},{2,1},{3,2},{4,7},{5,4},{6,5},{7,6},{8,11},{9,8},{10,9... | collective-permute-start | bytes 1179656 | tf_op jit(solution)/shard_map/ppermute | solution.py:42
  160.4 16.5 %collective-permute-start.23 = (bf16[512,384]{1,0:T(8,128)(2,1)S(1)}, bf16[512,384]{1,0:T(8,128)(2,1)S(1)}, u32[]{:S(2)}, u32[]{:S(2)}) collective-permute-start(bf16[512,384]{1,0:T(8,128)(2,1)S(1)} %collective-permute-done.22), channel_id=1, source_target_pairs={{0,3},{1,0},{2,1},{3,2},{4,7},{5,4},{6,5},{7,6},{8,11},{9,8},{10,9... | collective-permute-start | bytes 1179656 | tf_op jit(solution)/shard_map/ppermute | solution.py:42
  176.9 11.9 %collective-permute-start.24 = (bf16[512,384]{1,0:T(8,128)(2,1)S(1)}, bf16[512,384]{1,0:T(8,128)(2,1)S(1)}, u32[]{:S(2)}, u32[]{:S(2)}) collective-permute-start(bf16[512,384]{1,0:T(8,128)(2,1)S(1)} %collective-permute-done.23), channel_id=1, source_target_pairs={{0,3},{1,0},{2,1},{3,2},{4,7},{5,4},{6,5},{7,6},{8,11},{9,8},{10,9... | collective-permute-start | bytes 1179656 | tf_op jit(solution)/shard_map/ppermute | solution.py:42
  240.3 14.0 %collective-permute-start.34 = (bf16[128,1536]{1,0:T(8,128)(2,1)S(1)}, bf16[128,1536]{1,0:T(8,128)(2,1)S(1)}, u32[]{:S(2)}, u32[]{:S(2)}) collective-permute-start(bf16[128,1536]{1,0:T(8,128)(2,1)S(1)} %slice.760), channel_id=1, source_target_pairs={{0,1},{1,2},{2,3},{3,0},{4,5},{5,6},{6,7},{7,4},{8,9},{9,10},{10,1... | collective-permute-start | bytes 1179656 | tf_op jit(solution)/shard_map/ppermute | solution.py:47
  248.2 14.5 %collective-permute-start.28 = (bf16[128,1536]{1,0:T(8,128)(2,1)S(1)}, bf16[128,1536]{1,0:T(8,128)(2,1)S(1)}, u32[]{:S(2)}, u32[]{:S(2)}) collective-permute-start(bf16[128,1536]{1,0:T(8,128)(2,1)S(1)} %slice.761), channel_id=1, source_target_pairs={{0,1},{1,2},{2,3},{3,0},{4,5},{5,6},{6,7},{7,4},{8,9},{9,10},{10,1... | collective-permute-start | bytes 1179656 | tf_op jit(solution)/shard_map/ppermute | solution.py:47
  254.4 16.8 %collective-permute-start.35 = (bf16[128,1536]{1,0:T(8,128)(2,1)S(1)}, bf16[128,1536]{1,0:T(8,128)(2,1)S(1)}, u32[]{:S(2)}, u32[]{:S(2)}) collective-permute-start(bf16[128,1536]{1,0:T(8,128)(2,1)S(1)} %fusion.33), channel_id=1, source_target_pairs={{0,1},{1,2},{2,3},{3,0},{4,5},{5,6},{6,7},{7,4},{8,9},{9,10},{10,1... | collective-permute-start | bytes 1179656 | tf_op jit(solution)/shard_map/ppermute | solution.py:47
  262.8 16.8 %collective-permute-start.29 = (bf16[128,1536]{1,0:T(8,128)(2,1)S(1)}, bf16[128,1536]{1,0:T(8,128)(2,1)S(1)}, u32[]{:S(2)}, u32[]{:S(2)}) collective-permute-start(bf16[128,1536]{1,0:T(8,128)(2,1)S(1)} %fusion.35), channel_id=1, source_target_pairs={{0,1},{1,2},{2,3},{3,0},{4,5},{5,6},{6,7},{7,4},{8,9},{9,10},{10,1... | collective-permute-start | bytes 1179656 | tf_op jit(solution)/shard_map/ppermute | solution.py:47
  271.2 16.8 %collective-permute-start.36 = (bf16[128,1536]{1,0:T(8,128)(2,1)S(1)}, bf16[128,1536]{1,0:T(8,128)(2,1)S(1)}, u32[]{:S(2)}, u32[]{:S(2)}) collective-permute-start(bf16[128,1536]{1,0:T(8,128)(2,1)S(1)} %fusion.34), channel_id=1, source_target_pairs={{0,1},{1,2},{2,3},{3,0},{4,5},{5,6},{6,7},{7,4},{8,9},{9,10},{10,1... | collective-permute-start | bytes 1179656 | tf_op jit(solution)/shard_map/ppermute | solution.py:47
  279.7 16.1 %collective-permute-start.30 = (bf16[128,1536]{1,0:T(8,128)(2,1)S(1)}, bf16[128,1536]{1,0:T(8,128)(2,1)S(1)}, u32[]{:S(2)}, u32[]{:S(2)}) collective-permute-start(bf16[128,1536]{1,0:T(8,128)(2,1)S(1)} %fusion.36), channel_id=1, source_target_pairs={{0,1},{1,2},{2,3},{3,0},{4,5},{5,6},{6,7},{7,4},{8,9},{9,10},{10,1... | collective-permute-start | bytes 1179656 | tf_op jit(solution)/shard_map/ppermute | solution.py:47
  297.2 10.5 %collective-permute-start.63 = (bf16[128,1536]{1,0:T(8,128)(2,1)S(1)}, bf16[128,1536]{1,0:T(8,128)(2,1)S(1)}, u32[]{:S(2)}, u32[]{:S(2)}) collective-permute-start(bf16[128,1536]{1,0:T(8,128)(2,1)S(1)} %get-tuple-element.25), channel_id=1, source_target_pairs={{0,3},{1,0},{2,1},{3,2},{4,7},{5,4},{6,5},{7,6},{8,11},{9,8},{10,9... | collective-permute-start | bytes 1179656 | tf_op jit(solution)/shard_map/ppermute | solution.py:42
  307.7 10.4 %collective-permute-start.64 = (bf16[128,1536]{1,0:T(8,128)(2,1)S(1)}, bf16[128,1536]{1,0:T(8,128)(2,1)S(1)}, u32[]{:S(2)}, u32[]{:S(2)}) collective-permute-start(bf16[128,1536]{1,0:T(8,128)(2,1)S(1)} %collective-permute-done.63), channel_id=1, source_target_pairs={{0,3},{1,0},{2,1},{3,2},{4,7},{5,4},{6,5},{7,6},{8,11},{9,8},{10,9... | collective-permute-start | bytes 1179656 | tf_op jit(solution)/shard_map/ppermute | solution.py:42
  318.1 10.4 %collective-permute-start.65 = (bf16[128,1536]{1,0:T(8,128)(2,1)S(1)}, bf16[128,1536]{1,0:T(8,128)(2,1)S(1)}, u32[]{:S(2)}, u32[]{:S(2)}) collective-permute-start(bf16[128,1536]{1,0:T(8,128)(2,1)S(1)} %collective-permute-done.64), channel_id=1, source_target_pairs={{0,3},{1,0},{2,1},{3,2},{4,7},{5,4},{6,5},{7,6},{8,11},{9,8},{10,9... | collective-permute-start | bytes 1179656 | tf_op jit(solution)/shard_map/ppermute | solution.py:42
  330.5 163.0 %reduce-scatter.8.cloned.1.call-start = ((), (), s32[]{:S(2)}) async-start(), calls=%async_computation.8 | async-start | bytes 7962624 | tf_op jit(solution)/shard_map/reduce_scatter | solution.py:587
  339.6 207.9 %reduce-scatter.6.cloned.1.call-start = ((), (), s32[]{:S(2)}) async-start(), calls=%async_computation.7 | async-start | bytes 15482880 | tf_op jit(solution)/shard_map/reduce_scatter | solution.py:584
  356.9 7.1 %collective-permute-start.39 = (bf16[128,384]{1,0:T(8,128)(2,1)S(1)}, bf16[128,384]{1,0:T(8,128)(2,1)S(1)}, u32[]{:S(2)}, u32[]{:S(2)}) collective-permute-start(bf16[128,384]{1,0:T(8,128)(2,1)S(1)} %get-tuple-element.65), channel_id=1, source_target_pairs={{0,1},{1,2},{2,3},{3,0},{4,5},{5,6},{6,7},{7,4},{8,9},{9,10},{10,1... | collective-permute-start | bytes 294920 | tf_op jit(solution)/shard_map/ppermute | solution.py:42
  357.0 9.4 %collective-permute-start.38 = (bf16[128,384]{1,0:T(8,128)(2,1)S(1)}, bf16[128,384]{1,0:T(8,128)(2,1)S(1)}, u32[]{:S(2)}, u32[]{:S(2)}) collective-permute-start(bf16[128,384]{1,0:T(8,128)(2,1)S(1)} %get-tuple-element.66), channel_id=1, source_target_pairs={{0,2},{1,3},{2,0},{3,1},{4,6},{5,7},{6,4},{7,5},{8,10},{9,11},{10,... | collective-permute-start | bytes 294920 | tf_op jit(solution)/shard_map/ppermute | solution.py:42
  361.8 5.5 collective-permute-start.37
  393.8 12.3 %collective-permute-start.43 = (bf16[2,2,256,128]{3,2,1,0:T(8,128)(2,1)}, bf16[2,2,256,128]{3,2,1,0:T(8,128)(2,1)S(1)}, u32[]{:S(2)}, u32[]{:S(2)}) collective-permute-start(bf16[2,2,256,128]{3,2,1,0:T(8,128)(2,1)} %pad_maximum_fusion.21), channel_id=1, source_target_pairs={{0,16},{4,20},{8,24},{12,28},{16,0},{20,4},{24,8},{28,12},{1,17},{... | collective-permute-start | bytes 786440 | tf_op jit(solution)/shard_map/ppermute | solution.py:37
  395.7 14.1 %collective-permute-start.41 = (bf16[2,2,256,128]{3,2,1,0:T(8,128)(2,1)}, bf16[2,2,256,128]{3,2,1,0:T(8,128)(2,1)S(1)}, u32[]{:S(2)}, u32[]{:S(2)}) collective-permute-start(bf16[2,2,256,128]{3,2,1,0:T(8,128)(2,1)} %pad_maximum_fusion.20), channel_id=1, source_target_pairs={{0,8},{4,12},{8,0},{12,4},{16,24},{20,28},{24,16},{28,20},{1,9},{5... | collective-permute-start | bytes 786440 | tf_op jit(solution)/shard_map/ppermute | solution.py:37
  409.8 8.2 %collective-permute-start.44 = (bf16[1,2,256,128]{3,2,1,0:T(8,128)(2,1)S(1)}, bf16[1,2,256,128]{3,2,1,0:T(8,128)(2,1)S(1)}, u32[]{:S(2)}, u32[]{:S(2)}) collective-permute-start(bf16[1,2,256,128]{3,2,1,0:T(8,128)(2,1)S(1)} %get-tuple-element.36), channel_id=1, source_target_pairs={{0,8},{4,12},{8,0},{12,4},{16,24},{20,28},{24,16},{28,20},{1,9},{5... | collective-permute-start | bytes 393224 | tf_op jit(solution)/shard_map/ppermute | solution.py:37
  410.7 8.4 %collective-permute-start.42 = (bf16[1,2,256,128]{3,2,1,0:T(8,128)(2,1)S(1)}, bf16[1,2,256,128]{3,2,1,0:T(8,128)(2,1)S(1)}, u32[]{:S(2)}, u32[]{:S(2)}) collective-permute-start(bf16[1,2,256,128]{3,2,1,0:T(8,128)(2,1)S(1)} %get-tuple-element.35), channel_id=1, source_target_pairs={{0,16},{4,20},{8,24},{12,28},{16,0},{20,4},{24,8},{28,12},{1,17},{... | collective-permute-start | bytes 393224 | tf_op jit(solution)/shard_map/ppermute | solution.py:37
  419.3 5.0 collective-permute-start.45
  431.9 4.7 collective-permute-start.49
  439.0 15.2 %collective-permute-start.46 = (bf16[128,1536]{1,0:T(8,128)(2,1)S(1)}, bf16[128,1536]{1,0:T(8,128)(2,1)S(1)}, u32[]{:S(2)}, u32[]{:S(2)}) collective-permute-start(bf16[128,1536]{1,0:T(8,128)(2,1)S(1)} %slice.759), channel_id=1, source_target_pairs={{0,1},{1,2},{2,3},{3,0},{4,5},{5,6},{6,7},{7,4},{8,9},{9,10},{10,1... | collective-permute-start | bytes 1179656 | tf_op jit(solution)/shard_map/ppermute | solution.py:47
  444.1 4.7 collective-permute-start.52
  449.7 5.4 collective-permute-start.54
  449.8 5.3 collective-permute-start.57
  454.3 26.5 %collective-permute-start.47 = (bf16[128,1536]{1,0:T(8,128)(2,1)S(1)}, bf16[128,1536]{1,0:T(8,128)(2,1)S(1)}, u32[]{:S(2)}, u32[]{:S(2)}) collective-permute-start(bf16[128,1536]{1,0:T(8,128)(2,1)S(1)} %fusion.30), channel_id=1, source_target_pairs={{0,1},{1,2},{2,3},{3,0},{4,5},{5,6},{6,7},{7,4},{8,9},{9,10},{10,1... | collective-permute-start | bytes 1179656 | tf_op jit(solution)/shard_map/ppermute | solution.py:47
  455.4 5.7 %collective-permute-start.58 = (bf16[2,192,256]{2,1,0:T(8,128)(2,1)S(1)}, bf16[2,192,256]{2,1,0:T(8,128)(2,1)S(1)}, u32[]{:S(2)}, u32[]{:S(2)}) collective-permute-start(bf16[2,192,256]{2,1,0:T(8,128)(2,1)S(1)} %fusion.52), channel_id=1, source_target_pairs={{0,8},{4,12},{8,0},{12,4},{16,24},{20,28},{24,16},{28,20},{1,9},{5... | collective-permute-start | bytes 589832 | tf_op jit(solution)/shard_map/ppermute | solution.py:37
  457.2 6.8 %collective-permute-start.55 = (bf16[2,192,256]{2,1,0:T(8,128)(2,1)S(1)}, bf16[2,192,256]{2,1,0:T(8,128)(2,1)S(1)}, u32[]{:S(2)}, u32[]{:S(2)}) collective-permute-start(bf16[2,192,256]{2,1,0:T(8,128)(2,1)S(1)} %fusion.51), channel_id=1, source_target_pairs={{0,16},{4,20},{8,24},{12,28},{16,0},{20,4},{24,8},{28,12},{1,17},{... | collective-permute-start | bytes 589832 | tf_op jit(solution)/shard_map/ppermute | solution.py:37
  461.3 4.7 collective-permute-start.59
  464.1 4.7 collective-permute-start.56
  470.7 10.0 %collective-permute-start.61 = (bf16[48,512]{1,0:T(8,128)(2,1)S(1)}, bf16[48,512]{1,0:T(8,128)(2,1)S(1)}, u32[]{:S(2)}, u32[]{:S(2)}) collective-permute-start(bf16[48,512]{1,0:T(8,128)(2,1)S(1)} %get-tuple-element.62), channel_id=1, source_target_pairs={{0,2},{1,3},{2,0},{3,1},{4,6},{5,7},{6,4},{7,5},{8,10},{9,11},{10,... | collective-permute-start | bytes 147464 | tf_op jit(solution)/shard_map/ppermute | solution.py:42
  470.7 10.0 %collective-permute-start.62 = (bf16[48,512]{1,0:T(8,128)(2,1)S(1)}, bf16[48,512]{1,0:T(8,128)(2,1)S(1)}, u32[]{:S(2)}, u32[]{:S(2)}) collective-permute-start(bf16[48,512]{1,0:T(8,128)(2,1)S(1)} %get-tuple-element.61), channel_id=1, source_target_pairs={{0,1},{1,2},{2,3},{3,0},{4,5},{5,6},{6,7},{7,4},{8,9},{9,10},{10,1... | collective-permute-start | bytes 147464 | tf_op jit(solution)/shard_map/ppermute | solution.py:42
  480.9 9.6 %collective-permute-start.48 = (bf16[128,1536]{1,0:T(8,128)(2,1)S(1)}, bf16[128,1536]{1,0:T(8,128)(2,1)S(1)}, u32[]{:S(2)}, u32[]{:S(2)}) collective-permute-start(bf16[128,1536]{1,0:T(8,128)(2,1)S(1)} %fusion.31), channel_id=1, source_target_pairs={{0,1},{1,2},{2,3},{3,0},{4,5},{5,6},{6,7},{7,4},{8,9},{9,10},{10,1... | collective-permute-start | bytes 1179656 | tf_op jit(solution)/shard_map/ppermute | solution.py:47
  (68 other events, 682.0 us)
Sparse Core Ops, SparseCore 0:
  31.5 47.8 all-gather.3
  81.8 84.0 all-gather.5
  167.8 48.8 all-gather.7
  330.7 37.7 reduce-scatter.3
  372.3 73.2 reduce-scatter.7
  448.9 98.5 reduce-scatter.5

commit v2 on v1

v2 whole, which is shorter than its diff:
```python
import functools

import jax
import jax.numpy as jnp
from jax import lax
from jax.experimental import pallas as pl
from jax.experimental.layout import Layout, with_layout_constraint
from jax.experimental.pallas import tpu as pltpu
from jax.sharding import PartitionSpec as P

HEADS = 12
KV_HEADS = 2
HD = 128
QD = 1536
KD = 256
QKV = 2048


EPS = 1e-06
ROPE_BASE = 1000000.0
MASKED = -1e30
SEG_STEP = 1 << 20
TILE = 768
MIB = 2**20

BF = jnp.bfloat16
F32 = jnp.float32


def plain(values):
    return with_layout_constraint(values, Layout(major_to_minor=tuple(range(values.ndim))))


def bits_of(axis):
    return (lax.axis_size(axis) - 1).bit_length()


def bit_value(axis, bit):
    return (lax.axis_index(axis) >> bit) & 1


def send(block, axis, target):
    count = lax.axis_size(axis)
    return plain(lax.ppermute(plain(block), axis, [(j, target(j) % count) for j in range(count)]))


def swap(block, axis, bit):
    return send(block, axis, lambda j: j ^ (1 << bit))


def from_next(block, axis, apart=1):
    return send(block, axis, lambda j: j - apart)


def to_next(block, axis):
    return send(block, axis, lambda j: j + 1)


def tie_kernel(*refs):
    del refs


def tie_all(blocks, *others):
    count = len(blocks)
    return pl.pallas_call(
        tie_kernel,
        in_specs=[pl.BlockSpec(memory_space=pl.ANY)] * (count + len(others)),
        out_specs=[pl.BlockSpec(memory_space=pl.ANY)] * count,
        out_shape=[jax.ShapeDtypeStruct(block.shape, block.dtype) for block in blocks],
        input_output_aliases={i: i for i in range(count)},
        compiler_params=pltpu.CompilerParams(vmem_limit_bytes=MIB),
        name="tie",
    )(*blocks, *others)


def tie(block, *others):
    return tie_all([block], *others)[0]


def gather_blocks(block, axis, last=()):
    half = block.shape[0] // 2
    above = from_next(block, axis)
    below = to_next(block, axis)
    above, below = tie_all([above, below], *last)
    return [block, above, from_next(above[:half], axis), to_next(below[half:], axis), below]


def sum_first(far, axis):
    return from_next(far[0], axis), to_next(far[1], axis)


def sum_payload(ahead, behind, moved, last=()):
    half = ahead.shape[0] // 2
    from_above, from_below = tie_all(moved, *last)
    down = jnp.concatenate([behind[:half].astype(F32) + from_above.astype(F32), behind[half:].astype(F32)])
    up = jnp.concatenate([ahead[:half].astype(F32), ahead[half:].astype(F32) + from_below.astype(F32)])
    return down.astype(BF), up.astype(BF)


def gather_far(block, axis, last=()):
    count = lax.axis_size(axis) // 2
    if count != 4:
        blocks = [send(block, axis, lambda j: j ^ 2 * i) if i else plain(block) for i in range(count)]
        return jnp.stack(blocks), blocks[1:3]
    half = block.shape[0] // 2
    first = swap(block, axis, 1), swap(block, axis, 2)
    one, two = tie_all(first, *last)
    parts = [swap(one[:half], axis, 2), swap(two[half:], axis, 1)]
    return plain(jnp.stack([block, one, two, jnp.concatenate(parts)])), parts


def total(terms):
    result = terms[0].astype(F32)
    for term in terms[1:]:
        result = result + term.astype(F32)
    return result


def sum_step(terms, axis, bit, last=()):
    half = terms[0].shape[0] // 2
    sent = total([term[half:] for term in terms]).astype(BF)
    moved = swap(tie(sent, *last) if last else sent, axis, bit)
    return [term[:half] for term in terms] + [moved]


def sum_halving(terms, axis, bits):
    for bit in bits:
        terms = sum_step(terms, axis, bit)
    return total([term[0] for term in terms])


def sum_xor(blocks, axis, bits):
    blocks = dict(enumerate(blocks))
    for bit in bits:
        place = 1 << bit - 1
        sent = [m for m in sorted(blocks) if m & place]
        moved = swap(jnp.stack([blocks[m].astype(BF) for m in sent]), axis, bit)
        for i, m in enumerate(sent):
            blocks[m ^ place] = blocks[m ^ place] + moved[i].astype(F32)
            del blocks[m]
    return blocks[0], moved


def roll_blocks(stacked, shift, axis=0):
    count = stacked.shape[axis]
    return lax.dynamic_slice_in_dim(
        jnp.concatenate([stacked, stacked], axis=axis), shift, count, axis
    )


def dot_nn(left, right):
    return jnp.dot(left, right, preferred_element_type=F32)


def dot_nt(left, right):
    return lax.dot_general(left, right, (((1,), (1,)), ((), ())), preferred_element_type=F32)


def dot_tn(left, right):
    return lax.dot_general(left, right, (((0,), (0,)), ((), ())), preferred_element_type=F32)


def inverse_norm(values):
    return lax.rsqrt(jnp.mean(values * values, axis=-1, keepdims=True) + EPS)


def vmem():
    return pl.BlockSpec(memory_space=pltpu.VMEM)


def smem():
    return pl.BlockSpec(memory_space=pltpu.SMEM)


def anywhere():
    return pl.BlockSpec(memory_space=pl.ANY)


def shape_of(shape, dtype=BF):
    return jax.ShapeDtypeStruct(shape, dtype)


def fixed(shape):
    return pl.BlockSpec(shape, lambda *i: (0,) * len(shape))


def params(mib):
    return pltpu.CompilerParams(vmem_limit_bytes=mib * MIB)


def cost(micros):
    return pl.CostEstimate(flops=int(micros * 1153e6), bytes_accessed=0, transcendentals=0)


def cut(size, tile):
    return [(at, min(tile, size - at)) for at in range(0, size, tile)]


def start_blocks(own_ref, near_ref, other_ref, to_ref, sem):
    count = near_ref.shape[0]
    rows = to_ref.shape[0] // (2 * count)
    copies = []
    for side, source in enumerate((near_ref, other_ref)):
        for i in range(count):
            at = pl.multiple_of((own_ref[0] ^ (2 * i + side)) * rows, 16)
            copy = pltpu.make_async_copy(
                source.at[i, pl.ds(0, rows), :], to_ref.at[pl.ds(at, rows), :], sem.at[side, i]
            )
            copy.start()
            copies.append(copy)
    return copies


def masks_of(bits):
    masks = [0]
    for bit in bits[::-1]:
        masks += [mask | 1 << bit for mask in masks]
    return masks


def store_rows(refs, cols, values):
    at = 0
    for ref in refs:
        ref[:, cols] = values[at : at + ref.shape[0]].astype(ref.dtype)
        at += ref.shape[0]


def row_shapes(tok_rows, width):
    half = tok_rows // 2
    return [shape_of((tok_rows, width), F32), shape_of((tok_rows, width))] + [
        shape_of((rows, width)) for rows in (half, half, tok_rows)
    ]


def fill_rows(to_ref, parts):
    at = 0
    for part in parts:
        to_ref[at : at + part.shape[0], :] = part[...]
        at += part.shape[0]


def head_rows(tok_rows, blocks):
    half_block = tok_rows // 2
    return [
        (half, u * half_block, u * tok_rows + half * half_block, half_block)
        for u in range(blocks)
        for half in range(2)
    ]


def project_kernel(heads, own_ref, *refs):
    parts = refs[:5]
    gain_ref, bias_ref, cos_ref, sin_ref, near, other = refs[5:11]
    q_ref, kv_ref, x_ref, normed_ref, w_ref, sem = refs[11:]
    copies = start_blocks(own_ref, near, other, w_ref, sem)
    fill_rows(x_ref, parts)
    values = x_ref[...].astype(F32)
    normed_ref[...] = (values * inverse_norm(values) * gain_ref[...]).astype(BF)
    for copy in copies:
        copy.wait()
    joint = dot_nn(normed_ref[...], w_ref[...]) + bias_ref[...]
    tok_rows = parts[0].shape[0]
    blocks = x_ref.shape[0] // tok_rows
    half_rows = x_ref.shape[0] // 2
    for j in range(heads + 2):
        part = joint[:, j * HD : (j + 1) * HD]
        if j <= heads:
            part = part * cos_ref[...] + pltpu.roll(part, HD // 2, 1) * sin_ref[...]
        part = part.astype(BF)
        for half, low, row, count in head_rows(tok_rows, blocks):
            piece = part[row : row + count]
            if j < heads:
                q_ref[half, j * half_rows + low : j * half_rows + low + count, :] = piece
            else:
                kv_ref[j - heads, half, low : low + count, :] = piece


def project(own, parts, gain, bias, cos, sin, near, other, heads):
    width = parts[0].shape[1]
    rows = cos.shape[0]
    cols = near.shape[2]
    return pl.pallas_call(
        functools.partial(project_kernel, heads),
        in_specs=[smem()] + [vmem()] * 9 + [anywhere()] * 2,
        out_specs=[vmem()] * 5,
        out_shape=[
            shape_of((2, heads * rows // 2, HD)),
            shape_of((2, 2, rows // 2, HD)),
            shape_of((rows, width)),
            shape_of((rows, width)),
            shape_of((width, cols)),
        ],
        scratch_shapes=[pltpu.SemaphoreType.DMA((2, near.shape[0]))],
        compiler_params=params(60),
        cost_estimate=cost(2.8),
        name="project",
    )(own, *parts, gain, bias, cos, sin, near, other)


def project_back_kernel(heads, orders, own_ref, head_ref, *refs):
    dq_ref, dkv_ref, cos_ref, sin_ref, normed_ref, x_ref, w_ref, mixed_ref = refs[:8]
    parts = refs[8:13]
    gain_two_ref = refs[13]
    dn_refs = refs[14:19]
    cols_kept, cols_sent, outs_kept, outs_sent = refs[19:23]
    cols, branch, wide, wide_out, bias_v, small_v = refs[23:]
    rows = cos_ref.shape[0]
    half_rows = rows // 2
    tok_rows = parts[0].shape[0]
    blocks = rows // tok_rows
    head = head_ref[0]
    odd = (head & 1) == 1
    for half, low, row, count in head_rows(tok_rows, blocks):
        here = slice(row, row + count)
        for j in range(heads + 1):
            if j < heads:
                start = j * half_rows + low
                part = dq_ref[half, start : start + count, :]
            else:
                part = dkv_ref[half, low : low + count, :]
            part = part.astype(BF).astype(F32)
            turned = part * cos_ref[here, :] - pltpu.roll(part, HD // 2, 1) * sin_ref[here, :]
            if j == heads:
                turned = jnp.where(odd, part, turned)
            cols[here, j * HD : (j + 1) * HD] = turned.astype(BF)
    last = heads * HD
    bias = jnp.sum(cols[...].astype(F32), axis=0, keepdims=True)
    bias_v[...] = jnp.zeros(bias_v.shape, F32)
    bias_v[:, pl.ds(pl.multiple_of(head * last, HD), last)] = bias[:, :last]
    copies = (QD // last) // KV_HEADS
    slot = QD + (head & 1) * KD + (head // copies) * HD
    bias_v[:, pl.ds(pl.multiple_of(slot, HD), HD)] = bias[:, last:]
    key_w = jnp.where(odd, w_ref[:, last + HD :], w_ref[:, last : last + HD])
    grad = dot_nt(cols[:, :last], w_ref[:, :last]) + dot_nt(cols[:, last:], key_w)
    store_rows(dn_refs, slice(None), grad)
    values = x_ref[...].astype(F32)
    gain_one = jnp.sum(grad * (values * inverse_norm(values)), axis=0, keepdims=True)
    seq_dev = small_v.shape[0]
    small_v[...] = jnp.zeros(small_v.shape, BF)
    for row, vectors in enumerate(
        ((gain_one, gain_two_ref[...]), (bias_v[:, : QD + KD], bias_v[:, QD + KD :]))
    ):
        for i in range(seq_dev):
            at = 0
            for vector in vectors:
                size = vector.shape[1] // seq_dev
                small_v[i, row : row + 1, at : at + size] = vector[:, i * size : (i + 1) * size].astype(BF)
                at += size
    count = outs_kept.shape[1]
    fill_rows(branch, parts)
    wide[...] = dot_tn(normed_ref[...], cols[...]).astype(BF)
    wide_out[...] = dot_tn(branch[...], mixed_ref[...]).astype(BF)
    for i in range(cols_kept.shape[0]):
        for source, targets, order in (
            (wide, (cols_kept, cols_sent), orders[0]),
            (wide_out, (outs_kept, outs_sent), orders[1]),
        ):
            for side, to in enumerate(targets):
                block = own_ref[0] ^ order[i] ^ side
                to[i, :count] = source[pl.ds(pl.multiple_of(block * count, 16), count), :]
                if source is wide:
                    to[i, count:] = small_v[block]


MORE_ROWS = 16


def project_back(own, head, orders, dq, dkv, cos, sin, normed, x, w, mixed, parts, gain_two):
    rows, width = normed.shape
    heads = dq.shape[1] // (rows // 2)
    cols = (heads + 1) * HD
    tok_rows = parts[0].shape[0]
    far = len(orders[0])
    part_rows = width // (2 * far)
    return pl.pallas_call(
        functools.partial(project_back_kernel, heads, orders),
        in_specs=[smem()] * 2 + [vmem()] * 14,
        out_specs=[vmem()] * 9,
        out_shape=[
            *row_shapes(tok_rows, width),
            shape_of((far, part_rows + MORE_ROWS, cols)),
            shape_of((far, part_rows + MORE_ROWS, cols)),
            shape_of((far, part_rows, heads * HD)),
            shape_of((far, part_rows, heads * HD)),
        ],
        scratch_shapes=[
            pltpu.VMEM((rows, cols), BF),
            pltpu.VMEM((rows, width), BF),
            pltpu.VMEM((width, cols), BF),
            pltpu.VMEM((width, heads * HD), BF),
            pltpu.VMEM((1, QKV), F32),
            pltpu.VMEM((2 * far, MORE_ROWS, cols), BF),
        ],
        compiler_params=params(60),
        cost_estimate=cost(4.5),
        name="project_back",
    )(own, head, dq, dkv, cos, sin, normed, x, w, mixed, *parts, gain_two)


def visible_of(key_code, query_code, half):
    seen = key_code <= query_code
    if half == 1:
        seen &= key_code >= (query_code // SEG_STEP) * SEG_STEP
    return seen


PAIRS = ((0, 0), (0, 1), (1, 1))
SEQ_STEP = 2


def pick_side(first_steps, near_ref, other_ref, which, half):
    near = near_ref[:, which, half]
    other = other_ref[:, which, half]
    block = jnp.where(pl.program_id(0) < first_steps, near, other)
    return block.reshape(block.shape[0] * block.shape[1], block.shape[2])


def codes(code_ref, half):
    block = code_ref[:, half]
    return block.reshape(block.shape[0] * block.shape[1], 1)


def attend_kernel(scale, first_steps, tok_rows, q_ref, near_ref, other_ref, kc_ref, qc_ref, *refs):
    mixed_ref, wide_ref, lse_ref, top, total, acc = refs[-6:]
    step = pl.program_id(0)

    @pl.when(step == 0)
    def _():
        top[...] = jnp.full(top.shape, MASKED, F32)
        total[...] = jnp.zeros(total.shape, F32)
        acc[...] = jnp.zeros(acc.shape, F32)

    for key_half, query_half in PAIRS:
        keys = pick_side(first_steps, near_ref, other_ref, 0, key_half)
        values = pick_side(first_steps, near_ref, other_ref, 1, key_half)
        scores = dot_nt(keys, q_ref[query_half]) * scale
        if key_half == query_half:
            seen = visible_of(codes(kc_ref, key_half), qc_ref[query_half], key_half)
            scores = jnp.where(seen, scores, MASKED)
        old = top[query_half]
        new = jnp.maximum(old, jnp.max(scores, axis=0, keepdims=True))
        weights = jnp.exp(scores - new)
        if key_half == query_half:
            weights = jnp.where(seen, weights, 0.0)
        factor = jnp.exp(old - new)
        top[query_half] = new
        total[query_half] = total[query_half] * factor + jnp.sum(weights, axis=0, keepdims=True)
        acc[query_half] = acc[query_half] * factor + dot_tn(values, weights.astype(BF))

    @pl.when(step == pl.num_programs(0) - 1)
    def _():
        blocks = mixed_ref.shape[0] // tok_rows
        half_rows = mixed_ref.shape[0] // 2
        for half in range(2):
            wide_ref[half] = jnp.transpose(acc[half] / total[half])
            lse_ref[half] = top[half] + jnp.log(total[half])
        for half, low, row, count in head_rows(tok_rows, blocks):
            for j in range(mixed_ref.shape[1] // HD):
                at = j * half_rows + low
                mixed_ref[row : row + count, j * HD : (j + 1) * HD] = wide_ref[
                    half, at : at + count, :
                ].astype(BF)


def side_specs(shape, first_steps):
    block = (SEQ_STEP,) + shape[1:]
    rest = (0,) * (len(shape) - 1)
    return [
        pl.BlockSpec(block, lambda i: (jnp.minimum(i, first_steps - 1),) + rest),
        pl.BlockSpec(block, lambda i: (jnp.maximum(i - first_steps, 0),) + rest),
    ]


def code_spec(shape):
    return pl.BlockSpec((SEQ_STEP,) + shape[1:], lambda i: (i,) + (0,) * (len(shape) - 1))


def attend(queries, near, other, key_code, query_code, tok_rows, others):
    _, rows, _ = queries.shape
    half_rows = near.shape[3]
    heads = rows // half_rows
    first_steps = near.shape[0] // SEQ_STEP
    return pl.pallas_call(
        functools.partial(attend_kernel, HD**-0.5, first_steps, tok_rows),
        grid=(2 * first_steps,),
        in_specs=[fixed(queries.shape)]
        + side_specs(near.shape, first_steps)
        + [code_spec(key_code.shape), fixed(query_code.shape)]
        + [anywhere()] * len(others),
        out_specs=[fixed((2 * half_rows, heads * HD)), fixed((2, rows, HD)), fixed((2, 1, rows))],
        out_shape=[
            shape_of((2 * half_rows, heads * HD)),
            shape_of((2, rows, HD), F32),
            shape_of((2, 1, rows), F32),
        ],
        scratch_shapes=[
            pltpu.VMEM((2, 1, rows), F32),
            pltpu.VMEM((2, 1, rows), F32),
            pltpu.VMEM((2, HD, rows), F32),
        ],
        compiler_params=params(60),
        cost_estimate=cost(3),
        name="attend",
    )(queries, near, other, key_code, query_code, *others)


def attend_back_kernel(scale, first_steps, others, q_ref, *refs):
    grads = refs[:4]
    wide_ref, near_ref, other_ref, kc_ref, qc_ref, lse_ref = refs[4:10]
    dq_ref, own_ref, sent_ref, acc, do, delta = refs[10 + others :]
    step = pl.program_id(0)
    half_rows = near_ref.shape[3]
    tok_rows = grads[0].shape[0]

    @pl.when(step == 0)
    def _():
        acc[...] = jnp.zeros(acc.shape, F32)
        for u, grad in enumerate(grads):
            for half, low, row, count in head_rows(tok_rows, 1):
                for j in range(grad.shape[1] // HD):
                    at = j * half_rows + u * (tok_rows // 2)
                    do[half, at : at + count, :] = grad[row : row + count, j * HD : (j + 1) * HD]
        for half in range(2):
            product = do[half].astype(F32) * wide_ref[half]
            delta[half] = jnp.sum(jnp.transpose(product), axis=0, keepdims=True)

    results = []
    for key_half in range(2):
        keys = pick_side(first_steps, near_ref, other_ref, 0, key_half)
        values = pick_side(first_steps, near_ref, other_ref, 1, key_half)
        grad_keys, grad_values = None, None
        for query_half in range(key_half, 2):
            queries = q_ref[query_half]
            grad = do[query_half]
            scores = dot_nt(keys, queries) * scale
            weights = jnp.exp(scores - lse_ref[query_half])
            if key_half == query_half:
                seen = visible_of(codes(kc_ref, key_half), qc_ref[query_half], key_half)
                weights = jnp.where(seen, weights, 0.0)
            grad_weights = dot_nt(values, grad)
            grad_scores = (weights * (grad_weights - delta[query_half])).astype(BF)
            value_term = dot_nn(weights.astype(BF), grad)
            key_term = dot_nn(grad_scores, queries)
            grad_keys = key_term if grad_keys is None else grad_keys + key_term
            grad_values = value_term if grad_values is None else grad_values + value_term
            acc[query_half] += dot_tn(keys, grad_scores)
        shape = (SEQ_STEP, half_rows, HD)
        results.append((grad_keys * scale).reshape(shape).astype(BF))
        results.append(grad_values.reshape(shape).astype(BF))

    def store(ref):
        for key_half in range(2):
            ref[:, 0, key_half] = results[2 * key_half]
            ref[:, 1, key_half] = results[2 * key_half + 1]

    pl.when(step < first_steps)(lambda: store(own_ref))
    pl.when(step >= first_steps)(lambda: store(sent_ref))

    @pl.when(step == pl.num_programs(0) - 1)
    def _():
        for half in range(2):
            dq_ref[half] = jnp.transpose(acc[half] * scale)


def attend_back(queries, grads, wide, near, other, key_code, query_code, log_total, others):
    _, rows, _ = queries.shape
    first_steps = near.shape[0] // SEQ_STEP
    sides = side_specs(near.shape, first_steps)
    return pl.pallas_call(
        functools.partial(attend_back_kernel, HD**-0.5, first_steps, len(others)),
        grid=(2 * first_steps,),
        in_specs=[fixed(queries.shape)]
        + [fixed(grad.shape) for grad in grads]
        + [fixed(wide.shape)]
        + sides
        + [code_spec(key_code.shape), fixed(query_code.shape), fixed(log_total.shape)]
        + [anywhere()] * len(others),
        out_specs=[fixed((2, rows, HD))] + sides,
        out_shape=[shape_of((2, rows, HD), F32), shape_of(near.shape), shape_of(near.shape)],
        scratch_shapes=[
            pltpu.VMEM((2, HD, rows), F32),
            pltpu.VMEM((2, rows, HD), BF),
            pltpu.VMEM((2, 1, rows), F32),
        ],
        compiler_params=params(60),
        cost_estimate=cost(5.2),
        name="attend_back",
    )(queries, *grads, wide, near, other, key_code, query_code, log_total, *others)


OUT_TILE = 256
FEED_TILE = 512


def feed_forward_kernel(own_ref, gain_ref, *refs):
    x_hbm = refs[0]
    cot_parts = refs[1:6]
    mixed_parts = refs[6:11]
    near_w, other_w, joined_w = refs[11:14]
    refs = refs[14:]
    normed_ref, hidden_ref, middle_ref, dg_ref, du_ref, cot_ref = refs[:6]
    dx_refs = refs[6:11]
    x_v, out_v, gate_v, up_v, down_v, mixed_v, normed_v, middle_v, dg_v, du_v, cot_v = refs[11:22]
    in_sem, cot_sem, out_sem, w_sem, s_sem = refs[22:]
    rows, width = x_v.shape
    units = gate_v.shape[1]
    tok_rows = hidden_ref.shape[0]
    half = tok_rows // 2
    blocks = rows // tok_rows
    chunks = cut(units, FEED_TILE)
    cols = mixed_parts[0].shape[1]

    def begin(source, target, sem):
        copy = pltpu.make_async_copy(source, target, sem)
        copy.start()
        return copy

    first = [begin(x_hbm, x_v, in_sem.at[0])]
    for t, part, low in (
        (0, mixed_parts[0], 0),
        (1, mixed_parts[1], 0),
        (2, mixed_parts[2], 0),
        (2, mixed_parts[3], blocks // 2),
        (3, mixed_parts[4], 0),
    ):
        for b in range(part.shape[0] // tok_rows):
            u = (low + b + t) % blocks
            first.append(
                begin(
                    part.at[pl.ds(b * tok_rows, tok_rows), :],
                    mixed_v.at[pl.ds(u * tok_rows, tok_rows), pl.ds(t * cols, cols)],
                    in_sem.at[len(first)],
                )
            )
    first += start_blocks(own_ref, near_w, other_w, out_v, out_sem)
    cots, step = [], cot_parts[2].shape[0]
    for part in cot_parts:
        for low in range(0, part.shape[0], step):
            i = len(cots)
            cots.append(
                begin(
                    part.at[pl.ds(low, half), :], cot_v.at[pl.ds(i * half, half), :], cot_sem.at[i]
                )
            )
    loads = [
        [
            begin(
                joined_w.at[:, pl.ds(j * units + at, size)], dst.at[:, pl.ds(at, size)], w_sem.at[i, j]
            )
            for j, dst in enumerate((gate_v, up_v, down_v))
        ]
        for i, (at, size) in enumerate(chunks)
    ]
    for copy in first:
        copy.wait()
    hidden = x_v[...].astype(F32) + dot_nt(mixed_v[...], out_v[...])
    hidden_ref[...] = hidden[:tok_rows]
    normed_v[...] = (hidden * inverse_norm(hidden) * gain_ref[...]).astype(BF)
    for copy in cots:
        copy.wait()
    stores = [begin(normed_v, normed_ref, s_sem.at[0]), begin(cot_v, cot_ref, s_sem.at[1])]
    for i, (at, size) in enumerate(chunks):
        for copy in loads[i]:
            copy.wait()
        here = slice(at, at + size)
        gate = dot_nn(normed_v[...], gate_v[:, here])
        up = dot_nn(normed_v[...], up_v[:, here])
        grad = dot_nn(cot_v[...], down_v[:, here])
        sig = 1.0 / (1.0 + jnp.exp(-gate))
        active = gate * sig
        middle_v[:, here] = (active * up).astype(BF)
        dg_v[:, here] = (grad * up * sig * (1.0 + gate * (1.0 - sig))).astype(BF)
        du_v[:, here] = (grad * active).astype(BF)
    for j, (src, dst) in enumerate(((dg_v, dg_ref), (du_v, du_ref), (middle_v, middle_ref))):
        stores.append(begin(src, dst, s_sem.at[2 + j]))
    for at, size in cut(width, OUT_TILE):
        here = slice(at, at + size)
        grad = dot_nt(dg_v[...], gate_v[here, :]) + dot_nt(du_v[...], up_v[here, :])
        store_rows(dx_refs, here, grad)
    for copy in stores:
        copy.wait()


def feed_forward(own, x, gain, cot_parts, mixed_parts, near, other, joined_all, tok_rows):
    rows, width = x.shape
    units = joined_all.shape[1] // 3
    blocks = rows // tok_rows
    hidden_like = shape_of((rows, units))
    return pl.pallas_call(
        feed_forward_kernel,
        in_specs=[smem(), vmem()] + [anywhere()] * 14,
        out_specs=[anywhere(), vmem()] + [anywhere()] * 4 + [vmem()] * 5,
        out_shape=[
            shape_of((rows, width)),
            shape_of((tok_rows, width), F32),
            hidden_like,
            hidden_like,
            hidden_like,
            shape_of((rows, width)),
            *row_shapes(tok_rows, width),
        ],
        scratch_shapes=[
            pltpu.VMEM((rows, width), BF),
            pltpu.VMEM((width, QD), BF),
            pltpu.VMEM((width, units), BF),
            pltpu.VMEM((width, units), BF),
            pltpu.VMEM((width, units), BF),
            pltpu.VMEM((rows, QD), BF),
            pltpu.VMEM((rows, width), BF),
            pltpu.VMEM((rows, units), BF),
            pltpu.VMEM((rows, units), BF),
            pltpu.VMEM((rows, units), BF),
            pltpu.VMEM((rows, width), BF),
            pltpu.SemaphoreType.DMA((1 + blocks * blocks,)),
            pltpu.SemaphoreType.DMA((2 * blocks,)),
            pltpu.SemaphoreType.DMA((2, near.shape[0])),
            pltpu.SemaphoreType.DMA((len(cut(units, FEED_TILE)), 3)),
            pltpu.SemaphoreType.DMA((5,)),
        ],
        compiler_params=params(60),
        cost_estimate=cost(16),
        name="feed_forward",
    )(own, gain, x, *cot_parts, *mixed_parts, near, other, joined_all)


def down_grads_kernel(blocks, own_ref, c_ref, down_w, middle_ref, down_ref, out_ref, turned, acc):
    step = pl.program_id(0)

    @pl.when(step == 0)
    def _():
        turned[...] = jnp.transpose(c_ref[...])
        acc[...] = jnp.zeros(acc.shape, F32)

    down_ref[...] = dot_nn(turned[...], middle_ref[...]).astype(BF)
    acc[...] += dot_nt(middle_ref[...], down_w[...])

    @pl.when(step == pl.num_programs(0) - 1)
    def _():
        rows = acc.shape[0] // blocks
        for t in range(blocks):
            at = pl.multiple_of(lax.rem(own_ref[0] + t, blocks) * rows, 16)
            out_ref[pl.ds(at, rows), :] = acc[t * rows : (t + 1) * rows, :].astype(BF)


def down_grads(own, cot, middle, joined_all, blocks):
    rows, full = cot.shape
    units = middle.shape[1]
    steps = units // TILE

    def tiles(rows, first=0):
        return pl.BlockSpec((rows, TILE), lambda i, own: (0, first + i))

    return pl.pallas_call(
        functools.partial(down_grads_kernel, blocks),
        grid_spec=pltpu.PrefetchScalarGridSpec(
            num_scalar_prefetch=1,
            grid=(steps,),
            in_specs=[fixed(cot.shape), tiles(full, 2 * steps), tiles(rows)],
            out_specs=[tiles(full), fixed((rows, full))],
            scratch_shapes=[pltpu.VMEM((full, rows), BF), pltpu.VMEM((rows, full), F32)],
        ),
        out_shape=[shape_of((full, units)), shape_of((rows, full))],
        compiler_params=params(60),
        cost_estimate=cost(6.3),
        name="down_grads",
    )(own, cot, joined_all, middle)


def pair_grads_kernel(orders, others, own_ref, *refs):
    xs, gates, ups = refs[:2], refs[2:4], refs[4:6]
    outs, (one, two, turned) = refs[6 + others : -3], refs[-3:]
    count = len(outs) // 2
    blocks = len(orders[0])
    rows = one.shape[0] // blocks
    tokens = xs[0].shape[0]

    @pl.when(pl.program_id(0) == 0)
    def _():
        for side, x_ref in enumerate(xs):
            turned[...] = jnp.transpose(x_ref[...])
            where = slice(side * tokens, (side + 1) * tokens)
            for j in range(blocks):
                here = slice(j * rows, (j + 1) * rows)
                for to, which in ((one, 0), (two, 1)):
                    at = pl.multiple_of((own_ref[0] ^ orders[which][j]) * rows, 16)
                    to[here, where] = turned[pl.ds(at, rows), :]

    for left, grads, (low, high, sent) in ((one, gates, outs[:count]), (two, ups, outs[count:])):
        result = dot_nn(left[:, :tokens], grads[0][...]) + dot_nn(left[:, tokens:], grads[1][...])
        half = 2 * low.shape[0]
        low[...] = result[: half // 2].astype(BF)
        high[...] = result[half // 2 : half].astype(BF)
        sent[...] = result[half:].astype(BF)


def pair_grads(own, orders, xs, gates, ups, others):
    rows, full = xs[0].shape
    units = gates[0].shape[1]

    def tiles(rows):
        return pl.BlockSpec((rows, TILE), lambda i, order: (0, i))

    return pl.pallas_call(
        functools.partial(pair_grads_kernel, orders, len(others)),
        grid_spec=pltpu.PrefetchScalarGridSpec(
            num_scalar_prefetch=1,
            grid=(units // TILE,),
            in_specs=[fixed(xs[0].shape)] * 2 + [tiles(rows)] * 4 + [anywhere()] * len(others),
            out_specs=([tiles(full // 8)] * 2 + [tiles(full // 4)]) * 2,
            scratch_shapes=[pltpu.VMEM((full // 2, 2 * rows), BF)] * 2
            + [pltpu.VMEM((full, rows), BF)],
        ),
        out_shape=([shape_of((full // 8, units))] * 2 + [shape_of((full // 4, units))]) * 2,
        compiler_params=params(60),
        cost_estimate=cost(6.3),
        name="pair_grads",
    )(own, *xs, *gates, *ups, *others)


def norm_back_kernel(others, own_ref, *refs):
    near_w, other_w = refs[6:8]
    refs = refs[:6] + refs[8 + others :]
    first_ref, down_ref, up_ref, hidden_ref, gain_ref, cot_ref, dh_ref, branch_ref = refs[:8]
    mixed_refs = refs[8:-3]
    gain_grad_ref, out_v, sem = refs[-3:]
    copies = start_blocks(own_ref, near_w, other_w, out_v, sem)
    grad = first_ref[...] + down_ref[...].astype(F32) + up_ref[...].astype(F32)
    hidden = hidden_ref[...]
    inv = inverse_norm(hidden)
    scaled = grad * gain_ref[...]
    gain_grad_ref[...] = jnp.sum(grad * (hidden * inv), axis=0, keepdims=True)
    inner = jnp.mean(scaled * hidden, axis=-1, keepdims=True)
    d_hidden = cot_ref[...].astype(F32) + inv * scaled - hidden * (inv * inv * inv * inner)
    dh_ref[...] = d_hidden
    branch_ref[...] = d_hidden.astype(BF)
    for copy in copies:
        copy.wait()
    d_mixed = dot_nn(branch_ref[...], out_v[...]).astype(BF)
    cols = mixed_refs[0].shape[1]
    for t, ref in enumerate(mixed_refs):
        ref[...] = d_mixed[:, t * cols : (t + 1) * cols]


def norm_back(own, first, down, up, hidden, gain, cotangent, near, other, blocks, others):
    rows, width = hidden.shape
    return pl.pallas_call(
        functools.partial(norm_back_kernel, len(others)),
        in_specs=[smem()] + [vmem()] * 6 + [anywhere()] * (2 + len(others)),
        out_specs=[vmem()] * (3 + blocks),
        out_shape=[shape_of((rows, width), F32), shape_of((rows, width))]
        + [shape_of((rows, QD // blocks))] * blocks
        + [shape_of((1, width), F32)],
        scratch_shapes=[
            pltpu.VMEM((width, QD), BF),
            pltpu.SemaphoreType.DMA((2, near.shape[0])),
        ],
        compiler_params=params(60),
        cost_estimate=cost(2.3),
        name="norm_back",
    )(own, first, down, up, hidden, gain, cotangent, near, other, *others)


def per_device(
    inputs,
    norm_gain_attn,
    qkv_weight,
    qkv_bias,
    out_weight,
    norm_gain_mlp,
    gate_weight,
    up_weight,
    down_weight,
    cotangent,
    segment_ids,
    positions,
):
    tok_rows = inputs.shape[0]
    width = inputs.shape[1]
    seq_dev = lax.axis_size("seq")
    heads_dev = lax.axis_size("head")
    heads_here = HEADS // heads_dev
    copies = heads_dev // KV_HEADS
    group_rows = heads_dev * tok_rows
    half_rows = group_rows // 2
    query_cols = heads_here * HD
    head_index = lax.axis_index("head")
    seq_index = lax.axis_index("seq")
    odd = head_index % 2 == 1
    seq_bits = bits_of("seq")
    head_bits = bits_of("head")
    far = seq_dev // 2
    bits_down = list(range(seq_bits - 1, 0, -1))
    bits_up = bits_down[::-1]
    orders = (masks_of(bits_down), masks_of(bits_up))
    seq_own = seq_index.astype(jnp.int32).reshape(1)
    head_own = head_index.astype(jnp.int32).reshape(1)

    units = gate_weight.shape[1]
    padded = -(-units // TILE) * TILE
    joined = jnp.concatenate(
        [
            jnp.pad(part, ((0, 0), (0, padded - units)))
            for part in (gate_weight, up_weight, down_weight.T)
        ],
        axis=1,
    )
    joined_all = plain(lax.all_gather(plain(joined), "seq", axis=0, tiled=True))


    gain_cols = norm_gain_attn.shape[0]
    bias_cols = qkv_bias.shape[0]
    cols_here = query_cols + 2 * HD
    small = jnp.concatenate(
        [
            norm_gain_attn,
            norm_gain_mlp,
            qkv_bias,
            (positions >> 7).astype(BF),
            (positions & 127).astype(BF),
            segment_ids.astype(BF),
        ]
    )
    small_row = jnp.pad(small[None], ((0, MORE_ROWS - 1), (0, cols_here - small.shape[0])))

    def head_columns(values, head):
        last = values.ndim - 1
        slot = head // copies
        return [
            lax.dynamic_slice_in_dim(values, head * query_cols, query_cols, last),
            lax.dynamic_slice_in_dim(values, QD + slot * HD, HD, last),
            lax.dynamic_slice_in_dim(values, QD + KD + slot * HD, HD, last),
        ]

    rows_of = []
    for apart in range(heads_dev):
        target = (head_index - apart) % heads_dev
        block = jnp.concatenate(head_columns(qkv_weight, target), axis=1)
        block = jnp.concatenate([block, small_row])
        rows_of.append(from_next(block, "head", apart) if apart else block)
    own_wide = qkv_weight.shape[0]
    own_rows = own_wide * heads_dev
    inputs_parts = gather_blocks(tie(inputs, *rows_of[1:]), "head")
    rows_of = roll_blocks(jnp.stack(rows_of), (heads_dev - head_index) % heads_dev)
    small_grp = rows_of[:, own_wide]
    cols_own = jnp.concatenate(
        [
            rows_of[:, :own_wide].reshape(own_rows, cols_here),
            jnp.pad(small_grp, ((0, 2 * MORE_ROWS - heads_dev), (0, 0))),
        ]
    )
    cols_near, _ = gather_far(plain(cols_own), "seq", inputs_parts[2:4])
    cols_other = swap(cols_near, "seq", 0)

    def cut_small(values):
        cuts, start = [], 0
        for size in (gain_cols, gain_cols, bias_cols, tok_rows, tok_rows, tok_rows):
            cuts.append(values[..., start : start + size])
            start += size
        return cuts

    def places(cuts):
        pos = (cuts[3].astype(jnp.int32) << 7) + cuts[4].astype(jnp.int32)
        pos = roll_blocks(pos, head_index, pos.ndim - 2)
        seg = roll_blocks(cuts[5].astype(jnp.int32), head_index, pos.ndim - 2)
        return pos, seg * SEG_STEP + pos

    small_all = jnp.concatenate(
        [part[:, own_rows : own_rows + heads_dev] for part in (cols_near, cols_other)]
    )
    cuts = cut_small(small_all)
    _, key_code = places(cuts)
    query_pos, query_code = places(cut_small(small_grp))
    query_pos = query_pos.reshape(-1)

    def in_order(values):
        masks = [seq_index ^ j for j in range(seq_dev)]
        return jnp.stack(
            [
                lax.dynamic_index_in_dim(values, (m & 1) * far + (m >> 1), 0, keepdims=False)
                for m in masks
            ]
        ).reshape(-1)

    gain_attn = in_order(cuts[0]).reshape(1, -1).astype(F32)
    gain_mlp = in_order(cuts[1]).reshape(1, -1).astype(F32)
    bias_all = in_order(cuts[2]).astype(F32)

    def halves_first(values):
        tail = values.shape[1:]
        return jnp.swapaxes(
            values.reshape((heads_dev, 2, tok_rows // 2) + tail), 0, 1
        ).reshape((2, half_rows) + tail)

    query_code = jnp.broadcast_to(
        halves_first(query_code.reshape(-1))[:, None, None, :], (2, 1, heads_here, half_rows)
    ).reshape(2, 1, heads_here * half_rows)
    key_code = jnp.swapaxes(
        key_code.reshape(seq_dev, heads_dev, 2, tok_rows // 2), 1, 2
    ).reshape(seq_dev, 2, half_rows, 1)
    freq_index = jnp.arange(HD // 2, dtype=F32) * 2.0 / HD
    angles = query_pos.astype(F32)[:, None] * (1.0 / ROPE_BASE**freq_index)[None, :]
    cosine, sine = jnp.cos(angles), jnp.sin(angles)
    cosine_part = jnp.concatenate([cosine, cosine], axis=1)
    sine_part = jnp.concatenate([-sine, sine], axis=1)

    bias_here = jnp.concatenate(head_columns(bias_all, head_index))[None]
    queries, kv_own, inputs_grp, normed_one, cols_weight = project(
        seq_own,
        inputs_parts,
        gain_attn,
        bias_here,
        cosine_part,
        sine_part,
        cols_near,
        cols_other,
        heads_here,
    )
    half = tok_rows // 2
    out_flat = out_weight.reshape(-1, width)
    out_half = out_flat.shape[0] // 2
    out_pad = -out_half % 16
    cot_mixed = jnp.concatenate(
        [
            part
            for i in range(2)
            for part in (
                cotangent[i * half : (i + 1) * half],
                jnp.pad(out_flat[i * out_half : (i + 1) * out_half], ((0, out_pad), (0, 0))),
            )
        ]
    )
    cot_late = tie(plain(cot_mixed), inputs_parts[2], inputs_parts[3])
    cot_parts = gather_blocks(cot_late, "head", [queries])
    kv_near, _ = gather_far(kv_own, "seq", cot_parts[2:4])
    kv_other = swap(kv_near, "seq", 0)

    halves = jnp.concatenate(cot_parts).reshape(2 * heads_dev, half + out_half + out_pad, width)
    out_rows = plain(halves[:, half : half + out_half].reshape(QD, -1).T)
    out_first = tie(out_rows, kv_other)
    mixed, mixed_wide, log_total = attend(
        queries, kv_near, kv_other, key_code, query_code, tok_rows, []
    )
    out_near, out_came = gather_far(out_first, "seq", [mixed])
    mixed_parts = gather_blocks(mixed, "head", out_came)
    out_other = swap(tie(out_near, mixed_parts[1], mixed_parts[4]), "seq", 0)

    normed_two, own_hidden, middle, d_gate, d_up, cot_grp, *d_two = feed_forward(
        seq_own,
        inputs_grp,
        gain_mlp,
        cot_parts,
        mixed_parts,
        out_near,
        out_other,
        joined_all,
        tok_rows,
    )

    others = [swap(part, "seq", 0) for part in (normed_two, d_gate, d_up)]
    down_term, out_term = down_grads(
        head_own, cot_grp, middle, joined_all, heads_dev
    )
    moved = sum_first(d_two[2:4], "head")
    down_late = tie(down_term, *moved)
    down_sum = plain(lax.psum_scatter(plain(down_late), "seq", scatter_dimension=0, tiled=True))
    down, up = sum_payload(d_two[1], d_two[4], moved, others)
    parts = [
        part.reshape(-1, width // seq_dev, part.shape[1])
        for part in pair_grads(
            seq_own,
            orders,
            (normed_two, others[0]),
            (d_gate, others[1]),
            (d_up, others[2]),
            [down, up, down_late],
        )
    ]
    gate_low, gate_high, *gate_sent = parts[: len(parts) // 2]
    up_low, up_high, *up_sent = parts[len(parts) // 2 :]
    d_hidden, d_branch, *d_mixed_own, grad_gain_two = norm_back(
        seq_own,
        d_two[0],
        from_next(down, "head"),
        to_next(up, "head"),
        own_hidden,
        gain_mlp,
        cotangent,
        out_near,
        out_other,
        heads_dev,
        [gate_low],
    )
    d_mixed = [d_mixed_own[0]]
    for apart in range(1, heads_dev):
        d_mixed.append(from_next(d_mixed_own[heads_dev - apart], "head", apart))

    def move(t, *earlier):
        return (
            swap(tie(gate_sent[t], *earlier), "seq", bits_down[0]),
            swap(tie(up_sent[t], *earlier), "seq", bits_up[0]),
        )

    moved = [move(t, d_branch) for t in range(len(gate_sent))]
    branch_above = from_next(tie(d_branch, *d_mixed[1:]), "head")
    branch_below = to_next(tie(d_branch, *d_mixed[1:]), "head")
    d_queries, d_kv_own, d_kv_sent = attend_back(
        queries,
        d_mixed,
        mixed_wide,
        kv_near,
        kv_other,
        key_code,
        query_code,
        log_total,
        [],
    )
    d_kv_moved = swap(tie(d_kv_sent, branch_above, branch_below), "seq", 0)
    branch_above = tie(branch_above, d_queries)
    branch_below = tie(branch_below, d_queries)
    branch_parts = [
        d_branch,
        branch_above,
        from_next(branch_above[:half], "head"),
        to_next(branch_below[half:], "head"),
        branch_below,
    ]
    d_kv_moved = tie(d_kv_moved, *moved[-1], branch_parts[2], branch_parts[3])
    out_late = tie(out_term, down_sum)
    out_sum = plain(lax.psum_scatter(plain(out_late), "head", scatter_dimension=0, tiled=True))
    output = (own_hidden + out_sum.astype(F32)).astype(BF)
    d_kv = total([d_kv_own, d_kv_moved])
    d_keys, keys_last = sum_xor([d_kv[i, 0] for i in range(far)], "seq", bits_down)
    d_values, values_last = sum_xor([d_kv[i, 1] for i in range(far)], "seq", bits_up)
    d_other_raw = jnp.where(odd, d_keys, d_values).astype(BF)
    d_other_raw = swap(
        tie(d_other_raw, down_sum), "head", 0
    )
    d_other = d_other_raw.reshape(2, heads_dev, tok_rows // 2, HD)
    d_other = roll_blocks(d_other, jnp.where(odd, 1, heads_dev - 1), 1).reshape(2, half_rows, HD)
    d_kv_total = jnp.where(odd, d_values, d_keys) + d_other.astype(F32)


    def second(low, high, which, bit):
        half = high.shape[0]
        parts = [tie(pair[which], keys_last, values_last) for pair in moved]
        sent = total([high, jnp.concatenate([part[half:] for part in parts], axis=2)]).astype(BF)
        come = swap(sent, "seq", bit)
        return [low, jnp.concatenate([part[:half] for part in parts], axis=2), come]

    gate_terms = second(gate_low, gate_high, 0, bits_down[1])
    up_terms = second(up_low, up_high, 1, bits_up[1])
    *d_one, cols_kept, cols_sent, outs_kept, outs_sent = project_back(
        seq_own,
        head_own,
        orders,
        d_queries,
        d_kv_total,
        cosine_part,
        sine_part,
        normed_one,
        inputs_grp,
        cols_weight,
        mixed,
        branch_parts,
        grad_gain_two,
    )
    gate_terms[-1] = tie(gate_terms[-1], d_one[0])
    up_terms[-1] = tie(up_terms[-1], d_one[0])
    moved = sum_first(tie_all(d_one[2:4], gate_terms[-1], up_terms[-1]), "head")
    cols_moved, outs_moved = swap(cols_sent, "seq", 0), swap(outs_sent, "seq", 0)
    down, up = sum_payload(d_one[1], d_one[4], moved, [cols_moved, outs_moved])
    cols_terms = sum_step([cols_kept, cols_moved], "seq", bits_down[0])
    outs_terms = sum_step([outs_kept, outs_moved], "seq", bits_up[0])
    down, up = from_next(down, "head"), to_next(up, "head")
    d_normed_one = total([d_one[0], tie(down, cols_terms[-1], outs_terms[-1]), up])
    grad_cols = sum_halving(cols_terms, "seq", bits_down[1:]).astype(BF)
    grad_outs = sum_halving(outs_terms, "seq", bits_up[1:])
    inputs_f = inputs.astype(F32)
    inv_one = inverse_norm(inputs_f)
    scaled = d_normed_one * gain_attn
    inner = jnp.mean(scaled * inputs_f, axis=-1, keepdims=True)
    grad_inputs = (d_hidden + inv_one * scaled - inputs_f * (inv_one**3 * inner)).astype(BF)

    grad_out = grad_outs.T
    cols_wide = query_cols + HD
    more_rows = jnp.broadcast_to(grad_cols[own_rows:], (heads_dev, MORE_ROWS, cols_wide))
    grad_blocks = jnp.concatenate(
        [grad_cols[:own_rows].reshape(heads_dev, own_wide, cols_wide), more_rows], axis=1
    )
    grad_qkv = jnp.zeros((own_wide, QKV), F32)
    small_parts = []
    for apart in range(heads_dev):
        source = (head_index + apart) % heads_dev
        target = (head_index - apart) % heads_dev
        block = lax.dynamic_index_in_dim(grad_blocks, target, 0, keepdims=False)
        if apart:
            block = from_next(block, "head", apart)
        small_parts.append(block[own_wide : own_wide + 2])
        block = block[:own_wide].astype(F32)
        kv_place = QD + source % 2 * KD + source // copies * HD
        grad_qkv = lax.dynamic_update_slice_in_dim(
            grad_qkv, block[:, :query_cols], source * query_cols, 1
        )
        grad_qkv = lax.dynamic_update_slice_in_dim(grad_qkv, block[:, query_cols:], kv_place, 1)
    small_grads = total(small_parts)

    def own_part(row, start, size):
        return lax.dynamic_slice(small_grads, (row, start + head_index * size), (1, size)).reshape(size)

    key_bias = (QD + KD) // (seq_dev * heads_dev)
    value_bias = KD // (seq_dev * heads_dev)

    gate_sum = sum_halving(gate_terms, "seq", bits_down[2:])
    up_sum = sum_halving(up_terms, "seq", bits_up[2:])

    return (
        output,
        grad_inputs,
        own_part(0, 0, gain_cols),
        grad_qkv,
        own_part(1, 0, key_bias),
        own_part(1, heads_dev * key_bias, value_bias),
        grad_out,
        own_part(0, heads_dev * gain_cols, gain_cols),
        gate_sum[:, :units],
        up_sum[:, :units],
        down_sum[:, :units].T.astype(F32),
    )


def solution(mesh):
    both = ("seq", "head")
    in_specs = (
        P(both, None),
        P(both),
        P(both, None),
        P(both),
        P("head", "seq"),
        P(both),
        P("seq", "head"),
        P("seq", "head"),
        P("head", "seq"),
        P(both, None),
        P(both),
        P(both),
    )
    out_specs = (
        P(both, None),
        P(both, None),
        P(both),
        P(both, None),
        P(both),
        P(both),
        P("head", "seq"),
        P(both),
        P("seq", "head"),
        P("seq", "head"),
        P("head", "seq"),
    )
    return jax.shard_map(
        per_device, mesh=mesh, in_specs=in_specs, out_specs=out_specs, check_vma=False
    )
```

time: 566 us -> 454 us (0.80)
  matrix products: 91.3 us -> 0 us
  Pallas kernels: 28 us -> 119 us
  waiting for transfers between devices: 255 us -> 166 us
  other arithmetic: 47 us -> 27.5 us
  starting transfers between devices: 89.8 us -> 76.6 us
  local copies, waits for them, and re-layouts: 30.1 us -> 43 us
    dot_general x13 -> x0, matrix products: 91.3 us -> none  [the longest x5 33.5 us: dot_nn(): return jnp.dot(left, right, preferred_element_type=F32)]
    pallas_call x2 -> x36, Pallas kernels: 28 us -> 119 us  [the longest x1 36.2 us: feed_forward(): pl.pallas_call(feed_forward_kernel, in_specs=[smem(), vmem()] + [anywhere...]
    reduce_scatter x3 -> x2, waiting for transfers between devices: 51.4 us -> 0.02 us  [the longest x1 0.02 us: per_device(): lax.psum_scatter(plain(out_late), 'head', scatter_dimension=0, tiled=True)]
    ppermute x66 -> x67, waiting for transfers between devices: 198 us -> 166 us  [send(): lax.ppermute(plain(block), axis, [(j, target(j) % count) for j in range(c...]
    unnamed x138 -> x198, local copies, waits for them, and re-layouts: 10.7 us -> 29.3 us
    another operation x33 -> x13, other arithmetic: 17 us -> 3.36 us  [the longest x7 2.68 us: gather_far(): return (plain(jnp.stack([block, one, two, jnp.concatenate(parts)])), parts)]
    ppermute x66 -> x67, starting transfers between devices: 89.5 us -> 76.5 us  [send(): lax.ppermute(plain(block), axis, [(j, target(j) % count) for j in range(c...]
    slice x29 -> x32, local copies, waits for them, and re-layouts: 10.6 us -> 2.09 us  [the longest x1 0.94 us: per_device(): branch_below[half:]]
  transfers between devices with their start and end apart: 72 -> 70, of which waited for: 46 -> 42; matrix products, arithmetic and copies ran while one was open for 24% -> 9% of each run, Pallas kernels for 5% -> 18%
where the time goes in v2:
time: 454 us; the launch traced here: 447 us
  waiting for transfers between devices  166 us (37%)
  Pallas kernels  119 us (26%)
  starting transfers between devices  76.6 us (17%)
  local copies, waits for them, and re-layouts  43 us (9%)
  other arithmetic  27.5 us (6%)
  between operations  15.7 us (3%)
    ppermute x67, waiting for transfers between devices, send(): lax.ppermute(plain(block), axis, [(j, target(j) % count) for j in range(c...  166 us
    ppermute x67, starting transfers between devices, send(): lax.ppermute(plain(block), axis, [(j, target(j) % count) for j in range(c...  76.5 us
    pallas_call x1, Pallas kernels, feed_forward(): pl.pallas_call(feed_forward_kernel, in_specs=[smem(), vmem()] + [anywhere...  36.2 us
    unnamed x198, local copies, waits for them, and re-layouts  29.3 us
    pallas_call x1, Pallas kernels, attend_back(): pl.pallas_call(functools.partial(attend_back_kernel, HD ** (-0.5), first_...  17.9 us
    pallas_call x1, Pallas kernels, attend(): pl.pallas_call(functools.partial(attend_kernel, HD ** (-0.5), first_steps...  16.3 us
    pallas_call x1, Pallas kernels, pair_grads(): pl.pallas_call(functools.partial(pair_grads_kernel, orders, len(others)),...  14.5 us
    pallas_call x1, Pallas kernels, down_grads(): pl.pallas_call(functools.partial(down_grads_kernel, blocks), grid_spec=pl...  13 us
  transfers between devices with their start and end apart: 70, of which 42 were waited for; matrix products, arithmetic and copies ran while one was open for 9% of the time, Pallas kernels for 18%

profile of v2, /device:TPU:0, one launch (start us, length us, event | category | flops | bytes accessed | tf_op | source)
XLA Modules:
  0.0 447.3 jit_solution(5912629922859300541)
XLA Ops:
  7.2 2.9 fusion.5
  11.3 5.1 %collective-permute-start = (bf16[64,640]{1,0:T(8,128)(2,1)S(1)}, bf16[64,640]{1,0:T(8,128)(2,1)S(1)}, u32[]{:S(2)}, u32[]{:S(2)}) collective-permute-start(bf16[64,640]{1,0:T(8,128)(2,1)S(1)} %get-tuple-element.184), channel_id=1, source_target_pairs={{0,3},{1,0},{2,1},{3,2},{4,7},{5,4},{6,5},{7,6},{8,11},{9,8},{10,9... | collective-permute-start | bytes 245768 | tf_op jit(solution)/shard_map/ppermute | solution.py:44
  17.4 1.8 collective-permute-done.refs_1_
  19.2 4.7 %collective-permute-done.1.refs_2_ = bf16[64,640]{1,0:T(8,128)(2,1)S(1)} collective-permute-done((bf16[64,640]{1,0:T(8,128)(2,1)S(1)}, bf16[64,640]{1,0:T(8,128)(2,1)S(1)}, u32[]{:S(2)}, u32[]{:S(2)}) %collective-permute-start.1) | collective-permute-done | bytes 81952 | tf_op jit(solution)/shard_map/ppermute | solution.py:44
  23.9 2.1 collective-permute-start.5
  26.6 2.9 concatenate.113
  32.9 3.1 collective-permute-done.5.refs_0_
  35.9 7.9 %collective-permute-done.6.refs_1_ = bf16[128,1536]{1,0:T(8,128)(2,1)S(1)} collective-permute-done((bf16[128,1536]{1,0:T(8,128)(2,1)S(1)}, bf16[128,1536]{1,0:T(8,128)(2,1)S(1)}, u32[]{:S(2)}, u32[]{:S(2)}) %collective-permute-start.6) | collective-permute-done | bytes 393248 | tf_op jit(solution)/shard_map/ppermute | solution.py:44
  46.4 4.2 collective-permute-done.7.refs_2_.refs_1_
  50.6 4.3 collective-permute-done.8.refs_3_.refs_2_
  56.6 1.6 collective-permute-start.9
  58.9 4.2 collective-permute-done.10
  66.2 3.4 collective-permute-start.12
  72.4 6.1 %project.1 = (bf16[2,768,128]{2,1,0:T(8,128)(2,1)}, bf16[2,2,256,128]{3,2,1,0:T(8,128)(2,1)}, bf16[512,1536]{1,0:T(8,128)(2,1)}, bf16[512,1536]{1,0:T(8,128)(2,1)}, bf16[1536,640]{1,0:T(8,128)(2,1)}) custom-call(s32[1]{0:T(128)} %bitcast.own_ref, bf16[128,1536]{1,0:T(8,128)(2,1)} %copy-done.17, bf16[128,1536]{1,0:T(8,128)(2,1)} %copy-done.23, ...), custom_call_target="tpu_custom_call" | custom-call | flops 3228400128 | tf_op jit(solution)/shard_map/project/pallas_call | solution.py:282
  78.5 4.8 %collective-permute-done.12.refs_0_ = bf16[192,1536]{1,0:T(8,128)(2,1)S(1)} collective-permute-done((bf16[192,1536]{1,0:T(8,128)(2,1)S(1)}, bf16[192,1536]{1,0:T(8,128)(2,1)S(1)}, u32[]{:S(2)}, u32[]{:S(2)}) %collective-permute-start.12) | collective-permute-done | bytes 589856 | tf_op jit(solution)/shard_map/ppermute | solution.py:44
  83.3 13.0 %collective-permute-done.13.refs_1_ = bf16[192,1536]{1,0:T(8,128)(2,1)S(1)} collective-permute-done((bf16[192,1536]{1,0:T(8,128)(2,1)S(1)}, bf16[192,1536]{1,0:T(8,128)(2,1)S(1)}, u32[]{:S(2)}, u32[]{:S(2)}) %collective-permute-start.13) | collective-permute-done | bytes 589856 | tf_op jit(solution)/shard_map/ppermute | solution.py:44
  97.3 1.8 collective-permute-start.14
  102.0 12.1 %collective-permute-done.16.refs_0_ = bf16[2,2,256,128]{3,2,1,0:T(8,128)(2,1)S(1)} collective-permute-done((bf16[2,2,256,128]{3,2,1,0:T(8,128)(2,1)S(1)}, bf16[2,2,256,128]{3,2,1,0:T(8,128)(2,1)S(1)}, u32[]{:S(2)}, u32[]{:S(2)}) %collective-permute-start.16) | collective-permute-done | bytes 262176 | tf_op jit(solution)/shard_map/ppermute | solution.py:44
  117.7 5.8 %collective-permute-done.18 = bf16[1,2,256,128]{3,2,1,0:T(8,128)(2,1)} collective-permute-done((bf16[1,2,256,128]{3,2,1,0:T(8,128)(2,1)S(1)}, bf16[1,2,256,128]{3,2,1,0:T(8,128)(2,1)}, u32[]{:S(2)}, u32[]{:S(2)}) %collective-permute-start.18) | collective-permute-done | bytes 131104 | tf_op jit(solution)/shard_map/ppermute | solution.py:44
  127.7 1.8 collective-permute-done.20.other_ref.refs_1_.refs_6_
  132.0 2.0 copy.76.kc_ref.refs_7_
  134.1 16.3 %attend.1 = (bf16[512,384]{1,0:T(8,128)(2,1)}, f32[2,768,128]{2,1,0:T(8,128)}, f32[2,1,768]{2,1,0:T(1,128)}) custom-call(bf16[2,768,128]{2,1,0:T(8,128)(2,1)} %get-tuple-element.80.refs_2_.q_ref, bf16[4,2,2,256,128]{4,3,2,1,0:T(8,128)(2,1)} %pad_maximum_fusion.2.near_ref.refs_5_, ...), custom_call_target="tpu_custom_call" | custom-call | flops 3459000064 | tf_op jit(solution)/shard_map/attend/pallas_call | solution.py:483
  153.6 3.4 collective-permute-start.21
  157.0 3.0 collective-permute-done.25.refs_2_
  162.2 4.4 collective-permute-done.21.refs_0_
  166.6 7.2 %collective-permute-done.22.refs_1_ = bf16[512,384]{1,0:T(8,128)(2,1)S(1)} collective-permute-done((bf16[512,384]{1,0:T(8,128)(2,1)S(1)}, bf16[512,384]{1,0:T(8,128)(2,1)S(1)}, u32[]{:S(2)}, u32[]{:S(2)}) %collective-permute-start.22) | collective-permute-done | bytes 393248 | tf_op jit(solution)/shard_map/ppermute | solution.py:44
  174.6 1.8 collective-permute-start.27
  177.6 4.3 collective-permute-done.27.refs_8_
  181.9 4.3 collective-permute-done.28.refs_9_
  186.9 36.2 %feed_forward.1 = (bf16[512,1536]{1,0:T(8,128)(2,1)}, f32[128,1536]{1,0:T(8,128)}, bf16[512,2304]{1,0:T(8,128)(2,1)}, bf16[512,2304]{1,0:T(8,128)(2,1)}, bf16[51...) custom-call(s32[1]{0:T(128)} %bitcast.own_ref, ...), custom_call_target="tpu_custom_call" | custom-call | flops 18447998976 | tf_op jit(solution)/shard_map/feed_forward/pallas_call | solution.py:689
  223.1 2.1 collective-permute-start.30
  225.7 13.0 %down_grads.1 = (bf16[1536,2304]{1,0:T(8,128)(2,1)}, bf16[512,1536]{1,0:T(8,128)(2,1)}) custom-call(s32[1]{0:T(128)} %bitcast.25.own_ref.head_ref, bf16[512,1536]{1,0:T(8,128)(2,1)} %get-tuple-element.92.c_ref, bf16[1536,6912]{1,0:T(8,128)(2,1)} %all-gather.2.cloned.1.call-done.refs_13_.down_w, bf16[512,2304]{1,0:T(8,128)(2,1)} %get-tuple-element.93.middle_ref), custom_call_target="tpu_custom_call" | custom-call | flops 7263900160 | tf_op jit(solution)/shard_map/down_grads/pallas_call | solution.py:753
  238.7 3.0 copy-done
  241.7 2.9 copy-done.1
  245.8 2.6 collective-permute-done.32.refs_2_.refs_1_
  251.6 3.3 collective-permute-start.35
  254.9 14.5 %pair_grads.1 = (bf16[192,2304]{1,0:T(8,128)(2,1)}, bf16[192,2304]{1,0:T(8,128)(2,1)}, bf16[384,2304]{1,0:T(8,128)(2,1)}, bf16[192,2304]{1,0:T(8,128)(2,1)}, bf1...) custom-call(s32[1]{0:T(128)} %bitcast.own_ref, bf16[512,1536]{1,0:T(8,128)(2,1)} %get-tuple-element.100.refs_0_, ...), custom_call_target="tpu_custom_call" | custom-call | flops 7263900160 | tf_op jit(solution)/shard_map/pair_grads/pallas_call | solution.py:803
  269.4 1.9 collective-permute-done.35.refs_1_
  272.1 5.6 %norm_back.1 = (f32[128,1536]{1,0:T(8,128)}, bf16[128,1536]{1,0:T(8,128)(2,1)}, bf16[128,384]{1,0:T(8,128)(2,1)}, bf16[128,384]{1,0:T(8,128)(2,1)}, bf16[128,384...) custom-call(s32[1]{0:T(128)} %bitcast.own_ref, f32[128,1536]{1,0:T(8,128)} %get-tuple-element.98.refs_0_, ...), custom_call_target="tpu_custom_call" | custom-call | flops 2651899904 | tf_op jit(solution)/shard_map/norm_back/pallas_call | solution.py:846
  280.8 2.7 collective-permute-start.37
  286.8 5.6 %collective-permute-done.38.refs_2_ = bf16[128,384]{1,0:T(8,128)(2,1)S(1)} collective-permute-done((bf16[128,384]{1,0:T(8,128)(2,1)S(1)}, bf16[128,384]{1,0:T(8,128)(2,1)S(1)}, u32[]{:S(2)}, u32[]{:S(2)}) %collective-permute-start.38) | collective-permute-done | bytes 98336 | tf_op jit(solution)/shard_map/ppermute | solution.py:44
  295.7 17.9 %attend_back.1 = (f32[2,768,128]{2,1,0:T(8,128)}, bf16[4,2,2,256,128]{4,3,2,1,0:T(8,128)(2,1)}, bf16[4,2,2,256,128]{4,3,2,1,0:T(8,128)(2,1)}) custom-call(bf16[2,768,128]{2,1,0:T(8,128)(2,1)} %get-tuple-element.80.refs_2_.q_ref, bf16[128,384]{1,0:T(8,128)(2,1)} %get-tuple-element.108.refs_0_, bf16[128,384]{1,0:T(8,128)(2,1)} %copy-done.35, ...), custom_call_target="tpu_custom_call" | custom-call | flops 5995599872 | tf_op jit(solution)/shard_map/attend_back/pallas_call | solution.py:569
  317.3 4.0 collective-permute-start.45
  321.3 5.5 %collective-permute-done.46.refs_4_.refs_11_ = bf16[64,1536]{1,0:T(8,128)(2,1)S(1)} collective-permute-done((bf16[64,1536]{1,0:T(8,128)(2,1)S(1)}, bf16[64,1536]{1,0:T(8,128)(2,1)S(1)}, u32[]{:S(2)}, u32[]{:S(2)}) %collective-permute-start.46) | collective-permute-done | bytes 196640 | tf_op jit(solution)/shard_map/ppermute | solution.py:44
  326.8 2.3 collective-permute-done.45.refs_3_.refs_10_
  329.1 8.9 %collective-permute-done.44.refs_2_.refs_0_ = bf16[2,192,2304]{2,1,0:T(8,128)(2,1)S(1)} collective-permute-done((bf16[2,192,2304]{2,1,0:T(8,128)(2,1)}, bf16[2,192,2304]{2,1,0:T(8,128)(2,1)S(1)}, u32[]{:S(2)}, u32[]{:S(2)}) %collective-permute-start.44) | collective-permute-done | bytes 1769504 | tf_op jit(solution)/shard_map/ppermute | solution.py:44
  340.6 5.6 %collective-permute-done.47 = bf16[2,2,256,128]{3,2,1,0:T(8,128)(2,1)S(1)} collective-permute-done((bf16[2,2,256,128]{3,2,1,0:T(8,128)(2,1)S(1)}, bf16[2,2,256,128]{3,2,1,0:T(8,128)(2,1)S(1)}, u32[]{:S(2)}, u32[]{:S(2)}) %collective-permute-start.47) | collective-permute-done | bytes 262176 | tf_op jit(solution)/shard_map/ppermute | solution.py:44
  350.4 3.1 collective-permute-done.48.refs_2_
  359.1 1.9 select_convert_fusion.refs_0_
  364.1 1.7 collective-permute-start.51
  369.6 1.9 convert_add_fusion.7.refs_1_
  371.5 8.9 %project_back.1 = (f32[128,1536]{1,0:T(8,128)}, bf16[128,1536]{1,0:T(8,128)(2,1)}, bf16[64,1536]{1,0:T(8,128)(2,1)}, bf16[64,1536]{1,0:T(8,128)(2,1)}, bf16[128,...) custom-call(s32[1]{0:T(128)} %bitcast.own_ref, ...), custom_call_target="tpu_custom_call" | custom-call | flops 5188499968 | tf_op jit(solution)/shard_map/project_back/pallas_call | solution.py:375
  383.3 3.2 collective-permute-start.54
  386.6 2.8 convert_add_fusion.3
  389.5 2.8 convert_add_fusion.1
  394.5 7.2 %collective-permute-done.54.refs_0_ = bf16[64,1536]{1,0:T(8,128)(2,1)S(1)} collective-permute-done((bf16[64,1536]{1,0:T(8,128)(2,1)S(1)}, bf16[64,1536]{1,0:T(8,128)(2,1)S(1)}, u32[]{:S(2)}, u32[]{:S(2)}) %collective-permute-start.54) | collective-permute-done | bytes 196640 | tf_op jit(solution)/shard_map/ppermute | solution.py:44
  401.8 3.6 collective-permute-done.55.refs_1_
  405.5 2.5 collective-permute-start.58
  409.0 4.6 %collective-permute-done.66 = bf16[1,192,384]{2,1,0:T(8,128)(2,1)S(1)} collective-permute-done((bf16[1,192,384]{2,1,0:T(8,128)(2,1)S(1)}, bf16[1,192,384]{2,1,0:T(8,128)(2,1)S(1)}, u32[]{:S(2)}, u32[]{:S(2)}) %collective-permute-start.66) | collective-permute-done | bytes 147488 | tf_op jit(solution)/shard_map/ppermute | solution.py:44
  414.7 2.8 collective-permute-done.58.refs_0_
  417.5 8.9 %collective-permute-done.61 = bf16[128,1536]{1,0:T(8,128)(2,1)S(1)} collective-permute-done((bf16[128,1536]{1,0:T(8,128)(2,1)S(1)}, bf16[128,1536]{1,0:T(8,128)(2,1)S(1)}, u32[]{:S(2)}, u32[]{:S(2)}) %collective-permute-start.61) | collective-permute-done | bytes 393248 | tf_op jit(solution)/shard_map/ppermute | solution.py:44
  428.1 1.6 collective-permute-start.63
  432.9 3.0 collective-permute-done.64
  438.7 1.9 add_convert_fusion.1
  (451 shorter events, 90.9 us)
Async XLA Ops:
  7.2 179.0 %all-gather.2.cloned.1.call-start = ((), (), s32[]{:S(2)}) async-start(), calls=%async_computation.2 | async-start | bytes 23887872 | tf_op jit(solution)/shard_map/all_gather | solution.py:907
  10.2 352.7 %reduce-scatter.3.cloned.1.call-start = ((), (), s32[]{:S(2)}) async-start(), calls=%async_computation.3 | async-start | bytes 7962624 | tf_op jit(solution)/shard_map/reduce_scatter | solution.py:1065
  11.3 8.0 %collective-permute-start = (bf16[64,640]{1,0:T(8,128)(2,1)S(1)}, bf16[64,640]{1,0:T(8,128)(2,1)S(1)}, u32[]{:S(2)}, u32[]{:S(2)}) collective-permute-start(bf16[64,640]{1,0:T(8,128)(2,1)S(1)} %get-tuple-element.184), channel_id=1, source_target_pairs={{0,3},{1,0},{2,1},{3,2},{4,7},{5,4},{6,5},{7,6},{8,11},{9,8},{10,9... | collective-permute-start | bytes 245768 | tf_op jit(solution)/shard_map/ppermute | solution.py:44
  16.4 7.5 %collective-permute-start.1 = (bf16[64,640]{1,0:T(8,128)(2,1)S(1)}, bf16[64,640]{1,0:T(8,128)(2,1)S(1)}, u32[]{:S(2)}, u32[]{:S(2)}) collective-permute-start(bf16[64,640]{1,0:T(8,128)(2,1)S(1)} %get-tuple-element.185), channel_id=1, source_target_pairs={{0,2},{1,3},{2,0},{3,1},{4,6},{5,7},{6,4},{7,5},{8,10},{9,11},{10,... | collective-permute-start | bytes 245768 | tf_op jit(solution)/shard_map/ppermute | solution.py:44
  16.4 7.5 %collective-permute-start.2 = (bf16[64,640]{1,0:T(8,128)(2,1)S(1)}, bf16[64,640]{1,0:T(8,128)(2,1)S(1)}, u32[]{:S(2)}, u32[]{:S(2)}) collective-permute-start(bf16[64,640]{1,0:T(8,128)(2,1)S(1)} %get-tuple-element.182), channel_id=1, source_target_pairs={{0,1},{1,2},{2,3},{3,0},{4,5},{5,6},{6,7},{7,4},{8,9},{9,10},{10,1... | collective-permute-start | bytes 245768 | tf_op jit(solution)/shard_map/ppermute | solution.py:44
  23.9 12.1 %collective-permute-start.5 = (bf16[128,1536]{1,0:T(8,128)(2,1)S(1)}, bf16[128,1536]{1,0:T(8,128)(2,1)S(1)}, u32[]{:S(2)}, u32[]{:S(2)}) collective-permute-start(bf16[128,1536]{1,0:T(8,128)(2,1)S(1)} %tie.28.refs_0_), channel_id=1, source_target_pairs={{0,3},{1,0},{2,1},{3,2},{4,7},{5,4},{6,5},{7,6},{8,11},{9,8},{10,9... | collective-permute-start | bytes 1179656 | tf_op jit(solution)/shard_map/ppermute | solution.py:44
  26.0 17.8 %collective-permute-start.6 = (bf16[128,1536]{1,0:T(8,128)(2,1)S(1)}, bf16[128,1536]{1,0:T(8,128)(2,1)S(1)}, u32[]{:S(2)}, u32[]{:S(2)}) collective-permute-start(bf16[128,1536]{1,0:T(8,128)(2,1)S(1)} %tie.28.refs_0_), channel_id=1, source_target_pairs={{0,1},{1,2},{2,3},{3,0},{4,5},{5,6},{6,7},{7,4},{8,9},{9,10},{10,1... | collective-permute-start | bytes 1179656 | tf_op jit(solution)/shard_map/ppermute | solution.py:44
  29.8 16.2 %collective-permute-start.3 = (bf16[224,640]{1,0:T(8,128)(2,1)S(1)}, bf16[224,640]{1,0:T(8,128)(2,1)S(1)}, u32[]{:S(2)}, u32[]{:S(2)}) collective-permute-start(bf16[224,640]{1,0:T(8,128)(2,1)S(1)} %get-tuple-element.156), channel_id=1, source_target_pairs={{0,8},{4,12},{8,0},{12,4},{16,24},{20,28},{24,16},{28,20},{1,9},{5... | collective-permute-start | bytes 860168 | tf_op jit(solution)/shard_map/ppermute | solution.py:44
  31.3 15.1 %collective-permute-start.4 = (bf16[224,640]{1,0:T(8,128)(2,1)S(1)}, bf16[224,640]{1,0:T(8,128)(2,1)S(1)}, u32[]{:S(2)}, u32[]{:S(2)}) collective-permute-start(bf16[224,640]{1,0:T(8,128)(2,1)S(1)} %get-tuple-element.156), channel_id=1, source_target_pairs={{0,16},{4,20},{8,24},{12,28},{16,0},{20,4},{24,8},{28,12},{1,17},{... | collective-permute-start | bytes 860168 | tf_op jit(solution)/shard_map/ppermute | solution.py:44
  43.8 6.8 %collective-permute-start.7 = (bf16[64,1536]{1,0:T(8,128)(2,1)S(1)}, bf16[64,1536]{1,0:T(8,128)(2,1)S(1)}, u32[]{:S(2)}, u32[]{:S(2)}) collective-permute-start(bf16[64,1536]{1,0:T(8,128)(2,1)S(1)} %slice.309), channel_id=1, source_target_pairs={{0,3},{1,0},{2,1},{3,2},{4,7},{5,4},{6,5},{7,6},{8,11},{9,8},{10,9... | collective-permute-start | bytes 589832 | tf_op jit(solution)/shard_map/ppermute | solution.py:44
  45.3 9.7 %collective-permute-start.8 = (bf16[64,1536]{1,0:T(8,128)(2,1)S(1)}, bf16[64,1536]{1,0:T(8,128)(2,1)S(1)}, u32[]{:S(2)}, u32[]{:S(2)}) collective-permute-start(bf16[64,1536]{1,0:T(8,128)(2,1)S(1)} %slice.310), channel_id=1, source_target_pairs={{0,1},{1,2},{2,3},{3,0},{4,5},{5,6},{6,7},{7,4},{8,9},{9,10},{10,1... | collective-permute-start | bytes 589832 | tf_op jit(solution)/shard_map/ppermute | solution.py:44
  55.0 8.1 %collective-permute-start.10 = (bf16[112,640]{1,0:T(8,128)(2,1)S(1)}, bf16[112,640]{1,0:T(8,128)(2,1)S(1)}, u32[]{:S(2)}, u32[]{:S(2)}) collective-permute-start(bf16[112,640]{1,0:T(8,128)(2,1)S(1)} %slice.312), channel_id=1, source_target_pairs={{0,8},{4,12},{8,0},{12,4},{16,24},{20,28},{24,16},{28,20},{1,9},{5... | collective-permute-start | bytes 430088 | tf_op jit(solution)/shard_map/ppermute | solution.py:44
  56.6 7.0 %collective-permute-start.9 = (bf16[112,640]{1,0:T(8,128)(2,1)S(1)}, bf16[112,640]{1,0:T(8,128)(2,1)S(1)}, u32[]{:S(2)}, u32[]{:S(2)}) collective-permute-start(bf16[112,640]{1,0:T(8,128)(2,1)S(1)} %slice.311), channel_id=1, source_target_pairs={{0,16},{4,20},{8,24},{12,28},{16,0},{20,4},{24,8},{28,12},{1,17},{... | collective-permute-start | bytes 430088 | tf_op jit(solution)/shard_map/ppermute | solution.py:44
  63.8 5.8 %collective-permute-start.11 = (bf16[4,224,640]{2,1,0:T(8,128)(2,1)S(1)}, bf16[4,224,640]{2,1,0:T(8,128)(2,1)S(1)}, u32[]{:S(2)}, u32[]{:S(2)}) collective-permute-start(bf16[4,224,640]{2,1,0:T(8,128)(2,1)S(1)} %pad_maximum_fusion.1.refs_9_), channel_id=1, source_target_pairs={{0,4},{4,0},{8,12},{12,8},{16,20},{20,16},{24,28},{28,24},{1,5},{5... | collective-permute-start | bytes 3440648 | tf_op jit(solution)/shard_map/ppermute | solution.py:44
  66.2 17.1 %collective-permute-start.12 = (bf16[192,1536]{1,0:T(8,128)(2,1)S(1)}, bf16[192,1536]{1,0:T(8,128)(2,1)S(1)}, u32[]{:S(2)}, u32[]{:S(2)}) collective-permute-start(bf16[192,1536]{1,0:T(8,128)(2,1)S(1)} %tie.31.refs_1_), channel_id=1, source_target_pairs={{0,3},{1,0},{2,1},{3,2},{4,7},{5,4},{6,5},{7,6},{8,11},{9,8},{10,9... | collective-permute-start | bytes 1769480 | tf_op jit(solution)/shard_map/ppermute | solution.py:44
  69.6 26.7 %collective-permute-start.13 = (bf16[192,1536]{1,0:T(8,128)(2,1)S(1)}, bf16[192,1536]{1,0:T(8,128)(2,1)S(1)}, u32[]{:S(2)}, u32[]{:S(2)}) collective-permute-start(bf16[192,1536]{1,0:T(8,128)(2,1)S(1)} %tie.31.refs_1_), channel_id=1, source_target_pairs={{0,1},{1,2},{2,3},{3,0},{4,5},{5,6},{6,7},{7,4},{8,9},{9,10},{10,1... | collective-permute-start | bytes 1769480 | tf_op jit(solution)/shard_map/ppermute | solution.py:44
  97.3 17.7 %collective-permute-start.14 = (bf16[96,1536]{1,0:T(8,128)(2,1)S(1)}, bf16[96,1536]{1,0:T(8,128)(2,1)S(1)}, u32[]{:S(2)}, u32[]{:S(2)}) collective-permute-start(bf16[96,1536]{1,0:T(8,128)(2,1)S(1)} %slice.326), channel_id=1, source_target_pairs={{0,3},{1,0},{2,1},{3,2},{4,7},{5,4},{6,5},{7,6},{8,11},{9,8},{10,9... | collective-permute-start | bytes 884744 | tf_op jit(solution)/shard_map/ppermute | solution.py:44
  99.1 15.9 %collective-permute-start.15 = (bf16[96,1536]{1,0:T(8,128)(2,1)S(1)}, bf16[96,1536]{1,0:T(8,128)(2,1)S(1)}, u32[]{:S(2)}, u32[]{:S(2)}) collective-permute-start(bf16[96,1536]{1,0:T(8,128)(2,1)S(1)} %slice.327), channel_id=1, source_target_pairs={{0,1},{1,2},{2,3},{3,0},{4,5},{5,6},{6,7},{7,4},{8,9},{9,10},{10,1... | collective-permute-start | bytes 884744 | tf_op jit(solution)/shard_map/ppermute | solution.py:44
  99.9 14.2 %collective-permute-start.16 = (bf16[2,2,256,128]{3,2,1,0:T(8,128)(2,1)S(1)}, bf16[2,2,256,128]{3,2,1,0:T(8,128)(2,1)S(1)}, u32[]{:S(2)}, u32[]{:S(2)}) collective-permute-start(bf16[2,2,256,128]{3,2,1,0:T(8,128)(2,1)S(1)} %copy-done.70), channel_id=1, source_target_pairs={{0,8},{4,12},{8,0},{12,4},{16,24},{20,28},{24,16},{28,20},{1,9},{5... | collective-permute-start | bytes 786440 | tf_op jit(solution)/shard_map/ppermute | solution.py:44
  100.8 14.1 %collective-permute-start.17 = (bf16[2,2,256,128]{3,2,1,0:T(8,128)(2,1)S(1)}, bf16[2,2,256,128]{3,2,1,0:T(8,128)(2,1)S(1)}, u32[]{:S(2)}, u32[]{:S(2)}) collective-permute-start(bf16[2,2,256,128]{3,2,1,0:T(8,128)(2,1)S(1)} %copy-done.70), channel_id=1, source_target_pairs={{0,16},{4,20},{8,24},{12,28},{16,0},{20,4},{24,8},{28,12},{1,17},{... | collective-permute-start | bytes 786440 | tf_op jit(solution)/shard_map/ppermute | solution.py:44
  115.0 8.4 %collective-permute-start.18 = (bf16[1,2,256,128]{3,2,1,0:T(8,128)(2,1)S(1)}, bf16[1,2,256,128]{3,2,1,0:T(8,128)(2,1)}, u32[]{:S(2)}, u32[]{:S(2)}) collective-permute-start(bf16[1,2,256,128]{3,2,1,0:T(8,128)(2,1)S(1)} %slice.328), channel_id=1, source_target_pairs={{0,16},{4,20},{8,24},{12,28},{16,0},{20,4},{24,8},{28,12},{1,17},{... | collective-permute-start | bytes 393224 | tf_op jit(solution)/shard_map/ppermute | solution.py:44
  116.2 8.3 %collective-permute-start.19 = (bf16[1,2,256,128]{3,2,1,0:T(8,128)(2,1)S(1)}, bf16[1,2,256,128]{3,2,1,0:T(8,128)(2,1)}, u32[]{:S(2)}, u32[]{:S(2)}) collective-permute-start(bf16[1,2,256,128]{3,2,1,0:T(8,128)(2,1)S(1)} %slice.329), channel_id=1, source_target_pairs={{0,8},{4,12},{8,0},{12,4},{16,24},{20,28},{24,16},{28,20},{1,9},{5... | collective-permute-start | bytes 393224 | tf_op jit(solution)/shard_map/ppermute | solution.py:44
  129.6 20.8 %collective-permute-start.23 = (bf16[192,1536]{1,0:T(8,128)(2,1)S(1)}, bf16[192,1536]{1,0:T(8,128)(2,1)S(1)}, u32[]{:S(2)}, u32[]{:S(2)}) collective-permute-start(bf16[192,1536]{1,0:T(8,128)(2,1)S(1)} %tie.34), channel_id=1, source_target_pairs={{0,8},{4,12},{8,0},{12,4},{16,24},{20,28},{24,16},{28,20},{1,9},{5... | collective-permute-start | bytes 1769480 | tf_op jit(solution)/shard_map/ppermute | solution.py:44
  130.2 20.2 %collective-permute-start.24 = (bf16[192,1536]{1,0:T(8,128)(2,1)S(1)}, bf16[192,1536]{1,0:T(8,128)(2,1)S(1)}, u32[]{:S(2)}, u32[]{:S(2)}) collective-permute-start(bf16[192,1536]{1,0:T(8,128)(2,1)S(1)} %tie.34), channel_id=1, source_target_pairs={{0,16},{4,20},{8,24},{12,28},{16,0},{20,4},{24,8},{28,12},{1,17},{... | collective-permute-start | bytes 1769480 | tf_op jit(solution)/shard_map/ppermute | solution.py:44
  151.5 8.6 %collective-permute-start.25 = (bf16[96,1536]{1,0:T(8,128)(2,1)S(1)}, bf16[96,1536]{1,0:T(8,128)(2,1)S(1)}, u32[]{:S(2)}, u32[]{:S(2)}) collective-permute-start(bf16[96,1536]{1,0:T(8,128)(2,1)S(1)} %slice.335), channel_id=1, source_target_pairs={{0,16},{4,20},{8,24},{12,28},{16,0},{20,4},{24,8},{28,12},{1,17},{... | collective-permute-start | bytes 884744 | tf_op jit(solution)/shard_map/ppermute | solution.py:44
  152.2 8.3 %collective-permute-start.26 = (bf16[96,1536]{1,0:T(8,128)(2,1)S(1)}, bf16[96,1536]{1,0:T(8,128)(2,1)S(1)}, u32[]{:S(2)}, u32[]{:S(2)}) collective-permute-start(bf16[96,1536]{1,0:T(8,128)(2,1)S(1)} %slice.336), channel_id=1, source_target_pairs={{0,8},{4,12},{8,0},{12,4},{16,24},{20,28},{24,16},{28,20},{1,9},{5... | collective-permute-start | bytes 884744 | tf_op jit(solution)/shard_map/ppermute | solution.py:44
  153.6 13.0 %collective-permute-start.21 = (bf16[512,384]{1,0:T(8,128)(2,1)S(1)}, bf16[512,384]{1,0:T(8,128)(2,1)S(1)}, u32[]{:S(2)}, u32[]{:S(2)}) collective-permute-start(bf16[512,384]{1,0:T(8,128)(2,1)S(1)} %copy-done.29), channel_id=1, source_target_pairs={{0,3},{1,0},{2,1},{3,2},{4,7},{5,4},{6,5},{7,6},{8,11},{9,8},{10,9... | collective-permute-start | bytes 1179656 | tf_op jit(solution)/shard_map/ppermute | solution.py:44
  157.0 16.7 %collective-permute-start.22 = (bf16[512,384]{1,0:T(8,128)(2,1)S(1)}, bf16[512,384]{1,0:T(8,128)(2,1)S(1)}, u32[]{:S(2)}, u32[]{:S(2)}) collective-permute-start(bf16[512,384]{1,0:T(8,128)(2,1)S(1)} %copy-done.29), channel_id=1, source_target_pairs={{0,1},{1,2},{2,3},{3,0},{4,5},{5,6},{6,7},{7,4},{8,9},{9,10},{10,1... | collective-permute-start | bytes 1179656 | tf_op jit(solution)/shard_map/ppermute | solution.py:44
  173.7 12.5 %collective-permute-start.29 = (bf16[4,192,1536]{2,1,0:T(8,128)(2,1)S(1)}, bf16[4,192,1536]{2,1,0:T(8,128)(2,1)}, u32[]{:S(2)}, u32[]{:S(2)}) collective-permute-start(bf16[4,192,1536]{2,1,0:T(8,128)(2,1)S(1)} %tie.37), channel_id=1, source_target_pairs={{0,4},{4,0},{8,12},{12,8},{16,20},{20,16},{24,28},{28,24},{1,5},{5... | collective-permute-start | bytes 7077896 | tf_op jit(solution)/shard_map/ppermute | solution.py:44
  174.6 7.3 %collective-permute-start.27 = (bf16[256,384]{1,0:T(8,128)(2,1)S(1)}, bf16[256,384]{1,0:T(8,128)(2,1)S(1)}, u32[]{:S(2)}, u32[]{:S(2)}) collective-permute-start(bf16[256,384]{1,0:T(8,128)(2,1)S(1)} %slice.337), channel_id=1, source_target_pairs={{0,3},{1,0},{2,1},{3,2},{4,7},{5,4},{6,5},{7,6},{8,11},{9,8},{10,9... | collective-permute-start | bytes 589832 | tf_op jit(solution)/shard_map/ppermute | solution.py:44
  176.4 9.8 %collective-permute-start.28 = (bf16[256,384]{1,0:T(8,128)(2,1)S(1)}, bf16[256,384]{1,0:T(8,128)(2,1)S(1)}, u32[]{:S(2)}, u32[]{:S(2)}) collective-permute-start(bf16[256,384]{1,0:T(8,128)(2,1)S(1)} %slice.338), channel_id=1, source_target_pairs={{0,1},{1,2},{2,3},{3,0},{4,5},{5,6},{6,7},{7,4},{8,9},{9,10},{10,1... | collective-permute-start | bytes 589832 | tf_op jit(solution)/shard_map/ppermute | solution.py:44
  223.1 15.6 %collective-permute-start.30 = (bf16[64,1536]{1,0:T(8,128)(2,1)}, bf16[64,1536]{1,0:T(8,128)(2,1)S(1)}, u32[]{:S(2)}, u32[]{:S(2)}) collective-permute-start(bf16[64,1536]{1,0:T(8,128)(2,1)} %get-tuple-element.96), channel_id=1, source_target_pairs={{0,3},{1,0},{2,1},{3,2},{4,7},{5,4},{6,5},{7,6},{8,11},{9,8},{10,9... | collective-permute-start | bytes 589832 | tf_op jit(solution)/shard_map/ppermute | solution.py:44
  225.2 13.5 %collective-permute-start.31 = (bf16[64,1536]{1,0:T(8,128)(2,1)}, bf16[64,1536]{1,0:T(8,128)(2,1)S(1)}, u32[]{:S(2)}, u32[]{:S(2)}) collective-permute-start(bf16[64,1536]{1,0:T(8,128)(2,1)} %get-tuple-element.97), channel_id=1, source_target_pairs={{0,1},{1,2},{2,3},{3,0},{4,5},{5,6},{6,7},{7,4},{8,9},{9,10},{10,1... | collective-permute-start | bytes 589832 | tf_op jit(solution)/shard_map/ppermute | solution.py:44
  225.2 23.3 %collective-permute-start.33 = (bf16[512,2304]{1,0:T(8,128)(2,1)}, bf16[512,2304]{1,0:T(8,128)(2,1)S(1)}, u32[]{:S(2)}, u32[]{:S(2)}) collective-permute-start(bf16[512,2304]{1,0:T(8,128)(2,1)} %get-tuple-element.101.refs_2_), channel_id=1, source_target_pairs={{0,4},{4,0},{8,12},{12,8},{16,20},{20,16},{24,28},{28,24},{1,5},{5... | collective-permute-start | bytes 7077896 | tf_op jit(solution)/shard_map/ppermute | solution.py:44
  225.2 23.3 %collective-permute-start.34 = (bf16[512,2304]{1,0:T(8,128)(2,1)}, bf16[512,2304]{1,0:T(8,128)(2,1)}, u32[]{:S(2)}, u32[]{:S(2)}) collective-permute-start(bf16[512,2304]{1,0:T(8,128)(2,1)} %get-tuple-element.102.refs_4_), channel_id=1, source_target_pairs={{0,4},{4,0},{8,12},{12,8},{16,20},{20,16},{24,28},{28,24},{1,5},{5... | collective-permute-start | bytes 7077896 | tf_op jit(solution)/shard_map/ppermute | solution.py:44
  244.7 194.0 %reduce-scatter.5.cloned.1.call-start = ((), (), s32[]{:S(2)}) async-start(), calls=%async_computation.4 | async-start | bytes 1966080 | tf_op jit(solution)/shard_map/reduce_scatter | solution.py:1129
  250.4 19.0 %collective-permute-start.36 = (bf16[128,1536]{1,0:T(8,128)(2,1)S(1)}, bf16[128,1536]{1,0:T(8,128)(2,1)S(1)}, u32[]{:S(2)}, u32[]{:S(2)}) collective-permute-start(bf16[128,1536]{1,0:T(8,128)(2,1)S(1)} %pad_maximum_fusion.4.refs_7_), channel_id=1, source_target_pairs={{0,1},{1,2},{2,3},{3,0},{4,5},{5,6},{6,7},{7,4},{8,9},{9,10},{10,1... | collective-permute-start | bytes 1179656 | tf_op jit(solution)/shard_map/ppermute | solution.py:44
  251.6 19.8 %collective-permute-start.35 = (bf16[128,1536]{1,0:T(8,128)(2,1)S(1)}, bf16[128,1536]{1,0:T(8,128)(2,1)S(1)}, u32[]{:S(2)}, u32[]{:S(2)}) collective-permute-start(bf16[128,1536]{1,0:T(8,128)(2,1)S(1)} %pad_maximum_fusion.3.refs_6_), channel_id=1, source_target_pairs={{0,3},{1,0},{2,1},{3,2},{4,7},{5,4},{6,5},{7,6},{8,11},{9,8},{10,9... | collective-permute-start | bytes 1179656 | tf_op jit(solution)/shard_map/ppermute | solution.py:44
  278.7 59.2 %collective-permute-start.44 = (bf16[2,192,2304]{2,1,0:T(8,128)(2,1)}, bf16[2,192,2304]{2,1,0:T(8,128)(2,1)S(1)}, u32[]{:S(2)}, u32[]{:S(2)}) collective-permute-start(bf16[2,192,2304]{2,1,0:T(8,128)(2,1)} %tie.44), channel_id=1, source_target_pairs={{0,8},{4,12},{8,0},{12,4},{16,24},{20,28},{24,16},{28,20},{1,9},{5... | collective-permute-start | bytes 5308424 | tf_op jit(solution)/shard_map/ppermute | solution.py:44
  279.5 58.5 %collective-permute-start.43 = (bf16[2,192,2304]{2,1,0:T(8,128)(2,1)}, bf16[2,192,2304]{2,1,0:T(8,128)(2,1)S(1)}, u32[]{:S(2)}, u32[]{:S(2)}) collective-permute-start(bf16[2,192,2304]{2,1,0:T(8,128)(2,1)} %tie.43), channel_id=1, source_target_pairs={{0,16},{4,20},{8,24},{12,28},{16,0},{20,4},{24,8},{28,12},{1,17},{... | collective-permute-start | bytes 5308424 | tf_op jit(solution)/shard_map/ppermute | solution.py:44
  280.8 5.9 %collective-permute-start.37 = (bf16[128,384]{1,0:T(8,128)(2,1)S(1)}, bf16[128,384]{1,0:T(8,128)(2,1)S(1)}, u32[]{:S(2)}, u32[]{:S(2)}) collective-permute-start(bf16[128,384]{1,0:T(8,128)(2,1)S(1)} %copy-done.81), channel_id=1, source_target_pairs={{0,3},{1,0},{2,1},{3,2},{4,7},{5,4},{6,5},{7,6},{8,11},{9,8},{10,9... | collective-permute-start | bytes 294920 | tf_op jit(solution)/shard_map/ppermute | solution.py:44
  283.5 8.9 %collective-permute-start.38 = (bf16[128,384]{1,0:T(8,128)(2,1)S(1)}, bf16[128,384]{1,0:T(8,128)(2,1)S(1)}, u32[]{:S(2)}, u32[]{:S(2)}) collective-permute-start(bf16[128,384]{1,0:T(8,128)(2,1)S(1)} %copy-done.80), channel_id=1, source_target_pairs={{0,2},{1,3},{2,0},{3,1},{4,6},{5,7},{6,4},{7,5},{8,10},{9,11},{10,... | collective-permute-start | bytes 294920 | tf_op jit(solution)/shard_map/ppermute | solution.py:44
  283.6 8.8 %collective-permute-start.39 = (bf16[128,384]{1,0:T(8,128)(2,1)S(1)}, bf16[128,384]{1,0:T(8,128)(2,1)S(1)}, u32[]{:S(2)}, u32[]{:S(2)}) collective-permute-start(bf16[128,384]{1,0:T(8,128)(2,1)S(1)} %copy-done.79), channel_id=1, source_target_pairs={{0,1},{1,2},{2,3},{3,0},{4,5},{5,6},{6,7},{7,4},{8,9},{9,10},{10,1... | collective-permute-start | bytes 294920 | tf_op jit(solution)/shard_map/ppermute | solution.py:44
  293.6 20.0 %collective-permute-start.40 = (bf16[128,1536]{1,0:T(8,128)(2,1)}, bf16[128,1536]{1,0:T(8,128)(2,1)S(1)}, u32[]{:S(2)}, u32[]{:S(2)}) collective-permute-start(bf16[128,1536]{1,0:T(8,128)(2,1)} %tie.41), channel_id=1, source_target_pairs={{0,3},{1,0},{2,1},{3,2},{4,7},{5,4},{6,5},{7,6},{8,11},{9,8},{10,9... | collective-permute-start | bytes 1179656 | tf_op jit(solution)/shard_map/ppermute | solution.py:44
  295.0 19.0 %collective-permute-start.41 = (bf16[128,1536]{1,0:T(8,128)(2,1)}, bf16[128,1536]{1,0:T(8,128)(2,1)}, u32[]{:S(2)}, u32[]{:S(2)}) collective-permute-start(bf16[128,1536]{1,0:T(8,128)(2,1)} %tie.41), channel_id=1, source_target_pairs={{0,1},{1,2},{2,3},{3,0},{4,5},{5,6},{6,7},{7,4},{8,9},{9,10},{10,1... | collective-permute-start | bytes 1179656 | tf_op jit(solution)/shard_map/ppermute | solution.py:44
  316.2 12.8 %collective-permute-start.42 = (bf16[4,2,2,256,128]{4,3,2,1,0:T(8,128)(2,1)}, bf16[4,2,2,256,128]{4,3,2,1,0:T(8,128)(2,1)S(1)}, u32[]{:S(2)}, u32[]{:S(2)}) collective-permute-start(bf16[4,2,2,256,128]{4,3,2,1,0:T(8,128)(2,1)} %copy-done.22), channel_id=1, source_target_pairs={{0,4},{4,0},{8,12},{12,8},{16,20},{20,16},{24,28},{28,24},{1,5},{5... | collective-permute-start | bytes 3145736 | tf_op jit(solution)/shard_map/ppermute | solution.py:44
  317.2 9.6 %collective-permute-start.46 = (bf16[64,1536]{1,0:T(8,128)(2,1)S(1)}, bf16[64,1536]{1,0:T(8,128)(2,1)S(1)}, u32[]{:S(2)}, u32[]{:S(2)}) collective-permute-start(bf16[64,1536]{1,0:T(8,128)(2,1)S(1)} %slice.420), channel_id=1, source_target_pairs={{0,1},{1,2},{2,3},{3,0},{4,5},{5,6},{6,7},{7,4},{8,9},{9,10},{10,1... | collective-permute-start | bytes 589832 | tf_op jit(solution)/shard_map/ppermute | solution.py:44
  317.3 11.8 %collective-permute-start.45 = (bf16[64,1536]{1,0:T(8,128)(2,1)S(1)}, bf16[64,1536]{1,0:T(8,128)(2,1)S(1)}, u32[]{:S(2)}, u32[]{:S(2)}) collective-permute-start(bf16[64,1536]{1,0:T(8,128)(2,1)S(1)} %slice.419), channel_id=1, source_target_pairs={{0,3},{1,0},{2,1},{3,2},{4,7},{5,4},{6,5},{7,6},{8,11},{9,8},{10,9... | collective-permute-start | bytes 589832 | tf_op jit(solution)/shard_map/ppermute | solution.py:44
  338.4 7.8 %collective-permute-start.47 = (bf16[2,2,256,128]{3,2,1,0:T(8,128)(2,1)S(1)}, bf16[2,2,256,128]{3,2,1,0:T(8,128)(2,1)S(1)}, u32[]{:S(2)}, u32[]{:S(2)}) collective-permute-start(bf16[2,2,256,128]{3,2,1,0:T(8,128)(2,1)S(1)} %pad_maximum_fusion.9), channel_id=1, source_target_pairs={{0,8},{4,12},{8,0},{12,4},{16,24},{20,28},{24,16},{28,20},{1,9},{5... | collective-permute-start | bytes 786440 | tf_op jit(solution)/shard_map/ppermute | solution.py:44
  340.0 7.4 %collective-permute-start.49 = (bf16[2,2,256,128]{3,2,1,0:T(8,128)(2,1)S(1)}, bf16[2,2,256,128]{3,2,1,0:T(8,128)(2,1)S(1)}, u32[]{:S(2)}, u32[]{:S(2)}) collective-permute-start(bf16[2,2,256,128]{3,2,1,0:T(8,128)(2,1)S(1)} %pad_maximum_fusion.10), channel_id=1, source_target_pairs={{0,16},{4,20},{8,24},{12,28},{16,0},{20,4},{24,8},{28,12},{1,17},{... | collective-permute-start | bytes 786440 | tf_op jit(solution)/shard_map/ppermute | solution.py:44
  355.4 25.6 %collective-permute-start.53 = (bf16[1,192,2304]{2,1,0:T(8,128)(2,1)}, bf16[1,192,2304]{2,1,0:T(8,128)(2,1)}, u32[]{:S(2)}, u32[]{:S(2)}) collective-permute-start(bf16[1,192,2304]{2,1,0:T(8,128)(2,1)} %fusion.6), channel_id=1, source_target_pairs={{0,16},{4,20},{8,24},{12,28},{16,0},{20,4},{24,8},{28,12},{1,17},{... | collective-permute-start | bytes 2654216 | tf_op jit(solution)/shard_map/ppermute | solution.py:44
  357.8 24.3 %collective-permute-start.52 = (bf16[1,192,2304]{2,1,0:T(8,128)(2,1)}, bf16[1,192,2304]{2,1,0:T(8,128)(2,1)}, u32[]{:S(2)}, u32[]{:S(2)}) collective-permute-start(bf16[1,192,2304]{2,1,0:T(8,128)(2,1)} %fusion.7), channel_id=1, source_target_pairs={{0,8},{4,12},{8,0},{12,4},{16,24},{20,28},{24,16},{28,20},{1,9},{5... | collective-permute-start | bytes 2654216 | tf_op jit(solution)/shard_map/ppermute | solution.py:44
  380.5 11.9 %collective-permute-start.57 = (bf16[4,192,384]{2,1,0:T(8,128)(2,1)}, bf16[4,192,384]{2,1,0:T(8,128)(2,1)S(1)}, u32[]{:S(2)}, u32[]{:S(2)}) collective-permute-start(bf16[4,192,384]{2,1,0:T(8,128)(2,1)} %get-tuple-element.132), channel_id=1, source_target_pairs={{0,4},{4,0},{8,12},{12,8},{16,20},{20,16},{24,28},{28,24},{1,5},{5... | collective-permute-start | bytes 1769480 | tf_op jit(solution)/shard_map/ppermute | solution.py:44
  380.5 12.7 %collective-permute-start.56 = (bf16[4,208,512]{2,1,0:T(8,128)(2,1)}, bf16[4,208,512]{2,1,0:T(8,128)(2,1)S(1)}, u32[]{:S(2)}, u32[]{:S(2)}) collective-permute-start(bf16[4,208,512]{2,1,0:T(8,128)(2,1)} %get-tuple-element.131), channel_id=1, source_target_pairs={{0,4},{4,0},{8,12},{12,8},{16,20},{20,16},{24,28},{28,24},{1,5},{5... | collective-permute-start | bytes 2555912 | tf_op jit(solution)/shard_map/ppermute | solution.py:44
  383.3 18.4 %collective-permute-start.54 = (bf16[64,1536]{1,0:T(8,128)(2,1)S(1)}, bf16[64,1536]{1,0:T(8,128)(2,1)S(1)}, u32[]{:S(2)}, u32[]{:S(2)}) collective-permute-start(bf16[64,1536]{1,0:T(8,128)(2,1)S(1)} %get-tuple-element.129), channel_id=1, source_target_pairs={{0,3},{1,0},{2,1},{3,2},{4,7},{5,4},{6,5},{7,6},{8,11},{9,8},{10,9... | collective-permute-start | bytes 589832 | tf_op jit(solution)/shard_map/ppermute | solution.py:44
  386.5 18.9 %collective-permute-start.55 = (bf16[64,1536]{1,0:T(8,128)(2,1)S(1)}, bf16[64,1536]{1,0:T(8,128)(2,1)S(1)}, u32[]{:S(2)}, u32[]{:S(2)}) collective-permute-start(bf16[64,1536]{1,0:T(8,128)(2,1)S(1)} %get-tuple-element.130), channel_id=1, source_target_pairs={{0,1},{1,2},{2,3},{3,0},{4,5},{5,6},{6,7},{7,4},{8,9},{9,10},{10,1... | collective-permute-start | bytes 589832 | tf_op jit(solution)/shard_map/ppermute | solution.py:44
  392.4 15.6 %collective-permute-start.60 = (bf16[2,192,384]{2,1,0:T(8,128)(2,1)S(1)}, bf16[2,192,384]{2,1,0:T(8,128)(2,1)S(1)}, u32[]{:S(2)}, u32[]{:S(2)}) collective-permute-start(bf16[2,192,384]{2,1,0:T(8,128)(2,1)S(1)} %add_convert_fusion.2), channel_id=1, source_target_pairs={{0,8},{4,12},{8,0},{12,4},{16,24},{20,28},{24,16},{28,20},{1,9},{5... | collective-permute-start | bytes 884744 | tf_op jit(solution)/shard_map/ppermute | solution.py:44
  393.3 21.1 %collective-permute-start.59 = (bf16[2,208,512]{2,1,0:T(8,128)(2,1)S(1)}, bf16[2,208,512]{2,1,0:T(8,128)(2,1)S(1)}, u32[]{:S(2)}, u32[]{:S(2)}) collective-permute-start(bf16[2,208,512]{2,1,0:T(8,128)(2,1)S(1)} %add_convert_fusion), channel_id=1, source_target_pairs={{0,16},{4,20},{8,24},{12,28},{16,0},{20,4},{24,8},{28,12},{1,17},{... | collective-permute-start | bytes 1277960 | tf_op jit(solution)/shard_map/ppermute | solution.py:44
  405.5 12.1 %collective-permute-start.58 = (bf16[128,1536]{1,0:T(8,128)(2,1)S(1)}, bf16[128,1536]{1,0:T(8,128)(2,1)S(1)}, u32[]{:S(2)}, u32[]{:S(2)}) collective-permute-start(bf16[128,1536]{1,0:T(8,128)(2,1)S(1)} %pad_maximum_fusion.5), channel_id=1, source_target_pairs={{0,3},{1,0},{2,1},{3,2},{4,7},{5,4},{6,5},{7,6},{8,11},{9,8},{10,9... | collective-permute-start | bytes 1179656 | tf_op jit(solution)/shard_map/ppermute | solution.py:44
  408.1 5.5 %collective-permute-start.66 = (bf16[1,192,384]{2,1,0:T(8,128)(2,1)S(1)}, bf16[1,192,384]{2,1,0:T(8,128)(2,1)S(1)}, u32[]{:S(2)}, u32[]{:S(2)}) collective-permute-start(bf16[1,192,384]{2,1,0:T(8,128)(2,1)S(1)} %add_convert_fusion.9), channel_id=1, source_target_pairs={{0,16},{4,20},{8,24},{12,28},{16,0},{20,4},{24,8},{28,12},{1,17},{... | collective-permute-start | bytes 442376 | tf_op jit(solution)/shard_map/ppermute | solution.py:44
  408.9 17.5 %collective-permute-start.61 = (bf16[128,1536]{1,0:T(8,128)(2,1)S(1)}, bf16[128,1536]{1,0:T(8,128)(2,1)S(1)}, u32[]{:S(2)}, u32[]{:S(2)}) collective-permute-start(bf16[128,1536]{1,0:T(8,128)(2,1)S(1)} %pad_maximum_fusion.6), channel_id=1, source_target_pairs={{0,1},{1,2},{2,3},{3,0},{4,5},{5,6},{6,7},{7,4},{8,9},{9,10},{10,1... | collective-permute-start | bytes 1179656 | tf_op jit(solution)/shard_map/ppermute | solution.py:44
  414.5 13.3 %collective-permute-start.62 = (bf16[1,208,512]{2,1,0:T(8,128)(2,1)S(1)}, bf16[1,208,512]{2,1,0:T(8,128)(2,1)S(1)}, u32[]{:S(2)}, u32[]{:S(2)}) collective-permute-start(bf16[1,208,512]{2,1,0:T(8,128)(2,1)S(1)} %add_convert_fusion.4), channel_id=1, source_target_pairs={{0,8},{4,12},{8,0},{12,4},{16,24},{20,28},{24,16},{28,20},{1,9},{5... | collective-permute-start | bytes 638984 | tf_op jit(solution)/shard_map/ppermute | solution.py:44
  429.7 6.3 %collective-permute-start.64 = (bf16[64,512]{1,0:T(8,128)(2,1)S(1)}, bf16[64,512]{1,0:T(8,128)(2,1)S(1)}, u32[]{:S(2)}, u32[]{:S(2)}) collective-permute-start(bf16[64,512]{1,0:T(8,128)(2,1)S(1)} %get-tuple-element.153), channel_id=1, source_target_pairs={{0,2},{1,3},{2,0},{3,1},{4,6},{5,7},{6,4},{7,5},{8,10},{9,11},{10,... | collective-permute-start | bytes 196616 | tf_op jit(solution)/shard_map/ppermute | solution.py:44
  430.6 6.1 %collective-permute-start.65 = (bf16[64,512]{1,0:T(8,128)(2,1)S(1)}, bf16[64,512]{1,0:T(8,128)(2,1)S(1)}, u32[]{:S(2)}, u32[]{:S(2)}) collective-permute-start(bf16[64,512]{1,0:T(8,128)(2,1)S(1)} %get-tuple-element.154), channel_id=1, source_target_pairs={{0,1},{1,2},{2,3},{3,0},{4,5},{5,6},{6,7},{7,4},{8,9},{9,10},{10,1... | collective-permute-start | bytes 196616 | tf_op jit(solution)/shard_map/ppermute | solution.py:44
  (90 other events, 526.2 us)
Sparse Core Ops, SparseCore 0:
  10.3 132.8 all-gather.1
  244.8 85.6 reduce-scatter.2
  367.2 42.5 reduce-scatter.4

commit v3 on v2

--- a/solution.py
+++ b/solution.py
@@ -1,4 +1,5 @@
 import functools
+import math
 
 import jax
 import jax.numpy as jnp
@@ -19,10 +20,13 @@
 EPS = 1e-06
 ROPE_BASE = 1000000.0
 MASKED = -1e30
+LOWEST = -1e29
 SEG_STEP = 1 << 20
 TILE = 768
 MIB = 2**20
 
+TUNE = dict(x1=10, x2=30, mx=10, c2=8, g0=25, g1=10, wm=10, ct=15, project=7, project_back=9, attend=16, attend_back=18, feed_forward=36, down_product=8, pair_grads=7, norm_back=5.5, payload=2)
+
 BF = jnp.bfloat16
 F32 = jnp.float32
 
@@ -60,7 +64,7 @@
     del refs
 
 
-def tie_all(blocks, *others):
+def tie_all(blocks, *others, micros=0):
     count = len(blocks)
     return pl.pallas_call(
         tie_kernel,
@@ -68,7 +72,10 @@
         out_specs=[pl.BlockSpec(memory_space=pl.ANY)] * count,
         out_shape=[jax.ShapeDtypeStruct(block.shape, block.dtype) for block in blocks],
         input_output_aliases={i: i for i in range(count)},
-        compiler_params=pltpu.CompilerParams(vmem_limit_bytes=MIB),
+        compiler_params=pltpu.CompilerParams(
+            vmem_limit_bytes=60 * MIB if max(block.size for block in blocks) > MIB else MIB
+        ),
+        cost_estimate=cost(micros),
         name="tie",
     )(*blocks, *others)
 
@@ -77,11 +84,11 @@
     return tie_all([block], *others)[0]
 
 
-def gather_blocks(block, axis, last=()):
+def gather_blocks(block, axis, last=(), micros=0):
     half = block.shape[0] // 2
     above = from_next(block, axis)
     below = to_next(block, axis)
-    above, below = tie_all([above, below], *last)
+    above, below = tie_all([above, below], *last, micros=micros)
     return [block, above, from_next(above[:half], axis), to_next(below[half:], axis), below]
 
 
@@ -89,24 +96,42 @@
     return from_next(far[0], axis), to_next(far[1], axis)
 
 
-def sum_payload(ahead, behind, moved, last=()):
-    half = ahead.shape[0] // 2
-    from_above, from_below = tie_all(moved, *last)
-    down = jnp.concatenate([behind[:half].astype(F32) + from_above.astype(F32), behind[half:].astype(F32)])
-    up = jnp.concatenate([ahead[:half].astype(F32), ahead[half:].astype(F32) + from_below.astype(F32)])
-    return down.astype(BF), up.astype(BF)
-
-
-def gather_far(block, axis, last=()):
+def payload_kernel(ahead_ref, behind_ref, above_ref, below_ref, *refs):
+    down_ref, up_ref = refs[-2:]
+    half = ahead_ref.shape[0] // 2
+    down_ref[:half, :] = (behind_ref[:half, :].astype(F32) + above_ref[...].astype(F32)).astype(BF)
+    down_ref[half:, :] = behind_ref[half:, :]
+    up_ref[:half, :] = ahead_ref[:half, :]
+    up_ref[half:, :] = (ahead_ref[half:, :].astype(F32) + below_ref[...].astype(F32)).astype(BF)
+
+
+def sum_payload(ahead, behind, moved, others=()):
+    return pl.pallas_call(
+        payload_kernel,
+        in_specs=[vmem()] * 4 + [anywhere()] * len(others),
+        out_specs=[vmem()] * 2,
+        out_shape=[shape_of(ahead.shape)] * 2,
+        compiler_params=params(16),
+        cost_estimate=cost(TUNE["payload"]),
+        name="payload",
+    )(ahead, behind, *moved, *others)
+
+
+def far_first(block, axis):
+    return swap(block, axis, 1), swap(block, axis, 2)
+
+
+def far_last(block, first, axis, last=()):
     count = lax.axis_size(axis) // 2
-    if count != 4:
-        blocks = [send(block, axis, lambda j: j ^ 2 * i) if i else plain(block) for i in range(count)]
-        return jnp.stack(blocks), blocks[1:3]
-    half = block.shape[0] // 2
-    first = swap(block, axis, 1), swap(block, axis, 2)
     one, two = tie_all(first, *last)
-    parts = [swap(one[:half], axis, 2), swap(two[half:], axis, 1)]
-    return plain(jnp.stack([block, one, two, jnp.concatenate(parts)])), parts
+    if count == 4:
+        half = block.shape[0] // 2
+        parts = [swap(one[:half], axis, 2), swap(two[half:], axis, 1)]
+        blocks = [block, one, two, jnp.concatenate(parts)]
+    else:
+        more = [send(block, axis, lambda j: j ^ 2 * i) for i in range(3, count)]
+        blocks, parts = [block, one, two, *more], [one]
+    return plain(jnp.stack(blocks)), parts
 
 
 def total(terms):
@@ -221,7 +246,7 @@
 def store_rows(refs, cols, values):
     at = 0
     for ref in refs:
-        ref[:, cols] = values[at : at + ref.shape[0]].astype(ref.dtype)
+        ref[:, cols] = values[at : at + ref.shape[0], :].astype(ref.dtype)
         at += ref.shape[0]
 
 
@@ -233,10 +258,11 @@
 
 
 def fill_rows(to_ref, parts):
+    size = parts[0].shape[0]
     at = 0
-    for part in parts:
-        to_ref[at : at + part.shape[0], :] = part[...]
-        at += part.shape[0]
+    for part, rows in zip(parts, (size, size, size // 2, size // 2, size)):
+        to_ref[at : at + rows, :] = part[:rows, :]
+        at += rows
 
 
 def head_rows(tok_rows, blocks):
@@ -292,18 +318,19 @@
         ],
         scratch_shapes=[pltpu.SemaphoreType.DMA((2, near.shape[0]))],
         compiler_params=params(60),
-        cost_estimate=cost(2.8),
+        cost_estimate=cost(TUNE["project"]),
         name="project",
     )(own, *parts, gain, bias, cos, sin, near, other)
 
 
-def project_back_kernel(heads, orders, own_ref, head_ref, *refs):
+def project_back_kernel(heads, orders, others, own_ref, head_ref, *refs):
+    refs = refs[:14] + refs[14 + others :]
     dq_ref, dkv_ref, cos_ref, sin_ref, normed_ref, x_ref, w_ref, mixed_ref = refs[:8]
     parts = refs[8:13]
     gain_two_ref = refs[13]
     dn_refs = refs[14:19]
-    cols_kept, cols_sent, outs_kept, outs_sent = refs[19:23]
-    cols, branch, wide, wide_out, bias_v, small_v = refs[23:]
+    cols_kept, outs_kept, wide_sent = refs[19:22]
+    cols, branch, wide, wide_out, bias_v, small_v = refs[22:]
     rows = cos_ref.shape[0]
     half_rows = rows // 2
     tok_rows = parts[0].shape[0]
@@ -350,22 +377,32 @@
     fill_rows(branch, parts)
     wide[...] = dot_tn(normed_ref[...], cols[...]).astype(BF)
     wide_out[...] = dot_tn(branch[...], mixed_ref[...]).astype(BF)
+    split = cols.shape[1]
+    wide_sent[:, count:, split:] = jnp.zeros((wide_sent.shape[0], MORE_ROWS, wide_sent.shape[2] - split), BF)
     for i in range(cols_kept.shape[0]):
-        for source, targets, order in (
-            (wide, (cols_kept, cols_sent), orders[0]),
-            (wide_out, (outs_kept, outs_sent), orders[1]),
+        for source, order, kept, lanes in (
+            (wide, orders[0], cols_kept, slice(0, split)),
+            (wide_out, orders[1], outs_kept, slice(split, wide_sent.shape[2])),
         ):
-            for side, to in enumerate(targets):
+            for side in range(2):
                 block = own_ref[0] ^ order[i] ^ side
-                to[i, :count] = source[pl.ds(pl.multiple_of(block * count, 16), count), :]
+                rows = source[pl.ds(pl.multiple_of(block * count, 16), count), :]
+                if side == 0:
+                    kept[i, :count] = rows
+                else:
+                    wide_sent[i, :count, lanes] = rows
                 if source is wide:
-                    to[i, count:] = small_v[block]
+                    small = small_v[block]
+                    if side == 0:
+                        kept[i, count:] = small
+                    else:
+                        wide_sent[i, count:, lanes] = small
 
 
 MORE_ROWS = 16
 
 
-def project_back(own, head, orders, dq, dkv, cos, sin, normed, x, w, mixed, parts, gain_two):
+def project_back(own, head, orders, dq, dkv, cos, sin, normed, x, w, mixed, parts, gain_two, others):
     rows, width = normed.shape
     heads = dq.shape[1] // (rows // 2)
     cols = (heads + 1) * HD
@@ -373,15 +410,14 @@
     far = len(orders[0])
     part_rows = width // (2 * far)
     return pl.pallas_call(
-        functools.partial(project_back_kernel, heads, orders),
-        in_specs=[smem()] * 2 + [vmem()] * 14,
-        out_specs=[vmem()] * 9,
+        functools.partial(project_back_kernel, heads, orders, len(others)),
+        in_specs=[smem()] * 2 + [vmem()] * 14 + [anywhere()] * len(others),
+        out_specs=[vmem()] * 8,
         out_shape=[
             *row_shapes(tok_rows, width),
             shape_of((far, part_rows + MORE_ROWS, cols)),
-            shape_of((far, part_rows + MORE_ROWS, cols)),
             shape_of((far, part_rows, heads * HD)),
-            shape_of((far, part_rows, heads * HD)),
+            shape_of((far, part_rows + MORE_ROWS, cols + heads * HD)),
         ],
         scratch_shapes=[
             pltpu.VMEM((rows, cols), BF),
@@ -392,20 +428,20 @@
             pltpu.VMEM((2 * far, MORE_ROWS, cols), BF),
         ],
         compiler_params=params(60),
-        cost_estimate=cost(4.5),
+        cost_estimate=cost(TUNE["project_back"]),
         name="project_back",
-    )(own, head, dq, dkv, cos, sin, normed, x, w, mixed, *parts, gain_two)
+    )(own, head, dq, dkv, cos, sin, normed, x, w, mixed, *parts, gain_two, *others)
 
 
 def visible_of(key_code, query_code, half):
     seen = key_code <= query_code
     if half == 1:
-        seen &= key_code >= (query_code // SEG_STEP) * SEG_STEP
+        seen &= key_code >= (query_code & -SEG_STEP)
     return seen
 
 
 PAIRS = ((0, 0), (0, 1), (1, 1))
-SEQ_STEP = 2
+SEQ_STEP = 4
 
 
 def pick_side(first_steps, near_ref, other_ref, which, half):
@@ -426,23 +462,21 @@
 
     @pl.when(step == 0)
     def _():
-        top[...] = jnp.full(top.shape, MASKED, F32)
+        top[...] = jnp.full(top.shape, LOWEST, F32)
         total[...] = jnp.zeros(total.shape, F32)
         acc[...] = jnp.zeros(acc.shape, F32)
 
     for key_half, query_half in PAIRS:
         keys = pick_side(first_steps, near_ref, other_ref, 0, key_half)
         values = pick_side(first_steps, near_ref, other_ref, 1, key_half)
-        scores = dot_nt(keys, q_ref[query_half]) * scale
+        scores = dot_nt(keys, q_ref[query_half])
         if key_half == query_half:
             seen = visible_of(codes(kc_ref, key_half), qc_ref[query_half], key_half)
             scores = jnp.where(seen, scores, MASKED)
         old = top[query_half]
         new = jnp.maximum(old, jnp.max(scores, axis=0, keepdims=True))
-        weights = jnp.exp(scores - new)
-        if key_half == query_half:
-            weights = jnp.where(seen, weights, 0.0)
-        factor = jnp.exp(old - new)
+        weights = jnp.exp2((scores - new) * scale)
+        factor = jnp.exp2((old - new) * scale)
         top[query_half] = new
         total[query_half] = total[query_half] * factor + jnp.sum(weights, axis=0, keepdims=True)
         acc[query_half] = acc[query_half] * factor + dot_tn(values, weights.astype(BF))
@@ -453,7 +487,7 @@
         half_rows = mixed_ref.shape[0] // 2
         for half in range(2):
             wide_ref[half] = jnp.transpose(acc[half] / total[half])
-            lse_ref[half] = top[half] + jnp.log(total[half])
+            lse_ref[half] = top[half] * scale + jnp.log2(total[half])
         for half, low, row, count in head_rows(tok_rows, blocks):
             for j in range(mixed_ref.shape[1] // HD):
                 at = j * half_rows + low
@@ -481,7 +515,7 @@
     heads = rows // half_rows
     first_steps = near.shape[0] // SEQ_STEP
     return pl.pallas_call(
-        functools.partial(attend_kernel, HD**-0.5, first_steps, tok_rows),
+        functools.partial(attend_kernel, HD**-0.5 * math.log2(math.e), first_steps, tok_rows),
         grid=(2 * first_steps,),
         in_specs=[fixed(queries.shape)]
         + side_specs(near.shape, first_steps)
@@ -499,7 +533,7 @@
             pltpu.VMEM((2, HD, rows), F32),
         ],
         compiler_params=params(60),
-        cost_estimate=cost(3),
+        cost_estimate=cost(TUNE["attend"]),
         name="attend",
     )(queries, near, other, key_code, query_code, *others)
 
@@ -532,8 +566,8 @@
         for query_half in range(key_half, 2):
             queries = q_ref[query_half]
             grad = do[query_half]
-            scores = dot_nt(keys, queries) * scale
-            weights = jnp.exp(scores - lse_ref[query_half])
+            scores = dot_nt(keys, queries) * (scale * math.log2(math.e))
+            weights = jnp.exp2(scores - lse_ref[query_half])
             if key_half == query_half:
                 seen = visible_of(codes(kc_ref, key_half), qc_ref[query_half], key_half)
                 weights = jnp.where(seen, weights, 0.0)
@@ -583,7 +617,7 @@
             pltpu.VMEM((2, 1, rows), F32),
         ],
         compiler_params=params(60),
-        cost_estimate=cost(5.2),
+        cost_estimate=cost(TUNE["attend_back"]),
         name="attend_back",
     )(queries, *grads, wide, near, other, key_code, query_code, log_total, *others)
 
@@ -598,10 +632,10 @@
     mixed_parts = refs[6:11]
     near_w, other_w, joined_w = refs[11:14]
     refs = refs[14:]
-    normed_ref, hidden_ref, middle_ref, dg_ref, du_ref, cot_ref = refs[:6]
-    dx_refs = refs[6:11]
-    x_v, out_v, gate_v, up_v, down_v, mixed_v, normed_v, middle_v, dg_v, du_v, cot_v = refs[11:22]
-    in_sem, cot_sem, out_sem, w_sem, s_sem = refs[22:]
+    acts_ref, hidden_ref, middle_ref, cot_ref = refs[:4]
+    dx_refs = refs[4:9]
+    x_v, out_v, gate_v, up_v, down_v, mixed_v, normed_v, middle_v, dg_v, du_v, cot_v = refs[9:20]
+    in_sem, cot_sem, out_sem, w_sem, s_sem = refs[20:]
     rows, width = x_v.shape
     units = gate_v.shape[1]
     tok_rows = hidden_ref.shape[0]
@@ -642,6 +676,8 @@
                     part.at[pl.ds(low, half), :], cot_v.at[pl.ds(i * half, half), :], cot_sem.at[i]
                 )
             )
+    for copy in first:
+        copy.wait()
     loads = [
         [
             begin(
@@ -651,14 +687,13 @@
         ]
         for i, (at, size) in enumerate(chunks)
     ]
-    for copy in first:
-        copy.wait()
     hidden = x_v[...].astype(F32) + dot_nt(mixed_v[...], out_v[...])
     hidden_ref[...] = hidden[:tok_rows]
     normed_v[...] = (hidden * inverse_norm(hidden) * gain_ref[...]).astype(BF)
     for copy in cots:
         copy.wait()
-    stores = [begin(normed_v, normed_ref, s_sem.at[0]), begin(cot_v, cot_ref, s_sem.at[1])]
+    normed_to = acts_ref.at[:, pl.ds(2 * units, width)]
+    stores = [begin(normed_v, normed_to, s_sem.at[0]), begin(cot_v, cot_ref, s_sem.at[1])]
     for i, (at, size) in enumerate(chunks):
         for copy in loads[i]:
             copy.wait()
@@ -671,7 +706,13 @@
         middle_v[:, here] = (active * up).astype(BF)
         dg_v[:, here] = (grad * up * sig * (1.0 + gate * (1.0 - sig))).astype(BF)
         du_v[:, here] = (grad * active).astype(BF)
-    for j, (src, dst) in enumerate(((dg_v, dg_ref), (du_v, du_ref), (middle_v, middle_ref))):
+    for j, (src, dst) in enumerate(
+        (
+            (dg_v, acts_ref.at[:, pl.ds(0, units)]),
+            (du_v, acts_ref.at[:, pl.ds(units, units)]),
+            (middle_v, middle_ref),
+        )
+    ):
         stores.append(begin(src, dst, s_sem.at[2 + j]))
     for at, size in cut(width, OUT_TILE):
         here = slice(at, at + size)
@@ -685,17 +726,14 @@
     rows, width = x.shape
     units = joined_all.shape[1] // 3
     blocks = rows // tok_rows
-    hidden_like = shape_of((rows, units))
     return pl.pallas_call(
         feed_forward_kernel,
         in_specs=[smem(), vmem()] + [anywhere()] * 14,
-        out_specs=[anywhere(), vmem()] + [anywhere()] * 4 + [vmem()] * 5,
+        out_specs=[anywhere(), vmem()] + [anywhere()] * 2 + [vmem()] * 5,
         out_shape=[
-            shape_of((rows, width)),
+            shape_of((rows, 2 * units + width)),
             shape_of((tok_rows, width), F32),
-            hidden_like,
-            hidden_like,
-            hidden_like,
+            shape_of((rows, units)),
             shape_of((rows, width)),
             *row_shapes(tok_rows, width),
         ],
@@ -718,57 +756,52 @@
             pltpu.SemaphoreType.DMA((5,)),
         ],
         compiler_params=params(60),
-        cost_estimate=cost(16),
+        cost_estimate=cost(TUNE["feed_forward"]),
         name="feed_forward",
     )(own, gain, x, *cot_parts, *mixed_parts, near, other, joined_all)
 
 
-def down_grads_kernel(blocks, own_ref, c_ref, down_w, middle_ref, down_ref, out_ref, turned, acc):
+def down_product_kernel(down_w, middle_ref, *refs):
+    acc = refs[-1]
     step = pl.program_id(0)
 
     @pl.when(step == 0)
     def _():
-        turned[...] = jnp.transpose(c_ref[...])
         acc[...] = jnp.zeros(acc.shape, F32)
 
-    down_ref[...] = dot_nn(turned[...], middle_ref[...]).astype(BF)
     acc[...] += dot_nt(middle_ref[...], down_w[...])
 
     @pl.when(step == pl.num_programs(0) - 1)
     def _():
-        rows = acc.shape[0] // blocks
-        for t in range(blocks):
-            at = pl.multiple_of(lax.rem(own_ref[0] + t, blocks) * rows, 16)
-            out_ref[pl.ds(at, rows), :] = acc[t * rows : (t + 1) * rows, :].astype(BF)
-
-
-def down_grads(own, cot, middle, joined_all, blocks):
-    rows, full = cot.shape
-    units = middle.shape[1]
+        store_rows(refs[:-1], slice(None), acc)
+
+
+def down_product(middle, joined_all, tok_rows):
+    rows, units = middle.shape
+    full = joined_all.shape[0]
     steps = units // TILE
-
-    def tiles(rows, first=0):
-        return pl.BlockSpec((rows, TILE), lambda i, own: (0, first + i))
-
+    outs = row_shapes(tok_rows, full)
     return pl.pallas_call(
-        functools.partial(down_grads_kernel, blocks),
-        grid_spec=pltpu.PrefetchScalarGridSpec(
-            num_scalar_prefetch=1,
-            grid=(steps,),
-            in_specs=[fixed(cot.shape), tiles(full, 2 * steps), tiles(rows)],
-            out_specs=[tiles(full), fixed((rows, full))],
-            scratch_shapes=[pltpu.VMEM((full, rows), BF), pltpu.VMEM((rows, full), F32)],
-        ),
-        out_shape=[shape_of((full, units)), shape_of((rows, full))],
+        down_product_kernel,
+        grid=(steps,),
+        in_specs=[
+            pl.BlockSpec((full, TILE), lambda i: (0, 2 * steps + i)),
+            pl.BlockSpec((rows, TILE), lambda i: (0, i)),
+        ],
+        out_specs=[fixed(out.shape) for out in outs],
+        out_shape=outs,
+        scratch_shapes=[pltpu.VMEM((rows, full), F32)],
         compiler_params=params(60),
-        cost_estimate=cost(6.3),
-        name="down_grads",
-    )(own, cot, joined_all, middle)
+        cost_estimate=cost(TUNE["down_product"]),
+        name="down_product",
+    )(joined_all, middle)
 
 
 def pair_grads_kernel(orders, others, own_ref, *refs):
-    xs, gates, ups = refs[:2], refs[2:4], refs[4:6]
-    outs, (one, two, turned) = refs[6 + others : -3], refs[-3:]
+    xs, gates, ups = refs[:6:3], refs[1:6:3], refs[2:6:3]
+    cot_ref, middle_ref = refs[6:8]
+    *outs, down_ref = refs[8 + others : -4]
+    one, two, turned, cot_t = refs[-4:]
     count = len(outs) // 2
     blocks = len(orders[0])
     rows = one.shape[0] // blocks
@@ -776,6 +809,7 @@
 
     @pl.when(pl.program_id(0) == 0)
     def _():
+        cot_t[...] = jnp.transpose(cot_ref[...])
         for side, x_ref in enumerate(xs):
             turned[...] = jnp.transpose(x_ref[...])
             where = slice(side * tokens, (side + 1) * tokens)
@@ -785,36 +819,41 @@
                     at = pl.multiple_of((own_ref[0] ^ orders[which][j]) * rows, 16)
                     to[here, where] = turned[pl.ds(at, rows), :]
 
-    for left, grads, (low, high, sent) in ((one, gates, outs[:count]), (two, ups, outs[count:])):
+    for left, grads, quarters in ((one, gates, outs[:count]), (two, ups, outs[count:])):
         result = dot_nn(left[:, :tokens], grads[0][...]) + dot_nn(left[:, tokens:], grads[1][...])
-        half = 2 * low.shape[0]
-        low[...] = result[: half // 2].astype(BF)
-        high[...] = result[half // 2 : half].astype(BF)
-        sent[...] = result[half:].astype(BF)
-
-
-def pair_grads(own, orders, xs, gates, ups, others):
-    rows, full = xs[0].shape
-    units = gates[0].shape[1]
-
-    def tiles(rows):
-        return pl.BlockSpec((rows, TILE), lambda i, order: (0, i))
-
+        store_rows(quarters, slice(None), result)
+    down_ref[...] = dot_nn(cot_t[...], middle_ref[...]).astype(BF)
+
+
+def pair_grads(own, orders, acts, cot, middle, others):
+    rows, width = cot.shape
+    full = width
+    units = (acts[0].shape[1] - width) // 2
+    steps = units // TILE
+
+    def tiles(rows, first=0):
+        return pl.BlockSpec((rows, TILE), lambda i, own: (0, first + i))
+
+    one_side = [
+        pl.BlockSpec((rows, width), lambda i, own: (0, 2 * units // width)),
+        tiles(rows),
+        tiles(rows, steps),
+    ]
     return pl.pallas_call(
         functools.partial(pair_grads_kernel, orders, len(others)),
         grid_spec=pltpu.PrefetchScalarGridSpec(
             num_scalar_prefetch=1,
-            grid=(units // TILE,),
-            in_specs=[fixed(xs[0].shape)] * 2 + [tiles(rows)] * 4 + [anywhere()] * len(others),
-            out_specs=([tiles(full // 8)] * 2 + [tiles(full // 4)]) * 2,
+            grid=(steps,),
+            in_specs=one_side * 2 + [fixed(cot.shape), tiles(rows)] + [anywhere()] * len(others),
+            out_specs=[tiles(full // 8)] * 8 + [tiles(full)],
             scratch_shapes=[pltpu.VMEM((full // 2, 2 * rows), BF)] * 2
-            + [pltpu.VMEM((full, rows), BF)],
+            + [pltpu.VMEM((full, rows), BF)] * 2,
         ),
-        out_shape=([shape_of((full // 8, units))] * 2 + [shape_of((full // 4, units))]) * 2,
+        out_shape=[shape_of((full // 8, units))] * 8 + [shape_of((full, units))],
         compiler_params=params(60),
-        cost_estimate=cost(6.3),
+        cost_estimate=cost(TUNE["pair_grads"]),
         name="pair_grads",
-    )(own, *xs, *gates, *ups, *others)
+    )(own, *[side for side in acts for _ in range(3)], cot, middle, *others)
 
 
 def norm_back_kernel(others, own_ref, *refs):
@@ -855,7 +894,7 @@
             pltpu.SemaphoreType.DMA((2, near.shape[0])),
         ],
         compiler_params=params(60),
-        cost_estimate=cost(2.3),
+        cost_estimate=cost(TUNE["norm_back"]),
         name="norm_back",
     )(own, first, down, up, hidden, gain, cotangent, near, other, *others)
 
@@ -939,7 +978,7 @@
         rows_of.append(from_next(block, "head", apart) if apart else block)
     own_wide = qkv_weight.shape[0]
     own_rows = own_wide * heads_dev
-    inputs_parts = gather_blocks(tie(inputs, *rows_of[1:]), "head")
+    inputs_parts = gather_blocks(tie(inputs, *rows_of[1:]), "head", micros=TUNE["x1"])
     rows_of = roll_blocks(jnp.stack(rows_of), (heads_dev - head_index) % heads_dev)
     small_grp = rows_of[:, own_wide]
     cols_own = jnp.concatenate(
@@ -948,8 +987,10 @@
             jnp.pad(small_grp, ((0, 2 * MORE_ROWS - heads_dev), (0, 0))),
         ]
     )
-    cols_near, _ = gather_far(plain(cols_own), "seq", inputs_parts[2:4])
-    cols_other = swap(cols_near, "seq", 0)
+    cols_own = plain(cols_own)
+    cols_near, _ = far_last(cols_own, far_first(cols_own, "seq"), "seq")
+    inputs_parts[2:4] = tie_all(inputs_parts[2:4], micros=TUNE["x2"])
+    cols_other = swap(tie(cols_near, *inputs_parts[2:4]), "seq", 0)
 
     def cut_small(values):
         cuts, start = [], 0
@@ -1030,21 +1071,24 @@
         ]
     )
     cot_late = tie(plain(cot_mixed), inputs_parts[2], inputs_parts[3])
-    cot_parts = gather_blocks(cot_late, "head", [queries])
-    kv_near, _ = gather_far(kv_own, "seq", cot_parts[2:4])
+    kv_first = far_first(kv_own, "seq")
+    cot_parts = gather_blocks(cot_late, "head", kv_first)
+    kv_near, _ = far_last(kv_own, kv_first, "seq")
+    cot_parts[2:4] = tie_all(cot_parts[2:4], micros=TUNE["c2"])
     kv_other = swap(kv_near, "seq", 0)
 
-    halves = jnp.concatenate(cot_parts).reshape(2 * heads_dev, half + out_half + out_pad, width)
+    mixed, mixed_wide, log_total = attend(
+        queries, kv_near, kv_other, key_code, query_code, tok_rows, cot_parts[2:4]
+    )
+    late = tie_all([cot_mixed, *cot_parts[1:]], mixed)
+    halves = jnp.concatenate(late).reshape(2 * heads_dev, half + out_half + out_pad, width)
     out_rows = plain(halves[:, half : half + out_half].reshape(QD, -1).T)
-    out_first = tie(out_rows, kv_other)
-    mixed, mixed_wide, log_total = attend(
-        queries, kv_near, kv_other, key_code, query_code, tok_rows, []
-    )
-    out_near, out_came = gather_far(out_first, "seq", [mixed])
-    mixed_parts = gather_blocks(mixed, "head", out_came)
-    out_other = swap(tie(out_near, mixed_parts[1], mixed_parts[4]), "seq", 0)
-
-    normed_two, own_hidden, middle, d_gate, d_up, cot_grp, *d_two = feed_forward(
+    out_first = far_first(out_rows, "seq")
+    mixed_parts = gather_blocks(mixed, "head", micros=TUNE["mx"])
+    out_near, _ = far_last(out_rows, out_first, "seq", [mixed_parts[1], mixed_parts[4]])
+    out_other = swap(tie(out_near, *mixed_parts[2:4]), "seq", 0)
+
+    acts, own_hidden, middle, cot_grp, *d_two = feed_forward(
         seq_own,
         inputs_grp,
         gain_mlp,
@@ -1056,27 +1100,14 @@
         tok_rows,
     )
 
-    others = [swap(part, "seq", 0) for part in (normed_two, d_gate, d_up)]
-    down_term, out_term = down_grads(
-        head_own, cot_grp, middle, joined_all, heads_dev
-    )
+    acts_moved = swap(acts, "seq", 0)
     moved = sum_first(d_two[2:4], "head")
-    down_late = tie(down_term, *moved)
-    down_sum = plain(lax.psum_scatter(plain(down_late), "seq", scatter_dimension=0, tiled=True))
-    down, up = sum_payload(d_two[1], d_two[4], moved, others)
-    parts = [
-        part.reshape(-1, width // seq_dev, part.shape[1])
-        for part in pair_grads(
-            seq_own,
-            orders,
-            (normed_two, others[0]),
-            (d_gate, others[1]),
-            (d_up, others[2]),
-            [down, up, down_late],
-        )
-    ]
-    gate_low, gate_high, *gate_sent = parts[: len(parts) // 2]
-    up_low, up_high, *up_sent = parts[len(parts) // 2 :]
+    out_term = down_product(middle, joined_all, tok_rows)
+    down, up = sum_payload(d_two[1], d_two[4], moved, others=[out_term[0]])
+    *parts, down_term = pair_grads(seq_own, orders, (acts, acts_moved), cot_grp, middle, [down, up])
+    parts = [part.reshape(-1, width // seq_dev, padded) for part in parts]
+    gate_low, gate_high, *gate_sent = parts[:4]
+    up_low, up_high, *up_sent = parts[4:]
     d_hidden, d_branch, *d_mixed_own, grad_gain_two = norm_back(
         seq_own,
         d_two[0],
@@ -1094,15 +1125,15 @@
     for apart in range(1, heads_dev):
         d_mixed.append(from_next(d_mixed_own[heads_dev - apart], "head", apart))
 
-    def move(t, *earlier):
-        return (
-            swap(tie(gate_sent[t], *earlier), "seq", bits_down[0]),
-            swap(tie(up_sent[t], *earlier), "seq", bits_up[0]),
-        )
-
-    moved = [move(t, d_branch) for t in range(len(gate_sent))]
-    branch_above = from_next(tie(d_branch, *d_mixed[1:]), "head")
-    branch_below = to_next(tie(d_branch, *d_mixed[1:]), "head")
+    gate_moved = [swap(gate_sent[1], "seq", bits_down[0])]
+    up_moved = [swap(up_sent[1], "seq", bits_up[0])]
+    gate_moved[0], up_moved[0] = tie_all([gate_moved[0], up_moved[0]], micros=TUNE["g0"])
+    down_late = tie(down_term, *d_mixed[1:])
+    down_sum = plain(lax.psum_scatter(plain(down_late), "seq", scatter_dimension=0, tiled=True))
+    gate_moved.append(swap(tie(gate_sent[0], *d_mixed[1:], gate_moved[0], up_moved[0]), "seq", bits_down[0]))
+    up_moved.append(swap(tie(up_sent[0], *d_mixed[1:], gate_moved[0], up_moved[0]), "seq", bits_up[0]))
+    branch_late = tie(d_branch, *d_mixed[1:])
+    above, below = from_next(branch_late, "head"), to_next(branch_late, "head")
     d_queries, d_kv_own, d_kv_sent = attend_back(
         queries,
         d_mixed,
@@ -1112,44 +1143,37 @@
         key_code,
         query_code,
         log_total,
-        [],
-    )
-    d_kv_moved = swap(tie(d_kv_sent, branch_above, branch_below), "seq", 0)
-    branch_above = tie(branch_above, d_queries)
-    branch_below = tie(branch_below, d_queries)
-    branch_parts = [
-        d_branch,
-        branch_above,
-        from_next(branch_above[:half], "head"),
-        to_next(branch_below[half:], "head"),
-        branch_below,
-    ]
-    d_kv_moved = tie(d_kv_moved, *moved[-1], branch_parts[2], branch_parts[3])
-    out_late = tie(out_term, down_sum)
-    out_sum = plain(lax.psum_scatter(plain(out_late), "head", scatter_dimension=0, tiled=True))
-    output = (own_hidden + out_sum.astype(F32)).astype(BF)
+        [gate_moved[0], up_moved[0]],
+    )
+    d_kv_moved = swap(tie(d_kv_sent, above, below), "seq", 0)
+    half = tok_rows // 2
+    above, below = tie_all([above, below], d_queries)
+    above_far = from_next(jnp.concatenate([above[:half], out_term[2]]), "head")
+    below_far = to_next(jnp.concatenate([below[half:], out_term[3]]), "head")
+    down, up = sum_payload(out_term[1], out_term[4], [above_far[half:], below_far[half:]])
+    out_moved = [from_next(down, "head"), to_next(up, "head")]
+    branch_parts = [d_branch, above, above_far, below_far, below]
+    output = total([own_hidden, out_term[0], *out_moved]).astype(BF)
+    gate_moved[1], up_moved[1] = tie_all([gate_moved[1], up_moved[1]], micros=TUNE["g1"])
+    d_kv_moved = tie(d_kv_moved, gate_moved[1], up_moved[1])
     d_kv = total([d_kv_own, d_kv_moved])
     d_keys, keys_last = sum_xor([d_kv[i, 0] for i in range(far)], "seq", bits_down)
     d_values, values_last = sum_xor([d_kv[i, 1] for i in range(far)], "seq", bits_up)
     d_other_raw = jnp.where(odd, d_keys, d_values).astype(BF)
-    d_other_raw = swap(
-        tie(d_other_raw, down_sum), "head", 0
-    )
+    d_other_sent = d_other_raw
+    d_other_raw = swap(d_other_sent, "head", 0)
     d_other = d_other_raw.reshape(2, heads_dev, tok_rows // 2, HD)
     d_other = roll_blocks(d_other, jnp.where(odd, 1, heads_dev - 1), 1).reshape(2, half_rows, HD)
     d_kv_total = jnp.where(odd, d_values, d_keys) + d_other.astype(F32)
 
 
-    def second(low, high, which, bit):
-        half = high.shape[0]
-        parts = [tie(pair[which], keys_last, values_last) for pair in moved]
-        sent = total([high, jnp.concatenate([part[half:] for part in parts], axis=2)]).astype(BF)
-        come = swap(sent, "seq", bit)
-        return [low, jnp.concatenate([part[:half] for part in parts], axis=2), come]
-
-    gate_terms = second(gate_low, gate_high, 0, bits_down[1])
-    up_terms = second(up_low, up_high, 1, bits_up[1])
-    *d_one, cols_kept, cols_sent, outs_kept, outs_sent = project_back(
+    def second(low, high, moved, bit):
+        high_moved, low_moved = tie_all(moved, d_other_sent)
+        return [low, low_moved, swap(total([high, high_moved]).astype(BF), "seq", bit)]
+
+    gate_terms = second(gate_low, gate_high, gate_moved, bits_down[1])
+    up_terms = second(up_low, up_high, up_moved, bits_up[1])
+    *d_one, cols_kept, outs_kept, wide_sent = project_back(
         seq_own,
         head_own,
         orders,
@@ -1163,14 +1187,17 @@
         mixed,
         branch_parts,
         grad_gain_two,
-    )
-    gate_terms[-1] = tie(gate_terms[-1], d_one[0])
-    up_terms[-1] = tie(up_terms[-1], d_one[0])
-    moved = sum_first(tie_all(d_one[2:4], gate_terms[-1], up_terms[-1]), "head")
-    cols_moved, outs_moved = swap(cols_sent, "seq", 0), swap(outs_sent, "seq", 0)
-    down, up = sum_payload(d_one[1], d_one[4], moved, [cols_moved, outs_moved])
+        [down_sum, *out_moved],
+    )
+    moved = sum_first(d_one[2:4], "head")
+    wide_moved = tie_all([swap(wide_sent, "seq", 0)], micros=TUNE["wm"])[0]
+    down, up = sum_payload(d_one[1], d_one[4], moved, others=[wide_moved])
+    gate_terms[-1], up_terms[-1] = tie(gate_terms[-1], down), tie(up_terms[-1], down)
+    cols_moved = wide_moved[:, :, : query_cols + HD]
+    outs_moved = wide_moved[:, :own_rows, query_cols + HD :]
     cols_terms = sum_step([cols_kept, cols_moved], "seq", bits_down[0])
     outs_terms = sum_step([outs_kept, outs_moved], "seq", bits_up[0])
+    cols_terms[-1], outs_terms[-1] = tie_all([cols_terms[-1], outs_terms[-1]], micros=TUNE["ct"])
     down, up = from_next(down, "head"), to_next(up, "head")
     d_normed_one = total([d_one[0], tie(down, cols_terms[-1], outs_terms[-1]), up])
     grad_cols = sum_halving(cols_terms, "seq", bits_down[1:]).astype(BF)

time: 454 us -> 412 us (0.907)
  waiting for transfers between devices: 166 us -> 136 us
  local copies, waits for them, and re-layouts: 43 us -> 33.6 us
  Pallas kernels: 119 us -> 111 us
    ppermute x67 -> x68, waiting for transfers between devices: 166 us -> 136 us  [send(): lax.ppermute(plain(block), axis, [(j, target(j) % count) for j in range(c...]
    unnamed x198 -> x188, local copies, waits for them, and re-layouts: 29.3 us -> 17.8 us
    pallas_call x3 -> x6, Pallas kernels: 38.3 us -> 30.5 us  [the longest x1 13.1 us: attend(): pl.pallas_call(functools.partial(attend_kernel, HD ** (-0.5) * math.log2(...]
    pallas_call x1, Pallas kernels: 36.2 us -> 30.3 us  [feed_forward(): pl.pallas_call(feed_forward_kernel, in_specs=[smem(), vmem()] + [anywhere...]
    ppermute x67 -> x68, starting transfers between devices: 76.5 us -> 79.5 us  [send(): lax.ppermute(plain(block), axis, [(j, target(j) % count) for j in range(c...]
  transfers between devices with their start and end apart: 70 -> 70, of which waited for: 42 -> 38; matrix products, arithmetic and copies ran while one was open for 9% -> 10% of each run, Pallas kernels for 18% -> 20%
where the time goes in v3:
time: 412 us; the launch traced here: 405 us
  waiting for transfers between devices  136 us (33%)
  Pallas kernels  111 us (27%)
  starting transfers between devices  79.6 us (19%)
  local copies, waits for them, and re-layouts  33.6 us (8%)
  other arithmetic  27.7 us (7%)
  between operations  16.2 us (4%)
    ppermute x68, waiting for transfers between devices, send(): lax.ppermute(plain(block), axis, [(j, target(j) % count) for j in range(c...  136 us
    ppermute x68, starting transfers between devices, send(): lax.ppermute(plain(block), axis, [(j, target(j) % count) for j in range(c...  79.5 us
    pallas_call x1, Pallas kernels, feed_forward(): pl.pallas_call(feed_forward_kernel, in_specs=[smem(), vmem()] + [anywhere...  30.3 us
    pallas_call x1, Pallas kernels, pair_grads(): pl.pallas_call(functools.partial(pair_grads_kernel, orders, len(others)),...  18.8 us
    pallas_call x1, Pallas kernels, attend_back(): pl.pallas_call(functools.partial(attend_back_kernel, HD ** (-0.5), first_...  18.6 us
    unnamed x188, local copies, waits for them, and re-layouts  17.8 us
    pallas_call x1, Pallas kernels, attend(): pl.pallas_call(functools.partial(attend_kernel, HD ** (-0.5) * math.log2(...  13.1 us
    pallas_call x1, Pallas kernels, project_back(): pl.pallas_call(functools.partial(project_back_kernel, heads, orders, len(...  8.84 us
  transfers between devices with their start and end apart: 70, of which 38 were waited for; matrix products, arithmetic and copies ran while one was open for 10% of the time, Pallas kernels for 20%

profile of v3, /device:TPU:0, one launch (start us, length us, event | category | flops | bytes accessed | tf_op | source)
XLA Modules:
  0.0 404.6 jit_solution(10387003345518290080)
XLA Ops:
  7.2 2.9 fusion.5
  11.3 5.1 %collective-permute-start = (bf16[64,640]{1,0:T(8,128)(2,1)S(1)}, bf16[64,640]{1,0:T(8,128)(2,1)S(1)}, u32[]{:S(2)}, u32[]{:S(2)}) collective-permute-start(bf16[64,640]{1,0:T(8,128)(2,1)S(1)} %get-tuple-element.232), channel_id=1, source_target_pairs={{0,3},{1,0},{2,1},{3,2},{4,7},{5,4},{6,5},{7,6},{8,11},{9,8},{10,9... | collective-permute-start | bytes 245768 | tf_op jit(solution)/shard_map/ppermute | solution.py:48
  19.4 4.5 %collective-permute-done.1.refs_2_ = bf16[64,640]{1,0:T(8,128)(2,1)S(1)} collective-permute-done((bf16[64,640]{1,0:T(8,128)(2,1)S(1)}, bf16[64,640]{1,0:T(8,128)(2,1)S(1)}, u32[]{:S(2)}, u32[]{:S(2)}) %collective-permute-start.1) | collective-permute-done | bytes 81952 | tf_op jit(solution)/shard_map/ppermute | solution.py:48
  24.2 2.9 concatenate.103
  27.4 1.6 collective-permute-start.3
  30.4 2.1 collective-permute-start.7
  32.6 10.2 %collective-permute-done.3.refs_0_ = bf16[224,640]{1,0:T(8,128)(2,1)S(1)} collective-permute-done((bf16[224,640]{1,0:T(8,128)(2,1)S(1)}, bf16[224,640]{1,0:T(8,128)(2,1)S(1)}, u32[]{:S(2)}, u32[]{:S(2)}) %collective-permute-start.3) | collective-permute-done | bytes 286752 | tf_op jit(solution)/shard_map/ppermute | solution.py:48
  44.9 1.6 collective-permute-start.5
  46.4 3.2 collective-permute-done.8.refs_1_
  54.1 2.4 collective-permute-done.9.refs_0_
  56.5 4.4 %collective-permute-done.10.refs_1_ = bf16[64,1536]{1,0:T(8,128)(2,1)S(1)} collective-permute-done((bf16[64,1536]{1,0:T(8,128)(2,1)S(1)}, bf16[64,1536]{1,0:T(8,128)(2,1)S(1)}, u32[]{:S(2)}, u32[]{:S(2)}) %collective-permute-start.10) | collective-permute-done | bytes 196640 | tf_op jit(solution)/shard_map/ppermute | solution.py:48
  64.2 2.2 collective-permute-start.12
  69.3 7.4 %project.1 = (bf16[2,768,128]{2,1,0:T(8,128)(2,1)}, bf16[2,2,256,128]{3,2,1,0:T(8,128)(2,1)}, bf16[512,1536]{1,0:T(8,128)(2,1)}, bf16[512,1536]{1,0:T(8,128)(2,1)}, bf16[1536,640]{1,0:T(8,128)(2,1)}) custom-call(s32[1]{0:T(128)} %bitcast.own_ref, bf16[128,1536]{1,0:T(8,128)(2,1)} %copy-done.9, bf16[128,1536]{1,0:T(8,128)(2,1)} %copy-done.31, ...), custom_call_target="tpu_custom_call" | custom-call | flops 8071000064 | tf_op jit(solution)/shard_map/project/pallas_call | solution.py:308
  78.0 2.2 collective-permute-done.12.refs_0_
  80.1 13.4 %collective-permute-done.13.refs_1_ = bf16[192,1536]{1,0:T(8,128)(2,1)S(1)} collective-permute-done((bf16[192,1536]{1,0:T(8,128)(2,1)S(1)}, bf16[192,1536]{1,0:T(8,128)(2,1)S(1)}, u32[]{:S(2)}, u32[]{:S(2)}) %collective-permute-start.13) | collective-permute-done | bytes 589856 | tf_op jit(solution)/shard_map/ppermute | solution.py:48
  96.4 3.1 collective-permute-start.16
  100.4 2.0 collective-permute-done.19
  105.4 2.0 copy.86.kc_ref.refs_7_
  107.5 4.8 %collective-permute-done.17.refs_1_ = bf16[96,1536]{1,0:T(8,128)(2,1)S(1)} collective-permute-done((bf16[96,1536]{1,0:T(8,128)(2,1)}, bf16[96,1536]{1,0:T(8,128)(2,1)S(1)}, u32[]{:S(2)}, u32[]{:S(2)}) %collective-permute-start.17) | collective-permute-done | bytes 294944 | tf_op jit(solution)/shard_map/ppermute | solution.py:48
  114.6 13.1 %attend.1 = (bf16[512,384]{1,0:T(8,128)(2,1)}, f32[2,768,128]{2,1,0:T(8,128)}, f32[2,1,768]{2,1,0:T(1,128)}) custom-call(bf16[2,768,128]{2,1,0:T(8,128)(2,1)} %get-tuple-element.111.q_ref, bf16[4,2,2,256,128]{4,3,2,1,0:T(8,128)(2,1)} %pad_maximum_fusion.2.near_ref.refs_5_, bf16[4,2,2,256,128]{4,3,2,1,0:T(8,128)(2,1)} %collective-permute-done.20.other_ref.refs_6_, ...), custom_call_target="tpu_custom_call" | custom-call | flops 18447998976 | tf_op jit(solution)/shard_map/attend/pallas_call | solution.py:517
  127.7 2.7 collective-permute-start.21
  133.4 1.6 collective-permute-start.26
  135.1 5.2 %collective-permute-done.21.refs_0_ = bf16[512,384]{1,0:T(8,128)(2,1)S(1)} collective-permute-done((bf16[512,384]{1,0:T(8,128)(2,1)}, bf16[512,384]{1,0:T(8,128)(2,1)S(1)}, u32[]{:S(2)}, u32[]{:S(2)}) %collective-permute-start.21) | collective-permute-done | bytes 393248 | tf_op jit(solution)/shard_map/ppermute | solution.py:48
  140.2 8.5 %collective-permute-done.22.refs_1_ = bf16[512,384]{1,0:T(8,128)(2,1)S(1)} collective-permute-done((bf16[512,384]{1,0:T(8,128)(2,1)}, bf16[512,384]{1,0:T(8,128)(2,1)S(1)}, u32[]{:S(2)}, u32[]{:S(2)}) %collective-permute-start.22) | collective-permute-done | bytes 393248 | tf_op jit(solution)/shard_map/ppermute | solution.py:48
  151.5 3.4 collective-permute-start.23
  155.3 2.6 collective-permute-done.28
  161.6 1.9 collective-permute-done.24.refs_2_.refs_9_
  164.9 4.0 collective-permute-done.29.refs_12_.refs_7_
  170.3 30.3 %feed_forward.1 = (bf16[512,6144]{1,0:T(8,128)(2,1)}, f32[128,1536]{1,0:T(8,128)}, bf16[512,2304]{1,0:T(8,128)(2,1)}, bf16[512,1536]{1,0:T(8,128)(2,1)}, f32[128...) custom-call(s32[1]{0:T(128)} %bitcast.own_ref, ...), custom_call_target="tpu_custom_call" | custom-call | flops 41507999744 | tf_op jit(solution)/shard_map/feed_forward/pallas_call | solution.py:729
  200.8 2.1 collective-permute-start.30
  203.0 8.3 %down_product.1 = (f32[128,1536]{1,0:T(8,128)}, bf16[128,1536]{1,0:T(8,128)(2,1)}, bf16[64,1536]{1,0:T(8,128)(2,1)}, bf16[64,1536]{1,0:T(8,128)(2,1)}, bf16[128,1536]{1,0:T(8,128)(2,1)}) custom-call(bf16[1536,6912]{1,0:T(8,128)(2,1)} %all-gather.2.cloned.1.call-done.refs_13_.down_w, bf16[512,2304]{1,0:T(8,128)(2,1)} %get-tuple-element.125.middle_ref.refs_7_), custom_call_target="tpu_custom_call" | custom-call | flops 9223999488 | tf_op jit(solution)/shard_map/down_product/pallas_call | solution.py:784
  211.3 1.8 collective-permute-done.31.below_ref
  214.4 2.0 collective-permute-start.32
  216.5 18.8 %pair_grads.1 = (bf16[192,2304]{1,0:T(8,128)(2,1)}, bf16[192,2304]{1,0:T(8,128)(2,1)}, bf16[192,2304]{1,0:T(8,128)(2,1)}, bf16[192,2304]{1,0:T(8,128)(2,1)}, bf1...) custom-call(s32[1]{0:T(128)} %bitcast.own_ref, ...), custom_call_target="tpu_custom_call" | custom-call | flops 8071000064 | tf_op jit(solution)/shard_map/pair_grads/pallas_call | solution.py:842
  238.4 5.6 %norm_back.1 = (f32[128,1536]{1,0:T(8,128)}, bf16[128,1536]{1,0:T(8,128)(2,1)}, bf16[128,384]{1,0:T(8,128)(2,1)}, bf16[128,384]{1,0:T(8,128)(2,1)}, bf16[128,384...) custom-call(s32[1]{0:T(128)} %bitcast.own_ref, f32[128,1536]{1,0:T(8,128)} %get-tuple-element.129.refs_0_, ...), custom_call_target="tpu_custom_call" | custom-call | flops 6341499904 | tf_op jit(solution)/shard_map/norm_back/pallas_call | solution.py:885
  243.9 3.8 collective-permute-start.35
  248.3 2.7 collective-permute-done.35.refs_1_
  251.1 4.8 %collective-permute-done.36.refs_2_ = bf16[128,384]{1,0:T(8,128)(2,1)S(1)} collective-permute-done((bf16[128,384]{1,0:T(8,128)(2,1)}, bf16[128,384]{1,0:T(8,128)(2,1)S(1)}, u32[]{:S(2)}, u32[]{:S(2)}) %collective-permute-start.36) | collective-permute-done | bytes 98336 | tf_op jit(solution)/shard_map/ppermute | solution.py:48
  257.6 1.6 collective-permute-start.38
  262.5 18.6 %attend_back.1 = (f32[2,768,128]{2,1,0:T(8,128)}, bf16[4,2,2,256,128]{4,3,2,1,0:T(8,128)(2,1)}, bf16[4,2,2,256,128]{4,3,2,1,0:T(8,128)(2,1)}) custom-call(bf16[2,768,128]{2,1,0:T(8,128)(2,1)} %get-tuple-element.111.q_ref, bf16[128,384]{1,0:T(8,128)(2,1)} %get-tuple-element.143.refs_0_, bf16[128,384]{1,0:T(8,128)(2,1)} %copy-done.10, ...), custom_call_target="tpu_custom_call" | custom-call | flops 20753999872 | tf_op jit(solution)/shard_map/attend_back/pallas_call | solution.py:603
  283.5 3.4 collective-permute-start.42
  287.2 9.4 %collective-permute-done.42.refs_10_ = bf16[128,1536]{1,0:T(8,128)(2,1)S(1)} collective-permute-done((bf16[128,1536]{1,0:T(8,128)(2,1)S(1)}, bf16[128,1536]{1,0:T(8,128)(2,1)S(1)}, u32[]{:S(2)}, u32[]{:S(2)}) %collective-permute-start.42) | collective-permute-done | bytes 393248 | tf_op jit(solution)/shard_map/ppermute | solution.py:48
  296.5 5.9 %collective-permute-done.43.refs_11_ = bf16[128,1536]{1,0:T(8,128)(2,1)S(1)} collective-permute-done((bf16[128,1536]{1,0:T(8,128)(2,1)S(1)}, bf16[128,1536]{1,0:T(8,128)(2,1)S(1)}, u32[]{:S(2)}, u32[]{:S(2)}) %collective-permute-start.43) | collective-permute-done | bytes 393248 | tf_op jit(solution)/shard_map/ppermute | solution.py:48
  304.4 1.7 fusion.60
  310.5 3.3 collective-permute-start.44
  313.9 5.7 %collective-permute-done.51 = bf16[2,2,256,128]{3,2,1,0:T(8,128)(2,1)} collective-permute-done((bf16[2,2,256,128]{3,2,1,0:T(8,128)(2,1)}, bf16[2,2,256,128]{3,2,1,0:T(8,128)(2,1)}, u32[]{:S(2)}, u32[]{:S(2)}) %collective-permute-start.51) | collective-permute-done | bytes 262176 | tf_op jit(solution)/shard_map/ppermute | solution.py:48
  319.6 1.9 collective-permute-done.49
  324.8 2.7 collective-permute-done.44.refs_15_
  327.5 2.3 add_convert_fusion.1
  334.3 1.7 collective-permute-done.53
  336.1 1.8 convert_add_fusion.7.refs_1_
  337.9 8.8 %project_back.1 = (f32[128,1536]{1,0:T(8,128)}, bf16[128,1536]{1,0:T(8,128)(2,1)}, bf16[64,1536]{1,0:T(8,128)(2,1)}, bf16[64,1536]{1,0:T(8,128)(2,1)}, bf16[128,...) custom-call(s32[1]{0:T(128)} %bitcast.own_ref, ...), custom_call_target="tpu_custom_call" | custom-call | flops 10376999936 | tf_op jit(solution)/shard_map/project_back/pallas_call | solution.py:412
  349.2 2.5 collective-permute-start.54
  353.1 4.0 collective-permute-done.54.above_ref
  357.0 4.2 %collective-permute-done.55.below_ref = bf16[64,1536]{1,0:T(8,128)(2,1)S(1)} collective-permute-done((bf16[64,1536]{1,0:T(8,128)(2,1)S(1)}, bf16[64,1536]{1,0:T(8,128)(2,1)S(1)}, u32[]{:S(2)}, u32[]{:S(2)}) %collective-permute-start.55) | collective-permute-done | bytes 196640 | tf_op jit(solution)/shard_map/ppermute | solution.py:48
  361.4 1.7 collective-permute-start.60
  363.0 2.2 collective-permute-start.57
  368.9 1.9 collective-permute-done.67.refs_0_
  372.3 1.6 collective-permute-done.59.refs_1_
  374.0 5.4 %collective-permute-done.58.refs_0_ = bf16[2,208,512]{2,1,0:T(8,128)(2,1)S(1)} collective-permute-done((bf16[2,208,512]{2,1,0:T(8,128)(2,1)S(1)}, bf16[2,208,512]{2,1,0:T(8,128)(2,1)S(1)}, u32[]{:S(2)}, u32[]{:S(2)}) %collective-permute-start.58) | collective-permute-done | bytes 426016 | tf_op jit(solution)/shard_map/ppermute | solution.py:48
  382.9 2.7 collective-permute-done.65
  386.6 1.8 collective-permute-start.64
  391.0 1.8 collective-permute-done.64
  392.8 1.8 collective-permute-done.63
  (436 shorter events, 86.6 us)
Async XLA Ops:
  7.2 161.8 %all-gather.2.cloned.1.call-start = ((), (), s32[]{:S(2)}) async-start(), calls=%async_computation.1 | async-start | bytes 23887872 | tf_op jit(solution)/shard_map/all_gather | solution.py:946
  10.3 327.6 %reduce-scatter.2.cloned.1.call-start = ((), (), s32[]{:S(2)}) async-start(), calls=%async_computation.2 | async-start | bytes 7962624 | tf_op jit(solution)/shard_map/reduce_scatter | solution.py:1132
  11.3 8.0 %collective-permute-start = (bf16[64,640]{1,0:T(8,128)(2,1)S(1)}, bf16[64,640]{1,0:T(8,128)(2,1)S(1)}, u32[]{:S(2)}, u32[]{:S(2)}) collective-permute-start(bf16[64,640]{1,0:T(8,128)(2,1)S(1)} %get-tuple-element.232), channel_id=1, source_target_pairs={{0,3},{1,0},{2,1},{3,2},{4,7},{5,4},{6,5},{7,6},{8,11},{9,8},{10,9... | collective-permute-start | bytes 245768 | tf_op jit(solution)/shard_map/ppermute | solution.py:48
  16.4 7.5 %collective-permute-start.1 = (bf16[64,640]{1,0:T(8,128)(2,1)S(1)}, bf16[64,640]{1,0:T(8,128)(2,1)S(1)}, u32[]{:S(2)}, u32[]{:S(2)}) collective-permute-start(bf16[64,640]{1,0:T(8,128)(2,1)S(1)} %get-tuple-element.233), channel_id=1, source_target_pairs={{0,2},{1,3},{2,0},{3,1},{4,6},{5,7},{6,4},{7,5},{8,10},{9,11},{10,... | collective-permute-start | bytes 245768 | tf_op jit(solution)/shard_map/ppermute | solution.py:48
  16.4 7.6 %collective-permute-start.2 = (bf16[64,640]{1,0:T(8,128)(2,1)S(1)}, bf16[64,640]{1,0:T(8,128)(2,1)S(1)}, u32[]{:S(2)}, u32[]{:S(2)}) collective-permute-start(bf16[64,640]{1,0:T(8,128)(2,1)S(1)} %get-tuple-element.230), channel_id=1, source_target_pairs={{0,1},{1,2},{2,3},{3,0},{4,5},{5,6},{6,7},{7,4},{8,9},{9,10},{10,1... | collective-permute-start | bytes 245768 | tf_op jit(solution)/shard_map/ppermute | solution.py:48
  27.4 15.5 %collective-permute-start.3 = (bf16[224,640]{1,0:T(8,128)(2,1)S(1)}, bf16[224,640]{1,0:T(8,128)(2,1)S(1)}, u32[]{:S(2)}, u32[]{:S(2)}) collective-permute-start(bf16[224,640]{1,0:T(8,128)(2,1)S(1)} %get-tuple-element.204), channel_id=1, source_target_pairs={{0,8},{4,12},{8,0},{12,4},{16,24},{20,28},{24,16},{28,20},{1,9},{5... | collective-permute-start | bytes 860168 | tf_op jit(solution)/shard_map/ppermute | solution.py:48
  28.9 15.3 %collective-permute-start.4 = (bf16[224,640]{1,0:T(8,128)(2,1)S(1)}, bf16[224,640]{1,0:T(8,128)(2,1)S(1)}, u32[]{:S(2)}, u32[]{:S(2)}) collective-permute-start(bf16[224,640]{1,0:T(8,128)(2,1)S(1)} %get-tuple-element.204), channel_id=1, source_target_pairs={{0,16},{4,20},{8,24},{12,28},{16,0},{20,4},{24,8},{28,12},{1,17},{... | collective-permute-start | bytes 860168 | tf_op jit(solution)/shard_map/ppermute | solution.py:48
  30.4 16.0 %collective-permute-start.7 = (bf16[128,1536]{1,0:T(8,128)(2,1)S(1)}, bf16[128,1536]{1,0:T(8,128)(2,1)S(1)}, u32[]{:S(2)}, u32[]{:S(2)}) collective-permute-start(bf16[128,1536]{1,0:T(8,128)(2,1)S(1)} %tie.30.refs_0_), channel_id=1, source_target_pairs={{0,3},{1,0},{2,1},{3,2},{4,7},{5,4},{6,5},{7,6},{8,11},{9,8},{10,9... | collective-permute-start | bytes 1179656 | tf_op jit(solution)/shard_map/ppermute | solution.py:48
  32.6 17.1 %collective-permute-start.8 = (bf16[128,1536]{1,0:T(8,128)(2,1)S(1)}, bf16[128,1536]{1,0:T(8,128)(2,1)S(1)}, u32[]{:S(2)}, u32[]{:S(2)}) collective-permute-start(bf16[128,1536]{1,0:T(8,128)(2,1)S(1)} %tie.30.refs_0_), channel_id=1, source_target_pairs={{0,1},{1,2},{2,3},{3,0},{4,5},{5,6},{6,7},{7,4},{8,9},{9,10},{10,1... | collective-permute-start | bytes 1179656 | tf_op jit(solution)/shard_map/ppermute | solution.py:48
  44.2 9.0 %collective-permute-start.6 = (bf16[112,640]{1,0:T(8,128)(2,1)S(1)}, bf16[112,640]{1,0:T(8,128)(2,1)S(1)}, u32[]{:S(2)}, u32[]{:S(2)}) collective-permute-start(bf16[112,640]{1,0:T(8,128)(2,1)S(1)} %slice.286), channel_id=1, source_target_pairs={{0,8},{4,12},{8,0},{12,4},{16,24},{20,28},{24,16},{28,20},{1,9},{5... | collective-permute-start | bytes 430088 | tf_op jit(solution)/shard_map/ppermute | solution.py:48
  44.9 8.9 %collective-permute-start.5 = (bf16[112,640]{1,0:T(8,128)(2,1)S(1)}, bf16[112,640]{1,0:T(8,128)(2,1)S(1)}, u32[]{:S(2)}, u32[]{:S(2)}) collective-permute-start(bf16[112,640]{1,0:T(8,128)(2,1)S(1)} %slice.285), channel_id=1, source_target_pairs={{0,16},{4,20},{8,24},{12,28},{16,0},{20,4},{24,8},{28,12},{1,17},{... | collective-permute-start | bytes 430088 | tf_op jit(solution)/shard_map/ppermute | solution.py:48
  49.7 6.8 %collective-permute-start.9 = (bf16[64,1536]{1,0:T(8,128)(2,1)S(1)}, bf16[64,1536]{1,0:T(8,128)(2,1)S(1)}, u32[]{:S(2)}, u32[]{:S(2)}) collective-permute-start(bf16[64,1536]{1,0:T(8,128)(2,1)S(1)} %slice.288), channel_id=1, source_target_pairs={{0,3},{1,0},{2,1},{3,2},{4,7},{5,4},{6,5},{7,6},{8,11},{9,8},{10,9... | collective-permute-start | bytes 589832 | tf_op jit(solution)/shard_map/ppermute | solution.py:48
  51.2 9.7 %collective-permute-start.10 = (bf16[64,1536]{1,0:T(8,128)(2,1)S(1)}, bf16[64,1536]{1,0:T(8,128)(2,1)S(1)}, u32[]{:S(2)}, u32[]{:S(2)}) collective-permute-start(bf16[64,1536]{1,0:T(8,128)(2,1)S(1)} %slice.289), channel_id=1, source_target_pairs={{0,1},{1,2},{2,3},{3,0},{4,5},{5,6},{6,7},{7,4},{8,9},{9,10},{10,1... | collective-permute-start | bytes 589832 | tf_op jit(solution)/shard_map/ppermute | solution.py:48
  64.2 15.9 %collective-permute-start.12 = (bf16[192,1536]{1,0:T(8,128)(2,1)S(1)}, bf16[192,1536]{1,0:T(8,128)(2,1)S(1)}, u32[]{:S(2)}, u32[]{:S(2)}) collective-permute-start(bf16[192,1536]{1,0:T(8,128)(2,1)S(1)} %tie.34.refs_1_), channel_id=1, source_target_pairs={{0,3},{1,0},{2,1},{3,2},{4,7},{5,4},{6,5},{7,6},{8,11},{9,8},{10,9... | collective-permute-start | bytes 1769480 | tf_op jit(solution)/shard_map/ppermute | solution.py:48
  66.4 27.1 %collective-permute-start.13 = (bf16[192,1536]{1,0:T(8,128)(2,1)S(1)}, bf16[192,1536]{1,0:T(8,128)(2,1)S(1)}, u32[]{:S(2)}, u32[]{:S(2)}) collective-permute-start(bf16[192,1536]{1,0:T(8,128)(2,1)S(1)} %tie.34.refs_1_), channel_id=1, source_target_pairs={{0,1},{1,2},{2,3},{3,0},{4,5},{5,6},{6,7},{7,4},{8,9},{9,10},{10,1... | collective-permute-start | bytes 1769480 | tf_op jit(solution)/shard_map/ppermute | solution.py:48
  76.8 16.7 %collective-permute-start.14 = (bf16[2,2,256,128]{3,2,1,0:T(8,128)(2,1)}, bf16[2,2,256,128]{3,2,1,0:T(8,128)(2,1)S(1)}, u32[]{:S(2)}, u32[]{:S(2)}) collective-permute-start(bf16[2,2,256,128]{3,2,1,0:T(8,128)(2,1)} %get-tuple-element.106), channel_id=1, source_target_pairs={{0,8},{4,12},{8,0},{12,4},{16,24},{20,28},{24,16},{28,20},{1,9},{5... | collective-permute-start | bytes 786440 | tf_op jit(solution)/shard_map/ppermute | solution.py:48
  77.0 16.5 %collective-permute-start.15 = (bf16[2,2,256,128]{3,2,1,0:T(8,128)(2,1)}, bf16[2,2,256,128]{3,2,1,0:T(8,128)(2,1)S(1)}, u32[]{:S(2)}, u32[]{:S(2)}) collective-permute-start(bf16[2,2,256,128]{3,2,1,0:T(8,128)(2,1)} %get-tuple-element.106), channel_id=1, source_target_pairs={{0,16},{4,20},{8,24},{12,28},{16,0},{20,4},{24,8},{28,12},{1,17},{... | collective-permute-start | bytes 786440 | tf_op jit(solution)/shard_map/ppermute | solution.py:48
  93.6 8.9 %collective-permute-start.19 = (bf16[1,2,256,128]{3,2,1,0:T(8,128)(2,1)S(1)}, bf16[1,2,256,128]{3,2,1,0:T(8,128)(2,1)}, u32[]{:S(2)}, u32[]{:S(2)}) collective-permute-start(bf16[1,2,256,128]{3,2,1,0:T(8,128)(2,1)S(1)} %slice.305), channel_id=1, source_target_pairs={{0,8},{4,12},{8,0},{12,4},{16,24},{20,28},{24,16},{28,20},{1,9},{5... | collective-permute-start | bytes 393224 | tf_op jit(solution)/shard_map/ppermute | solution.py:48
  94.2 8.8 %collective-permute-start.18 = (bf16[1,2,256,128]{3,2,1,0:T(8,128)(2,1)S(1)}, bf16[1,2,256,128]{3,2,1,0:T(8,128)(2,1)}, u32[]{:S(2)}, u32[]{:S(2)}) collective-permute-start(bf16[1,2,256,128]{3,2,1,0:T(8,128)(2,1)S(1)} %slice.304), channel_id=1, source_target_pairs={{0,16},{4,20},{8,24},{12,28},{16,0},{20,4},{24,8},{28,12},{1,17},{... | collective-permute-start | bytes 393224 | tf_op jit(solution)/shard_map/ppermute | solution.py:48
  96.4 11.1 %collective-permute-start.16 = (bf16[96,1536]{1,0:T(8,128)(2,1)}, bf16[96,1536]{1,0:T(8,128)(2,1)S(1)}, u32[]{:S(2)}, u32[]{:S(2)}) collective-permute-start(bf16[96,1536]{1,0:T(8,128)(2,1)} %slice.302), channel_id=1, source_target_pairs={{0,3},{1,0},{2,1},{3,2},{4,7},{5,4},{6,5},{7,6},{8,11},{9,8},{10,9... | collective-permute-start | bytes 884744 | tf_op jit(solution)/shard_map/ppermute | solution.py:48
  100.2 12.0 %collective-permute-start.17 = (bf16[96,1536]{1,0:T(8,128)(2,1)}, bf16[96,1536]{1,0:T(8,128)(2,1)S(1)}, u32[]{:S(2)}, u32[]{:S(2)}) collective-permute-start(bf16[96,1536]{1,0:T(8,128)(2,1)} %slice.303), channel_id=1, source_target_pairs={{0,1},{1,2},{2,3},{3,0},{4,5},{5,6},{6,7},{7,4},{8,9},{9,10},{10,1... | collective-permute-start | bytes 884744 | tf_op jit(solution)/shard_map/ppermute | solution.py:48
  105.1 9.6 %collective-permute-start.20 = (bf16[4,2,2,256,128]{4,3,2,1,0:T(8,128)(2,1)}, bf16[4,2,2,256,128]{4,3,2,1,0:T(8,128)(2,1)}, u32[]{:S(2)}, u32[]{:S(2)}) collective-permute-start(bf16[4,2,2,256,128]{4,3,2,1,0:T(8,128)(2,1)} %pad_maximum_fusion.2.near_ref.refs_5_), channel_id=1, source_target_pairs={{0,4},{4,0},{8,12},{12,8},{16,20},{20,16},{24,28},{28,24},{1,5},{5... | collective-permute-start | bytes 3145736 | tf_op jit(solution)/shard_map/ppermute | solution.py:48
  127.7 12.5 %collective-permute-start.21 = (bf16[512,384]{1,0:T(8,128)(2,1)}, bf16[512,384]{1,0:T(8,128)(2,1)S(1)}, u32[]{:S(2)}, u32[]{:S(2)}) collective-permute-start(bf16[512,384]{1,0:T(8,128)(2,1)} %get-tuple-element.114.refs_5_.refs_6_.refs_7_), channel_id=1, source_target_pairs={{0,3},{1,0},{2,1},{3,2},{4,7},{5,4},{6,5},{7,6},{8,11},{9,8},{10,9... | collective-permute-start | bytes 1179656 | tf_op jit(solution)/shard_map/ppermute | solution.py:48
  130.4 18.3 %collective-permute-start.22 = (bf16[512,384]{1,0:T(8,128)(2,1)}, bf16[512,384]{1,0:T(8,128)(2,1)S(1)}, u32[]{:S(2)}, u32[]{:S(2)}) collective-permute-start(bf16[512,384]{1,0:T(8,128)(2,1)} %get-tuple-element.114.refs_5_.refs_6_.refs_7_), channel_id=1, source_target_pairs={{0,1},{1,2},{2,3},{3,0},{4,5},{5,6},{6,7},{7,4},{8,9},{9,10},{10,1... | collective-permute-start | bytes 1179656 | tf_op jit(solution)/shard_map/ppermute | solution.py:48
  132.6 16.7 %collective-permute-start.25 = (bf16[192,1536]{1,0:T(8,128)(2,1)S(1)}, bf16[192,1536]{1,0:T(8,128)(2,1)S(1)}, u32[]{:S(2)}, u32[]{:S(2)}) collective-permute-start(bf16[192,1536]{1,0:T(8,128)(2,1)S(1)} %bitcast.181), channel_id=1, source_target_pairs={{0,8},{4,12},{8,0},{12,4},{16,24},{20,28},{24,16},{28,20},{1,9},{5... | collective-permute-start | bytes 1769480 | tf_op jit(solution)/shard_map/ppermute | solution.py:48
  133.4 15.8 %collective-permute-start.26 = (bf16[192,1536]{1,0:T(8,128)(2,1)S(1)}, bf16[192,1536]{1,0:T(8,128)(2,1)S(1)}, u32[]{:S(2)}, u32[]{:S(2)}) collective-permute-start(bf16[192,1536]{1,0:T(8,128)(2,1)S(1)} %bitcast.182), channel_id=1, source_target_pairs={{0,16},{4,20},{8,24},{12,28},{16,0},{20,4},{24,8},{28,12},{1,17},{... | collective-permute-start | bytes 1769480 | tf_op jit(solution)/shard_map/ppermute | solution.py:48
  149.3 8.7 %collective-permute-start.28 = (bf16[96,1536]{1,0:T(8,128)(2,1)S(1)}, bf16[96,1536]{1,0:T(8,128)(2,1)S(1)}, u32[]{:S(2)}, u32[]{:S(2)}) collective-permute-start(bf16[96,1536]{1,0:T(8,128)(2,1)S(1)} %slice.314), channel_id=1, source_target_pairs={{0,8},{4,12},{8,0},{12,4},{16,24},{20,28},{24,16},{28,20},{1,9},{5... | collective-permute-start | bytes 884744 | tf_op jit(solution)/shard_map/ppermute | solution.py:48
  150.8 8.3 %collective-permute-start.27 = (bf16[96,1536]{1,0:T(8,128)(2,1)S(1)}, bf16[96,1536]{1,0:T(8,128)(2,1)S(1)}, u32[]{:S(2)}, u32[]{:S(2)}) collective-permute-start(bf16[96,1536]{1,0:T(8,128)(2,1)S(1)} %slice.313), channel_id=1, source_target_pairs={{0,16},{4,20},{8,24},{12,28},{16,0},{20,4},{24,8},{28,12},{1,17},{... | collective-permute-start | bytes 884744 | tf_op jit(solution)/shard_map/ppermute | solution.py:48
  151.5 10.1 %collective-permute-start.23 = (bf16[256,384]{1,0:T(8,128)(2,1)S(1)}, bf16[256,384]{1,0:T(8,128)(2,1)S(1)}, u32[]{:S(2)}, u32[]{:S(2)}) collective-permute-start(bf16[256,384]{1,0:T(8,128)(2,1)S(1)} %slice.310), channel_id=1, source_target_pairs={{0,3},{1,0},{2,1},{3,2},{4,7},{5,4},{6,5},{7,6},{8,11},{9,8},{10,9... | collective-permute-start | bytes 589832 | tf_op jit(solution)/shard_map/ppermute | solution.py:48
  154.9 8.6 %collective-permute-start.24 = (bf16[256,384]{1,0:T(8,128)(2,1)S(1)}, bf16[256,384]{1,0:T(8,128)(2,1)S(1)}, u32[]{:S(2)}, u32[]{:S(2)}) collective-permute-start(bf16[256,384]{1,0:T(8,128)(2,1)S(1)} %slice.311), channel_id=1, source_target_pairs={{0,1},{1,2},{2,3},{3,0},{4,5},{5,6},{6,7},{7,4},{8,9},{9,10},{10,1... | collective-permute-start | bytes 589832 | tf_op jit(solution)/shard_map/ppermute | solution.py:48
  200.6 15.8 %collective-permute-start.34 = (bf16[512,6144]{1,0:T(8,128)(2,1)}, bf16[512,6144]{1,0:T(8,128)(2,1)}, u32[]{:S(2)}, u32[]{:S(2)}) collective-permute-start(bf16[512,6144]{1,0:T(8,128)(2,1)} %get-tuple-element.136.refs_0_.refs_1_.refs_2_), channel_id=1, source_target_pairs={{0,4},{4,0},{8,12},{12,8},{16,20},{20,16},{24,28},{28,24},{1,5},{5... | collective-permute-start | bytes 18874376 | tf_op jit(solution)/shard_map/ppermute | solution.py:48
  200.8 10.4 %collective-permute-start.30 = (bf16[64,1536]{1,0:T(8,128)(2,1)}, bf16[64,1536]{1,0:T(8,128)(2,1)S(1)}, u32[]{:S(2)}, u32[]{:S(2)}) collective-permute-start(bf16[64,1536]{1,0:T(8,128)(2,1)} %get-tuple-element.132), channel_id=1, source_target_pairs={{0,3},{1,0},{2,1},{3,2},{4,7},{5,4},{6,5},{7,6},{8,11},{9,8},{10,9... | collective-permute-start | bytes 589832 | tf_op jit(solution)/shard_map/ppermute | solution.py:48
  203.0 10.1 %collective-permute-start.31 = (bf16[64,1536]{1,0:T(8,128)(2,1)}, bf16[64,1536]{1,0:T(8,128)(2,1)S(1)}, u32[]{:S(2)}, u32[]{:S(2)}) collective-permute-start(bf16[64,1536]{1,0:T(8,128)(2,1)} %get-tuple-element.133), channel_id=1, source_target_pairs={{0,1},{1,2},{2,3},{3,0},{4,5},{5,6},{6,7},{7,4},{8,9},{9,10},{10,1... | collective-permute-start | bytes 589832 | tf_op jit(solution)/shard_map/ppermute | solution.py:48
  214.4 23.1 %collective-permute-start.32 = (bf16[128,1536]{1,0:T(8,128)(2,1)S(1)}, bf16[128,1536]{1,0:T(8,128)(2,1)S(1)}, u32[]{:S(2)}, u32[]{:S(2)}) collective-permute-start(bf16[128,1536]{1,0:T(8,128)(2,1)S(1)} %get-tuple-element.134.refs_8_), channel_id=1, source_target_pairs={{0,3},{1,0},{2,1},{3,2},{4,7},{5,4},{6,5},{7,6},{8,11},{9,8},{10,9... | collective-permute-start | bytes 1179656 | tf_op jit(solution)/shard_map/ppermute | solution.py:48
  216.4 21.1 %collective-permute-start.33 = (bf16[128,1536]{1,0:T(8,128)(2,1)S(1)}, bf16[128,1536]{1,0:T(8,128)(2,1)S(1)}, u32[]{:S(2)}, u32[]{:S(2)}) collective-permute-start(bf16[128,1536]{1,0:T(8,128)(2,1)S(1)} %get-tuple-element.135.refs_9_), channel_id=1, source_target_pairs={{0,1},{1,2},{2,3},{3,0},{4,5},{5,6},{6,7},{7,4},{8,9},{9,10},{10,1... | collective-permute-start | bytes 1179656 | tf_op jit(solution)/shard_map/ppermute | solution.py:48
  235.3 24.6 %collective-permute-start.40 = (bf16[1,192,2304]{2,1,0:T(8,128)(2,1)}, bf16[1,192,2304]{2,1,0:T(8,128)(2,1)S(1)}, u32[]{:S(2)}, u32[]{:S(2)}) collective-permute-start(bf16[1,192,2304]{2,1,0:T(8,128)(2,1)} %bitcast.194), channel_id=1, source_target_pairs={{0,16},{4,20},{8,24},{12,28},{16,0},{20,4},{24,8},{28,12},{1,17},{... | collective-permute-start | bytes 2654216 | tf_op jit(solution)/shard_map/ppermute | solution.py:48
  236.7 23.1 %collective-permute-start.41 = (bf16[1,192,2304]{2,1,0:T(8,128)(2,1)}, bf16[1,192,2304]{2,1,0:T(8,128)(2,1)S(1)}, u32[]{:S(2)}, u32[]{:S(2)}) collective-permute-start(bf16[1,192,2304]{2,1,0:T(8,128)(2,1)} %bitcast.193), channel_id=1, source_target_pairs={{0,8},{4,12},{8,0},{12,4},{16,24},{20,28},{24,16},{28,20},{1,9},{5... | collective-permute-start | bytes 2654216 | tf_op jit(solution)/shard_map/ppermute | solution.py:48
  243.9 7.1 %collective-permute-start.35 = (bf16[128,384]{1,0:T(8,128)(2,1)}, bf16[128,384]{1,0:T(8,128)(2,1)S(1)}, u32[]{:S(2)}, u32[]{:S(2)}) collective-permute-start(bf16[128,384]{1,0:T(8,128)(2,1)} %get-tuple-element.140), channel_id=1, source_target_pairs={{0,3},{1,0},{2,1},{3,2},{4,7},{5,4},{6,5},{7,6},{8,11},{9,8},{10,9... | collective-permute-start | bytes 294920 | tf_op jit(solution)/shard_map/ppermute | solution.py:48
  247.7 8.2 %collective-permute-start.36 = (bf16[128,384]{1,0:T(8,128)(2,1)}, bf16[128,384]{1,0:T(8,128)(2,1)S(1)}, u32[]{:S(2)}, u32[]{:S(2)}) collective-permute-start(bf16[128,384]{1,0:T(8,128)(2,1)} %get-tuple-element.141), channel_id=1, source_target_pairs={{0,2},{1,3},{2,0},{3,1},{4,6},{5,7},{6,4},{7,5},{8,10},{9,11},{10,... | collective-permute-start | bytes 294920 | tf_op jit(solution)/shard_map/ppermute | solution.py:48
  247.7 8.2 %collective-permute-start.37 = (bf16[128,384]{1,0:T(8,128)(2,1)}, bf16[128,384]{1,0:T(8,128)(2,1)S(1)}, u32[]{:S(2)}, u32[]{:S(2)}) collective-permute-start(bf16[128,384]{1,0:T(8,128)(2,1)} %get-tuple-element.142), channel_id=1, source_target_pairs={{0,1},{1,2},{2,3},{3,0},{4,5},{5,6},{6,7},{7,4},{8,9},{9,10},{10,1... | collective-permute-start | bytes 294920 | tf_op jit(solution)/shard_map/ppermute | solution.py:48
  257.6 23.4 %collective-permute-start.38 = (bf16[128,1536]{1,0:T(8,128)(2,1)S(1)}, bf16[128,1536]{1,0:T(8,128)(2,1)S(1)}, u32[]{:S(2)}, u32[]{:S(2)}) collective-permute-start(bf16[128,1536]{1,0:T(8,128)(2,1)S(1)} %tie.42), channel_id=1, source_target_pairs={{0,3},{1,0},{2,1},{3,2},{4,7},{5,4},{6,5},{7,6},{8,11},{9,8},{10,9... | collective-permute-start | bytes 1179656 | tf_op jit(solution)/shard_map/ppermute | solution.py:48
  259.3 21.8 %collective-permute-start.39 = (bf16[128,1536]{1,0:T(8,128)(2,1)S(1)}, bf16[128,1536]{1,0:T(8,128)(2,1)S(1)}, u32[]{:S(2)}, u32[]{:S(2)}) collective-permute-start(bf16[128,1536]{1,0:T(8,128)(2,1)S(1)} %tie.42), channel_id=1, source_target_pairs={{0,1},{1,2},{2,3},{3,0},{4,5},{5,6},{6,7},{7,4},{8,9},{9,10},{10,1... | collective-permute-start | bytes 1179656 | tf_op jit(solution)/shard_map/ppermute | solution.py:48
  259.9 42.5 %collective-permute-start.47 = (bf16[1,192,2304]{2,1,0:T(8,128)(2,1)}, bf16[1,192,2304]{2,1,0:T(8,128)(2,1)S(1)}, u32[]{:S(2)}, u32[]{:S(2)}) collective-permute-start(bf16[1,192,2304]{2,1,0:T(8,128)(2,1)} %tie.46), channel_id=1, source_target_pairs={{0,16},{4,20},{8,24},{12,28},{16,0},{20,4},{24,8},{28,12},{1,17},{... | collective-permute-start | bytes 2654216 | tf_op jit(solution)/shard_map/ppermute | solution.py:48
  261.5 41.0 %collective-permute-start.48 = (bf16[1,192,2304]{2,1,0:T(8,128)(2,1)}, bf16[1,192,2304]{2,1,0:T(8,128)(2,1)S(1)}, u32[]{:S(2)}, u32[]{:S(2)}) collective-permute-start(bf16[1,192,2304]{2,1,0:T(8,128)(2,1)} %tie.47), channel_id=1, source_target_pairs={{0,8},{4,12},{8,0},{12,4},{16,24},{20,28},{24,16},{28,20},{1,9},{5... | collective-permute-start | bytes 2654216 | tf_op jit(solution)/shard_map/ppermute | solution.py:48
  283.5 13.0 %collective-permute-start.42 = (bf16[128,1536]{1,0:T(8,128)(2,1)S(1)}, bf16[128,1536]{1,0:T(8,128)(2,1)S(1)}, u32[]{:S(2)}, u32[]{:S(2)}) collective-permute-start(bf16[128,1536]{1,0:T(8,128)(2,1)S(1)} %pad_maximum_fusion.3), channel_id=1, source_target_pairs={{0,3},{1,0},{2,1},{3,2},{4,7},{5,4},{6,5},{7,6},{8,11},{9,8},{10,9... | collective-permute-start | bytes 1179656 | tf_op jit(solution)/shard_map/ppermute | solution.py:48
  287.0 15.4 %collective-permute-start.43 = (bf16[128,1536]{1,0:T(8,128)(2,1)S(1)}, bf16[128,1536]{1,0:T(8,128)(2,1)S(1)}, u32[]{:S(2)}, u32[]{:S(2)}) collective-permute-start(bf16[128,1536]{1,0:T(8,128)(2,1)S(1)} %pad_maximum_fusion.4), channel_id=1, source_target_pairs={{0,1},{1,2},{2,3},{3,0},{4,5},{5,6},{6,7},{7,4},{8,9},{9,10},{10,1... | collective-permute-start | bytes 1179656 | tf_op jit(solution)/shard_map/ppermute | solution.py:48
  287.1 16.1 %collective-permute-start.46 = (bf16[4,2,2,256,128]{4,3,2,1,0:T(8,128)(2,1)S(1)}, bf16[4,2,2,256,128]{4,3,2,1,0:T(8,128)(2,1)S(1)}, u32[]{:S(2)}, u32[]{:S(2)}) collective-permute-start(bf16[4,2,2,256,128]{4,3,2,1,0:T(8,128)(2,1)S(1)} %tie.45), channel_id=1, source_target_pairs={{0,4},{4,0},{8,12},{12,8},{16,20},{20,16},{24,28},{28,24},{1,5},{5... | collective-permute-start | bytes 3145736 | tf_op jit(solution)/shard_map/ppermute | solution.py:48
  306.9 12.7 %collective-permute-start.51 = (bf16[2,2,256,128]{3,2,1,0:T(8,128)(2,1)}, bf16[2,2,256,128]{3,2,1,0:T(8,128)(2,1)}, u32[]{:S(2)}, u32[]{:S(2)}) collective-permute-start(bf16[2,2,256,128]{3,2,1,0:T(8,128)(2,1)} %pad_maximum_fusion.8), channel_id=1, source_target_pairs={{0,16},{4,20},{8,24},{12,28},{16,0},{20,4},{24,8},{28,12},{1,17},{... | collective-permute-start | bytes 786440 | tf_op jit(solution)/shard_map/ppermute | solution.py:48
  308.3 13.3 %collective-permute-start.49 = (bf16[2,2,256,128]{3,2,1,0:T(8,128)(2,1)}, bf16[2,2,256,128]{3,2,1,0:T(8,128)(2,1)}, u32[]{:S(2)}, u32[]{:S(2)}) collective-permute-start(bf16[2,2,256,128]{3,2,1,0:T(8,128)(2,1)} %pad_maximum_fusion.7), channel_id=1, source_target_pairs={{0,8},{4,12},{8,0},{12,4},{16,24},{20,28},{24,16},{28,20},{1,9},{5... | collective-permute-start | bytes 786440 | tf_op jit(solution)/shard_map/ppermute | solution.py:48
  309.7 15.1 %collective-permute-start.45 = (bf16[128,1536]{1,0:T(8,128)(2,1)S(1)}, bf16[128,1536]{1,0:T(8,128)(2,1)}, u32[]{:S(2)}, u32[]{:S(2)}) collective-permute-start(bf16[128,1536]{1,0:T(8,128)(2,1)S(1)} %get-tuple-element.156), channel_id=1, source_target_pairs={{0,1},{1,2},{2,3},{3,0},{4,5},{5,6},{6,7},{7,4},{8,9},{9,10},{10,1... | collective-permute-start | bytes 1179656 | tf_op jit(solution)/shard_map/ppermute | solution.py:48
  310.5 17.0 %collective-permute-start.44 = (bf16[128,1536]{1,0:T(8,128)(2,1)S(1)}, bf16[128,1536]{1,0:T(8,128)(2,1)}, u32[]{:S(2)}, u32[]{:S(2)}) collective-permute-start(bf16[128,1536]{1,0:T(8,128)(2,1)S(1)} %get-tuple-element.155), channel_id=1, source_target_pairs={{0,3},{1,0},{2,1},{3,2},{4,7},{5,4},{6,5},{7,6},{8,11},{9,8},{10,9... | collective-permute-start | bytes 1179656 | tf_op jit(solution)/shard_map/ppermute | solution.py:48
  322.9 6.9 %collective-permute-start.50 = (bf16[1,2,256,128]{3,2,1,0:T(8,128)(2,1)S(1)}, bf16[1,2,256,128]{3,2,1,0:T(8,128)(2,1)S(1)}, u32[]{:S(2)}, u32[]{:S(2)}) collective-permute-start(bf16[1,2,256,128]{3,2,1,0:T(8,128)(2,1)S(1)} %get-tuple-element.190), channel_id=1, source_target_pairs={{0,16},{4,20},{8,24},{12,28},{16,0},{20,4},{24,8},{28,12},{1,17},{... | collective-permute-start | bytes 393224 | tf_op jit(solution)/shard_map/ppermute | solution.py:48
  333.6 33.1 %collective-permute-start.66 = (bf16[1,192,2304]{2,1,0:T(8,128)(2,1)}, bf16[1,192,2304]{2,1,0:T(8,128)(2,1)S(1)}, u32[]{:S(2)}, u32[]{:S(2)}) collective-permute-start(bf16[1,192,2304]{2,1,0:T(8,128)(2,1)} %fusion.7), channel_id=1, source_target_pairs={{0,8},{4,12},{8,0},{12,4},{16,24},{20,28},{24,16},{28,20},{1,9},{5... | collective-permute-start | bytes 2654216 | tf_op jit(solution)/shard_map/ppermute | solution.py:48
  346.7 6.3 %collective-permute-start.56 = (bf16[4,208,896]{2,1,0:T(8,128)(2,1)}, bf16[4,208,896]{2,1,0:T(8,128)(2,1)S(1)}, u32[]{:S(2)}, u32[]{:S(2)}) collective-permute-start(bf16[4,208,896]{2,1,0:T(8,128)(2,1)} %get-tuple-element.173), channel_id=1, source_target_pairs={{0,4},{4,0},{8,12},{12,8},{16,20},{20,16},{24,28},{28,24},{1,5},{5... | collective-permute-start | bytes 4472840 | tf_op jit(solution)/shard_map/ppermute | solution.py:48
  348.3 22.5 %collective-permute-start.67 = (bf16[1,192,2304]{2,1,0:T(8,128)(2,1)S(1)}, bf16[1,192,2304]{2,1,0:T(8,128)(2,1)S(1)}, u32[]{:S(2)}, u32[]{:S(2)}) collective-permute-start(bf16[1,192,2304]{2,1,0:T(8,128)(2,1)S(1)} %fusion.6), channel_id=1, source_target_pairs={{0,16},{4,20},{8,24},{12,28},{16,0},{20,4},{24,8},{28,12},{1,17},{... | collective-permute-start | bytes 2654216 | tf_op jit(solution)/shard_map/ppermute | solution.py:48
  349.2 7.8 %collective-permute-start.54 = (bf16[64,1536]{1,0:T(8,128)(2,1)S(1)}, bf16[64,1536]{1,0:T(8,128)(2,1)S(1)}, u32[]{:S(2)}, u32[]{:S(2)}) collective-permute-start(bf16[64,1536]{1,0:T(8,128)(2,1)S(1)} %copy-done.74), channel_id=1, source_target_pairs={{0,3},{1,0},{2,1},{3,2},{4,7},{5,4},{6,5},{7,6},{8,11},{9,8},{10,9... | collective-permute-start | bytes 589832 | tf_op jit(solution)/shard_map/ppermute | solution.py:48
  351.7 9.5 %collective-permute-start.55 = (bf16[64,1536]{1,0:T(8,128)(2,1)S(1)}, bf16[64,1536]{1,0:T(8,128)(2,1)S(1)}, u32[]{:S(2)}, u32[]{:S(2)}) collective-permute-start(bf16[64,1536]{1,0:T(8,128)(2,1)S(1)} %copy-done.73), channel_id=1, source_target_pairs={{0,1},{1,2},{2,3},{3,0},{4,5},{5,6},{6,7},{7,4},{8,9},{9,10},{10,1... | collective-permute-start | bytes 589832 | tf_op jit(solution)/shard_map/ppermute | solution.py:48
  361.4 20.1 %collective-permute-start.60 = (bf16[128,1536]{1,0:T(8,128)(2,1)S(1)}, bf16[128,1536]{1,0:T(8,128)(2,1)S(1)}, u32[]{:S(2)}, u32[]{:S(2)}) collective-permute-start(bf16[128,1536]{1,0:T(8,128)(2,1)S(1)} %get-tuple-element.179), channel_id=1, source_target_pairs={{0,1},{1,2},{2,3},{3,0},{4,5},{5,6},{6,7},{7,4},{8,9},{9,10},{10,1... | collective-permute-start | bytes 1179656 | tf_op jit(solution)/shard_map/ppermute | solution.py:48
  363.0 18.4 %collective-permute-start.57 = (bf16[128,1536]{1,0:T(8,128)(2,1)S(1)}, bf16[128,1536]{1,0:T(8,128)(2,1)S(1)}, u32[]{:S(2)}, u32[]{:S(2)}) collective-permute-start(bf16[128,1536]{1,0:T(8,128)(2,1)S(1)} %get-tuple-element.174.refs_1_), channel_id=1, source_target_pairs={{0,3},{1,0},{2,1},{3,2},{4,7},{5,4},{6,5},{7,6},{8,11},{9,8},{10,9... | collective-permute-start | bytes 1179656 | tf_op jit(solution)/shard_map/ppermute | solution.py:48
  365.3 14.1 %collective-permute-start.58 = (bf16[2,208,512]{2,1,0:T(8,128)(2,1)S(1)}, bf16[2,208,512]{2,1,0:T(8,128)(2,1)S(1)}, u32[]{:S(2)}, u32[]{:S(2)}) collective-permute-start(bf16[2,208,512]{2,1,0:T(8,128)(2,1)S(1)} %add_convert_fusion), channel_id=1, source_target_pairs={{0,16},{4,20},{8,24},{12,28},{16,0},{20,4},{24,8},{28,12},{1,17},{... | collective-permute-start | bytes 1277960 | tf_op jit(solution)/shard_map/ppermute | solution.py:48
  366.7 7.3 %collective-permute-start.59 = (bf16[2,192,384]{2,1,0:T(8,128)(2,1)S(1)}, bf16[2,192,384]{2,1,0:T(8,128)(2,1)S(1)}, u32[]{:S(2)}, u32[]{:S(2)}) collective-permute-start(bf16[2,192,384]{2,1,0:T(8,128)(2,1)S(1)} %add_convert_fusion.2), channel_id=1, source_target_pairs={{0,8},{4,12},{8,0},{12,4},{16,24},{20,28},{24,16},{28,20},{1,9},{5... | collective-permute-start | bytes 884744 | tf_op jit(solution)/shard_map/ppermute | solution.py:48
  379.5 6.9 %collective-permute-start.61 = (bf16[1,208,512]{2,1,0:T(8,128)(2,1)S(1)}, bf16[1,208,512]{2,1,0:T(8,128)(2,1)S(1)}, u32[]{:S(2)}, u32[]{:S(2)}) collective-permute-start(bf16[1,208,512]{2,1,0:T(8,128)(2,1)S(1)} %add_convert_fusion.4), channel_id=1, source_target_pairs={{0,8},{4,12},{8,0},{12,4},{16,24},{20,28},{24,16},{28,20},{1,9},{5... | collective-permute-start | bytes 638984 | tf_op jit(solution)/shard_map/ppermute | solution.py:48
  386.6 6.2 %collective-permute-start.64 = (bf16[64,512]{1,0:T(8,128)(2,1)S(1)}, bf16[64,512]{1,0:T(8,128)(2,1)S(1)}, u32[]{:S(2)}, u32[]{:S(2)}) collective-permute-start(bf16[64,512]{1,0:T(8,128)(2,1)S(1)} %get-tuple-element.202), channel_id=1, source_target_pairs={{0,1},{1,2},{2,3},{3,0},{4,5},{5,6},{6,7},{7,4},{8,9},{9,10},{10,1... | collective-permute-start | bytes 196616 | tf_op jit(solution)/shard_map/ppermute | solution.py:48
  388.4 6.2 %collective-permute-start.63 = (bf16[64,512]{1,0:T(8,128)(2,1)S(1)}, bf16[64,512]{1,0:T(8,128)(2,1)S(1)}, u32[]{:S(2)}, u32[]{:S(2)}) collective-permute-start(bf16[64,512]{1,0:T(8,128)(2,1)S(1)} %get-tuple-element.201), channel_id=1, source_target_pairs={{0,2},{1,3},{2,0},{3,1},{4,6},{5,7},{6,4},{7,5},{8,10},{9,11},{10,... | collective-permute-start | bytes 196616 | tf_op jit(solution)/shard_map/ppermute | solution.py:48
  (83 other events, 364.1 us)
Sparse Core Ops, SparseCore 0:
  10.4 129.8 all-gather.1
  256.7 68.4 reduce-scatter.1

commit v4 on v3

--- a/solution.py
+++ b/solution.py
@@ -12,6 +12,7 @@
 HEADS = 12
 KV_HEADS = 2
 HD = 128
+MORE_ROWS = 16
 QD = 1536
 KD = 256
 QKV = 2048
@@ -25,7 +26,7 @@
 TILE = 768
 MIB = 2**20
 
-TUNE = dict(x1=10, x2=30, mx=10, c2=8, g0=25, g1=10, wm=10, ct=15, project=7, project_back=9, attend=16, attend_back=18, feed_forward=36, down_product=8, pair_grads=7, norm_back=5.5, payload=2)
+TUNE = dict(x1=10, x2=30, mx=10, c2=8, g1=25, wm=0, ct=0, s2=20, project=7, project_back=9, attend=16, attend_back=18, feed_forward=36, down_product=8, pair_grads=7, wide_grads=11, norm_back=5.5, payload=2, far=25)
 
 BF = jnp.bfloat16
 F32 = jnp.float32
@@ -85,36 +86,26 @@
 
 
 def gather_blocks(block, axis, last=(), micros=0):
-    half = block.shape[0] // 2
     above = from_next(block, axis)
     below = to_next(block, axis)
     above, below = tie_all([above, below], *last, micros=micros)
-    return [block, above, from_next(above[:half], axis), to_next(below[half:], axis), below]
-
-
-def sum_first(far, axis):
-    return from_next(far[0], axis), to_next(far[1], axis)
-
-
-def payload_kernel(ahead_ref, behind_ref, above_ref, below_ref, *refs):
-    down_ref, up_ref = refs[-2:]
-    half = ahead_ref.shape[0] // 2
-    down_ref[:half, :] = (behind_ref[:half, :].astype(F32) + above_ref[...].astype(F32)).astype(BF)
-    down_ref[half:, :] = behind_ref[half:, :]
-    up_ref[:half, :] = ahead_ref[:half, :]
-    up_ref[half:, :] = (ahead_ref[half:, :].astype(F32) + below_ref[...].astype(F32)).astype(BF)
-
-
-def sum_payload(ahead, behind, moved, others=()):
+    return [block, above, from_next(above, axis), below]
+
+
+def payload_kernel(behind_ref, moved_ref, *refs):
+    refs[-1][...] = (behind_ref[...].astype(F32) + moved_ref[...].astype(F32)).astype(BF)
+
+
+def sum_payload(behind, moved, others=()):
     return pl.pallas_call(
         payload_kernel,
-        in_specs=[vmem()] * 4 + [anywhere()] * len(others),
-        out_specs=[vmem()] * 2,
-        out_shape=[shape_of(ahead.shape)] * 2,
+        in_specs=[vmem()] * 2 + [anywhere()] * len(others),
+        out_specs=vmem(),
+        out_shape=shape_of(behind.shape),
         compiler_params=params(16),
         cost_estimate=cost(TUNE["payload"]),
         name="payload",
-    )(ahead, behind, *moved, *others)
+    )(behind, moved, *others)
 
 
 def far_first(block, axis):
@@ -251,18 +242,13 @@
 
 
 def row_shapes(tok_rows, width):
-    half = tok_rows // 2
-    return [shape_of((tok_rows, width), F32), shape_of((tok_rows, width))] + [
-        shape_of((rows, width)) for rows in (half, half, tok_rows)
-    ]
+    return [shape_of((tok_rows, width), F32)] + [shape_of((tok_rows, width))] * 3
 
 
 def fill_rows(to_ref, parts):
     size = parts[0].shape[0]
-    at = 0
-    for part, rows in zip(parts, (size, size, size // 2, size // 2, size)):
-        to_ref[at : at + rows, :] = part[:rows, :]
-        at += rows
+    for t, part in enumerate(parts):
+        to_ref[t * size : (t + 1) * size, :] = part[:size, :]
 
 
 def head_rows(tok_rows, blocks):
@@ -274,17 +260,74 @@
     ]
 
 
-def project_kernel(heads, own_ref, *refs):
-    parts = refs[:5]
-    gain_ref, bias_ref, cos_ref, sin_ref, near, other = refs[5:11]
-    q_ref, kv_ref, x_ref, normed_ref, w_ref, sem = refs[11:]
+def arrange_kernel(head_ref, *refs):
+    to_ref = refs[-1]
+    count = len(refs) - 1
+    rows = refs[0].shape[0] - MORE_ROWS
+    line = lax.broadcasted_iota(jnp.int32, (MORE_ROWS, to_ref.shape[1]), 0)
+    small = jnp.zeros(line.shape, F32)
+    for apart, ref in enumerate(refs[:-1]):
+        place = lax.rem(head_ref[0] + apart, count)
+        to_ref[pl.ds(pl.multiple_of(place * rows, rows), rows), :] = ref[:rows, :]
+        small = jnp.where(line == place, ref[rows : rows + 1, :].astype(F32), small)
+    to_ref[count * rows : count * rows + MORE_ROWS, :] = small.astype(BF)
+    to_ref[count * rows + MORE_ROWS :, :] = jnp.zeros(line.shape, BF)
+
+
+def arrange(head, blocks):
+    rows, cols = blocks[0].shape
+    if (rows - MORE_ROWS) % 16:
+        count = len(blocks)
+        ordered = roll_blocks(jnp.stack(blocks), (count - head[0]) % count)
+        small = jnp.pad(ordered[:, rows - MORE_ROWS], ((0, 2 * MORE_ROWS - count), (0, 0)))
+        return jnp.concatenate([ordered[:, : rows - MORE_ROWS].reshape(-1, cols), small])
+    return pl.pallas_call(
+        arrange_kernel,
+        in_specs=[smem()] + [vmem()] * len(blocks),
+        out_specs=vmem(),
+        out_shape=shape_of((len(blocks) * (rows - MORE_ROWS) + 2 * MORE_ROWS, cols)),
+        compiler_params=params(60),
+        cost_estimate=cost(1),
+        name="arrange",
+    )(head, *blocks)
+
+
+def project_kernel(heads, gain_cols, bias_cols, own_ref, head_ref, *refs):
+    parts = refs[:4]
+    cos_ref, sin_ref, near, other = refs[4:8]
+    q_ref, kv_ref, x_ref, normed_ref, w_ref, small_v, gain_v, all_v, bias_v, sem, small_sem = refs[8:]
+    rows = w_ref.shape[0] // small_v.shape[0]
+    smalls = []
+    for side, source in enumerate((near, other)):
+        for i in range(source.shape[0]):
+            copy = pltpu.make_async_copy(
+                source.at[i, pl.ds(rows, MORE_ROWS), :],
+                small_v.at[own_ref[0] ^ (2 * i + side)],
+                small_sem.at[side, i],
+            )
+            copy.start()
+            smalls.append(copy)
     copies = start_blocks(own_ref, near, other, w_ref, sem)
+    for copy in smalls:
+        copy.wait()
+    devices = gain_v.shape[1] // gain_cols
+    per = devices // small_v.shape[0]
+    for d in range(devices):
+        row = small_v[d // per, d % per : d % per + 1, :].astype(F32)
+        gain_v[:, d * gain_cols : (d + 1) * gain_cols] = row[:, :gain_cols]
+        all_v[:, d * bias_cols : (d + 1) * bias_cols] = row[:, 2 * gain_cols : 2 * gain_cols + bias_cols]
+    head = head_ref[0]
+    last = heads * HD
+    slot = (head // ((QD // last) // KV_HEADS)) * HD
+    bias_v[:, :last] = all_v[:, pl.ds(pl.multiple_of(head * last, HD), last)]
+    bias_v[:, last : last + HD] = all_v[:, pl.ds(pl.multiple_of(QD + slot, HD), HD)]
+    bias_v[:, last + HD :] = all_v[:, pl.ds(pl.multiple_of(QD + KD + slot, HD), HD)]
     fill_rows(x_ref, parts)
     values = x_ref[...].astype(F32)
-    normed_ref[...] = (values * inverse_norm(values) * gain_ref[...]).astype(BF)
+    normed_ref[...] = (values * inverse_norm(values) * gain_v[...]).astype(BF)
     for copy in copies:
         copy.wait()
-    joint = dot_nn(normed_ref[...], w_ref[...]) + bias_ref[...]
+    joint = dot_nn(normed_ref[...], w_ref[...]) + bias_v[...]
     tok_rows = parts[0].shape[0]
     blocks = x_ref.shape[0] // tok_rows
     half_rows = x_ref.shape[0] // 2
@@ -301,13 +344,13 @@
                 kv_ref[j - heads, half, low : low + count, :] = piece
 
 
-def project(own, parts, gain, bias, cos, sin, near, other, heads):
+def project(own, head, parts, cos, sin, near, other, heads, gain_cols, bias_cols):
     width = parts[0].shape[1]
     rows = cos.shape[0]
     cols = near.shape[2]
     return pl.pallas_call(
-        functools.partial(project_kernel, heads),
-        in_specs=[smem()] + [vmem()] * 9 + [anywhere()] * 2,
+        functools.partial(project_kernel, heads, gain_cols, bias_cols),
+        in_specs=[smem()] * 2 + [vmem()] * 6 + [anywhere()] * 2,
         out_specs=[vmem()] * 5,
         out_shape=[
             shape_of((2, heads * rows // 2, HD)),
@@ -316,21 +359,28 @@
             shape_of((rows, width)),
             shape_of((width, cols)),
         ],
-        scratch_shapes=[pltpu.SemaphoreType.DMA((2, near.shape[0]))],
+        scratch_shapes=[
+            pltpu.VMEM((2 * near.shape[0], MORE_ROWS, cols), BF),
+            pltpu.VMEM((1, width), F32),
+            pltpu.VMEM((1, QKV), F32),
+            pltpu.VMEM((1, cols), F32),
+            pltpu.SemaphoreType.DMA((2, near.shape[0])),
+            pltpu.SemaphoreType.DMA((2, near.shape[0])),
+        ],
         compiler_params=params(60),
         cost_estimate=cost(TUNE["project"]),
         name="project",
-    )(own, *parts, gain, bias, cos, sin, near, other)
+    )(own, head, *parts, cos, sin, near, other)
 
 
 def project_back_kernel(heads, orders, others, own_ref, head_ref, *refs):
-    refs = refs[:14] + refs[14 + others :]
+    refs = refs[:13] + refs[13 + others :]
     dq_ref, dkv_ref, cos_ref, sin_ref, normed_ref, x_ref, w_ref, mixed_ref = refs[:8]
-    parts = refs[8:13]
-    gain_two_ref = refs[13]
-    dn_refs = refs[14:19]
-    cols_kept, outs_kept, wide_sent = refs[19:22]
-    cols, branch, wide, wide_out, bias_v, small_v = refs[22:]
+    parts = refs[8:12]
+    gain_two_ref = refs[12]
+    dn_refs = refs[13:17]
+    cols_kept, outs_kept, wide_sent = refs[17:20]
+    cols, branch, wide, wide_out, bias_v, small_v = refs[20:]
     rows = cos_ref.shape[0]
     half_rows = rows // 2
     tok_rows = parts[0].shape[0]
@@ -399,9 +449,6 @@
                         wide_sent[i, count:, lanes] = small
 
 
-MORE_ROWS = 16
-
-
 def project_back(own, head, orders, dq, dkv, cos, sin, normed, x, w, mixed, parts, gain_two, others):
     rows, width = normed.shape
     heads = dq.shape[1] // (rows // 2)
@@ -411,8 +458,8 @@
     part_rows = width // (2 * far)
     return pl.pallas_call(
         functools.partial(project_back_kernel, heads, orders, len(others)),
-        in_specs=[smem()] * 2 + [vmem()] * 14 + [anywhere()] * len(others),
-        out_specs=[vmem()] * 8,
+        in_specs=[smem()] * 2 + [vmem()] * 13 + [anywhere()] * len(others),
+        out_specs=[vmem()] * 7,
         out_shape=[
             *row_shapes(tok_rows, width),
             shape_of((far, part_rows + MORE_ROWS, cols)),
@@ -628,14 +675,14 @@
 
 def feed_forward_kernel(own_ref, gain_ref, *refs):
     x_hbm = refs[0]
-    cot_parts = refs[1:6]
-    mixed_parts = refs[6:11]
-    near_w, other_w, joined_w = refs[11:14]
-    refs = refs[14:]
+    cot_parts = refs[1:5]
+    mixed_parts = refs[5:9]
+    near_w, other_w, joined_w = refs[9:12]
+    refs = refs[12:]
     acts_ref, hidden_ref, middle_ref, cot_ref = refs[:4]
-    dx_refs = refs[4:9]
-    x_v, out_v, gate_v, up_v, down_v, mixed_v, normed_v, middle_v, dg_v, du_v, cot_v = refs[9:20]
-    in_sem, cot_sem, out_sem, w_sem, s_sem = refs[20:]
+    dx_refs = refs[4:8]
+    x_v, out_v, gate_v, up_v, down_v, mixed_v, normed_v, middle_v, dg_v, du_v, cot_v = refs[8:19]
+    in_sem, cot_sem, out_sem, w_sem, s_sem = refs[19:]
     rows, width = x_v.shape
     units = gate_v.shape[1]
     tok_rows = hidden_ref.shape[0]
@@ -650,15 +697,9 @@
         return copy
 
     first = [begin(x_hbm, x_v, in_sem.at[0])]
-    for t, part, low in (
-        (0, mixed_parts[0], 0),
-        (1, mixed_parts[1], 0),
-        (2, mixed_parts[2], 0),
-        (2, mixed_parts[3], blocks // 2),
-        (3, mixed_parts[4], 0),
-    ):
-        for b in range(part.shape[0] // tok_rows):
-            u = (low + b + t) % blocks
+    for t, part in enumerate(mixed_parts):
+        for b in range(blocks):
+            u = (b + t) % blocks
             first.append(
                 begin(
                     part.at[pl.ds(b * tok_rows, tok_rows), :],
@@ -667,7 +708,7 @@
                 )
             )
     first += start_blocks(own_ref, near_w, other_w, out_v, out_sem)
-    cots, step = [], cot_parts[2].shape[0]
+    cots, step = [], cot_parts[0].shape[0] // 2
     for part in cot_parts:
         for low in range(0, part.shape[0], step):
             i = len(cots)
@@ -728,8 +769,8 @@
     blocks = rows // tok_rows
     return pl.pallas_call(
         feed_forward_kernel,
-        in_specs=[smem(), vmem()] + [anywhere()] * 14,
-        out_specs=[anywhere(), vmem()] + [anywhere()] * 2 + [vmem()] * 5,
+        in_specs=[smem(), vmem()] + [anywhere()] * 12,
+        out_specs=[anywhere(), vmem()] + [anywhere()] * 2 + [vmem()] * 4,
         out_shape=[
             shape_of((rows, 2 * units + width)),
             shape_of((tok_rows, width), F32),
@@ -761,7 +802,8 @@
     )(own, gain, x, *cot_parts, *mixed_parts, near, other, joined_all)
 
 
-def down_product_kernel(down_w, middle_ref, *refs):
+def down_product_kernel(others, down_w, middle_ref, *refs):
+    refs = refs[others:]
     acc = refs[-1]
     step = pl.program_id(0)
 
@@ -776,84 +818,92 @@
         store_rows(refs[:-1], slice(None), acc)
 
 
-def down_product(middle, joined_all, tok_rows):
+def down_product(middle, joined_all, tok_rows, others):
     rows, units = middle.shape
     full = joined_all.shape[0]
     steps = units // TILE
     outs = row_shapes(tok_rows, full)
     return pl.pallas_call(
-        down_product_kernel,
+        functools.partial(down_product_kernel, len(others)),
         grid=(steps,),
         in_specs=[
             pl.BlockSpec((full, TILE), lambda i: (0, 2 * steps + i)),
             pl.BlockSpec((rows, TILE), lambda i: (0, i)),
-        ],
+        ]
+        + [anywhere()] * len(others),
         out_specs=[fixed(out.shape) for out in outs],
         out_shape=outs,
         scratch_shapes=[pltpu.VMEM((rows, full), F32)],
         compiler_params=params(60),
         cost_estimate=cost(TUNE["down_product"]),
         name="down_product",
-    )(joined_all, middle)
+    )(joined_all, middle, *others)
+
+
+def wide_grads_kernel(x_ref, acts_ref, out_ref, turned):
+    @pl.when(pl.program_id(0) == 0)
+    def _():
+        turned[...] = jnp.transpose(x_ref[...])
+
+    out_ref[...] = dot_nn(turned[...], acts_ref[...]).astype(BF)
+
+
+def wide_grads(acts, width):
+    rows = acts.shape[0]
+    units = acts.shape[1] - width
+    return pl.pallas_call(
+        wide_grads_kernel,
+        grid=(units // TILE,),
+        in_specs=[
+            pl.BlockSpec((rows, width), lambda i: (0, units // width)),
+            pl.BlockSpec((rows, TILE), lambda i: (0, i)),
+        ],
+        out_specs=pl.BlockSpec((width, TILE), lambda i: (0, i)),
+        out_shape=shape_of((width, units)),
+        scratch_shapes=[pltpu.VMEM((width, rows), BF)],
+        compiler_params=params(60),
+        cost_estimate=cost(TUNE["wide_grads"]),
+        name="wide_grads",
+    )(acts, acts)
 
 
 def pair_grads_kernel(orders, others, own_ref, *refs):
-    xs, gates, ups = refs[:6:3], refs[1:6:3], refs[2:6:3]
-    cot_ref, middle_ref = refs[6:8]
-    *outs, down_ref = refs[8 + others : -4]
-    one, two, turned, cot_t = refs[-4:]
+    cots, middles = refs[:2], refs[2:4]
+    outs = refs[4 + others : -2]
+    one, two, turned = refs[-3:]
     count = len(outs) // 2
     blocks = len(orders[0])
     rows = one.shape[0] // blocks
-    tokens = xs[0].shape[0]
-
-    @pl.when(pl.program_id(0) == 0)
-    def _():
-        cot_t[...] = jnp.transpose(cot_ref[...])
-        for side, x_ref in enumerate(xs):
-            turned[...] = jnp.transpose(x_ref[...])
-            where = slice(side * tokens, (side + 1) * tokens)
+    tokens = cots[0].shape[0]
+    cols = outs[0].shape[1]
+    for side, cot_ref in enumerate(cots):
+        turned[side] = jnp.transpose(cot_ref[...])
+        for left, order in ((one, orders[0]), (two, orders[1])):
             for j in range(blocks):
-                here = slice(j * rows, (j + 1) * rows)
-                for to, which in ((one, 0), (two, 1)):
-                    at = pl.multiple_of((own_ref[0] ^ orders[which][j]) * rows, 16)
-                    to[here, where] = turned[pl.ds(at, rows), :]
-
-    for left, grads, quarters in ((one, gates, outs[:count]), (two, ups, outs[count:])):
-        result = dot_nn(left[:, :tokens], grads[0][...]) + dot_nn(left[:, tokens:], grads[1][...])
-        store_rows(quarters, slice(None), result)
-    down_ref[...] = dot_nn(cot_t[...], middle_ref[...]).astype(BF)
-
-
-def pair_grads(own, orders, acts, cot, middle, others):
-    rows, width = cot.shape
-    full = width
-    units = (acts[0].shape[1] - width) // 2
-    steps = units // TILE
-
-    def tiles(rows, first=0):
-        return pl.BlockSpec((rows, TILE), lambda i, own: (0, first + i))
-
-    one_side = [
-        pl.BlockSpec((rows, width), lambda i, own: (0, 2 * units // width)),
-        tiles(rows),
-        tiles(rows, steps),
-    ]
+                at = pl.multiple_of((own_ref[0] ^ order[j]) * rows, 16)
+                left[j * rows : (j + 1) * rows, side * tokens : (side + 1) * tokens] = turned[
+                    side, pl.ds(at, rows), :
+                ]
+    for which, left in enumerate((one, two)):
+        here = slice(which * cols, (which + 1) * cols)
+        result = dot_nn(left[:, :tokens], middles[0][:, here]) + dot_nn(left[:, tokens:], middles[1][:, here])
+        store_rows(outs[which * count : (which + 1) * count], slice(None), result)
+
+
+def pair_grads(own, orders, cots, middles, others):
+    rows, full = cots[0].shape
+    cols = middles[0].shape[1] // 2
+    outs = [shape_of((n, cols)) for n in (full // 8, full // 8, full // 4)] * 2
     return pl.pallas_call(
         functools.partial(pair_grads_kernel, orders, len(others)),
-        grid_spec=pltpu.PrefetchScalarGridSpec(
-            num_scalar_prefetch=1,
-            grid=(steps,),
-            in_specs=one_side * 2 + [fixed(cot.shape), tiles(rows)] + [anywhere()] * len(others),
-            out_specs=[tiles(full // 8)] * 8 + [tiles(full)],
-            scratch_shapes=[pltpu.VMEM((full // 2, 2 * rows), BF)] * 2
-            + [pltpu.VMEM((full, rows), BF)] * 2,
-        ),
-        out_shape=[shape_of((full // 8, units))] * 8 + [shape_of((full, units))],
+        in_specs=[smem()] + [vmem()] * 4 + [anywhere()] * len(others),
+        out_specs=[vmem()] * 6,
+        out_shape=outs,
+        scratch_shapes=[pltpu.VMEM((full // 2, 2 * rows), BF)] * 2 + [pltpu.VMEM((2, full, rows), BF)],
         compiler_params=params(60),
         cost_estimate=cost(TUNE["pair_grads"]),
         name="pair_grads",
-    )(own, *[side for side in acts for _ in range(3)], cot, middle, *others)
+    )(own, *cots, *middles, *others)
 
 
 def norm_back_kernel(others, own_ref, *refs):
@@ -970,24 +1020,17 @@
             lax.dynamic_slice_in_dim(values, QD + KD + slot * HD, HD, last),
         ]
 
+    own_wide = qkv_weight.shape[0]
+    own_rows = own_wide * heads_dev
     rows_of = []
     for apart in range(heads_dev):
         target = (head_index - apart) % heads_dev
         block = jnp.concatenate(head_columns(qkv_weight, target), axis=1)
         block = jnp.concatenate([block, small_row])
         rows_of.append(from_next(block, "head", apart) if apart else block)
-    own_wide = qkv_weight.shape[0]
-    own_rows = own_wide * heads_dev
     inputs_parts = gather_blocks(tie(inputs, *rows_of[1:]), "head", micros=TUNE["x1"])
-    rows_of = roll_blocks(jnp.stack(rows_of), (heads_dev - head_index) % heads_dev)
-    small_grp = rows_of[:, own_wide]
-    cols_own = jnp.concatenate(
-        [
-            rows_of[:, :own_wide].reshape(own_rows, cols_here),
-            jnp.pad(small_grp, ((0, 2 * MORE_ROWS - heads_dev), (0, 0))),
-        ]
-    )
-    cols_own = plain(cols_own)
+    cols_own = arrange(head_own, rows_of)
+    small_grp = cols_own[own_rows : own_rows + heads_dev]
     cols_near, _ = far_last(cols_own, far_first(cols_own, "seq"), "seq")
     inputs_parts[2:4] = tie_all(inputs_parts[2:4], micros=TUNE["x2"])
     cols_other = swap(tie(cols_near, *inputs_parts[2:4]), "seq", 0)
@@ -1024,7 +1067,6 @@
 
     gain_attn = in_order(cuts[0]).reshape(1, -1).astype(F32)
     gain_mlp = in_order(cuts[1]).reshape(1, -1).astype(F32)
-    bias_all = in_order(cuts[2]).astype(F32)
 
     def halves_first(values):
         tail = values.shape[1:]
@@ -1044,17 +1086,17 @@
     cosine_part = jnp.concatenate([cosine, cosine], axis=1)
     sine_part = jnp.concatenate([-sine, sine], axis=1)
 
-    bias_here = jnp.concatenate(head_columns(bias_all, head_index))[None]
     queries, kv_own, inputs_grp, normed_one, cols_weight = project(
         seq_own,
+        head_own,
         inputs_parts,
-        gain_attn,
-        bias_here,
         cosine_part,
         sine_part,
         cols_near,
         cols_other,
         heads_here,
+        gain_cols,
+        bias_cols,
     )
     half = tok_rows // 2
     out_flat = out_weight.reshape(-1, width)
@@ -1085,7 +1127,7 @@
     out_rows = plain(halves[:, half : half + out_half].reshape(QD, -1).T)
     out_first = far_first(out_rows, "seq")
     mixed_parts = gather_blocks(mixed, "head", micros=TUNE["mx"])
-    out_near, _ = far_last(out_rows, out_first, "seq", [mixed_parts[1], mixed_parts[4]])
+    out_near, _ = far_last(out_rows, out_first, "seq", [mixed_parts[1], mixed_parts[3]])
     out_other = swap(tie(out_near, *mixed_parts[2:4]), "seq", 0)
 
     acts, own_hidden, middle, cot_grp, *d_two = feed_forward(
@@ -1100,38 +1142,37 @@
         tok_rows,
     )
 
-    acts_moved = swap(acts, "seq", 0)
-    moved = sum_first(d_two[2:4], "head")
-    out_term = down_product(middle, joined_all, tok_rows)
-    down, up = sum_payload(d_two[1], d_two[4], moved, others=[out_term[0]])
-    *parts, down_term = pair_grads(seq_own, orders, (acts, acts_moved), cot_grp, middle, [down, up])
-    parts = [part.reshape(-1, width // seq_dev, padded) for part in parts]
-    gate_low, gate_high, *gate_sent = parts[:4]
-    up_low, up_high, *up_sent = parts[4:]
+    cots, middles = [[part, swap(part, "seq", 0)] for part in (cot_grp, middle)]
+    moved = from_next(d_two[2], "head")
+    up = to_next(d_two[1], "head")
+    wide_term = wide_grads(acts, width)
+    wide_late = tie(wide_term, moved)
+    down = sum_payload(d_two[3], moved, others=[cots[1], middles[1]])
+    wide_sum = plain(lax.psum_scatter(plain(wide_late), "seq", scatter_dimension=0, tiled=True))
+    out_term = down_product(middle, joined_all, tok_rows, [down])
+    one_low, one_high, one_sent, two_low, two_high, two_sent = [
+        part.reshape(-1, width // seq_dev, part.shape[1])
+        for part in pair_grads(seq_own, orders, cots, middles, [down])
+    ]
     d_hidden, d_branch, *d_mixed_own, grad_gain_two = norm_back(
         seq_own,
         d_two[0],
         from_next(down, "head"),
-        to_next(up, "head"),
+        up,
         own_hidden,
         gain_mlp,
         cotangent,
         out_near,
         out_other,
         heads_dev,
-        [gate_low],
+        [one_low, out_term[0]],
     )
     d_mixed = [d_mixed_own[0]]
     for apart in range(1, heads_dev):
         d_mixed.append(from_next(d_mixed_own[heads_dev - apart], "head", apart))
 
-    gate_moved = [swap(gate_sent[1], "seq", bits_down[0])]
-    up_moved = [swap(up_sent[1], "seq", bits_up[0])]
-    gate_moved[0], up_moved[0] = tie_all([gate_moved[0], up_moved[0]], micros=TUNE["g0"])
-    down_late = tie(down_term, *d_mixed[1:])
-    down_sum = plain(lax.psum_scatter(plain(down_late), "seq", scatter_dimension=0, tiled=True))
-    gate_moved.append(swap(tie(gate_sent[0], *d_mixed[1:], gate_moved[0], up_moved[0]), "seq", bits_down[0]))
-    up_moved.append(swap(tie(up_sent[0], *d_mixed[1:], gate_moved[0], up_moved[0]), "seq", bits_up[0]))
+    one_moved = swap(one_sent, "seq", bits_down[0])
+    two_moved = swap(two_sent, "seq", bits_up[0])
     branch_late = tie(d_branch, *d_mixed[1:])
     above, below = from_next(branch_late, "head"), to_next(branch_late, "head")
     d_queries, d_kv_own, d_kv_sent = attend_back(
@@ -1143,19 +1184,19 @@
         key_code,
         query_code,
         log_total,
-        [gate_moved[0], up_moved[0]],
+        [],
     )
     d_kv_moved = swap(tie(d_kv_sent, above, below), "seq", 0)
     half = tok_rows // 2
     above, below = tie_all([above, below], d_queries)
-    above_far = from_next(jnp.concatenate([above[:half], out_term[2]]), "head")
-    below_far = to_next(jnp.concatenate([below[half:], out_term[3]]), "head")
-    down, up = sum_payload(out_term[1], out_term[4], [above_far[half:], below_far[half:]])
-    out_moved = [from_next(down, "head"), to_next(up, "head")]
-    branch_parts = [d_branch, above, above_far, below_far, below]
-    output = total([own_hidden, out_term[0], *out_moved]).astype(BF)
-    gate_moved[1], up_moved[1] = tie_all([gate_moved[1], up_moved[1]], micros=TUNE["g1"])
-    d_kv_moved = tie(d_kv_moved, gate_moved[1], up_moved[1])
+    out_up = to_next(tie(out_term[1], *d_mixed[1:]), "head")
+    far_both = from_next(jnp.concatenate([above, out_term[2]]), "head")
+    far_both = tie_all([far_both], micros=TUNE["far"])[0]
+    branch_parts = [d_branch, above, far_both, below]
+    down = sum_payload(out_term[3], far_both[tok_rows:], others=[out_up])
+    out_moved = [from_next(down, "head"), out_up]
+    one_moved, two_moved = tie_all([one_moved, two_moved], micros=TUNE["g1"])
+    d_kv_moved = tie(d_kv_moved, one_moved, two_moved)
     d_kv = total([d_kv_own, d_kv_moved])
     d_keys, keys_last = sum_xor([d_kv[i, 0] for i in range(far)], "seq", bits_down)
     d_values, values_last = sum_xor([d_kv[i, 1] for i in range(far)], "seq", bits_up)
@@ -1168,11 +1209,13 @@
 
 
     def second(low, high, moved, bit):
-        high_moved, low_moved = tie_all(moved, d_other_sent)
-        return [low, low_moved, swap(total([high, high_moved]).astype(BF), "seq", bit)]
-
-    gate_terms = second(gate_low, gate_high, gate_moved, bits_down[1])
-    up_terms = second(up_low, up_high, up_moved, bits_up[1])
+        half = high.shape[0]
+        moved = tie(moved, d_other_sent)
+        return [low, moved[:half], swap(total([high, moved[half:]]).astype(BF), "seq", bit)]
+
+    one_terms = second(one_low, one_high, one_moved, bits_down[1])
+    two_terms = second(two_low, two_high, two_moved, bits_up[1])
+    one_terms[-1], two_terms[-1] = tie_all([one_terms[-1], two_terms[-1]], micros=TUNE["s2"])
     *d_one, cols_kept, outs_kept, wide_sent = project_back(
         seq_own,
         head_own,
@@ -1187,18 +1230,21 @@
         mixed,
         branch_parts,
         grad_gain_two,
-        [down_sum, *out_moved],
-    )
-    moved = sum_first(d_one[2:4], "head")
+        out_moved,
+    )
+    ahead, across = tie_all(d_one[1:3], one_terms[-1], two_terms[-1])
+    moved = from_next(across, "head")
+    up = to_next(ahead, "head")
     wide_moved = tie_all([swap(wide_sent, "seq", 0)], micros=TUNE["wm"])[0]
-    down, up = sum_payload(d_one[1], d_one[4], moved, others=[wide_moved])
-    gate_terms[-1], up_terms[-1] = tie(gate_terms[-1], down), tie(up_terms[-1], down)
+    down = sum_payload(d_one[3], moved, others=[wide_moved, up])
+    one_terms[-1], two_terms[-1] = tie(one_terms[-1], down), tie(two_terms[-1], down)
+    output = total([own_hidden, out_term[0], *out_moved]).astype(BF)
     cols_moved = wide_moved[:, :, : query_cols + HD]
     outs_moved = wide_moved[:, :own_rows, query_cols + HD :]
     cols_terms = sum_step([cols_kept, cols_moved], "seq", bits_down[0])
     outs_terms = sum_step([outs_kept, outs_moved], "seq", bits_up[0])
     cols_terms[-1], outs_terms[-1] = tie_all([cols_terms[-1], outs_terms[-1]], micros=TUNE["ct"])
-    down, up = from_next(down, "head"), to_next(up, "head")
+    down = from_next(down, "head")
     d_normed_one = total([d_one[0], tie(down, cols_terms[-1], outs_terms[-1]), up])
     grad_cols = sum_halving(cols_terms, "seq", bits_down[1:]).astype(BF)
     grad_outs = sum_halving(outs_terms, "seq", bits_up[1:])
@@ -1221,7 +1267,7 @@
         target = (head_index - apart) % heads_dev
         block = lax.dynamic_index_in_dim(grad_blocks, target, 0, keepdims=False)
         if apart:
-            block = from_next(block, "head", apart)
+            block = from_next(tie(block, wide_sum), "head", apart)
         small_parts.append(block[own_wide : own_wide + 2])
         block = block[:own_wide].astype(F32)
         kv_place = QD + source % 2 * KD + source // copies * HD
@@ -1237,8 +1283,13 @@
     key_bias = (QD + KD) // (seq_dev * heads_dev)
     value_bias = KD // (seq_dev * heads_dev)
 
-    gate_sum = sum_halving(gate_terms, "seq", bits_down[2:])
-    up_sum = sum_halving(up_terms, "seq", bits_up[2:])
+    grad_down = jnp.concatenate(
+        [
+            sum_halving(one_terms, "seq", bits_down[2:]),
+            sum_halving(two_terms, "seq", bits_up[2:]),
+        ],
+        axis=1,
+    )[:, :units].T
 
     return (
         output,
@@ -1249,9 +1300,9 @@
         own_part(1, heads_dev * key_bias, value_bias),
         grad_out,
         own_part(0, heads_dev * gain_cols, gain_cols),
-        gate_sum[:, :units],
-        up_sum[:, :units],
-        down_sum[:, :units].T.astype(F32),
+        wide_sum[:, :units].astype(F32),
+        wide_sum[:, padded : padded + units].astype(F32),
+        grad_down,
     )
 
 

time: 412 us -> 402 us (0.976)
  waiting for transfers between devices: 136 us -> 123 us
  Pallas kernels: 111 us -> 119 us
  other arithmetic: 27.7 us -> 19.7 us
    pallas_call x5 -> x7, Pallas kernels: 16 us -> 31.7 us  [the longest x1 12.9 us: wide_grads(): pl.pallas_call(wide_grads_kernel, grid=(units // TILE,), in_specs=[pl.Blo...]
    ppermute x68 -> x61, waiting for transfers between devices: 136 us -> 123 us  [send(): lax.ppermute(plain(block), axis, [(j, target(j) % count) for j in range(c...]
    pallas_call x1, Pallas kernels: 18.8 us -> 11.4 us  [pair_grads(): pl.pallas_call(functools.partial(pair_grads_kernel, orders, len(others)),...]
    unnamed x188 -> x166, local copies, waits for them, and re-layouts: 17.8 us -> 23.2 us
    ppermute x68 -> x61, starting transfers between devices: 79.5 us -> 83.2 us  [send(): lax.ppermute(plain(block), axis, [(j, target(j) % count) for j in range(c...]
  transfers between devices with their start and end apart: 70 -> 63, of which waited for: 38 -> 37; matrix products, arithmetic and copies ran while one was open for 10% -> 7% of each run, Pallas kernels for 20% -> 22%
where the time goes in v4:
time: 402 us; the launch traced here: 396 us
  waiting for transfers between devices  123 us (31%)
  Pallas kernels  119 us (30%)
  starting transfers between devices  83.3 us (21%)
  local copies, waits for them, and re-layouts  35 us (9%)
  other arithmetic  19.7 us (5%)
  between operations  15.7 us (4%)
    ppermute x61, waiting for transfers between devices, send(): lax.ppermute(plain(block), axis, [(j, target(j) % count) for j in range(c...  123 us
    ppermute x61, starting transfers between devices, send(): lax.ppermute(plain(block), axis, [(j, target(j) % count) for j in range(c...  83.2 us
    pallas_call x1, Pallas kernels, feed_forward(): pl.pallas_call(feed_forward_kernel, in_specs=[smem(), vmem()] + [anywhere...  30.3 us
    unnamed x166, local copies, waits for them, and re-layouts  23.2 us
    pallas_call x1, Pallas kernels, attend_back(): pl.pallas_call(functools.partial(attend_back_kernel, HD ** (-0.5), first_...  17.7 us
    pallas_call x1, Pallas kernels, attend(): pl.pallas_call(functools.partial(attend_kernel, HD ** (-0.5) * math.log2(...  13.2 us
    pallas_call x1, Pallas kernels, wide_grads(): pl.pallas_call(wide_grads_kernel, grid=(units // TILE,), in_specs=[pl.Blo...  12.9 us
    pallas_call x1, Pallas kernels, pair_grads(): pl.pallas_call(functools.partial(pair_grads_kernel, orders, len(others)),...  11.4 us
  transfers between devices with their start and end apart: 63, of which 37 were waited for; matrix products, arithmetic and copies ran while one was open for 7% of the time, Pallas kernels for 22%

profile of v4, /device:TPU:0, one launch (start us, length us, event | category | flops | bytes accessed | tf_op | source)
XLA Modules:
  0.0 395.6 jit_solution(1276127307119950102)
XLA Ops:
  7.2 2.9 fusion.5
  11.9 5.0 %collective-permute-start = (bf16[64,640]{1,0:T(8,128)(2,1)S(1)}, bf16[64,640]{1,0:T(8,128)(2,1)S(1)}, u32[]{:S(2)}, u32[]{:S(2)}) collective-permute-start(bf16[64,640]{1,0:T(8,128)(2,1)S(1)} %get-tuple-element.198), channel_id=1, source_target_pairs={{0,3},{1,0},{2,1},{3,2},{4,7},{5,4},{6,5},{7,6},{8,11},{9,8},{10,9... | collective-permute-start | bytes 245768 | tf_op jit(solution)/shard_map/ppermute | solution.py:49
  18.0 1.8 collective-permute-done.refs_1_
  19.8 4.7 %collective-permute-done.1.refs_2_ = bf16[64,640]{1,0:T(8,128)(2,1)S(1)} collective-permute-done((bf16[64,640]{1,0:T(8,128)(2,1)S(1)}, bf16[64,640]{1,0:T(8,128)(2,1)S(1)}, u32[]{:S(2)}, u32[]{:S(2)}) %collective-permute-start.1) | collective-permute-done | bytes 81952 | tf_op jit(solution)/shard_map/ppermute | solution.py:49
  25.1 1.9 arrange.1
  28.5 1.5 collective-permute-start.4
  32.7 2.0 collective-permute-start.7
  35.5 7.1 %collective-permute-done.3.refs_0_ = bf16[224,640]{1,0:T(8,128)(2,1)S(1)} collective-permute-done((bf16[224,640]{1,0:T(8,128)(2,1)}, bf16[224,640]{1,0:T(8,128)(2,1)S(1)}, u32[]{:S(2)}, u32[]{:S(2)}) %collective-permute-start.3) | collective-permute-done | bytes 286752 | tf_op jit(solution)/shard_map/ppermute | solution.py:49
  44.7 1.6 collective-permute-start.5
  46.3 5.7 %collective-permute-done.8.refs_1_ = bf16[128,1536]{1,0:T(8,128)(2,1)S(1)} collective-permute-done((bf16[128,1536]{1,0:T(8,128)(2,1)S(1)}, bf16[128,1536]{1,0:T(8,128)(2,1)S(1)}, u32[]{:S(2)}, u32[]{:S(2)}) %collective-permute-start.8) | collective-permute-done | bytes 393248 | tf_op jit(solution)/shard_map/ppermute | solution.py:49
  55.7 6.4 %collective-permute-done.9.refs_0_ = bf16[128,1536]{1,0:T(8,128)(2,1)S(1)} collective-permute-done((bf16[128,1536]{1,0:T(8,128)(2,1)S(1)}, bf16[128,1536]{1,0:T(8,128)(2,1)S(1)}, u32[]{:S(2)}, u32[]{:S(2)}) %collective-permute-start.9) | collective-permute-done | bytes 393248 | tf_op jit(solution)/shard_map/ppermute | solution.py:49
  67.3 4.3 %collective-permute-start.11 = (bf16[192,1536]{1,0:T(8,128)(2,1)S(1)}, bf16[192,1536]{1,0:T(8,128)(2,1)S(1)}, u32[]{:S(2)}, u32[]{:S(2)}) collective-permute-start(bf16[192,1536]{1,0:T(8,128)(2,1)S(1)} %tie.38.refs_1_), channel_id=1, source_target_pairs={{0,3},{1,0},{2,1},{3,2},{4,7},{5,4},{6,5},{7,6},{8,11},{9,8},{10,9... | collective-permute-start | bytes 1769480 | tf_op jit(solution)/shard_map/ppermute | solution.py:49
  71.6 6.8 %project.1 = (bf16[2,768,128]{2,1,0:T(8,128)(2,1)}, bf16[2,2,256,128]{3,2,1,0:T(8,128)(2,1)}, bf16[512,1536]{1,0:T(8,128)(2,1)}, bf16[512,1536]{1,0:T(8,128)(2,1)}, bf16[1536,640]{1,0:T(8,128)(2,1)}) custom-call(s32[1]{0:T(128)} %bitcast.own_ref, s32[1]{0:T(128)} %bitcast.1.head_ref, bf16[128,1536]{1,0:T(8,128)(2,1)} %copy-done.7, ...), custom_call_target="tpu_custom_call" | custom-call | flops 8071000064 | tf_op jit(solution)/shard_map/project/pallas_call | solution.py:351
  80.6 4.8 %collective-permute-done.11.refs_0_ = bf16[192,1536]{1,0:T(8,128)(2,1)S(1)} collective-permute-done((bf16[192,1536]{1,0:T(8,128)(2,1)S(1)}, bf16[192,1536]{1,0:T(8,128)(2,1)S(1)}, u32[]{:S(2)}, u32[]{:S(2)}) %collective-permute-start.11) | collective-permute-done | bytes 589856 | tf_op jit(solution)/shard_map/ppermute | solution.py:49
  85.4 11.6 %collective-permute-done.12.refs_1_ = bf16[192,1536]{1,0:T(8,128)(2,1)S(1)} collective-permute-done((bf16[192,1536]{1,0:T(8,128)(2,1)S(1)}, bf16[192,1536]{1,0:T(8,128)(2,1)S(1)}, u32[]{:S(2)}, u32[]{:S(2)}) %collective-permute-start.12) | collective-permute-done | bytes 589856 | tf_op jit(solution)/shard_map/ppermute | solution.py:49
  100.6 2.3 collective-permute-start.15
  103.0 2.5 collective-permute-done.17
  108.6 2.0 copy.79.kc_ref.refs_7_
  110.5 3.9 collective-permute-done.15.refs_0_
  116.1 13.2 %attend.1 = (bf16[512,384]{1,0:T(8,128)(2,1)}, f32[2,768,128]{2,1,0:T(8,128)}, f32[2,1,768]{2,1,0:T(1,128)}) custom-call(bf16[2,768,128]{2,1,0:T(8,128)(2,1)} %get-tuple-element.96.q_ref, bf16[4,2,2,256,128]{4,3,2,1,0:T(8,128)(2,1)} %pad_maximum_fusion.4.near_ref.refs_5_, bf16[4,2,2,256,128]{4,3,2,1,0:T(8,128)(2,1)} %collective-permute-done.18.other_ref.refs_6_, ...), custom_call_target="tpu_custom_call" | custom-call | flops 18447998976 | tf_op jit(solution)/shard_map/attend/pallas_call | solution.py:564
  129.3 3.5 collective-permute-start.19
  134.0 1.6 collective-permute-start.22
  137.0 5.6 %collective-permute-done.19.refs_0_ = bf16[512,384]{1,0:T(8,128)(2,1)S(1)} collective-permute-done((bf16[512,384]{1,0:T(8,128)(2,1)}, bf16[512,384]{1,0:T(8,128)(2,1)S(1)}, u32[]{:S(2)}, u32[]{:S(2)}) %collective-permute-start.19) | collective-permute-done | bytes 393248 | tf_op jit(solution)/shard_map/ppermute | solution.py:49
  142.6 5.0 %collective-permute-done.20.refs_1_ = bf16[512,384]{1,0:T(8,128)(2,1)S(1)} collective-permute-done((bf16[512,384]{1,0:T(8,128)(2,1)}, bf16[512,384]{1,0:T(8,128)(2,1)S(1)}, u32[]{:S(2)}, u32[]{:S(2)}) %collective-permute-start.20) | collective-permute-done | bytes 393248 | tf_op jit(solution)/shard_map/ppermute | solution.py:49
  147.6 1.6 collective-permute-done.22.refs_0_
  149.2 1.5 collective-permute-start.25
  151.4 3.5 collective-permute-start.21
  154.9 2.0 collective-permute-done.25
  162.8 3.8 collective-permute-done.26.refs_10_.refs_7_
  168.1 30.3 %feed_forward.1 = (bf16[512,6144]{1,0:T(8,128)(2,1)}, f32[128,1536]{1,0:T(8,128)}, bf16[512,2304]{1,0:T(8,128)(2,1)}, bf16[512,1536]{1,0:T(8,128)(2,1)}, f32[128...) custom-call(s32[1]{0:T(128)} %bitcast.own_ref, ...), custom_call_target="tpu_custom_call" | custom-call | flops 41507999744 | tf_op jit(solution)/shard_map/feed_forward/pallas_call | solution.py:770
  199.0 4.3 %collective-permute-start.27 = (bf16[128,1536]{1,0:T(8,128)(2,1)}, bf16[128,1536]{1,0:T(8,128)(2,1)S(1)}, u32[]{:S(2)}, u32[]{:S(2)}) collective-permute-start(bf16[128,1536]{1,0:T(8,128)(2,1)} %get-tuple-element.111), channel_id=1, source_target_pairs={{0,3},{1,0},{2,1},{3,2},{4,7},{5,4},{6,5},{7,6},{8,11},{9,8},{10,9... | collective-permute-start | bytes 1179656 | tf_op jit(solution)/shard_map/ppermute | solution.py:49
  203.4 12.9 %wide_grads.1.refs_0_ = bf16[1536,4608]{1,0:T(8,128)(2,1)} custom-call(bf16[512,6144]{1,0:T(8,128)(2,1)} %get-tuple-element.155.x_ref.acts_ref, bf16[512,6144]{1,0:T(8,128)(2,1)} %get-tuple-element.155.x_ref.acts_ref), custom_call_target="tpu_custom_call" | custom-call | flops 12682999808 | tf_op jit(solution)/shard_map/wide_grads/pallas_call | solution.py:854
  218.7 4.1 %collective-permute-start.30 = (bf16[128,1536]{1,0:T(8,128)(2,1)S(1)}, bf16[128,1536]{1,0:T(8,128)(2,1)S(1)}, u32[]{:S(2)}, u32[]{:S(2)}) collective-permute-start(bf16[128,1536]{1,0:T(8,128)(2,1)S(1)} %payload.3.refs_0_.refs_4_), channel_id=1, source_target_pairs={{0,3},{1,0},{2,1},{3,2},{4,7},{5,4},{6,5},{7,6},{8,11},{9,8},{10,9... | collective-permute-start | bytes 1179656 | tf_op jit(solution)/shard_map/ppermute | solution.py:49
  222.9 9.8 %down_product.1 = (f32[128,1536]{1,0:T(8,128)}, bf16[128,1536]{1,0:T(8,128)(2,1)}, bf16[128,1536]{1,0:T(8,128)(2,1)}, bf16[128,1536]{1,0:T(8,128)(2,1)}) custom-call(bf16[1536,6912]{1,0:T(8,128)(2,1)} %all-gather.2.cloned.1.call-done.refs_11_.down_w, bf16[512,2304]{1,0:T(8,128)(2,1)} %get-tuple-element.109.middle_ref.refs_2_, bf16[128,1536]{1,0:T(8,128)(2,1)} %copy-done.36), custom_call_target="tpu_custom_call" | custom-call | flops 9223999488 | tf_op jit(solution)/shard_map/down_product/pallas_call | solution.py:826
  232.6 11.4 %pair_grads.1 = (bf16[192,1152]{1,0:T(8,128)(2,1)}, bf16[192,1152]{1,0:T(8,128)(2,1)}, bf16[384,1152]{1,0:T(8,128)(2,1)}, bf16[192,1152]{1,0:T(8,128)(2,1)}, bf1...) custom-call(s32[1]{0:T(128)} %bitcast.own_ref, bf16[512,1536]{1,0:T(8,128)(2,1)} %get-tuple-element.112.refs_0_, ...), custom_call_target="tpu_custom_call" | custom-call | flops 8071000064 | tf_op jit(solution)/shard_map/pair_grads/pallas_call | solution.py:897
  244.8 6.0 %norm_back.1 = (f32[128,1536]{1,0:T(8,128)}, bf16[128,1536]{1,0:T(8,128)(2,1)}, bf16[128,384]{1,0:T(8,128)(2,1)}, bf16[128,384]{1,0:T(8,128)(2,1)}, bf16[128,384...) custom-call(s32[1]{0:T(128)} %bitcast.own_ref, f32[128,1536]{1,0:T(8,128)} %get-tuple-element.115.refs_0_, ...), custom_call_target="tpu_custom_call" | custom-call | flops 6341499904 | tf_op jit(solution)/shard_map/norm_back/pallas_call | solution.py:935
  251.0 1.9 collective-permute-start.34
  257.2 2.5 collective-permute-done.33.refs_2_
  259.8 1.6 collective-permute-start.35
  263.1 17.7 %attend_back.1 = (f32[2,768,128]{2,1,0:T(8,128)}, bf16[4,2,2,256,128]{4,3,2,1,0:T(8,128)(2,1)}, bf16[4,2,2,256,128]{4,3,2,1,0:T(8,128)(2,1)}) custom-call(bf16[2,768,128]{2,1,0:T(8,128)(2,1)} %get-tuple-element.96.q_ref, bf16[128,384]{1,0:T(8,128)(2,1)} %get-tuple-element.122.refs_0_, bf16[128,384]{1,0:T(8,128)(2,1)} %copy-done.19, ...), custom_call_target="tpu_custom_call" | custom-call | flops 20753999872 | tf_op jit(solution)/shard_map/attend_back/pallas_call | solution.py:650
  284.8 1.9 collective-permute-start.37
  286.8 7.0 %collective-permute-done.41.refs_0_ = bf16[2,192,1152]{2,1,0:T(8,128)(2,1)S(1)} collective-permute-done((bf16[2,192,1152]{2,1,0:T(8,128)(2,1)}, bf16[2,192,1152]{2,1,0:T(8,128)(2,1)S(1)}, u32[]{:S(2)}, u32[]{:S(2)}) %collective-permute-start.41) | collective-permute-done | bytes 884768 | tf_op jit(solution)/shard_map/ppermute | solution.py:49
  297.5 1.8 collective-permute-start.43
  299.4 7.0 %collective-permute-done.37.refs_0_ = bf16[256,1536]{1,0:T(8,128)(2,1)S(1)} collective-permute-done((bf16[256,1536]{1,0:T(8,128)(2,1)S(1)}, bf16[256,1536]{1,0:T(8,128)(2,1)S(1)}, u32[]{:S(2)}, u32[]{:S(2)}) %collective-permute-start.37) | collective-permute-done | bytes 786464 | tf_op jit(solution)/shard_map/ppermute | solution.py:49
  306.4 3.0 collective-permute-done.45
  309.4 1.9 collective-permute-done.43
  311.6 1.6 collective-permute-start.46
  313.4 2.6 collective-permute-start.39
  316.7 2.2 collective-permute-start.47
  320.2 2.0 collective-permute-start.49
  322.3 1.9 collective-permute-done.47
  325.8 8.9 %project_back.1 = (f32[128,1536]{1,0:T(8,128)}, bf16[128,1536]{1,0:T(8,128)(2,1)}, bf16[128,1536]{1,0:T(8,128)(2,1)}, bf16[128,1536]{1,0:T(8,128)(2,1)}, bf16[4,...) custom-call(s32[1]{0:T(128)} %bitcast.own_ref, s32[1]{0:T(128)} %bitcast.1.head_ref, ...), custom_call_target="tpu_custom_call" | custom-call | flops 10376999936 | tf_op jit(solution)/shard_map/project_back/pallas_call | solution.py:459
  334.8 1.5 collective-permute-done.48.refs_0_
  336.4 2.5 collective-permute-done.49.refs_1_
  339.6 3.2 collective-permute-start.50
  342.8 1.9 add_convert_fusion.1
  344.7 7.9 %collective-permute-done.52.refs_1_ = bf16[128,1536]{1,0:T(8,128)(2,1)S(1)} collective-permute-done((bf16[128,1536]{1,0:T(8,128)(2,1)S(1)}, bf16[128,1536]{1,0:T(8,128)(2,1)S(1)}, u32[]{:S(2)}, u32[]{:S(2)}) %collective-permute-start.52) | collective-permute-done | bytes 393248 | tf_op jit(solution)/shard_map/ppermute | solution.py:49
  352.5 3.8 collective-permute-done.50.moved_ref
  356.5 2.1 collective-permute-start.53
  362.6 4.7 %collective-permute-done.55.refs_1_ = bf16[2,192,384]{2,1,0:T(8,128)(2,1)S(1)} collective-permute-done((bf16[2,192,384]{2,1,0:T(8,128)(2,1)S(1)}, bf16[2,192,384]{2,1,0:T(8,128)(2,1)S(1)}, u32[]{:S(2)}, u32[]{:S(2)}) %collective-permute-start.55) | collective-permute-done | bytes 294944 | tf_op jit(solution)/shard_map/ppermute | solution.py:49
  367.3 1.7 collective-permute-done.54.refs_0_
  372.8 3.1 collective-permute-done.60
  381.1 2.2 collective-permute-start.57
  383.4 2.0 slice_convert_fusion
  (390 shorter events, 78.6 us)
Async XLA Ops:
  7.2 159.5 %all-gather.2.cloned.1.call-start = ((), (), s32[]{:S(2)}) async-start(), calls=%async_computation.1 | async-start | bytes 23887872 | tf_op jit(solution)/shard_map/all_gather | solution.py:996
  10.2 366.7 %reduce-scatter.2.cloned.1.call-start = ((), (), s32[]{:S(2)}) async-start(), calls=%async_computation.2 | async-start | bytes 15925248 | tf_op jit(solution)/shard_map/reduce_scatter | solution.py:1151
  11.9 7.9 %collective-permute-start = (bf16[64,640]{1,0:T(8,128)(2,1)S(1)}, bf16[64,640]{1,0:T(8,128)(2,1)S(1)}, u32[]{:S(2)}, u32[]{:S(2)}) collective-permute-start(bf16[64,640]{1,0:T(8,128)(2,1)S(1)} %get-tuple-element.198), channel_id=1, source_target_pairs={{0,3},{1,0},{2,1},{3,2},{4,7},{5,4},{6,5},{7,6},{8,11},{9,8},{10,9... | collective-permute-start | bytes 245768 | tf_op jit(solution)/shard_map/ppermute | solution.py:49
  17.0 7.5 %collective-permute-start.1 = (bf16[64,640]{1,0:T(8,128)(2,1)S(1)}, bf16[64,640]{1,0:T(8,128)(2,1)S(1)}, u32[]{:S(2)}, u32[]{:S(2)}) collective-permute-start(bf16[64,640]{1,0:T(8,128)(2,1)S(1)} %get-tuple-element.199), channel_id=1, source_target_pairs={{0,2},{1,3},{2,0},{3,1},{4,6},{5,7},{6,4},{7,5},{8,10},{9,11},{10,... | collective-permute-start | bytes 245768 | tf_op jit(solution)/shard_map/ppermute | solution.py:49
  17.0 7.5 %collective-permute-start.2 = (bf16[64,640]{1,0:T(8,128)(2,1)S(1)}, bf16[64,640]{1,0:T(8,128)(2,1)S(1)}, u32[]{:S(2)}, u32[]{:S(2)}) collective-permute-start(bf16[64,640]{1,0:T(8,128)(2,1)S(1)} %get-tuple-element.196), channel_id=1, source_target_pairs={{0,1},{1,2},{2,3},{3,0},{4,5},{5,6},{6,7},{7,4},{8,9},{9,10},{10,1... | collective-permute-start | bytes 245768 | tf_op jit(solution)/shard_map/ppermute | solution.py:49
  27.0 15.6 %collective-permute-start.3 = (bf16[224,640]{1,0:T(8,128)(2,1)}, bf16[224,640]{1,0:T(8,128)(2,1)S(1)}, u32[]{:S(2)}, u32[]{:S(2)}) collective-permute-start(bf16[224,640]{1,0:T(8,128)(2,1)} %arrange.1), channel_id=1, source_target_pairs={{0,8},{4,12},{8,0},{12,4},{16,24},{20,28},{24,16},{28,20},{1,9},{5... | collective-permute-start | bytes 860168 | tf_op jit(solution)/shard_map/ppermute | solution.py:49
  28.5 15.5 %collective-permute-start.4 = (bf16[224,640]{1,0:T(8,128)(2,1)}, bf16[224,640]{1,0:T(8,128)(2,1)S(1)}, u32[]{:S(2)}, u32[]{:S(2)}) collective-permute-start(bf16[224,640]{1,0:T(8,128)(2,1)} %arrange.1), channel_id=1, source_target_pairs={{0,16},{4,20},{8,24},{12,28},{16,0},{20,4},{24,8},{28,12},{1,17},{... | collective-permute-start | bytes 860168 | tf_op jit(solution)/shard_map/ppermute | solution.py:49
  32.7 13.6 %collective-permute-start.7 = (bf16[128,1536]{1,0:T(8,128)(2,1)S(1)}, bf16[128,1536]{1,0:T(8,128)(2,1)S(1)}, u32[]{:S(2)}, u32[]{:S(2)}) collective-permute-start(bf16[128,1536]{1,0:T(8,128)(2,1)S(1)} %tie.34.refs_0_), channel_id=1, source_target_pairs={{0,3},{1,0},{2,1},{3,2},{4,7},{5,4},{6,5},{7,6},{8,11},{9,8},{10,9... | collective-permute-start | bytes 1179656 | tf_op jit(solution)/shard_map/ppermute | solution.py:49
  34.8 17.3 %collective-permute-start.8 = (bf16[128,1536]{1,0:T(8,128)(2,1)S(1)}, bf16[128,1536]{1,0:T(8,128)(2,1)S(1)}, u32[]{:S(2)}, u32[]{:S(2)}) collective-permute-start(bf16[128,1536]{1,0:T(8,128)(2,1)S(1)} %tie.34.refs_0_), channel_id=1, source_target_pairs={{0,1},{1,2},{2,3},{3,0},{4,5},{5,6},{6,7},{7,4},{8,9},{9,10},{10,1... | collective-permute-start | bytes 1179656 | tf_op jit(solution)/shard_map/ppermute | solution.py:49
  44.1 11.3 %collective-permute-start.6 = (bf16[112,640]{1,0:T(8,128)(2,1)S(1)}, bf16[112,640]{1,0:T(8,128)(2,1)S(1)}, u32[]{:S(2)}, u32[]{:S(2)}) collective-permute-start(bf16[112,640]{1,0:T(8,128)(2,1)S(1)} %slice.264), channel_id=1, source_target_pairs={{0,8},{4,12},{8,0},{12,4},{16,24},{20,28},{24,16},{28,20},{1,9},{5... | collective-permute-start | bytes 430088 | tf_op jit(solution)/shard_map/ppermute | solution.py:49
  44.7 10.6 %collective-permute-start.5 = (bf16[112,640]{1,0:T(8,128)(2,1)S(1)}, bf16[112,640]{1,0:T(8,128)(2,1)S(1)}, u32[]{:S(2)}, u32[]{:S(2)}) collective-permute-start(bf16[112,640]{1,0:T(8,128)(2,1)S(1)} %slice.263), channel_id=1, source_target_pairs={{0,16},{4,20},{8,24},{12,28},{16,0},{20,4},{24,8},{28,12},{1,17},{... | collective-permute-start | bytes 430088 | tf_op jit(solution)/shard_map/ppermute | solution.py:49
  52.0 10.1 %collective-permute-start.9 = (bf16[128,1536]{1,0:T(8,128)(2,1)S(1)}, bf16[128,1536]{1,0:T(8,128)(2,1)S(1)}, u32[]{:S(2)}, u32[]{:S(2)}) collective-permute-start(bf16[128,1536]{1,0:T(8,128)(2,1)S(1)} %get-tuple-element.86.refs_1_), channel_id=1, source_target_pairs={{0,3},{1,0},{2,1},{3,2},{4,7},{5,4},{6,5},{7,6},{8,11},{9,8},{10,9... | collective-permute-start | bytes 1179656 | tf_op jit(solution)/shard_map/ppermute | solution.py:49
  62.2 9.5 %collective-permute-start.10 = (bf16[4,224,640]{2,1,0:T(8,128)(2,1)S(1)}, bf16[4,224,640]{2,1,0:T(8,128)(2,1)}, u32[]{:S(2)}, u32[]{:S(2)}) collective-permute-start(bf16[4,224,640]{2,1,0:T(8,128)(2,1)S(1)} %tie.37), channel_id=1, source_target_pairs={{0,4},{4,0},{8,12},{12,8},{16,20},{20,16},{24,28},{28,24},{1,5},{5... | collective-permute-start | bytes 3440648 | tf_op jit(solution)/shard_map/ppermute | solution.py:49
  67.3 18.1 %collective-permute-start.11 = (bf16[192,1536]{1,0:T(8,128)(2,1)S(1)}, bf16[192,1536]{1,0:T(8,128)(2,1)S(1)}, u32[]{:S(2)}, u32[]{:S(2)}) collective-permute-start(bf16[192,1536]{1,0:T(8,128)(2,1)S(1)} %tie.38.refs_1_), channel_id=1, source_target_pairs={{0,3},{1,0},{2,1},{3,2},{4,7},{5,4},{6,5},{7,6},{8,11},{9,8},{10,9... | collective-permute-start | bytes 1769480 | tf_op jit(solution)/shard_map/ppermute | solution.py:49
  71.6 25.4 %collective-permute-start.12 = (bf16[192,1536]{1,0:T(8,128)(2,1)S(1)}, bf16[192,1536]{1,0:T(8,128)(2,1)S(1)}, u32[]{:S(2)}, u32[]{:S(2)}) collective-permute-start(bf16[192,1536]{1,0:T(8,128)(2,1)S(1)} %tie.38.refs_1_), channel_id=1, source_target_pairs={{0,1},{1,2},{2,3},{3,0},{4,5},{5,6},{6,7},{7,4},{8,9},{9,10},{10,1... | collective-permute-start | bytes 1769480 | tf_op jit(solution)/shard_map/ppermute | solution.py:49
  78.5 18.6 %collective-permute-start.13 = (bf16[2,2,256,128]{3,2,1,0:T(8,128)(2,1)}, bf16[2,2,256,128]{3,2,1,0:T(8,128)(2,1)S(1)}, u32[]{:S(2)}, u32[]{:S(2)}) collective-permute-start(bf16[2,2,256,128]{3,2,1,0:T(8,128)(2,1)} %get-tuple-element.91), channel_id=1, source_target_pairs={{0,8},{4,12},{8,0},{12,4},{16,24},{20,28},{24,16},{28,20},{1,9},{5... | collective-permute-start | bytes 786440 | tf_op jit(solution)/shard_map/ppermute | solution.py:49
  79.5 17.5 %collective-permute-start.14 = (bf16[2,2,256,128]{3,2,1,0:T(8,128)(2,1)}, bf16[2,2,256,128]{3,2,1,0:T(8,128)(2,1)S(1)}, u32[]{:S(2)}, u32[]{:S(2)}) collective-permute-start(bf16[2,2,256,128]{3,2,1,0:T(8,128)(2,1)} %get-tuple-element.91), channel_id=1, source_target_pairs={{0,16},{4,20},{8,24},{12,28},{16,0},{20,4},{24,8},{28,12},{1,17},{... | collective-permute-start | bytes 786440 | tf_op jit(solution)/shard_map/ppermute | solution.py:49
  97.0 35.7 %copy-start.4 = (bf16[192,1536]{1,0:T(8,128)(2,1)}, bf16[192,1536]{1,0:T(8,128)(2,1)S(1)}, u32[]{:S(2)}) copy-start(bf16[192,1536]{1,0:T(8,128)(2,1)S(1)} %get-tuple-element.92.refs_2_) | copy-start | bytes 1769476
  97.1 8.5 %collective-permute-start.17 = (bf16[1,2,256,128]{3,2,1,0:T(8,128)(2,1)S(1)}, bf16[1,2,256,128]{3,2,1,0:T(8,128)(2,1)}, u32[]{:S(2)}, u32[]{:S(2)}) collective-permute-start(bf16[1,2,256,128]{3,2,1,0:T(8,128)(2,1)S(1)} %slice.277), channel_id=1, source_target_pairs={{0,8},{4,12},{8,0},{12,4},{16,24},{20,28},{24,16},{28,20},{1,9},{5... | collective-permute-start | bytes 393224 | tf_op jit(solution)/shard_map/ppermute | solution.py:49
  97.7 8.4 %collective-permute-start.16 = (bf16[1,2,256,128]{3,2,1,0:T(8,128)(2,1)S(1)}, bf16[1,2,256,128]{3,2,1,0:T(8,128)(2,1)}, u32[]{:S(2)}, u32[]{:S(2)}) collective-permute-start(bf16[1,2,256,128]{3,2,1,0:T(8,128)(2,1)S(1)} %slice.276), channel_id=1, source_target_pairs={{0,16},{4,20},{8,24},{12,28},{16,0},{20,4},{24,8},{28,12},{1,17},{... | collective-permute-start | bytes 393224 | tf_op jit(solution)/shard_map/ppermute | solution.py:49
  100.6 13.8 %collective-permute-start.15 = (bf16[192,1536]{1,0:T(8,128)(2,1)S(1)}, bf16[192,1536]{1,0:T(8,128)(2,1)S(1)}, u32[]{:S(2)}, u32[]{:S(2)}) collective-permute-start(bf16[192,1536]{1,0:T(8,128)(2,1)S(1)} %get-tuple-element.92.refs_2_), channel_id=1, source_target_pairs={{0,3},{1,0},{2,1},{3,2},{4,7},{5,4},{6,5},{7,6},{8,11},{9,8},{10,9... | collective-permute-start | bytes 1769480 | tf_op jit(solution)/shard_map/ppermute | solution.py:49
  108.2 7.8 %collective-permute-start.18 = (bf16[4,2,2,256,128]{4,3,2,1,0:T(8,128)(2,1)}, bf16[4,2,2,256,128]{4,3,2,1,0:T(8,128)(2,1)}, u32[]{:S(2)}, u32[]{:S(2)}) collective-permute-start(bf16[4,2,2,256,128]{4,3,2,1,0:T(8,128)(2,1)} %pad_maximum_fusion.4.near_ref.refs_5_), channel_id=1, source_target_pairs={{0,4},{4,0},{8,12},{12,8},{16,20},{20,16},{24,28},{28,24},{1,5},{5... | collective-permute-start | bytes 3145736 | tf_op jit(solution)/shard_map/ppermute | solution.py:49
  129.3 13.3 %collective-permute-start.19 = (bf16[512,384]{1,0:T(8,128)(2,1)}, bf16[512,384]{1,0:T(8,128)(2,1)S(1)}, u32[]{:S(2)}, u32[]{:S(2)}) collective-permute-start(bf16[512,384]{1,0:T(8,128)(2,1)} %get-tuple-element.99.refs_4_.refs_5_.refs_7_), channel_id=1, source_target_pairs={{0,3},{1,0},{2,1},{3,2},{4,7},{5,4},{6,5},{7,6},{8,11},{9,8},{10,9... | collective-permute-start | bytes 1179656 | tf_op jit(solution)/shard_map/ppermute | solution.py:49
  132.7 14.8 %collective-permute-start.20 = (bf16[512,384]{1,0:T(8,128)(2,1)}, bf16[512,384]{1,0:T(8,128)(2,1)S(1)}, u32[]{:S(2)}, u32[]{:S(2)}) collective-permute-start(bf16[512,384]{1,0:T(8,128)(2,1)} %get-tuple-element.99.refs_4_.refs_5_.refs_7_), channel_id=1, source_target_pairs={{0,1},{1,2},{2,3},{3,0},{4,5},{5,6},{6,7},{7,4},{8,9},{9,10},{10,1... | collective-permute-start | bytes 1179656 | tf_op jit(solution)/shard_map/ppermute | solution.py:49
  134.0 15.2 %collective-permute-start.22 = (bf16[192,1536]{1,0:T(8,128)(2,1)S(1)}, bf16[192,1536]{1,0:T(8,128)(2,1)S(1)}, u32[]{:S(2)}, u32[]{:S(2)}) collective-permute-start(bf16[192,1536]{1,0:T(8,128)(2,1)S(1)} %bitcast.172), channel_id=1, source_target_pairs={{0,8},{4,12},{8,0},{12,4},{16,24},{20,28},{24,16},{28,20},{1,9},{5... | collective-permute-start | bytes 1769480 | tf_op jit(solution)/shard_map/ppermute | solution.py:49
  135.6 13.7 %collective-permute-start.23 = (bf16[192,1536]{1,0:T(8,128)(2,1)S(1)}, bf16[192,1536]{1,0:T(8,128)(2,1)S(1)}, u32[]{:S(2)}, u32[]{:S(2)}) collective-permute-start(bf16[192,1536]{1,0:T(8,128)(2,1)S(1)} %bitcast.173), channel_id=1, source_target_pairs={{0,16},{4,20},{8,24},{12,28},{16,0},{20,4},{24,8},{28,12},{1,17},{... | collective-permute-start | bytes 1769480 | tf_op jit(solution)/shard_map/ppermute | solution.py:49
  149.2 7.7 %collective-permute-start.25 = (bf16[96,1536]{1,0:T(8,128)(2,1)S(1)}, bf16[96,1536]{1,0:T(8,128)(2,1)S(1)}, u32[]{:S(2)}, u32[]{:S(2)}) collective-permute-start(bf16[96,1536]{1,0:T(8,128)(2,1)S(1)} %slice.284), channel_id=1, source_target_pairs={{0,8},{4,12},{8,0},{12,4},{16,24},{20,28},{24,16},{28,20},{1,9},{5... | collective-permute-start | bytes 884744 | tf_op jit(solution)/shard_map/ppermute | solution.py:49
  150.8 7.1 %collective-permute-start.24 = (bf16[96,1536]{1,0:T(8,128)(2,1)S(1)}, bf16[96,1536]{1,0:T(8,128)(2,1)S(1)}, u32[]{:S(2)}, u32[]{:S(2)}) collective-permute-start(bf16[96,1536]{1,0:T(8,128)(2,1)S(1)} %slice.283), channel_id=1, source_target_pairs={{0,16},{4,20},{8,24},{12,28},{16,0},{20,4},{24,8},{28,12},{1,17},{... | collective-permute-start | bytes 884744 | tf_op jit(solution)/shard_map/ppermute | solution.py:49
  151.4 9.7 %collective-permute-start.21 = (bf16[512,384]{1,0:T(8,128)(2,1)S(1)}, bf16[512,384]{1,0:T(8,128)(2,1)S(1)}, u32[]{:S(2)}, u32[]{:S(2)}) collective-permute-start(bf16[512,384]{1,0:T(8,128)(2,1)S(1)} %get-tuple-element.100.refs_2_.refs_6_), channel_id=1, source_target_pairs={{0,3},{1,0},{2,1},{3,2},{4,7},{5,4},{6,5},{7,6},{8,11},{9,8},{10,9... | collective-permute-start | bytes 1179656 | tf_op jit(solution)/shard_map/ppermute | solution.py:49
  161.9 4.7 %collective-permute-start.26 = (bf16[4,192,1536]{2,1,0:T(8,128)(2,1)}, bf16[4,192,1536]{2,1,0:T(8,128)(2,1)S(1)}, u32[]{:S(2)}, u32[]{:S(2)}) collective-permute-start(bf16[4,192,1536]{2,1,0:T(8,128)(2,1)} %tie.45), channel_id=1, source_target_pairs={{0,4},{4,0},{8,12},{12,8},{16,20},{20,16},{24,28},{28,24},{1,5},{5... | collective-permute-start | bytes 7077896 | tf_op jit(solution)/shard_map/ppermute | solution.py:49
  198.3 18.8 %collective-permute-start.29 = (bf16[512,2304]{1,0:T(8,128)(2,1)}, bf16[512,2304]{1,0:T(8,128)(2,1)S(1)}, u32[]{:S(2)}, u32[]{:S(2)}) collective-permute-start(bf16[512,2304]{1,0:T(8,128)(2,1)} %get-tuple-element.109.middle_ref.refs_2_), channel_id=1, source_target_pairs={{0,4},{4,0},{8,12},{12,8},{16,20},{20,16},{24,28},{28,24},{1,5},{5... | collective-permute-start | bytes 7077896 | tf_op jit(solution)/shard_map/ppermute | solution.py:49
  198.7 18.4 %collective-permute-start.28 = (bf16[512,1536]{1,0:T(8,128)(2,1)}, bf16[512,1536]{1,0:T(8,128)(2,1)}, u32[]{:S(2)}, u32[]{:S(2)}) collective-permute-start(bf16[512,1536]{1,0:T(8,128)(2,1)} %get-tuple-element.112.refs_0_), channel_id=1, source_target_pairs={{0,4},{4,0},{8,12},{12,8},{16,20},{20,16},{24,28},{28,24},{1,5},{5... | collective-permute-start | bytes 4718600 | tf_op jit(solution)/shard_map/ppermute | solution.py:49
  199.0 17.3 %collective-permute-start.27 = (bf16[128,1536]{1,0:T(8,128)(2,1)}, bf16[128,1536]{1,0:T(8,128)(2,1)S(1)}, u32[]{:S(2)}, u32[]{:S(2)}) collective-permute-start(bf16[128,1536]{1,0:T(8,128)(2,1)} %get-tuple-element.111), channel_id=1, source_target_pairs={{0,3},{1,0},{2,1},{3,2},{4,7},{5,4},{6,5},{7,6},{8,11},{9,8},{10,9... | collective-permute-start | bytes 1179656 | tf_op jit(solution)/shard_map/ppermute | solution.py:49
  203.4 40.7 %collective-permute-start.31 = (bf16[128,1536]{1,0:T(8,128)(2,1)}, bf16[128,1536]{1,0:T(8,128)(2,1)}, u32[]{:S(2)}, u32[]{:S(2)}) collective-permute-start(bf16[128,1536]{1,0:T(8,128)(2,1)} %get-tuple-element.116), channel_id=1, source_target_pairs={{0,1},{1,2},{2,3},{3,0},{4,5},{5,6},{6,7},{7,4},{8,9},{9,10},{10,1... | collective-permute-start | bytes 1179656 | tf_op jit(solution)/shard_map/ppermute | solution.py:49
  218.7 25.3 %collective-permute-start.30 = (bf16[128,1536]{1,0:T(8,128)(2,1)S(1)}, bf16[128,1536]{1,0:T(8,128)(2,1)S(1)}, u32[]{:S(2)}, u32[]{:S(2)}) collective-permute-start(bf16[128,1536]{1,0:T(8,128)(2,1)S(1)} %payload.3.refs_0_.refs_4_), channel_id=1, source_target_pairs={{0,3},{1,0},{2,1},{3,2},{4,7},{5,4},{6,5},{7,6},{8,11},{9,8},{10,9... | collective-permute-start | bytes 1179656 | tf_op jit(solution)/shard_map/ppermute | solution.py:49
  250.9 6.4 %collective-permute-start.32 = (bf16[128,384]{1,0:T(8,128)(2,1)}, bf16[128,384]{1,0:T(8,128)(2,1)S(1)}, u32[]{:S(2)}, u32[]{:S(2)}) collective-permute-start(bf16[128,384]{1,0:T(8,128)(2,1)} %get-tuple-element.119), channel_id=1, source_target_pairs={{0,3},{1,0},{2,1},{3,2},{4,7},{5,4},{6,5},{7,6},{8,11},{9,8},{10,9... | collective-permute-start | bytes 294920 | tf_op jit(solution)/shard_map/ppermute | solution.py:49
  250.9 8.8 %collective-permute-start.33 = (bf16[128,384]{1,0:T(8,128)(2,1)}, bf16[128,384]{1,0:T(8,128)(2,1)S(1)}, u32[]{:S(2)}, u32[]{:S(2)}) collective-permute-start(bf16[128,384]{1,0:T(8,128)(2,1)} %get-tuple-element.120), channel_id=1, source_target_pairs={{0,2},{1,3},{2,0},{3,1},{4,6},{5,7},{6,4},{7,5},{8,10},{9,11},{10,... | collective-permute-start | bytes 294920 | tf_op jit(solution)/shard_map/ppermute | solution.py:49
  251.0 8.8 %collective-permute-start.34 = (bf16[128,384]{1,0:T(8,128)(2,1)}, bf16[128,384]{1,0:T(8,128)(2,1)S(1)}, u32[]{:S(2)}, u32[]{:S(2)}) collective-permute-start(bf16[128,384]{1,0:T(8,128)(2,1)} %get-tuple-element.121), channel_id=1, source_target_pairs={{0,1},{1,2},{2,3},{3,0},{4,5},{5,6},{6,7},{7,4},{8,9},{9,10},{10,1... | collective-permute-start | bytes 294920 | tf_op jit(solution)/shard_map/ppermute | solution.py:49
  253.0 40.7 %collective-permute-start.41 = (bf16[2,192,1152]{2,1,0:T(8,128)(2,1)}, bf16[2,192,1152]{2,1,0:T(8,128)(2,1)S(1)}, u32[]{:S(2)}, u32[]{:S(2)}) collective-permute-start(bf16[2,192,1152]{2,1,0:T(8,128)(2,1)} %bitcast.21), channel_id=1, source_target_pairs={{0,16},{4,20},{8,24},{12,28},{16,0},{20,4},{24,8},{28,12},{1,17},{... | collective-permute-start | bytes 2654216 | tf_op jit(solution)/shard_map/ppermute | solution.py:49
  253.7 40.5 %collective-permute-start.42 = (bf16[2,192,1152]{2,1,0:T(8,128)(2,1)}, bf16[2,192,1152]{2,1,0:T(8,128)(2,1)S(1)}, u32[]{:S(2)}, u32[]{:S(2)}) collective-permute-start(bf16[2,192,1152]{2,1,0:T(8,128)(2,1)} %bitcast.183), channel_id=1, source_target_pairs={{0,8},{4,12},{8,0},{12,4},{16,24},{20,28},{24,16},{28,20},{1,9},{5... | collective-permute-start | bytes 2654216 | tf_op jit(solution)/shard_map/ppermute | solution.py:49
  259.8 21.1 %collective-permute-start.35 = (bf16[128,1536]{1,0:T(8,128)(2,1)S(1)}, bf16[128,1536]{1,0:T(8,128)(2,1)S(1)}, u32[]{:S(2)}, u32[]{:S(2)}) collective-permute-start(bf16[128,1536]{1,0:T(8,128)(2,1)S(1)} %tie.46), channel_id=1, source_target_pairs={{0,3},{1,0},{2,1},{3,2},{4,7},{5,4},{6,5},{7,6},{8,11},{9,8},{10,9... | collective-permute-start | bytes 1179656 | tf_op jit(solution)/shard_map/ppermute | solution.py:49
  261.4 20.6 %collective-permute-start.36 = (bf16[128,1536]{1,0:T(8,128)(2,1)S(1)}, bf16[128,1536]{1,0:T(8,128)(2,1)S(1)}, u32[]{:S(2)}, u32[]{:S(2)}) collective-permute-start(bf16[128,1536]{1,0:T(8,128)(2,1)S(1)} %tie.46), channel_id=1, source_target_pairs={{0,1},{1,2},{2,3},{3,0},{4,5},{5,6},{6,7},{7,4},{8,9},{9,10},{10,1... | collective-permute-start | bytes 1179656 | tf_op jit(solution)/shard_map/ppermute | solution.py:49
  261.9 51.4 %collective-permute-start.38 = (bf16[128,1536]{1,0:T(8,128)(2,1)S(1)}, bf16[128,1536]{1,0:T(8,128)(2,1)}, u32[]{:S(2)}, u32[]{:S(2)}) collective-permute-start(bf16[128,1536]{1,0:T(8,128)(2,1)S(1)} %tie.49), channel_id=1, source_target_pairs={{0,1},{1,2},{2,3},{3,0},{4,5},{5,6},{6,7},{7,4},{8,9},{9,10},{10,1... | collective-permute-start | bytes 1179656 | tf_op jit(solution)/shard_map/ppermute | solution.py:49
  284.2 10.1 %collective-permute-start.40 = (bf16[4,2,2,256,128]{4,3,2,1,0:T(8,128)(2,1)}, bf16[4,2,2,256,128]{4,3,2,1,0:T(8,128)(2,1)S(1)}, u32[]{:S(2)}, u32[]{:S(2)}) collective-permute-start(bf16[4,2,2,256,128]{4,3,2,1,0:T(8,128)(2,1)} %copy-done.13), channel_id=1, source_target_pairs={{0,4},{4,0},{8,12},{12,8},{16,20},{20,16},{24,28},{28,24},{1,5},{5... | collective-permute-start | bytes 3145736 | tf_op jit(solution)/shard_map/ppermute | solution.py:49
  284.8 21.5 %collective-permute-start.37 = (bf16[256,1536]{1,0:T(8,128)(2,1)S(1)}, bf16[256,1536]{1,0:T(8,128)(2,1)S(1)}, u32[]{:S(2)}, u32[]{:S(2)}) collective-permute-start(bf16[256,1536]{1,0:T(8,128)(2,1)S(1)} %pad_maximum_fusion.5), channel_id=1, source_target_pairs={{0,3},{1,0},{2,1},{3,2},{4,7},{5,4},{6,5},{7,6},{8,11},{9,8},{10,9... | collective-permute-start | bytes 2359304 | tf_op jit(solution)/shard_map/ppermute | solution.py:49
  296.0 13.4 %collective-permute-start.45 = (bf16[2,2,256,128]{3,2,1,0:T(8,128)(2,1)S(1)}, bf16[2,2,256,128]{3,2,1,0:T(8,128)(2,1)S(1)}, u32[]{:S(2)}, u32[]{:S(2)}) collective-permute-start(bf16[2,2,256,128]{3,2,1,0:T(8,128)(2,1)S(1)} %pad_maximum_fusion.9), channel_id=1, source_target_pairs={{0,16},{4,20},{8,24},{12,28},{16,0},{20,4},{24,8},{28,12},{1,17},{... | collective-permute-start | bytes 786440 | tf_op jit(solution)/shard_map/ppermute | solution.py:49
  297.5 13.8 %collective-permute-start.43 = (bf16[2,2,256,128]{3,2,1,0:T(8,128)(2,1)S(1)}, bf16[2,2,256,128]{3,2,1,0:T(8,128)(2,1)S(1)}, u32[]{:S(2)}, u32[]{:S(2)}) collective-permute-start(bf16[2,2,256,128]{3,2,1,0:T(8,128)(2,1)S(1)} %pad_maximum_fusion.8), channel_id=1, source_target_pairs={{0,8},{4,12},{8,0},{12,4},{16,24},{20,28},{24,16},{28,20},{1,9},{5... | collective-permute-start | bytes 786440 | tf_op jit(solution)/shard_map/ppermute | solution.py:49
  311.4 5.0 %collective-permute-start.44 = (bf16[1,2,256,128]{3,2,1,0:T(8,128)(2,1)S(1)}, bf16[1,2,256,128]{3,2,1,0:T(8,128)(2,1)S(1)}, u32[]{:S(2)}, u32[]{:S(2)}) collective-permute-start(bf16[1,2,256,128]{3,2,1,0:T(8,128)(2,1)S(1)} %get-tuple-element.160), channel_id=1, source_target_pairs={{0,16},{4,20},{8,24},{12,28},{16,0},{20,4},{24,8},{28,12},{1,17},{... | collective-permute-start | bytes 393224 | tf_op jit(solution)/shard_map/ppermute | solution.py:49
  311.6 5.0 %collective-permute-start.46 = (bf16[1,2,256,128]{3,2,1,0:T(8,128)(2,1)S(1)}, bf16[1,2,256,128]{3,2,1,0:T(8,128)(2,1)S(1)}, u32[]{:S(2)}, u32[]{:S(2)}) collective-permute-start(bf16[1,2,256,128]{3,2,1,0:T(8,128)(2,1)S(1)} %get-tuple-element.159), channel_id=1, source_target_pairs={{0,8},{4,12},{8,0},{12,4},{16,24},{20,28},{24,16},{28,20},{1,9},{5... | collective-permute-start | bytes 393224 | tf_op jit(solution)/shard_map/ppermute | solution.py:49
  313.4 11.7 %collective-permute-start.39 = (bf16[128,1536]{1,0:T(8,128)(2,1)S(1)}, bf16[128,1536]{1,0:T(8,128)(2,1)S(1)}, u32[]{:S(2)}, u32[]{:S(2)}) collective-permute-start(bf16[128,1536]{1,0:T(8,128)(2,1)S(1)} %payload.4), channel_id=1, source_target_pairs={{0,3},{1,0},{2,1},{3,2},{4,7},{5,4},{6,5},{7,6},{8,11},{9,8},{10,9... | collective-permute-start | bytes 1179656 | tf_op jit(solution)/shard_map/ppermute | solution.py:49
  316.7 7.5 %collective-permute-start.47 = (bf16[2,256,128]{2,1,0:T(8,128)(2,1)S(1)}, bf16[2,256,128]{2,1,0:T(8,128)(2,1)S(1)}, u32[]{:S(2)}, u32[]{:S(2)}) collective-permute-start(bf16[2,256,128]{2,1,0:T(8,128)(2,1)S(1)} %select_convert_fusion.refs_1_), channel_id=1, source_target_pairs={{0,1},{1,0},{2,3},{3,2},{4,5},{5,4},{6,7},{7,6},{8,9},{9,8},{10,11... | collective-permute-start | bytes 393224 | tf_op jit(solution)/shard_map/ppermute | solution.py:49
  319.0 17.3 %collective-permute-start.48 = (bf16[1,192,1152]{2,1,0:T(8,128)(2,1)S(1)}, bf16[1,192,1152]{2,1,0:T(8,128)(2,1)S(1)}, u32[]{:S(2)}, u32[]{:S(2)}) collective-permute-start(bf16[1,192,1152]{2,1,0:T(8,128)(2,1)S(1)} %fusion.11), channel_id=1, source_target_pairs={{0,8},{4,12},{8,0},{12,4},{16,24},{20,28},{24,16},{28,20},{1,9},{5... | collective-permute-start | bytes 1327112 | tf_op jit(solution)/shard_map/ppermute | solution.py:49
  320.2 18.6 %collective-permute-start.49 = (bf16[1,192,1152]{2,1,0:T(8,128)(2,1)S(1)}, bf16[1,192,1152]{2,1,0:T(8,128)(2,1)S(1)}, u32[]{:S(2)}, u32[]{:S(2)}) collective-permute-start(bf16[1,192,1152]{2,1,0:T(8,128)(2,1)S(1)} %fusion.10), channel_id=1, source_target_pairs={{0,16},{4,20},{8,24},{12,28},{16,0},{20,4},{24,8},{28,12},{1,17},{... | collective-permute-start | bytes 1327112 | tf_op jit(solution)/shard_map/ppermute | solution.py:49
  334.7 9.9 %collective-permute-start.51 = (bf16[4,208,896]{2,1,0:T(8,128)(2,1)}, bf16[4,208,896]{2,1,0:T(8,128)(2,1)S(1)}, u32[]{:S(2)}, u32[]{:S(2)}) collective-permute-start(bf16[4,208,896]{2,1,0:T(8,128)(2,1)} %get-tuple-element.149), channel_id=1, source_target_pairs={{0,4},{4,0},{8,12},{12,8},{16,20},{20,16},{24,28},{28,24},{1,5},{5... | collective-permute-start | bytes 4472840 | tf_op jit(solution)/shard_map/ppermute | solution.py:49
  338.9 13.7 %collective-permute-start.52 = (bf16[128,1536]{1,0:T(8,128)(2,1)S(1)}, bf16[128,1536]{1,0:T(8,128)(2,1)S(1)}, u32[]{:S(2)}, u32[]{:S(2)}) collective-permute-start(bf16[128,1536]{1,0:T(8,128)(2,1)S(1)} %get-tuple-element.150), channel_id=1, source_target_pairs={{0,1},{1,2},{2,3},{3,0},{4,5},{5,6},{6,7},{7,4},{8,9},{9,10},{10,1... | collective-permute-start | bytes 1179656 | tf_op jit(solution)/shard_map/ppermute | solution.py:49
  339.6 16.8 %collective-permute-start.50 = (bf16[128,1536]{1,0:T(8,128)(2,1)S(1)}, bf16[128,1536]{1,0:T(8,128)(2,1)S(1)}, u32[]{:S(2)}, u32[]{:S(2)}) collective-permute-start(bf16[128,1536]{1,0:T(8,128)(2,1)S(1)} %get-tuple-element.148), channel_id=1, source_target_pairs={{0,3},{1,0},{2,1},{3,2},{4,7},{5,4},{6,5},{7,6},{8,11},{9,8},{10,9... | collective-permute-start | bytes 1179656 | tf_op jit(solution)/shard_map/ppermute | solution.py:49
  356.5 14.7 %collective-permute-start.53 = (bf16[128,1536]{1,0:T(8,128)(2,1)S(1)}, bf16[128,1536]{1,0:T(8,128)(2,1)S(1)}, u32[]{:S(2)}, u32[]{:S(2)}) collective-permute-start(bf16[128,1536]{1,0:T(8,128)(2,1)S(1)} %payload.5.refs_1_), channel_id=1, source_target_pairs={{0,3},{1,0},{2,1},{3,2},{4,7},{5,4},{6,5},{7,6},{8,11},{9,8},{10,9... | collective-permute-start | bytes 1179656 | tf_op jit(solution)/shard_map/ppermute | solution.py:49
  358.7 10.3 %collective-permute-start.54 = (bf16[2,208,512]{2,1,0:T(8,128)(2,1)S(1)}, bf16[2,208,512]{2,1,0:T(8,128)(2,1)S(1)}, u32[]{:S(2)}, u32[]{:S(2)}) collective-permute-start(bf16[2,208,512]{2,1,0:T(8,128)(2,1)S(1)} %add_convert_fusion), channel_id=1, source_target_pairs={{0,16},{4,20},{8,24},{12,28},{16,0},{20,4},{24,8},{28,12},{1,17},{... | collective-permute-start | bytes 1277960 | tf_op jit(solution)/shard_map/ppermute | solution.py:49
  360.2 7.1 %collective-permute-start.55 = (bf16[2,192,384]{2,1,0:T(8,128)(2,1)S(1)}, bf16[2,192,384]{2,1,0:T(8,128)(2,1)S(1)}, u32[]{:S(2)}, u32[]{:S(2)}) collective-permute-start(bf16[2,192,384]{2,1,0:T(8,128)(2,1)S(1)} %add_convert_fusion.2), channel_id=1, source_target_pairs={{0,8},{4,12},{8,0},{12,4},{16,24},{20,28},{24,16},{28,20},{1,9},{5... | collective-permute-start | bytes 884744 | tf_op jit(solution)/shard_map/ppermute | solution.py:49
  369.1 7.5 %collective-permute-start.56 = (bf16[1,208,512]{2,1,0:T(8,128)(2,1)S(1)}, bf16[1,208,512]{2,1,0:T(8,128)(2,1)S(1)}, u32[]{:S(2)}, u32[]{:S(2)}) collective-permute-start(bf16[1,208,512]{2,1,0:T(8,128)(2,1)S(1)} %add_convert_fusion.4), channel_id=1, source_target_pairs={{0,8},{4,12},{8,0},{12,4},{16,24},{20,28},{24,16},{28,20},{1,9},{5... | collective-permute-start | bytes 638984 | tf_op jit(solution)/shard_map/ppermute | solution.py:49
  370.7 5.2 %collective-permute-start.60 = (bf16[1,192,384]{2,1,0:T(8,128)(2,1)S(1)}, bf16[1,192,384]{2,1,0:T(8,128)(2,1)S(1)}, u32[]{:S(2)}, u32[]{:S(2)}) collective-permute-start(bf16[1,192,384]{2,1,0:T(8,128)(2,1)S(1)} %add_convert_fusion.5), channel_id=1, source_target_pairs={{0,16},{4,20},{8,24},{12,28},{16,0},{20,4},{24,8},{28,12},{1,17},{... | collective-permute-start | bytes 442376 | tf_op jit(solution)/shard_map/ppermute | solution.py:49
  378.4 6.9 %collective-permute-start.59 = (bf16[64,512]{1,0:T(8,128)(2,1)S(1)}, bf16[64,512]{1,0:T(8,128)(2,1)S(1)}, u32[]{:S(2)}, u32[]{:S(2)}) collective-permute-start(bf16[64,512]{1,0:T(8,128)(2,1)S(1)} %tie.63), channel_id=1, source_target_pairs={{0,1},{1,2},{2,3},{3,0},{4,5},{5,6},{6,7},{7,4},{8,9},{9,10},{10,1... | collective-permute-start | bytes 196616 | tf_op jit(solution)/shard_map/ppermute | solution.py:49
  379.9 6.0 %collective-permute-start.58 = (bf16[64,512]{1,0:T(8,128)(2,1)S(1)}, bf16[64,512]{1,0:T(8,128)(2,1)S(1)}, u32[]{:S(2)}, u32[]{:S(2)}) collective-permute-start(bf16[64,512]{1,0:T(8,128)(2,1)S(1)} %tie.62), channel_id=1, source_target_pairs={{0,2},{1,3},{2,0},{3,1},{4,6},{5,7},{6,4},{7,5},{8,10},{9,11},{10,... | collective-permute-start | bytes 196616 | tf_op jit(solution)/shard_map/ppermute | solution.py:49
  381.1 4.8 %collective-permute-start.57 = (bf16[64,512]{1,0:T(8,128)(2,1)S(1)}, bf16[64,512]{1,0:T(8,128)(2,1)S(1)}, u32[]{:S(2)}, u32[]{:S(2)}) collective-permute-start(bf16[64,512]{1,0:T(8,128)(2,1)S(1)} %tie.61), channel_id=1, source_target_pairs={{0,3},{1,0},{2,1},{3,2},{4,7},{5,4},{6,5},{7,6},{8,11},{9,8},{10,9... | collective-permute-start | bytes 196616 | tf_op jit(solution)/shard_map/ppermute | solution.py:49
  (75 other events, 321.3 us)
Sparse Core Ops, SparseCore 0:
  10.4 130.1 all-gather.1
  217.2 133.0 reduce-scatter.1

commit v5 on v4

--- a/solution.py
+++ b/solution.py
@@ -869,9 +869,15 @@
 
 def pair_grads_kernel(orders, others, own_ref, *refs):
     cots, middles = refs[:2], refs[2:4]
-    outs = refs[4 + others : -2]
-    one, two, turned = refs[-3:]
+    outs = refs[4 + others : -5]
+    one, two, turned, middles_v, sem = refs[-5:]
     count = len(outs) // 2
+    copies = [
+        pltpu.make_async_copy(ref, middles_v.at[side], sem.at[side])
+        for side, ref in enumerate(middles)
+    ]
+    for copy in copies:
+        copy.start()
     blocks = len(orders[0])
     rows = one.shape[0] // blocks
     tokens = cots[0].shape[0]
@@ -884,9 +890,13 @@
                 left[j * rows : (j + 1) * rows, side * tokens : (side + 1) * tokens] = turned[
                     side, pl.ds(at, rows), :
                 ]
+    for copy in copies:
+        copy.wait()
     for which, left in enumerate((one, two)):
         here = slice(which * cols, (which + 1) * cols)
-        result = dot_nn(left[:, :tokens], middles[0][:, here]) + dot_nn(left[:, tokens:], middles[1][:, here])
+        result = dot_nn(left[:, :tokens], middles_v[0, :, here]) + dot_nn(
+            left[:, tokens:], middles_v[1, :, here]
+        )
         store_rows(outs[which * count : (which + 1) * count], slice(None), result)
 
 
@@ -896,10 +906,14 @@
     outs = [shape_of((n, cols)) for n in (full // 8, full // 8, full // 4)] * 2
     return pl.pallas_call(
         functools.partial(pair_grads_kernel, orders, len(others)),
-        in_specs=[smem()] + [vmem()] * 4 + [anywhere()] * len(others),
+        in_specs=[smem()] + [vmem()] * 2 + [anywhere()] * (2 + len(others)),
         out_specs=[vmem()] * 6,
         out_shape=outs,
-        scratch_shapes=[pltpu.VMEM((full // 2, 2 * rows), BF)] * 2 + [pltpu.VMEM((2, full, rows), BF)],
+        scratch_shapes=[pltpu.VMEM((full // 2, 2 * rows), BF)] * 2 + [
+            pltpu.VMEM((2, full, rows), BF),
+            pltpu.VMEM((2,) + middles[0].shape, BF),
+            pltpu.SemaphoreType.DMA((2,)),
+        ],
         compiler_params=params(60),
         cost_estimate=cost(TUNE["pair_grads"]),
         name="pair_grads",

time: 402 us -> 402 us (level)
  no operation moved by 1% of the time
where the time goes in v5:
time: 402 us; the launch traced here: 396 us
  waiting for transfers between devices  124 us (31%)
  Pallas kernels  119 us (30%)
  starting transfers between devices  82.3 us (20%)
  local copies, waits for them, and re-layouts  35.5 us (9%)
  other arithmetic  19.7 us (5%)
  between operations  15.7 us (4%)
    ppermute x61, waiting for transfers between devices, send(): lax.ppermute(plain(block), axis, [(j, target(j) % count) for j in range(c...  124 us
    ppermute x61, starting transfers between devices, send(): lax.ppermute(plain(block), axis, [(j, target(j) % count) for j in range(c...  82.2 us
    pallas_call x1, Pallas kernels, feed_forward(): pl.pallas_call(feed_forward_kernel, in_specs=[smem(), vmem()] + [anywhere...  30.3 us
    unnamed x166, local copies, waits for them, and re-layouts  23.8 us
    pallas_call x1, Pallas kernels, attend_back(): pl.pallas_call(functools.partial(attend_back_kernel, HD ** (-0.5), first_...  17.7 us
    pallas_call x1, Pallas kernels, attend(): pl.pallas_call(functools.partial(attend_kernel, HD ** (-0.5) * math.log2(...  13.2 us
    pallas_call x1, Pallas kernels, wide_grads(): pl.pallas_call(wide_grads_kernel, grid=(units // TILE,), in_specs=[pl.Blo...  12.9 us
    pallas_call x1, Pallas kernels, pair_grads(): pl.pallas_call(functools.partial(pair_grads_kernel, orders, len(others)),...  11.3 us
  transfers between devices with their start and end apart: 63, of which 37 were waited for; matrix products, arithmetic and copies ran while one was open for 7% of the time, Pallas kernels for 22%

profile of v5, /device:TPU:0, one launch (start us, length us, event | category | flops | bytes accessed | tf_op | source)
XLA Modules:
  0.0 396.0 jit_solution(7983541313924486933)
XLA Ops:
  7.2 2.9 fusion.5
  11.9 5.0 %collective-permute-start = (bf16[64,640]{1,0:T(8,128)(2,1)S(1)}, bf16[64,640]{1,0:T(8,128)(2,1)S(1)}, u32[]{:S(2)}, u32[]{:S(2)}) collective-permute-start(bf16[64,640]{1,0:T(8,128)(2,1)S(1)} %get-tuple-element.198), channel_id=1, source_target_pairs={{0,3},{1,0},{2,1},{3,2},{4,7},{5,4},{6,5},{7,6},{8,11},{9,8},{10,9... | collective-permute-start | bytes 245768 | tf_op jit(solution)/shard_map/ppermute | solution.py:49
  18.0 1.8 collective-permute-done.refs_1_
  19.8 4.7 %collective-permute-done.1.refs_2_ = bf16[64,640]{1,0:T(8,128)(2,1)S(1)} collective-permute-done((bf16[64,640]{1,0:T(8,128)(2,1)S(1)}, bf16[64,640]{1,0:T(8,128)(2,1)S(1)}, u32[]{:S(2)}, u32[]{:S(2)}) %collective-permute-start.1) | collective-permute-done | bytes 81952 | tf_op jit(solution)/shard_map/ppermute | solution.py:49
  25.1 1.9 arrange.1
  28.5 1.5 collective-permute-start.4
  32.7 2.0 collective-permute-start.7
  35.5 7.1 %collective-permute-done.3.refs_0_ = bf16[224,640]{1,0:T(8,128)(2,1)S(1)} collective-permute-done((bf16[224,640]{1,0:T(8,128)(2,1)}, bf16[224,640]{1,0:T(8,128)(2,1)S(1)}, u32[]{:S(2)}, u32[]{:S(2)}) %collective-permute-start.3) | collective-permute-done | bytes 286752 | tf_op jit(solution)/shard_map/ppermute | solution.py:49
  44.7 1.6 collective-permute-start.5
  46.3 5.7 %collective-permute-done.8.refs_1_ = bf16[128,1536]{1,0:T(8,128)(2,1)S(1)} collective-permute-done((bf16[128,1536]{1,0:T(8,128)(2,1)S(1)}, bf16[128,1536]{1,0:T(8,128)(2,1)S(1)}, u32[]{:S(2)}, u32[]{:S(2)}) %collective-permute-start.8) | collective-permute-done | bytes 393248 | tf_op jit(solution)/shard_map/ppermute | solution.py:49
  55.7 6.4 %collective-permute-done.9.refs_0_ = bf16[128,1536]{1,0:T(8,128)(2,1)S(1)} collective-permute-done((bf16[128,1536]{1,0:T(8,128)(2,1)S(1)}, bf16[128,1536]{1,0:T(8,128)(2,1)S(1)}, u32[]{:S(2)}, u32[]{:S(2)}) %collective-permute-start.9) | collective-permute-done | bytes 393248 | tf_op jit(solution)/shard_map/ppermute | solution.py:49
  67.3 4.3 %collective-permute-start.11 = (bf16[192,1536]{1,0:T(8,128)(2,1)S(1)}, bf16[192,1536]{1,0:T(8,128)(2,1)S(1)}, u32[]{:S(2)}, u32[]{:S(2)}) collective-permute-start(bf16[192,1536]{1,0:T(8,128)(2,1)S(1)} %tie.38.refs_1_), channel_id=1, source_target_pairs={{0,3},{1,0},{2,1},{3,2},{4,7},{5,4},{6,5},{7,6},{8,11},{9,8},{10,9... | collective-permute-start | bytes 1769480 | tf_op jit(solution)/shard_map/ppermute | solution.py:49
  71.6 6.8 %project.1 = (bf16[2,768,128]{2,1,0:T(8,128)(2,1)}, bf16[2,2,256,128]{3,2,1,0:T(8,128)(2,1)}, bf16[512,1536]{1,0:T(8,128)(2,1)}, bf16[512,1536]{1,0:T(8,128)(2,1)}, bf16[1536,640]{1,0:T(8,128)(2,1)}) custom-call(s32[1]{0:T(128)} %bitcast.own_ref, s32[1]{0:T(128)} %bitcast.1.head_ref, bf16[128,1536]{1,0:T(8,128)(2,1)} %copy-done.7, ...), custom_call_target="tpu_custom_call" | custom-call | flops 8071000064 | tf_op jit(solution)/shard_map/project/pallas_call | solution.py:351
  80.6 4.8 %collective-permute-done.11.refs_0_ = bf16[192,1536]{1,0:T(8,128)(2,1)S(1)} collective-permute-done((bf16[192,1536]{1,0:T(8,128)(2,1)S(1)}, bf16[192,1536]{1,0:T(8,128)(2,1)S(1)}, u32[]{:S(2)}, u32[]{:S(2)}) %collective-permute-start.11) | collective-permute-done | bytes 589856 | tf_op jit(solution)/shard_map/ppermute | solution.py:49
  85.4 11.6 %collective-permute-done.12.refs_1_ = bf16[192,1536]{1,0:T(8,128)(2,1)S(1)} collective-permute-done((bf16[192,1536]{1,0:T(8,128)(2,1)S(1)}, bf16[192,1536]{1,0:T(8,128)(2,1)S(1)}, u32[]{:S(2)}, u32[]{:S(2)}) %collective-permute-start.12) | collective-permute-done | bytes 589856 | tf_op jit(solution)/shard_map/ppermute | solution.py:49
  100.6 2.3 collective-permute-start.15
  103.0 2.5 collective-permute-done.17
  108.6 2.0 copy.79.kc_ref.refs_7_
  110.5 3.9 collective-permute-done.15.refs_0_
  116.1 13.2 %attend.1 = (bf16[512,384]{1,0:T(8,128)(2,1)}, f32[2,768,128]{2,1,0:T(8,128)}, f32[2,1,768]{2,1,0:T(1,128)}) custom-call(bf16[2,768,128]{2,1,0:T(8,128)(2,1)} %get-tuple-element.96.q_ref, bf16[4,2,2,256,128]{4,3,2,1,0:T(8,128)(2,1)} %pad_maximum_fusion.4.near_ref.refs_5_, bf16[4,2,2,256,128]{4,3,2,1,0:T(8,128)(2,1)} %collective-permute-done.18.other_ref.refs_6_, ...), custom_call_target="tpu_custom_call" | custom-call | flops 18447998976 | tf_op jit(solution)/shard_map/attend/pallas_call | solution.py:564
  129.3 3.5 collective-permute-start.19
  134.0 1.6 collective-permute-start.22
  137.0 5.6 %collective-permute-done.19.refs_0_ = bf16[512,384]{1,0:T(8,128)(2,1)S(1)} collective-permute-done((bf16[512,384]{1,0:T(8,128)(2,1)}, bf16[512,384]{1,0:T(8,128)(2,1)S(1)}, u32[]{:S(2)}, u32[]{:S(2)}) %collective-permute-start.19) | collective-permute-done | bytes 393248 | tf_op jit(solution)/shard_map/ppermute | solution.py:49
  142.6 5.0 %collective-permute-done.20.refs_1_ = bf16[512,384]{1,0:T(8,128)(2,1)S(1)} collective-permute-done((bf16[512,384]{1,0:T(8,128)(2,1)}, bf16[512,384]{1,0:T(8,128)(2,1)S(1)}, u32[]{:S(2)}, u32[]{:S(2)}) %collective-permute-start.20) | collective-permute-done | bytes 393248 | tf_op jit(solution)/shard_map/ppermute | solution.py:49
  147.6 1.6 collective-permute-done.22.refs_0_
  149.2 1.5 collective-permute-start.25
  151.4 3.5 collective-permute-start.21
  154.9 2.0 collective-permute-done.25
  162.8 3.8 collective-permute-done.26.refs_10_.refs_7_
  168.1 30.3 %feed_forward.1 = (bf16[512,6144]{1,0:T(8,128)(2,1)}, f32[128,1536]{1,0:T(8,128)}, bf16[512,2304]{1,0:T(8,128)(2,1)}, bf16[512,1536]{1,0:T(8,128)(2,1)}, f32[128...) custom-call(s32[1]{0:T(128)} %bitcast.own_ref, ...), custom_call_target="tpu_custom_call" | custom-call | flops 41507999744 | tf_op jit(solution)/shard_map/feed_forward/pallas_call | solution.py:770
  199.0 4.3 %collective-permute-start.27 = (bf16[128,1536]{1,0:T(8,128)(2,1)}, bf16[128,1536]{1,0:T(8,128)(2,1)S(1)}, u32[]{:S(2)}, u32[]{:S(2)}) collective-permute-start(bf16[128,1536]{1,0:T(8,128)(2,1)} %get-tuple-element.111), channel_id=1, source_target_pairs={{0,3},{1,0},{2,1},{3,2},{4,7},{5,4},{6,5},{7,6},{8,11},{9,8},{10,9... | collective-permute-start | bytes 1179656 | tf_op jit(solution)/shard_map/ppermute | solution.py:49
  203.4 12.9 %wide_grads.1.refs_0_ = bf16[1536,4608]{1,0:T(8,128)(2,1)} custom-call(bf16[512,6144]{1,0:T(8,128)(2,1)} %get-tuple-element.155.x_ref.acts_ref, bf16[512,6144]{1,0:T(8,128)(2,1)} %get-tuple-element.155.x_ref.acts_ref), custom_call_target="tpu_custom_call" | custom-call | flops 12682999808 | tf_op jit(solution)/shard_map/wide_grads/pallas_call | solution.py:854
  218.7 4.1 %collective-permute-start.30 = (bf16[128,1536]{1,0:T(8,128)(2,1)S(1)}, bf16[128,1536]{1,0:T(8,128)(2,1)S(1)}, u32[]{:S(2)}, u32[]{:S(2)}) collective-permute-start(bf16[128,1536]{1,0:T(8,128)(2,1)S(1)} %payload.3.refs_0_.refs_4_), channel_id=1, source_target_pairs={{0,3},{1,0},{2,1},{3,2},{4,7},{5,4},{6,5},{7,6},{8,11},{9,8},{10,9... | collective-permute-start | bytes 1179656 | tf_op jit(solution)/shard_map/ppermute | solution.py:49
  222.9 9.8 %down_product.1 = (f32[128,1536]{1,0:T(8,128)}, bf16[128,1536]{1,0:T(8,128)(2,1)}, bf16[128,1536]{1,0:T(8,128)(2,1)}, bf16[128,1536]{1,0:T(8,128)(2,1)}) custom-call(bf16[1536,6912]{1,0:T(8,128)(2,1)} %all-gather.2.cloned.1.call-done.refs_11_.down_w, bf16[512,2304]{1,0:T(8,128)(2,1)} %get-tuple-element.109.middle_ref.refs_2_, bf16[128,1536]{1,0:T(8,128)(2,1)} %copy-done.36), custom_call_target="tpu_custom_call" | custom-call | flops 9223999488 | tf_op jit(solution)/shard_map/down_product/pallas_call | solution.py:826
  232.6 11.3 %pair_grads.1 = (bf16[192,1152]{1,0:T(8,128)(2,1)}, bf16[192,1152]{1,0:T(8,128)(2,1)}, bf16[384,1152]{1,0:T(8,128)(2,1)}, bf16[192,1152]{1,0:T(8,128)(2,1)}, bf1...) custom-call(s32[1]{0:T(128)} %bitcast.own_ref, bf16[512,1536]{1,0:T(8,128)(2,1)} %get-tuple-element.112.refs_0_, ...), custom_call_target="tpu_custom_call" | custom-call | flops 8071000064 | tf_op jit(solution)/shard_map/pair_grads/pallas_call | solution.py:907
  244.7 5.9 %norm_back.1 = (f32[128,1536]{1,0:T(8,128)}, bf16[128,1536]{1,0:T(8,128)(2,1)}, bf16[128,384]{1,0:T(8,128)(2,1)}, bf16[128,384]{1,0:T(8,128)(2,1)}, bf16[128,384...) custom-call(s32[1]{0:T(128)} %bitcast.own_ref, f32[128,1536]{1,0:T(8,128)} %get-tuple-element.115.refs_0_, ...), custom_call_target="tpu_custom_call" | custom-call | flops 6341499904 | tf_op jit(solution)/shard_map/norm_back/pallas_call | solution.py:949
  250.7 1.9 collective-permute-start.34
  255.8 4.1 %collective-permute-done.33.refs_2_ = bf16[128,384]{1,0:T(8,128)(2,1)S(1)} collective-permute-done((bf16[128,384]{1,0:T(8,128)(2,1)}, bf16[128,384]{1,0:T(8,128)(2,1)S(1)}, u32[]{:S(2)}, u32[]{:S(2)}) %collective-permute-start.33) | collective-permute-done | bytes 98336 | tf_op jit(solution)/shard_map/ppermute | solution.py:49
  259.9 1.6 collective-permute-start.35
  263.3 17.7 %attend_back.1 = (f32[2,768,128]{2,1,0:T(8,128)}, bf16[4,2,2,256,128]{4,3,2,1,0:T(8,128)(2,1)}, bf16[4,2,2,256,128]{4,3,2,1,0:T(8,128)(2,1)}) custom-call(bf16[2,768,128]{2,1,0:T(8,128)(2,1)} %get-tuple-element.96.q_ref, bf16[128,384]{1,0:T(8,128)(2,1)} %get-tuple-element.122.refs_0_, bf16[128,384]{1,0:T(8,128)(2,1)} %copy-done.19, ...), custom_call_target="tpu_custom_call" | custom-call | flops 20753999872 | tf_op jit(solution)/shard_map/attend_back/pallas_call | solution.py:650
  285.0 1.9 collective-permute-start.37
  286.9 6.7 %collective-permute-done.41.refs_0_ = bf16[2,192,1152]{2,1,0:T(8,128)(2,1)S(1)} collective-permute-done((bf16[2,192,1152]{2,1,0:T(8,128)(2,1)}, bf16[2,192,1152]{2,1,0:T(8,128)(2,1)S(1)}, u32[]{:S(2)}, u32[]{:S(2)}) %collective-permute-start.41) | collective-permute-done | bytes 884768 | tf_op jit(solution)/shard_map/ppermute | solution.py:49
  297.4 1.8 collective-permute-start.43
  299.2 7.4 %collective-permute-done.37.refs_0_ = bf16[256,1536]{1,0:T(8,128)(2,1)S(1)} collective-permute-done((bf16[256,1536]{1,0:T(8,128)(2,1)S(1)}, bf16[256,1536]{1,0:T(8,128)(2,1)S(1)}, u32[]{:S(2)}, u32[]{:S(2)}) %collective-permute-start.37) | collective-permute-done | bytes 786464 | tf_op jit(solution)/shard_map/ppermute | solution.py:49
  306.6 3.0 collective-permute-done.45
  309.6 1.6 collective-permute-done.43
  313.3 2.6 collective-permute-start.39
  316.9 2.0 collective-permute-start.47
  320.2 1.9 collective-permute-start.49
  322.1 2.0 collective-permute-done.47
  325.7 8.9 %project_back.1 = (f32[128,1536]{1,0:T(8,128)}, bf16[128,1536]{1,0:T(8,128)(2,1)}, bf16[128,1536]{1,0:T(8,128)(2,1)}, bf16[128,1536]{1,0:T(8,128)(2,1)}, bf16[4,...) custom-call(s32[1]{0:T(128)} %bitcast.own_ref, s32[1]{0:T(128)} %bitcast.1.head_ref, ...), custom_call_target="tpu_custom_call" | custom-call | flops 10376999936 | tf_op jit(solution)/shard_map/project_back/pallas_call | solution.py:459
  336.3 2.7 collective-permute-done.49.refs_1_
  339.8 3.1 collective-permute-start.50
  342.9 1.9 add_convert_fusion.1
  344.8 7.8 %collective-permute-done.52.refs_1_ = bf16[128,1536]{1,0:T(8,128)(2,1)S(1)} collective-permute-done((bf16[128,1536]{1,0:T(8,128)(2,1)S(1)}, bf16[128,1536]{1,0:T(8,128)(2,1)S(1)}, u32[]{:S(2)}, u32[]{:S(2)}) %collective-permute-start.52) | collective-permute-done | bytes 393248 | tf_op jit(solution)/shard_map/ppermute | solution.py:49
  352.6 3.8 collective-permute-done.50.moved_ref
  356.5 2.2 collective-permute-start.53
  358.7 1.5 collective-permute-start.54
  362.6 4.7 %collective-permute-done.55.refs_1_ = bf16[2,192,384]{2,1,0:T(8,128)(2,1)S(1)} collective-permute-done((bf16[2,192,384]{2,1,0:T(8,128)(2,1)S(1)}, bf16[2,192,384]{2,1,0:T(8,128)(2,1)S(1)}, u32[]{:S(2)}, u32[]{:S(2)}) %collective-permute-start.55) | collective-permute-done | bytes 294944 | tf_op jit(solution)/shard_map/ppermute | solution.py:49
  367.3 1.7 collective-permute-done.54.refs_0_
  369.1 1.8 collective-permute-start.56
  373.1 3.1 collective-permute-done.60
  381.1 2.2 collective-permute-start.57
  383.3 2.0 slice_convert_fusion
  (390 shorter events, 77.9 us)
Async XLA Ops:
  7.2 159.5 %all-gather.2.cloned.1.call-start = ((), (), s32[]{:S(2)}) async-start(), calls=%async_computation.1 | async-start | bytes 23887872 | tf_op jit(solution)/shard_map/all_gather | solution.py:1010
  10.2 367.1 %reduce-scatter.2.cloned.1.call-start = ((), (), s32[]{:S(2)}) async-start(), calls=%async_computation.2 | async-start | bytes 15925248 | tf_op jit(solution)/shard_map/reduce_scatter | solution.py:1165
  11.9 7.9 %collective-permute-start = (bf16[64,640]{1,0:T(8,128)(2,1)S(1)}, bf16[64,640]{1,0:T(8,128)(2,1)S(1)}, u32[]{:S(2)}, u32[]{:S(2)}) collective-permute-start(bf16[64,640]{1,0:T(8,128)(2,1)S(1)} %get-tuple-element.198), channel_id=1, source_target_pairs={{0,3},{1,0},{2,1},{3,2},{4,7},{5,4},{6,5},{7,6},{8,11},{9,8},{10,9... | collective-permute-start | bytes 245768 | tf_op jit(solution)/shard_map/ppermute | solution.py:49
  17.0 7.5 %collective-permute-start.1 = (bf16[64,640]{1,0:T(8,128)(2,1)S(1)}, bf16[64,640]{1,0:T(8,128)(2,1)S(1)}, u32[]{:S(2)}, u32[]{:S(2)}) collective-permute-start(bf16[64,640]{1,0:T(8,128)(2,1)S(1)} %get-tuple-element.199), channel_id=1, source_target_pairs={{0,2},{1,3},{2,0},{3,1},{4,6},{5,7},{6,4},{7,5},{8,10},{9,11},{10,... | collective-permute-start | bytes 245768 | tf_op jit(solution)/shard_map/ppermute | solution.py:49
  17.0 7.5 %collective-permute-start.2 = (bf16[64,640]{1,0:T(8,128)(2,1)S(1)}, bf16[64,640]{1,0:T(8,128)(2,1)S(1)}, u32[]{:S(2)}, u32[]{:S(2)}) collective-permute-start(bf16[64,640]{1,0:T(8,128)(2,1)S(1)} %get-tuple-element.196), channel_id=1, source_target_pairs={{0,1},{1,2},{2,3},{3,0},{4,5},{5,6},{6,7},{7,4},{8,9},{9,10},{10,1... | collective-permute-start | bytes 245768 | tf_op jit(solution)/shard_map/ppermute | solution.py:49
  27.0 15.6 %collective-permute-start.3 = (bf16[224,640]{1,0:T(8,128)(2,1)}, bf16[224,640]{1,0:T(8,128)(2,1)S(1)}, u32[]{:S(2)}, u32[]{:S(2)}) collective-permute-start(bf16[224,640]{1,0:T(8,128)(2,1)} %arrange.1), channel_id=1, source_target_pairs={{0,8},{4,12},{8,0},{12,4},{16,24},{20,28},{24,16},{28,20},{1,9},{5... | collective-permute-start | bytes 860168 | tf_op jit(solution)/shard_map/ppermute | solution.py:49
  28.5 15.5 %collective-permute-start.4 = (bf16[224,640]{1,0:T(8,128)(2,1)}, bf16[224,640]{1,0:T(8,128)(2,1)S(1)}, u32[]{:S(2)}, u32[]{:S(2)}) collective-permute-start(bf16[224,640]{1,0:T(8,128)(2,1)} %arrange.1), channel_id=1, source_target_pairs={{0,16},{4,20},{8,24},{12,28},{16,0},{20,4},{24,8},{28,12},{1,17},{... | collective-permute-start | bytes 860168 | tf_op jit(solution)/shard_map/ppermute | solution.py:49
  32.7 13.6 %collective-permute-start.7 = (bf16[128,1536]{1,0:T(8,128)(2,1)S(1)}, bf16[128,1536]{1,0:T(8,128)(2,1)S(1)}, u32[]{:S(2)}, u32[]{:S(2)}) collective-permute-start(bf16[128,1536]{1,0:T(8,128)(2,1)S(1)} %tie.34.refs_0_), channel_id=1, source_target_pairs={{0,3},{1,0},{2,1},{3,2},{4,7},{5,4},{6,5},{7,6},{8,11},{9,8},{10,9... | collective-permute-start | bytes 1179656 | tf_op jit(solution)/shard_map/ppermute | solution.py:49
  34.8 17.3 %collective-permute-start.8 = (bf16[128,1536]{1,0:T(8,128)(2,1)S(1)}, bf16[128,1536]{1,0:T(8,128)(2,1)S(1)}, u32[]{:S(2)}, u32[]{:S(2)}) collective-permute-start(bf16[128,1536]{1,0:T(8,128)(2,1)S(1)} %tie.34.refs_0_), channel_id=1, source_target_pairs={{0,1},{1,2},{2,3},{3,0},{4,5},{5,6},{6,7},{7,4},{8,9},{9,10},{10,1... | collective-permute-start | bytes 1179656 | tf_op jit(solution)/shard_map/ppermute | solution.py:49
  44.1 11.3 %collective-permute-start.6 = (bf16[112,640]{1,0:T(8,128)(2,1)S(1)}, bf16[112,640]{1,0:T(8,128)(2,1)S(1)}, u32[]{:S(2)}, u32[]{:S(2)}) collective-permute-start(bf16[112,640]{1,0:T(8,128)(2,1)S(1)} %slice.264), channel_id=1, source_target_pairs={{0,8},{4,12},{8,0},{12,4},{16,24},{20,28},{24,16},{28,20},{1,9},{5... | collective-permute-start | bytes 430088 | tf_op jit(solution)/shard_map/ppermute | solution.py:49
  44.7 10.6 %collective-permute-start.5 = (bf16[112,640]{1,0:T(8,128)(2,1)S(1)}, bf16[112,640]{1,0:T(8,128)(2,1)S(1)}, u32[]{:S(2)}, u32[]{:S(2)}) collective-permute-start(bf16[112,640]{1,0:T(8,128)(2,1)S(1)} %slice.263), channel_id=1, source_target_pairs={{0,16},{4,20},{8,24},{12,28},{16,0},{20,4},{24,8},{28,12},{1,17},{... | collective-permute-start | bytes 430088 | tf_op jit(solution)/shard_map/ppermute | solution.py:49
  52.0 10.1 %collective-permute-start.9 = (bf16[128,1536]{1,0:T(8,128)(2,1)S(1)}, bf16[128,1536]{1,0:T(8,128)(2,1)S(1)}, u32[]{:S(2)}, u32[]{:S(2)}) collective-permute-start(bf16[128,1536]{1,0:T(8,128)(2,1)S(1)} %get-tuple-element.86.refs_1_), channel_id=1, source_target_pairs={{0,3},{1,0},{2,1},{3,2},{4,7},{5,4},{6,5},{7,6},{8,11},{9,8},{10,9... | collective-permute-start | bytes 1179656 | tf_op jit(solution)/shard_map/ppermute | solution.py:49
  62.2 9.5 %collective-permute-start.10 = (bf16[4,224,640]{2,1,0:T(8,128)(2,1)S(1)}, bf16[4,224,640]{2,1,0:T(8,128)(2,1)}, u32[]{:S(2)}, u32[]{:S(2)}) collective-permute-start(bf16[4,224,640]{2,1,0:T(8,128)(2,1)S(1)} %tie.37), channel_id=1, source_target_pairs={{0,4},{4,0},{8,12},{12,8},{16,20},{20,16},{24,28},{28,24},{1,5},{5... | collective-permute-start | bytes 3440648 | tf_op jit(solution)/shard_map/ppermute | solution.py:49
  67.3 18.1 %collective-permute-start.11 = (bf16[192,1536]{1,0:T(8,128)(2,1)S(1)}, bf16[192,1536]{1,0:T(8,128)(2,1)S(1)}, u32[]{:S(2)}, u32[]{:S(2)}) collective-permute-start(bf16[192,1536]{1,0:T(8,128)(2,1)S(1)} %tie.38.refs_1_), channel_id=1, source_target_pairs={{0,3},{1,0},{2,1},{3,2},{4,7},{5,4},{6,5},{7,6},{8,11},{9,8},{10,9... | collective-permute-start | bytes 1769480 | tf_op jit(solution)/shard_map/ppermute | solution.py:49
  71.6 25.4 %collective-permute-start.12 = (bf16[192,1536]{1,0:T(8,128)(2,1)S(1)}, bf16[192,1536]{1,0:T(8,128)(2,1)S(1)}, u32[]{:S(2)}, u32[]{:S(2)}) collective-permute-start(bf16[192,1536]{1,0:T(8,128)(2,1)S(1)} %tie.38.refs_1_), channel_id=1, source_target_pairs={{0,1},{1,2},{2,3},{3,0},{4,5},{5,6},{6,7},{7,4},{8,9},{9,10},{10,1... | collective-permute-start | bytes 1769480 | tf_op jit(solution)/shard_map/ppermute | solution.py:49
  78.5 18.6 %collective-permute-start.13 = (bf16[2,2,256,128]{3,2,1,0:T(8,128)(2,1)}, bf16[2,2,256,128]{3,2,1,0:T(8,128)(2,1)S(1)}, u32[]{:S(2)}, u32[]{:S(2)}) collective-permute-start(bf16[2,2,256,128]{3,2,1,0:T(8,128)(2,1)} %get-tuple-element.91), channel_id=1, source_target_pairs={{0,8},{4,12},{8,0},{12,4},{16,24},{20,28},{24,16},{28,20},{1,9},{5... | collective-permute-start | bytes 786440 | tf_op jit(solution)/shard_map/ppermute | solution.py:49
  79.5 17.5 %collective-permute-start.14 = (bf16[2,2,256,128]{3,2,1,0:T(8,128)(2,1)}, bf16[2,2,256,128]{3,2,1,0:T(8,128)(2,1)S(1)}, u32[]{:S(2)}, u32[]{:S(2)}) collective-permute-start(bf16[2,2,256,128]{3,2,1,0:T(8,128)(2,1)} %get-tuple-element.91), channel_id=1, source_target_pairs={{0,16},{4,20},{8,24},{12,28},{16,0},{20,4},{24,8},{28,12},{1,17},{... | collective-permute-start | bytes 786440 | tf_op jit(solution)/shard_map/ppermute | solution.py:49
  97.0 35.7 %copy-start.4 = (bf16[192,1536]{1,0:T(8,128)(2,1)}, bf16[192,1536]{1,0:T(8,128)(2,1)S(1)}, u32[]{:S(2)}) copy-start(bf16[192,1536]{1,0:T(8,128)(2,1)S(1)} %get-tuple-element.92.refs_2_) | copy-start | bytes 1769476
  97.1 8.5 %collective-permute-start.17 = (bf16[1,2,256,128]{3,2,1,0:T(8,128)(2,1)S(1)}, bf16[1,2,256,128]{3,2,1,0:T(8,128)(2,1)}, u32[]{:S(2)}, u32[]{:S(2)}) collective-permute-start(bf16[1,2,256,128]{3,2,1,0:T(8,128)(2,1)S(1)} %slice.277), channel_id=1, source_target_pairs={{0,8},{4,12},{8,0},{12,4},{16,24},{20,28},{24,16},{28,20},{1,9},{5... | collective-permute-start | bytes 393224 | tf_op jit(solution)/shard_map/ppermute | solution.py:49
  97.7 8.4 %collective-permute-start.16 = (bf16[1,2,256,128]{3,2,1,0:T(8,128)(2,1)S(1)}, bf16[1,2,256,128]{3,2,1,0:T(8,128)(2,1)}, u32[]{:S(2)}, u32[]{:S(2)}) collective-permute-start(bf16[1,2,256,128]{3,2,1,0:T(8,128)(2,1)S(1)} %slice.276), channel_id=1, source_target_pairs={{0,16},{4,20},{8,24},{12,28},{16,0},{20,4},{24,8},{28,12},{1,17},{... | collective-permute-start | bytes 393224 | tf_op jit(solution)/shard_map/ppermute | solution.py:49
  100.6 13.8 %collective-permute-start.15 = (bf16[192,1536]{1,0:T(8,128)(2,1)S(1)}, bf16[192,1536]{1,0:T(8,128)(2,1)S(1)}, u32[]{:S(2)}, u32[]{:S(2)}) collective-permute-start(bf16[192,1536]{1,0:T(8,128)(2,1)S(1)} %get-tuple-element.92.refs_2_), channel_id=1, source_target_pairs={{0,3},{1,0},{2,1},{3,2},{4,7},{5,4},{6,5},{7,6},{8,11},{9,8},{10,9... | collective-permute-start | bytes 1769480 | tf_op jit(solution)/shard_map/ppermute | solution.py:49
  108.2 7.8 %collective-permute-start.18 = (bf16[4,2,2,256,128]{4,3,2,1,0:T(8,128)(2,1)}, bf16[4,2,2,256,128]{4,3,2,1,0:T(8,128)(2,1)}, u32[]{:S(2)}, u32[]{:S(2)}) collective-permute-start(bf16[4,2,2,256,128]{4,3,2,1,0:T(8,128)(2,1)} %pad_maximum_fusion.4.near_ref.refs_5_), channel_id=1, source_target_pairs={{0,4},{4,0},{8,12},{12,8},{16,20},{20,16},{24,28},{28,24},{1,5},{5... | collective-permute-start | bytes 3145736 | tf_op jit(solution)/shard_map/ppermute | solution.py:49
  129.3 13.3 %collective-permute-start.19 = (bf16[512,384]{1,0:T(8,128)(2,1)}, bf16[512,384]{1,0:T(8,128)(2,1)S(1)}, u32[]{:S(2)}, u32[]{:S(2)}) collective-permute-start(bf16[512,384]{1,0:T(8,128)(2,1)} %get-tuple-element.99.refs_4_.refs_5_.refs_7_), channel_id=1, source_target_pairs={{0,3},{1,0},{2,1},{3,2},{4,7},{5,4},{6,5},{7,6},{8,11},{9,8},{10,9... | collective-permute-start | bytes 1179656 | tf_op jit(solution)/shard_map/ppermute | solution.py:49
  132.7 14.8 %collective-permute-start.20 = (bf16[512,384]{1,0:T(8,128)(2,1)}, bf16[512,384]{1,0:T(8,128)(2,1)S(1)}, u32[]{:S(2)}, u32[]{:S(2)}) collective-permute-start(bf16[512,384]{1,0:T(8,128)(2,1)} %get-tuple-element.99.refs_4_.refs_5_.refs_7_), channel_id=1, source_target_pairs={{0,1},{1,2},{2,3},{3,0},{4,5},{5,6},{6,7},{7,4},{8,9},{9,10},{10,1... | collective-permute-start | bytes 1179656 | tf_op jit(solution)/shard_map/ppermute | solution.py:49
  134.0 15.2 %collective-permute-start.22 = (bf16[192,1536]{1,0:T(8,128)(2,1)S(1)}, bf16[192,1536]{1,0:T(8,128)(2,1)S(1)}, u32[]{:S(2)}, u32[]{:S(2)}) collective-permute-start(bf16[192,1536]{1,0:T(8,128)(2,1)S(1)} %bitcast.172), channel_id=1, source_target_pairs={{0,8},{4,12},{8,0},{12,4},{16,24},{20,28},{24,16},{28,20},{1,9},{5... | collective-permute-start | bytes 1769480 | tf_op jit(solution)/shard_map/ppermute | solution.py:49
  135.6 13.7 %collective-permute-start.23 = (bf16[192,1536]{1,0:T(8,128)(2,1)S(1)}, bf16[192,1536]{1,0:T(8,128)(2,1)S(1)}, u32[]{:S(2)}, u32[]{:S(2)}) collective-permute-start(bf16[192,1536]{1,0:T(8,128)(2,1)S(1)} %bitcast.173), channel_id=1, source_target_pairs={{0,16},{4,20},{8,24},{12,28},{16,0},{20,4},{24,8},{28,12},{1,17},{... | collective-permute-start | bytes 1769480 | tf_op jit(solution)/shard_map/ppermute | solution.py:49
  149.2 7.7 %collective-permute-start.25 = (bf16[96,1536]{1,0:T(8,128)(2,1)S(1)}, bf16[96,1536]{1,0:T(8,128)(2,1)S(1)}, u32[]{:S(2)}, u32[]{:S(2)}) collective-permute-start(bf16[96,1536]{1,0:T(8,128)(2,1)S(1)} %slice.284), channel_id=1, source_target_pairs={{0,8},{4,12},{8,0},{12,4},{16,24},{20,28},{24,16},{28,20},{1,9},{5... | collective-permute-start | bytes 884744 | tf_op jit(solution)/shard_map/ppermute | solution.py:49
  150.8 7.1 %collective-permute-start.24 = (bf16[96,1536]{1,0:T(8,128)(2,1)S(1)}, bf16[96,1536]{1,0:T(8,128)(2,1)S(1)}, u32[]{:S(2)}, u32[]{:S(2)}) collective-permute-start(bf16[96,1536]{1,0:T(8,128)(2,1)S(1)} %slice.283), channel_id=1, source_target_pairs={{0,16},{4,20},{8,24},{12,28},{16,0},{20,4},{24,8},{28,12},{1,17},{... | collective-permute-start | bytes 884744 | tf_op jit(solution)/shard_map/ppermute | solution.py:49
  151.4 9.7 %collective-permute-start.21 = (bf16[512,384]{1,0:T(8,128)(2,1)S(1)}, bf16[512,384]{1,0:T(8,128)(2,1)S(1)}, u32[]{:S(2)}, u32[]{:S(2)}) collective-permute-start(bf16[512,384]{1,0:T(8,128)(2,1)S(1)} %get-tuple-element.100.refs_2_.refs_6_), channel_id=1, source_target_pairs={{0,3},{1,0},{2,1},{3,2},{4,7},{5,4},{6,5},{7,6},{8,11},{9,8},{10,9... | collective-permute-start | bytes 1179656 | tf_op jit(solution)/shard_map/ppermute | solution.py:49
  161.9 4.7 %collective-permute-start.26 = (bf16[4,192,1536]{2,1,0:T(8,128)(2,1)}, bf16[4,192,1536]{2,1,0:T(8,128)(2,1)S(1)}, u32[]{:S(2)}, u32[]{:S(2)}) collective-permute-start(bf16[4,192,1536]{2,1,0:T(8,128)(2,1)} %tie.45), channel_id=1, source_target_pairs={{0,4},{4,0},{8,12},{12,8},{16,20},{20,16},{24,28},{28,24},{1,5},{5... | collective-permute-start | bytes 7077896 | tf_op jit(solution)/shard_map/ppermute | solution.py:49
  198.3 18.8 %collective-permute-start.29 = (bf16[512,2304]{1,0:T(8,128)(2,1)}, bf16[512,2304]{1,0:T(8,128)(2,1)S(1)}, u32[]{:S(2)}, u32[]{:S(2)}) collective-permute-start(bf16[512,2304]{1,0:T(8,128)(2,1)} %get-tuple-element.109.middle_ref.refs_2_), channel_id=1, source_target_pairs={{0,4},{4,0},{8,12},{12,8},{16,20},{20,16},{24,28},{28,24},{1,5},{5... | collective-permute-start | bytes 7077896 | tf_op jit(solution)/shard_map/ppermute | solution.py:49
  198.7 18.4 %collective-permute-start.28 = (bf16[512,1536]{1,0:T(8,128)(2,1)}, bf16[512,1536]{1,0:T(8,128)(2,1)}, u32[]{:S(2)}, u32[]{:S(2)}) collective-permute-start(bf16[512,1536]{1,0:T(8,128)(2,1)} %get-tuple-element.112.refs_0_), channel_id=1, source_target_pairs={{0,4},{4,0},{8,12},{12,8},{16,20},{20,16},{24,28},{28,24},{1,5},{5... | collective-permute-start | bytes 4718600 | tf_op jit(solution)/shard_map/ppermute | solution.py:49
  199.0 17.3 %collective-permute-start.27 = (bf16[128,1536]{1,0:T(8,128)(2,1)}, bf16[128,1536]{1,0:T(8,128)(2,1)S(1)}, u32[]{:S(2)}, u32[]{:S(2)}) collective-permute-start(bf16[128,1536]{1,0:T(8,128)(2,1)} %get-tuple-element.111), channel_id=1, source_target_pairs={{0,3},{1,0},{2,1},{3,2},{4,7},{5,4},{6,5},{7,6},{8,11},{9,8},{10,9... | collective-permute-start | bytes 1179656 | tf_op jit(solution)/shard_map/ppermute | solution.py:49
  203.4 40.5 %collective-permute-start.31 = (bf16[128,1536]{1,0:T(8,128)(2,1)}, bf16[128,1536]{1,0:T(8,128)(2,1)}, u32[]{:S(2)}, u32[]{:S(2)}) collective-permute-start(bf16[128,1536]{1,0:T(8,128)(2,1)} %get-tuple-element.116), channel_id=1, source_target_pairs={{0,1},{1,2},{2,3},{3,0},{4,5},{5,6},{6,7},{7,4},{8,9},{9,10},{10,1... | collective-permute-start | bytes 1179656 | tf_op jit(solution)/shard_map/ppermute | solution.py:49
  218.7 25.2 %collective-permute-start.30 = (bf16[128,1536]{1,0:T(8,128)(2,1)S(1)}, bf16[128,1536]{1,0:T(8,128)(2,1)S(1)}, u32[]{:S(2)}, u32[]{:S(2)}) collective-permute-start(bf16[128,1536]{1,0:T(8,128)(2,1)S(1)} %payload.3.refs_0_.refs_4_), channel_id=1, source_target_pairs={{0,3},{1,0},{2,1},{3,2},{4,7},{5,4},{6,5},{7,6},{8,11},{9,8},{10,9... | collective-permute-start | bytes 1179656 | tf_op jit(solution)/shard_map/ppermute | solution.py:49
  250.6 5.2 %collective-permute-start.32 = (bf16[128,384]{1,0:T(8,128)(2,1)}, bf16[128,384]{1,0:T(8,128)(2,1)S(1)}, u32[]{:S(2)}, u32[]{:S(2)}) collective-permute-start(bf16[128,384]{1,0:T(8,128)(2,1)} %get-tuple-element.119), channel_id=1, source_target_pairs={{0,3},{1,0},{2,1},{3,2},{4,7},{5,4},{6,5},{7,6},{8,11},{9,8},{10,9... | collective-permute-start | bytes 294920 | tf_op jit(solution)/shard_map/ppermute | solution.py:49
  250.6 9.3 %collective-permute-start.33 = (bf16[128,384]{1,0:T(8,128)(2,1)}, bf16[128,384]{1,0:T(8,128)(2,1)S(1)}, u32[]{:S(2)}, u32[]{:S(2)}) collective-permute-start(bf16[128,384]{1,0:T(8,128)(2,1)} %get-tuple-element.120), channel_id=1, source_target_pairs={{0,2},{1,3},{2,0},{3,1},{4,6},{5,7},{6,4},{7,5},{8,10},{9,11},{10,... | collective-permute-start | bytes 294920 | tf_op jit(solution)/shard_map/ppermute | solution.py:49
  250.7 9.2 %collective-permute-start.34 = (bf16[128,384]{1,0:T(8,128)(2,1)}, bf16[128,384]{1,0:T(8,128)(2,1)S(1)}, u32[]{:S(2)}, u32[]{:S(2)}) collective-permute-start(bf16[128,384]{1,0:T(8,128)(2,1)} %get-tuple-element.121), channel_id=1, source_target_pairs={{0,1},{1,2},{2,3},{3,0},{4,5},{5,6},{6,7},{7,4},{8,9},{9,10},{10,1... | collective-permute-start | bytes 294920 | tf_op jit(solution)/shard_map/ppermute | solution.py:49
  252.7 40.9 %collective-permute-start.41 = (bf16[2,192,1152]{2,1,0:T(8,128)(2,1)}, bf16[2,192,1152]{2,1,0:T(8,128)(2,1)S(1)}, u32[]{:S(2)}, u32[]{:S(2)}) collective-permute-start(bf16[2,192,1152]{2,1,0:T(8,128)(2,1)} %bitcast.21), channel_id=1, source_target_pairs={{0,16},{4,20},{8,24},{12,28},{16,0},{20,4},{24,8},{28,12},{1,17},{... | collective-permute-start | bytes 2654216 | tf_op jit(solution)/shard_map/ppermute | solution.py:49
  253.7 40.6 %collective-permute-start.42 = (bf16[2,192,1152]{2,1,0:T(8,128)(2,1)}, bf16[2,192,1152]{2,1,0:T(8,128)(2,1)S(1)}, u32[]{:S(2)}, u32[]{:S(2)}) collective-permute-start(bf16[2,192,1152]{2,1,0:T(8,128)(2,1)} %bitcast.183), channel_id=1, source_target_pairs={{0,8},{4,12},{8,0},{12,4},{16,24},{20,28},{24,16},{28,20},{1,9},{5... | collective-permute-start | bytes 2654216 | tf_op jit(solution)/shard_map/ppermute | solution.py:49
  259.9 21.1 %collective-permute-start.35 = (bf16[128,1536]{1,0:T(8,128)(2,1)S(1)}, bf16[128,1536]{1,0:T(8,128)(2,1)S(1)}, u32[]{:S(2)}, u32[]{:S(2)}) collective-permute-start(bf16[128,1536]{1,0:T(8,128)(2,1)S(1)} %tie.46), channel_id=1, source_target_pairs={{0,3},{1,0},{2,1},{3,2},{4,7},{5,4},{6,5},{7,6},{8,11},{9,8},{10,9... | collective-permute-start | bytes 1179656 | tf_op jit(solution)/shard_map/ppermute | solution.py:49
  261.5 20.6 %collective-permute-start.36 = (bf16[128,1536]{1,0:T(8,128)(2,1)S(1)}, bf16[128,1536]{1,0:T(8,128)(2,1)S(1)}, u32[]{:S(2)}, u32[]{:S(2)}) collective-permute-start(bf16[128,1536]{1,0:T(8,128)(2,1)S(1)} %tie.46), channel_id=1, source_target_pairs={{0,1},{1,2},{2,3},{3,0},{4,5},{5,6},{6,7},{7,4},{8,9},{9,10},{10,1... | collective-permute-start | bytes 1179656 | tf_op jit(solution)/shard_map/ppermute | solution.py:49
  262.0 51.2 %collective-permute-start.38 = (bf16[128,1536]{1,0:T(8,128)(2,1)S(1)}, bf16[128,1536]{1,0:T(8,128)(2,1)}, u32[]{:S(2)}, u32[]{:S(2)}) collective-permute-start(bf16[128,1536]{1,0:T(8,128)(2,1)S(1)} %tie.49), channel_id=1, source_target_pairs={{0,1},{1,2},{2,3},{3,0},{4,5},{5,6},{6,7},{7,4},{8,9},{9,10},{10,1... | collective-permute-start | bytes 1179656 | tf_op jit(solution)/shard_map/ppermute | solution.py:49
  284.3 10.0 %collective-permute-start.40 = (bf16[4,2,2,256,128]{4,3,2,1,0:T(8,128)(2,1)}, bf16[4,2,2,256,128]{4,3,2,1,0:T(8,128)(2,1)S(1)}, u32[]{:S(2)}, u32[]{:S(2)}) collective-permute-start(bf16[4,2,2,256,128]{4,3,2,1,0:T(8,128)(2,1)} %copy-done.13), channel_id=1, source_target_pairs={{0,4},{4,0},{8,12},{12,8},{16,20},{20,16},{24,28},{28,24},{1,5},{5... | collective-permute-start | bytes 3145736 | tf_op jit(solution)/shard_map/ppermute | solution.py:49
  285.0 21.6 %collective-permute-start.37 = (bf16[256,1536]{1,0:T(8,128)(2,1)S(1)}, bf16[256,1536]{1,0:T(8,128)(2,1)S(1)}, u32[]{:S(2)}, u32[]{:S(2)}) collective-permute-start(bf16[256,1536]{1,0:T(8,128)(2,1)S(1)} %pad_maximum_fusion.5), channel_id=1, source_target_pairs={{0,3},{1,0},{2,1},{3,2},{4,7},{5,4},{6,5},{7,6},{8,11},{9,8},{10,9... | collective-permute-start | bytes 2359304 | tf_op jit(solution)/shard_map/ppermute | solution.py:49
  296.0 13.5 %collective-permute-start.45 = (bf16[2,2,256,128]{3,2,1,0:T(8,128)(2,1)S(1)}, bf16[2,2,256,128]{3,2,1,0:T(8,128)(2,1)S(1)}, u32[]{:S(2)}, u32[]{:S(2)}) collective-permute-start(bf16[2,2,256,128]{3,2,1,0:T(8,128)(2,1)S(1)} %pad_maximum_fusion.9), channel_id=1, source_target_pairs={{0,16},{4,20},{8,24},{12,28},{16,0},{20,4},{24,8},{28,12},{1,17},{... | collective-permute-start | bytes 786440 | tf_op jit(solution)/shard_map/ppermute | solution.py:49
  297.4 13.8 %collective-permute-start.43 = (bf16[2,2,256,128]{3,2,1,0:T(8,128)(2,1)S(1)}, bf16[2,2,256,128]{3,2,1,0:T(8,128)(2,1)S(1)}, u32[]{:S(2)}, u32[]{:S(2)}) collective-permute-start(bf16[2,2,256,128]{3,2,1,0:T(8,128)(2,1)S(1)} %pad_maximum_fusion.8), channel_id=1, source_target_pairs={{0,8},{4,12},{8,0},{12,4},{16,24},{20,28},{24,16},{28,20},{1,9},{5... | collective-permute-start | bytes 786440 | tf_op jit(solution)/shard_map/ppermute | solution.py:49
  311.3 5.0 %collective-permute-start.44 = (bf16[1,2,256,128]{3,2,1,0:T(8,128)(2,1)S(1)}, bf16[1,2,256,128]{3,2,1,0:T(8,128)(2,1)S(1)}, u32[]{:S(2)}, u32[]{:S(2)}) collective-permute-start(bf16[1,2,256,128]{3,2,1,0:T(8,128)(2,1)S(1)} %get-tuple-element.160), channel_id=1, source_target_pairs={{0,16},{4,20},{8,24},{12,28},{16,0},{20,4},{24,8},{28,12},{1,17},{... | collective-permute-start | bytes 393224 | tf_op jit(solution)/shard_map/ppermute | solution.py:49
  311.8 5.0 %collective-permute-start.46 = (bf16[1,2,256,128]{3,2,1,0:T(8,128)(2,1)S(1)}, bf16[1,2,256,128]{3,2,1,0:T(8,128)(2,1)S(1)}, u32[]{:S(2)}, u32[]{:S(2)}) collective-permute-start(bf16[1,2,256,128]{3,2,1,0:T(8,128)(2,1)S(1)} %get-tuple-element.159), channel_id=1, source_target_pairs={{0,8},{4,12},{8,0},{12,4},{16,24},{20,28},{24,16},{28,20},{1,9},{5... | collective-permute-start | bytes 393224 | tf_op jit(solution)/shard_map/ppermute | solution.py:49
  313.3 11.7 %collective-permute-start.39 = (bf16[128,1536]{1,0:T(8,128)(2,1)S(1)}, bf16[128,1536]{1,0:T(8,128)(2,1)S(1)}, u32[]{:S(2)}, u32[]{:S(2)}) collective-permute-start(bf16[128,1536]{1,0:T(8,128)(2,1)S(1)} %payload.4), channel_id=1, source_target_pairs={{0,3},{1,0},{2,1},{3,2},{4,7},{5,4},{6,5},{7,6},{8,11},{9,8},{10,9... | collective-permute-start | bytes 1179656 | tf_op jit(solution)/shard_map/ppermute | solution.py:49
  316.9 7.2 %collective-permute-start.47 = (bf16[2,256,128]{2,1,0:T(8,128)(2,1)S(1)}, bf16[2,256,128]{2,1,0:T(8,128)(2,1)S(1)}, u32[]{:S(2)}, u32[]{:S(2)}) collective-permute-start(bf16[2,256,128]{2,1,0:T(8,128)(2,1)S(1)} %select_convert_fusion.refs_1_), channel_id=1, source_target_pairs={{0,1},{1,0},{2,3},{3,2},{4,5},{5,4},{6,7},{7,6},{8,9},{9,8},{10,11... | collective-permute-start | bytes 393224 | tf_op jit(solution)/shard_map/ppermute | solution.py:49
  319.0 17.3 %collective-permute-start.48 = (bf16[1,192,1152]{2,1,0:T(8,128)(2,1)S(1)}, bf16[1,192,1152]{2,1,0:T(8,128)(2,1)S(1)}, u32[]{:S(2)}, u32[]{:S(2)}) collective-permute-start(bf16[1,192,1152]{2,1,0:T(8,128)(2,1)S(1)} %fusion.11), channel_id=1, source_target_pairs={{0,8},{4,12},{8,0},{12,4},{16,24},{20,28},{24,16},{28,20},{1,9},{5... | collective-permute-start | bytes 1327112 | tf_op jit(solution)/shard_map/ppermute | solution.py:49
  320.2 18.8 %collective-permute-start.49 = (bf16[1,192,1152]{2,1,0:T(8,128)(2,1)S(1)}, bf16[1,192,1152]{2,1,0:T(8,128)(2,1)S(1)}, u32[]{:S(2)}, u32[]{:S(2)}) collective-permute-start(bf16[1,192,1152]{2,1,0:T(8,128)(2,1)S(1)} %fusion.10), channel_id=1, source_target_pairs={{0,16},{4,20},{8,24},{12,28},{16,0},{20,4},{24,8},{28,12},{1,17},{... | collective-permute-start | bytes 1327112 | tf_op jit(solution)/shard_map/ppermute | solution.py:49
  334.7 10.1 %collective-permute-start.51 = (bf16[4,208,896]{2,1,0:T(8,128)(2,1)}, bf16[4,208,896]{2,1,0:T(8,128)(2,1)S(1)}, u32[]{:S(2)}, u32[]{:S(2)}) collective-permute-start(bf16[4,208,896]{2,1,0:T(8,128)(2,1)} %get-tuple-element.149), channel_id=1, source_target_pairs={{0,4},{4,0},{8,12},{12,8},{16,20},{20,16},{24,28},{28,24},{1,5},{5... | collective-permute-start | bytes 4472840 | tf_op jit(solution)/shard_map/ppermute | solution.py:49
  339.0 13.6 %collective-permute-start.52 = (bf16[128,1536]{1,0:T(8,128)(2,1)S(1)}, bf16[128,1536]{1,0:T(8,128)(2,1)S(1)}, u32[]{:S(2)}, u32[]{:S(2)}) collective-permute-start(bf16[128,1536]{1,0:T(8,128)(2,1)S(1)} %get-tuple-element.150), channel_id=1, source_target_pairs={{0,1},{1,2},{2,3},{3,0},{4,5},{5,6},{6,7},{7,4},{8,9},{9,10},{10,1... | collective-permute-start | bytes 1179656 | tf_op jit(solution)/shard_map/ppermute | solution.py:49
  339.8 16.6 %collective-permute-start.50 = (bf16[128,1536]{1,0:T(8,128)(2,1)S(1)}, bf16[128,1536]{1,0:T(8,128)(2,1)S(1)}, u32[]{:S(2)}, u32[]{:S(2)}) collective-permute-start(bf16[128,1536]{1,0:T(8,128)(2,1)S(1)} %get-tuple-element.148), channel_id=1, source_target_pairs={{0,3},{1,0},{2,1},{3,2},{4,7},{5,4},{6,5},{7,6},{8,11},{9,8},{10,9... | collective-permute-start | bytes 1179656 | tf_op jit(solution)/shard_map/ppermute | solution.py:49
  356.5 14.9 %collective-permute-start.53 = (bf16[128,1536]{1,0:T(8,128)(2,1)S(1)}, bf16[128,1536]{1,0:T(8,128)(2,1)S(1)}, u32[]{:S(2)}, u32[]{:S(2)}) collective-permute-start(bf16[128,1536]{1,0:T(8,128)(2,1)S(1)} %payload.5.refs_1_), channel_id=1, source_target_pairs={{0,3},{1,0},{2,1},{3,2},{4,7},{5,4},{6,5},{7,6},{8,11},{9,8},{10,9... | collective-permute-start | bytes 1179656 | tf_op jit(solution)/shard_map/ppermute | solution.py:49
  358.7 10.3 %collective-permute-start.54 = (bf16[2,208,512]{2,1,0:T(8,128)(2,1)S(1)}, bf16[2,208,512]{2,1,0:T(8,128)(2,1)S(1)}, u32[]{:S(2)}, u32[]{:S(2)}) collective-permute-start(bf16[2,208,512]{2,1,0:T(8,128)(2,1)S(1)} %add_convert_fusion), channel_id=1, source_target_pairs={{0,16},{4,20},{8,24},{12,28},{16,0},{20,4},{24,8},{28,12},{1,17},{... | collective-permute-start | bytes 1277960 | tf_op jit(solution)/shard_map/ppermute | solution.py:49
  360.3 7.0 %collective-permute-start.55 = (bf16[2,192,384]{2,1,0:T(8,128)(2,1)S(1)}, bf16[2,192,384]{2,1,0:T(8,128)(2,1)S(1)}, u32[]{:S(2)}, u32[]{:S(2)}) collective-permute-start(bf16[2,192,384]{2,1,0:T(8,128)(2,1)S(1)} %add_convert_fusion.2), channel_id=1, source_target_pairs={{0,8},{4,12},{8,0},{12,4},{16,24},{20,28},{24,16},{28,20},{1,9},{5... | collective-permute-start | bytes 884744 | tf_op jit(solution)/shard_map/ppermute | solution.py:49
  369.1 7.9 %collective-permute-start.56 = (bf16[1,208,512]{2,1,0:T(8,128)(2,1)S(1)}, bf16[1,208,512]{2,1,0:T(8,128)(2,1)S(1)}, u32[]{:S(2)}, u32[]{:S(2)}) collective-permute-start(bf16[1,208,512]{2,1,0:T(8,128)(2,1)S(1)} %add_convert_fusion.4), channel_id=1, source_target_pairs={{0,8},{4,12},{8,0},{12,4},{16,24},{20,28},{24,16},{28,20},{1,9},{5... | collective-permute-start | bytes 638984 | tf_op jit(solution)/shard_map/ppermute | solution.py:49
  371.0 5.2 %collective-permute-start.60 = (bf16[1,192,384]{2,1,0:T(8,128)(2,1)S(1)}, bf16[1,192,384]{2,1,0:T(8,128)(2,1)S(1)}, u32[]{:S(2)}, u32[]{:S(2)}) collective-permute-start(bf16[1,192,384]{2,1,0:T(8,128)(2,1)S(1)} %add_convert_fusion.5), channel_id=1, source_target_pairs={{0,16},{4,20},{8,24},{12,28},{16,0},{20,4},{24,8},{28,12},{1,17},{... | collective-permute-start | bytes 442376 | tf_op jit(solution)/shard_map/ppermute | solution.py:49
  378.8 6.6 %collective-permute-start.59 = (bf16[64,512]{1,0:T(8,128)(2,1)S(1)}, bf16[64,512]{1,0:T(8,128)(2,1)S(1)}, u32[]{:S(2)}, u32[]{:S(2)}) collective-permute-start(bf16[64,512]{1,0:T(8,128)(2,1)S(1)} %tie.63), channel_id=1, source_target_pairs={{0,1},{1,2},{2,3},{3,0},{4,5},{5,6},{6,7},{7,4},{8,9},{9,10},{10,1... | collective-permute-start | bytes 196616 | tf_op jit(solution)/shard_map/ppermute | solution.py:49
  380.3 6.0 %collective-permute-start.58 = (bf16[64,512]{1,0:T(8,128)(2,1)S(1)}, bf16[64,512]{1,0:T(8,128)(2,1)S(1)}, u32[]{:S(2)}, u32[]{:S(2)}) collective-permute-start(bf16[64,512]{1,0:T(8,128)(2,1)S(1)} %tie.62), channel_id=1, source_target_pairs={{0,2},{1,3},{2,0},{3,1},{4,6},{5,7},{6,4},{7,5},{8,10},{9,11},{10,... | collective-permute-start | bytes 196616 | tf_op jit(solution)/shard_map/ppermute | solution.py:49
  381.1 5.2 %collective-permute-start.57 = (bf16[64,512]{1,0:T(8,128)(2,1)S(1)}, bf16[64,512]{1,0:T(8,128)(2,1)S(1)}, u32[]{:S(2)}, u32[]{:S(2)}) collective-permute-start(bf16[64,512]{1,0:T(8,128)(2,1)S(1)} %tie.61), channel_id=1, source_target_pairs={{0,3},{1,0},{2,1},{3,2},{4,7},{5,4},{6,5},{7,6},{8,11},{9,8},{10,9... | collective-permute-start | bytes 196616 | tf_op jit(solution)/shard_map/ppermute | solution.py:49
  (75 other events, 323.7 us)
Sparse Core Ops, SparseCore 0:
  10.4 130.1 all-gather.1
  217.2 133.2 reduce-scatter.1
